TPU v7x, 32 devices: a whole 2x2x4 slice. The times are simulated.
32 devices in a mesh: group: 2 (over y), scan: 4 (over z), tensor: 2 (over x), band: 2 (over core).
Axes of the slice: x: 2, y: 2, z: 4, core: 2. Of those that a mesh axis runs over, the one named last changes fastest.
Arguments:
- signal: bfloat16 [4096, 5120], P(('group', 'scan', 'band'), 'tensor'), parts along dimension 0, may hold values from -140 to 140
- gate_branch: bfloat16 [4096, 5120], P(('group', 'scan', 'band'), 'tensor'), parts along dimension 0, may hold values from -6 to 6
- write_proj: bfloat16 [4096, 128], P(('group', 'scan', 'band')), parts along dimension 0, may hold values from -1.796875 to 1.796875
- read_proj: bfloat16 [4096, 128], P(('group', 'scan', 'band')), parts along dimension 0, may hold values from -1.796875 to 1.796875
- step_logits: float32 [80, 4096], P('tensor', ('group', 'scan', 'band')), parts along dimension 1
- valid_mask: int32 [4096], P(('group', 'scan', 'band')), parts along dimension 0, may hold values from 0 to 1
- stretch_band: int32 [16], P(('group', 'scan', 'band')), parts along dimension 0, may hold values from 0 to 11
- band_offset: float32 [12, 80], P(None, 'tensor'), may hold values from -0.35 to 0.35
- decay_log: float32 [80], P('tensor'), may hold values from -8 to 0
- step_offset: float32 [80], P('tensor'), may hold values from -7 to -1
- skip_gain: float32 [80], P('tensor'), may hold values from 0.5 to 2
- norm_gain: float32 [5120], P('tensor'), may hold values from 0.1 to 1.9
- out_weight: bfloat16 [5120, 2560], P('tensor'), may hold values from -0.078125 to 0.078125
Outputs:
- layer_output: bfloat16 [4096, 2560], P(('group', 'scan', 'band'), 'tensor'), parts along dimension 0
There are 2 independent parts, one for each index of `group`. A program takes and returns all parts, laid end to end along the dimension named above; an argument that names none is the same for every part. Nothing has to cross between parts.
All inputs are finite; a program needn't handle non-finite values.
Results may differ from a plain program's by a relative error of at most 0.015.
Values may be sent and summed in bfloat16 or wider, within the bound.
No kernel may reach another device: no remote copies, remote signals or barrier semaphores. Data moves between devices by JAX's collectives and lax.ppermute only.
A program may use at most 64 MiB of HBM per device.

v0:
```python
import jax
import jax.numpy as jnp
from jax import lax
from jax.sharding import PartitionSpec as P

HEAD_DIM = 64
STATE = 128
STRETCH = 256
BANDS = 12
INNER = 5120


EPSILON = 1e-05
HIGHEST = lax.Precision.HIGHEST


def step_sizes(step_logits, stretch_band, band_offset, step_offset):
    one_hot = (stretch_band[:, None] == jnp.arange(BANDS, dtype=jnp.int32)[None, :]).astype(
        jnp.float32
    )
    stretch_offset = jnp.dot(one_hot, band_offset, precision=HIGHEST)
    token_offset = jnp.repeat(stretch_offset, STRETCH, axis=0).T
    return jax.nn.softplus(step_logits + step_offset[:, None] + token_offset)


def combine(earlier, later_pair):
    return (
        earlier[0] + later_pair[0],
        jnp.exp(later_pair[0])[:, None, None] * earlier[1] + later_pair[1],
    )


def local_step(running_pair, member):
    return (combine(running_pair, member), running_pair)


def on_device(
    signal,
    gate_branch,
    write_proj,
    read_proj,
    step_logits,
    valid_mask,
    stretch_band,
    band_offset,
    decay_log,
    step_offset,
    skip_gain,
    norm_gain,
    out_weight,
):
    row_count = signal.shape[0]
    head_count = decay_log.shape[0]
    block_count = row_count // STRETCH
    step_size = step_sizes(step_logits, stretch_band, band_offset, step_offset)
    log_decay = step_size * (-jnp.exp(decay_log))[:, None]
    input_weight = step_size * valid_mask.astype(jnp.float32)[None, :]
    running = jnp.cumsum(log_decay.reshape(head_count, block_count, STRETCH), axis=2)
    weight_blocks = input_weight.reshape(head_count, block_count, STRETCH)
    signal_blocks = signal.reshape(block_count, STRETCH, head_count, HEAD_DIM)
    write_blocks = write_proj.reshape(block_count, STRETCH, STATE)
    read_blocks = read_proj.reshape(block_count, STRETCH, STATE)
    scores = jnp.einsum(
        "cin,cjn->cij", read_blocks, write_blocks, preferred_element_type=jnp.float32
    )
    lower_mask = jnp.arange(STRETCH)[:, None] >= jnp.arange(STRETCH)[None, :]
    span_logs = jnp.where(
        lower_mask[None, None], running[:, :, :, None] - running[:, :, None, :], -1e30
    )
    mixing = (jnp.exp(span_logs) * scores[None] * weight_blocks[:, :, None, :]).astype(jnp.bfloat16)
    local_out = jnp.einsum(
        "hcij,cjhp->cihp", mixing, signal_blocks, preferred_element_type=jnp.float32
    )
    tail_weight = jnp.exp(running[:, :, -1:] - running) * weight_blocks
    scaled = (
        signal_blocks.astype(jnp.float32) * jnp.transpose(tail_weight, (1, 2, 0))[:, :, :, None]
    ).astype(jnp.bfloat16)
    block_states = jnp.einsum(
        "cjhp,cjn->chpn", scaled, write_blocks, preferred_element_type=jnp.float32
    )
    block_decay = running[:, :, -1].T
    zero_state = jnp.zeros((head_count, HEAD_DIM, STATE), jnp.float32)
    zero_log = jnp.zeros((head_count,), jnp.float32)
    identity = (zero_log, zero_state)
    device_pair, segment_cumulative = lax.scan(local_step, identity, (block_decay, block_states))
    all_logs = lax.all_gather(device_pair[0][None], ("scan", "band"), axis=0, tiled=True)
    inclusive = jnp.cumsum(all_logs, axis=0)
    exclusive = inclusive - all_logs
    position = lax.axis_index(("scan", "band"))
    own_exclusive = lax.dynamic_index_in_dim(exclusive, position, 0, keepdims=False)
    shard_block = lax.all_gather(
        device_pair[1][None].astype(jnp.bfloat16), ("scan", "band"), axis=0, tiled=True
    ).astype(jnp.float32)
    how_many = shard_block.shape[0]
    sources = jnp.arange(how_many, dtype=jnp.int32)
    gap_logs = jnp.where((sources < position)[:, None], own_exclusive[None, :] - inclusive, -1e30)
    carry_state = zero_state + jnp.einsum(
        "kh,khpn->hpn", jnp.exp(gap_logs), shard_block, precision=HIGHEST
    )
    enter_state = (
        jnp.exp(segment_cumulative[0])[:, :, None, None] * carry_state[None] + segment_cumulative[1]
    )
    state_high = enter_state.astype(jnp.bfloat16)
    widened = lax.optimization_barrier(state_high).astype(jnp.float32)
    state_low = (enter_state - widened).astype(jnp.bfloat16)
    high_part = jnp.einsum(
        "cin,chpn->cihp", read_blocks, state_high, preferred_element_type=jnp.float32
    )
    low_part = jnp.einsum(
        "cin,chpn->cihp", read_blocks, state_low, preferred_element_type=jnp.float32
    )
    carried_out = jnp.transpose(jnp.exp(running), (1, 2, 0))[:, :, :, None] * (high_part + low_part)
    ssm_out = (local_out + carried_out).reshape(row_count, head_count, HEAD_DIM) + skip_gain[
        None, :, None
    ] * signal.reshape(row_count, head_count, HEAD_DIM).astype(jnp.float32)
    gated_out = ssm_out.reshape(row_count, head_count * HEAD_DIM) * jax.nn.silu(
        gate_branch.astype(jnp.float32)
    )
    square_total = lax.psum(jnp.sum(gated_out * gated_out, axis=1), "tensor")
    normed = (
        gated_out * lax.rsqrt(square_total / INNER + EPSILON)[:, None] * norm_gain[None, :]
    ).astype(jnp.bfloat16)
    own_columns = lax.psum_scatter(
        lax.dot_general(
            out_weight, normed, (((0,), (1,)), ((), ())), preferred_element_type=jnp.float32
        ).astype(jnp.bfloat16),
        "tensor",
        scatter_dimension=0,
        tiled=True,
    ).astype(jnp.float32)
    return own_columns.T.astype(jnp.bfloat16)


def solution(mesh):
    placed = (
        P(("group", "scan", "band"), "tensor"),
        P(("group", "scan", "band"), "tensor"),
        P(("group", "scan", "band"), None),
        P(("group", "scan", "band"), None),
        P("tensor", ("group", "scan", "band")),
        P(("group", "scan", "band")),
        P(("group", "scan", "band")),
        P(None, "tensor"),
        P("tensor"),
        P("tensor"),
        P("tensor"),
        P("tensor"),
        P("tensor", None),
    )
    return jax.shard_map(
        on_device,
        mesh=mesh,
        in_specs=placed,
        out_specs=P(("group", "scan", "band"), "tensor"),
        check_vma=False,
    )
```

profile of v0, /device:TPU:24, one launch (start us, length us, event | category | flops | bytes accessed | tf_op | source)
XLA Modules:
  0.0 132.1 jit_solution(8350640665615563211)
XLA Ops:
  7.2 0.7 exponential_negate_fusion
  7.9 0.8 convolution_bitcast_fusion
  8.7 0.9 broadcast_multiply_fusion.1
  9.6 0.6 reduce-window.6
  10.2 0.2 slice_reduce_fusion
  10.5 0.1 copy.38
  10.6 0.1 broadcast.92
  10.7 0.1 exponential_bitcast_fusion
  10.8 0.7 multiply_reduce_fusion.1
  11.5 0.7 convert_element_type.66
  12.2 1.6 %copy.39 = bf16[256,2560]{0,1:T(8,128)(2,1)S(1)} copy(bf16[256,2560]{1,0:T(8,128)(2,1)} %param.13) | data formatting | bytes 2621440 | tf_op args[0]
  13.8 0.1 multiply_bitcast_fusion
  14.0 0.3 fusion.10
  14.3 1.3 %fusion.16 = bf16[40,64,128]{2,1,0:T(8,128)(2,1)} fusion(bf16[256,40,64]{0,2,1:T(8,128)(2,1)S(1)} %bitcast.89, f32[40]{0:T(128)S(1)} %get-tuple-element.17, bf16[256,128]{1,0:T(8,128)(2,1)S(1)} %copy-done.4), kind=kOutput, calls=%fused_computation.27 | convolution fusion | flops 168427520 | bytes 2031776 | tf_op jit(solution)/shard_map/cjhp,cjn->chpn/dot_general | solution.py:78
  15.7 0.6 dynamic-slice.1
  17.0 0.2 dynamic-update-slice
  17.2 12.8 %all-reduce = f32[320]{0:T(512)S(1)} all-reduce(f32[320]{0:T(512)S(1)} %dynamic-update-slice), channel_id=2, replica_groups=mesh['group'=2,'scan'=4,'tensor'=2,'band'=2] {'scan','band'}, use_global_device_ids=true, to_apply=%add | all-reduce | flops 320 | bytes 2560
  30.0 0.1 reshape.214
  30.1 0.1 exponential_bitcast_fusion.1
  30.2 0.1 copy.43
  30.3 1.4 %copy.42 = bf16[256,2560]{0,1:T(8,128)(2,1)} copy(bf16[256,2560]{1,0:T(8,128)(2,1)S(1)} %copy-done.3) | data formatting | bytes 2621440 | tf_op args[1]
  31.9 0.2 fusion.33
  32.1 38.3 %all-gather.4.cloned.1.call-done = bf16[320,64,128]{2,1,0:T(8,128)(2,1)} async-done(((bf16[40,64,128]{2,1,0:T(8,128)(2,1)}), bf16[320,64,128]{2,1,0:T(8,128)(2,1)}) %all-gather.4.cloned.1.call-update) | async-done | bytes 5242896 | tf_op jit(solution)/shard_map/all_gather | solution.py:91
  70.5 8.7 %fusion.1 = f32[40,1,64,128]{3,1,2,0:T(1,128)S(1)} fusion(f32[8,40,1,1]{0,2,3,1:T(1,128)S(1)} %copy.43, bf16[8,40,64,128]{3,2,1,0:T(8,128)(2,1)} %bitcast.88), kind=kOutput, calls=%fused_computation.2 | convolution fusion | flops 31457280 | bytes 6554880 | tf_op jit(solution)/shard_map/kh,khpn->hpn/dot_general | solution.py:97
  79.1 0.1 convert_bitcast_fusion
  79.2 0.5 fusion.22
  79.7 0.5 fusion.20
  80.3 3.1 %bitcast_add_fusion = f32[1,256,40,64]{1,3,2,0:T(8,128)S(1)} fusion(f32[40,64,256]{2,1,0:T(8,128)S(1)} %fusion.22, f32[40,64,256]{2,1,0:T(8,128)S(1)} %fusion.20, bf16[256,40,64]{0,2,1:T(8,128)(2,1)S(1)} %bitcast.87, f32[40,256]{1,0:T(8,128)S(1)} %get-tuple-element.34, f32[256,256]{1,0:T(8,128)S(1)} %fusion.33, f32[40,256]{1,0:T(8,128)S(1)} %get-tuple-element.33, ...), kind=kOutput, calls=%fused_computation.22 | convolution fusion | flops 350617600 | bytes 9625600 | tf_op jit(solution)/shard_map/hcij,cjhp->cihp/dot_general | solution.py:71
  83.4 2.6 %multiply_reduce_fusion = (f32[256]{0:T(256)S(1)}, f32[256,2560]{0,1:T(8,128)S(1)}) fusion(bf16[256,2560]{0,1:T(8,128)(2,1)S(1)} %copy-done.2, bf16[256,2560]{0,1:T(8,128)(2,1)} %copy-done.1, f32[2560]{0:T(1024)S(1)} %mul.162, f32[1,256,40,64]{1,3,2,0:T(8,128)S(1)} %bitcast_add_fusion), kind=kLoop, calls=%fused_computation.25 | loop fusion | flops 7208704 | bytes 7875584 | tf_op jit(solution)/shard_map/reduce_sum | solution.py:119
  86.0 5.2 %psum.7 = f32[256]{0:T(256)S(1)} all-reduce(f32[256]{0:T(256)S(1)} %get-tuple-element.19), channel_id=1, replica_groups=mesh['group'=2,'scan'=4,'tensor'=2,'band'=2] {'tensor'}, use_global_device_ids=true, to_apply=%region_4.5 | all-reduce | flops 256 | bytes 2048 | tf_op jit(solution)/shard_map/psum | solution.py:119
  91.2 9.5 %fusion.9 = bf16[2560,256]{0,1:T(8,128)(2,1)} fusion(bf16[2560,2560]{1,0:T(8,128)(2,1)} %param.25, f32[256,2560]{0,1:T(8,128)S(1)} %get-tuple-element.20, f32[2560]{0:T(1024)S(1)} %copy-done.6, f32[256]{0:T(256)S(1)} %add_rsqrt_fusion), kind=kOutput, calls=%fused_computation.11 | convolution fusion | flops 3358064640 | bytes 17050624 | tf_op jit(solution)/shard_map/dot_general | solution.py:124
  100.7 24.6 %reduce-scatter.2.cloned.1.call-done = bf16[1280,256]{0,1:T(8,128)(2,1)} async-done(((bf16[2560,256]{0,1:T(8,128)(2,1)}), bf16[1280,256]{0,1:T(8,128)(2,1)}) %reduce-scatter.2.cloned.1.call-update) | async-done | bytes 655376 | tf_op jit(solution)/shard_map/reduce_scatter | solution.py:123
  (40 shorter events, 0.5 us)
Async XLA Ops:
  6.5 25.4 %copy-start = (bf16[256,128]{1,0:T(8,128)(2,1)S(1)}, bf16[256,128]{1,0:T(8,128)(2,1)}, u32[]{:S(2)}) copy-start(bf16[256,128]{1,0:T(8,128)(2,1)} %param.16) | copy-start | bytes 196612
  6.5 7.3 %copy-start.5 = (f32[40,256]{1,0:T(8,128)S(1)}, f32[40,256]{1,0:T(8,128)}, u32[]{:S(2)}) copy-start(f32[40,256]{1,0:T(8,128)} %param.17) | copy-start | bytes 122884
  6.5 7.3 %copy-start.7 = (f32[40]{0:T(128)S(1)}, f32[40]{0:T(128)}, u32[]{:S(2)}) copy-start(f32[40]{0:T(128)} %param.22) | copy-start | bytes 484
  6.5 63.9 %all-gather.4.cloned.1.call-start = ((), (), s32[]{:S(2)}) async-start(), calls=%async_computation.2 | async-start | bytes 5898240 | tf_op jit(solution)/shard_map/all_gather | solution.py:91
  12.2 2.1 %copy-start.4 = (bf16[256,128]{1,0:T(8,128)(2,1)S(1)}, bf16[256,128]{1,0:T(8,128)(2,1)}, u32[]{:S(2)}) copy-start(bf16[256,128]{1,0:T(8,128)(2,1)} %param.15) | copy-start | bytes 196612
  13.8 66.5 %copy-start.1 = (bf16[256,2560]{0,1:T(8,128)(2,1)}, bf16[256,2560]{0,1:T(8,128)(2,1)S(1)}, u32[]{:S(2)}) copy-start(bf16[256,2560]{0,1:T(8,128)(2,1)S(1)} %copy.39) | copy-start | bytes 3932164
  13.9 1.8 %copy-start.9 = (u32[32]{0:T(128)S(1)}, u32[32]{0:T(128)}, u32[]{:S(2)}) copy-start(u32[32]{0:T(128)} %constant.58) | copy-start | bytes 388
  14.0 16.3 %copy-start.3 = (bf16[256,2560]{1,0:T(8,128)(2,1)S(1)}, bf16[256,2560]{1,0:T(8,128)(2,1)}, u32[]{:S(2)}) copy-start(bf16[256,2560]{1,0:T(8,128)(2,1)} %param.14) | copy-start | bytes 3932164
  14.3 17.5 %copy-start.8 = (f32[40]{0:T(128)S(1)}, f32[40]{0:T(128)}, u32[]{:S(2)}) copy-start(f32[40]{0:T(128)} %param.23) | copy-start | bytes 484
  15.6 109.7 %reduce-scatter.2.cloned.1.call-start = ((), (), s32[]{:S(2)}) async-start(), calls=%async_computation.1 | async-start | bytes 1966080 | tf_op jit(solution)/shard_map/reduce_scatter | solution.py:123
  80.3 3.1 %copy-start.2 = (bf16[256,2560]{0,1:T(8,128)(2,1)S(1)}, bf16[256,2560]{0,1:T(8,128)(2,1)}, u32[]{:S(2)}) copy-start(bf16[256,2560]{0,1:T(8,128)(2,1)} %copy.42) | copy-start | bytes 3932164
  83.4 7.8 %copy-start.6 = (f32[2560]{0:T(1024)S(1)}, f32[2560]{0:T(1024)}, u32[]{:S(2)}) copy-start(f32[2560]{0:T(1024)} %param.24) | copy-start | bytes 30724
Sparse Core Ops, SparseCore 0:
  15.8 54.6 all-gather.3
  100.8 24.4 reduce-scatter.1
where the time goes:
time: 134 us; the launch traced here: 132 us
  waiting for transfers between devices  63 us (47%)
  matrix products  24.6 us (18%)
  blocking collectives  17.9 us (13%)
  between operations  15 us (11%)
  other arithmetic  6.85 us (5%)
  local copies, waits for them, and re-layouts  4.72 us (4%)
    all_gather x1, waiting for transfers between devices, on_device(): lax.all_gather(device_pair[1][None].astype(jnp.bfloat16), ('scan', 'band'...  38.3 us
    reduce_scatter x1, waiting for transfers between devices, on_device(): lax.psum_scatter(lax.dot_general(out_weight, normed, (((0,), (1,)), ((),...  24.6 us
    unnamed x1, blocking collectives  12.8 us
    dot_general x1, matrix products, on_device(): lax.dot_general(out_weight, normed, (((0,), (1,)), ((), ())), preferred_e...  9.46 us
    dot_general x1, matrix products, on_device(): jnp.einsum('kh,khpn->hpn', jnp.exp(gap_logs), shard_block, precision=HIGH...  8.66 us
    psum x1, blocking collectives, on_device(): square_total = lax.psum(jnp.sum(gated_out * gated_out, axis=1), 'tensor')  5.16 us
    unnamed x26, local copies, waits for them, and re-layouts  3.97 us
    dot_general x1, matrix products, on_device(): jnp.einsum('hcij,cjhp->cihp', mixing, signal_blocks, preferred_element_ty...  3.11 us
  transfers between devices with their start and end apart: 2, of which 2 were waited for; matrix products, arithmetic and copies ran while one was open for 2% of the time, Pallas kernels for 0%

commit v1 on v0

v1 whole, which is shorter than its diff:
```python
import functools

import jax
import jax.numpy as jnp
from jax import lax
from jax.experimental import pallas as pl
from jax.experimental.pallas import tpu as pltpu
from jax.sharding import PartitionSpec as P

HEAD_DIM = 64
STATE = 128
HALF = STATE // 2
PART = HALF // 2
STRETCH = 256
BANDS = 12
INNER = 5120
LANES = 128
CHUNK = 256

EPSILON = 1e-05
HIGHEST = lax.Precision.HIGHEST
F32 = jnp.float32
BF16 = jnp.bfloat16
MIB = 1 << 20


def dot(a, b):
    return lax.dot_general(a, b, (((1,), (0,)), ((), ())), preferred_element_type=F32)


def dot_rows(a, b):
    return lax.dot_general(a, b, (((0,), (0,)), ((), ())), preferred_element_type=F32)


def pieces(x):
    high = x.astype(BF16)
    rest = x - high.astype(F32)
    middle = rest.astype(BF16)
    return high, middle, (rest - middle.astype(F32)).astype(BF16)


def head_of_lane(heads, lanes, group, first=0):
    row = lax.broadcasted_iota(jnp.int32, (heads, lanes), 0)
    lane = lax.broadcasted_iota(jnp.int32, (heads, lanes), 1)
    return (row == first + lax.shift_right_logical(lane, group)).astype(F32).astype(BF16)


def spread_tokens(values, heads_map):
    return sum(dot_rows(piece, heads_map) for piece in pieces(values))


def spread_heads(row, heads_map):
    return sum(dot(piece, heads_map) for piece in pieces(jnp.broadcast_to(row, (8, row.shape[1]))))[:1]


def diagonal(rows, lanes):
    return lax.broadcasted_iota(jnp.int32, (rows, lanes), 0) == lax.broadcasted_iota(
        jnp.int32, (rows, lanes), 1
    )


def to_column(row):
    count = row.shape[1]
    return jnp.sum(jnp.where(diagonal(count, count), row, 0.0), axis=1, keepdims=True)


def decay_block(row, rows):
    place = lax.broadcasted_iota(jnp.int32, (rows, LANES), 0)
    high, middle, low = (piece.astype(F32) for piece in pieces(row))
    block = jnp.where(place == 0, high, jnp.where(place == 1, middle, jnp.where(place == 2, low, 0.0)))
    return block.astype(BF16)


def decay_row(block):
    return jnp.sum(block.astype(F32), axis=0, keepdims=True)


def decay_lanes(block, heads_map):
    return jnp.sum(dot(block[:16], heads_map), axis=0, keepdims=True)


def column_block(width):
    return width // 5 if width % (5 * LANES) == 0 else width


def local_call(body, name, outs, args, scratch=(), smem=(), limit=32 * MIB, flops=0):
    size = sum(a.size * a.dtype.itemsize for a in args) + sum(o.size * o.dtype.itemsize for o in outs)
    return pl.pallas_call(
        body,
        name=name,
        out_shape=outs,
        in_specs=[
            pl.BlockSpec(memory_space=pltpu.SMEM if i in smem else pltpu.VMEM) for i in range(len(args))
        ],
        out_specs=[pl.BlockSpec(memory_space=pltpu.VMEM)] * len(outs),
        scratch_shapes=list(scratch),
        compiler_params=pltpu.CompilerParams(vmem_limit_bytes=limit),
        cost_estimate=pl.CostEstimate(flops=flops, bytes_accessed=size, transcendentals=0),
    )(*args)


def state_kernel(
    band_ref,
    logits_ref,
    mask_ref,
    offset_ref,
    decay_log_ref,
    step_offset_ref,
    write_ref,
    signal_ref,
    running_ref,
    weight_ref,
    decay_ref,
    keep_ref,
    send_ref,
    state_ref,
):
    heads, tokens = logits_ref.shape
    width = signal_ref.shape[1]
    core = lax.axis_index("band")
    offset = to_column(step_offset_ref[...] + offset_ref[pl.ds(band_ref[0], 1), :])
    raw = logits_ref[...] + offset
    step_size = jnp.maximum(raw, 0.0) + jnp.log1p(jnp.exp(-jnp.abs(raw)))
    log_decay = step_size * to_column(-jnp.exp(decay_log_ref[...]))
    earlier = lax.broadcasted_iota(jnp.int32, (tokens, tokens), 0)
    later = lax.broadcasted_iota(jnp.int32, (tokens, tokens), 1)
    running = lax.dot_general(
        log_decay,
        (earlier <= later).astype(F32),
        (((1,), (0,)), ((), ())),
        precision=HIGHEST,
        preferred_element_type=F32,
    )
    weight = step_size * mask_ref[...].astype(F32)
    running_ref[...] = running
    weight_ref[...] = weight
    total = running[:, tokens - 1 : tokens]
    tail = jnp.exp(total - running) * weight
    block = column_block(width)
    for first in range(0, width, block):
        lanes = slice(first, first + block)
        heads_map = head_of_lane(heads, block, 6, first // HEAD_DIM)
        scaled = (signal_ref[:, lanes].astype(F32) * spread_tokens(tail, heads_map)).astype(BF16)
        state_ref[:, lanes] = dot_rows(write_ref[...], scaled)
    own = pl.multiple_of(core * HALF, HALF)
    other = pl.multiple_of((1 - core) * HALF, HALF)
    keep_ref[...] = state_ref[pl.ds(own, HALF), :]
    send_ref[:, :width] = state_ref[pl.ds(other, HALF), :].astype(BF16)
    row = jnp.sum(jnp.where(diagonal(heads, LANES), jnp.exp(total), 0.0), axis=0, keepdims=True)
    send_ref[:, width:] = decay_block(row, HALF)
    decay_ref[...] = decay_block(row, 16)


def local_kernel(
    running_ref,
    weight_ref,
    skip_ref,
    write_ref,
    read_ref,
    signal_ref,
    gate_ref,
    base_ref,
    factor_ref,
    scores_ref,
):
    heads, tokens = running_ref.shape
    block = signal_ref.shape[1]
    pairs = block // LANES
    at = pl.program_id(0)
    half = tokens // 2

    @pl.when(at == 0)
    def _():
        scores = lax.dot_general(
            read_ref[...], write_ref[...], (((1,), (1,)), ((), ())), preferred_element_type=F32
        )
        row = lax.broadcasted_iota(jnp.int32, scores.shape, 0)
        lane = lax.broadcasted_iota(jnp.int32, scores.shape, 1)
        scores_ref[...] = jnp.where(row >= lane, scores, 0.0)

    running = running_ref[...]
    first_head = at * (block // HEAD_DIM)
    wide = spread_tokens(running, head_of_lane(heads, block * 2, 7, first_head))
    heads_map = head_of_lane(heads, block, 6, first_head)
    gate = gate_ref[...].astype(F32)
    gate = gate / (1.0 + jnp.exp(-gate))
    factor_ref[...] = spread_tokens(jnp.exp(running), heads_map) * gate
    skip = spread_heads(skip_ref[...], heads_map)
    low_lanes = lax.broadcasted_iota(jnp.int32, (half, LANES), 1) < HEAD_DIM
    for pair in range(pairs):
        lanes = slice(pair * LANES, (pair + 1) * LANES)
        values = signal_ref[:, lanes]
        top, bottom = [], []
        for k in (2 * pair, 2 * pair + 1):
            row = running_ref[pl.ds(first_head + k, 1), :]
            weight = weight_ref[pl.ds(first_head + k, 1), :]
            column = wide[:, k * LANES : (k + 1) * LANES]

            def mixing(rows, cols):
                span = jnp.minimum(column[rows] - row[:, cols], 0.0)
                return (jnp.exp(span) * scores_ref[rows, cols] * weight[:, cols]).astype(BF16)

            early, late = slice(0, half), slice(half, tokens)
            top.append(dot(mixing(early, early), values[early]))
            bottom.append(
                dot(mixing(late, early), values[early]) + dot(mixing(late, late), values[late])
            )
        wide_values = values.astype(F32) * skip[:, lanes]
        base_ref[:half, lanes] = (
            jnp.where(low_lanes, top[0], top[1]) + wide_values[:half]
        ) * gate[:half, lanes]
        base_ref[half:, lanes] = (
            jnp.where(low_lanes, bottom[0], bottom[1]) + wide_values[half:]
        ) * gate[half:, lanes]


def local_part(running, weight, skip_gain, write_proj, read_proj, signal, gate_branch):
    tokens, width = signal.shape
    heads = running.shape[0]
    block = column_block(width)
    whole = lambda a: pl.BlockSpec(a.shape, lambda i: (0, 0))
    cols = pl.BlockSpec((tokens, block), lambda i: (0, i))
    return pl.pallas_call(
        local_kernel,
        name="local_part",
        out_shape=[jax.ShapeDtypeStruct((tokens, width), F32)] * 2,
        grid=(width // block,),
        in_specs=[whole(a) for a in (running, weight, skip_gain, write_proj, read_proj)] + [cols, cols],
        out_specs=[cols, cols],
        scratch_shapes=[pltpu.VMEM((tokens, tokens), F32)],
        compiler_params=pltpu.CompilerParams(vmem_limit_bytes=24 * MIB),
        cost_estimate=pl.CostEstimate(
            flops=6 * heads * tokens * tokens * HEAD_DIM,
            bytes_accessed=tokens * width * 12,
            transcendentals=heads * tokens * tokens,
        ),
    )(running, weight, skip_gain, write_proj, read_proj, signal, gate_branch)


def chip_kernel(keep_ref, got_ref, decay_ref, state_ref, first_ref, second_ref):
    width = keep_ref.shape[1]
    core = lax.axis_index("band")
    chip = lax.axis_index("scan")
    heads_map = head_of_lane(LANES, width, 6)
    got_decay = got_ref[:16, width:]
    mine = decay_ref[...]
    later = jnp.where(core == 0, got_decay.astype(F32), mine.astype(F32)).astype(BF16)
    lanes = decay_lanes(later, heads_map)
    got = got_ref[:, :width].astype(F32)
    keep = keep_ref[...]
    early, late = jnp.where(core == 0, keep, got), jnp.where(core == 0, got, keep)
    state_ref[:, :width] = (early * lanes + late).astype(BF16)
    block = decay_block(decay_row(got_decay) * decay_row(mine), PART)
    state_ref[:PART, width:] = block
    state_ref[PART:, width:] = block
    second_ref[...] = state_ref[PART:, :]
    first_ref[...] = state_ref[pl.ds(pl.multiple_of(jnp.where(chip == 1, PART, 0), PART), PART), :]


def middle_kernel(state_ref, near_ref, far_ref, out_ref):
    width = out_ref.shape[1]
    chip = lax.axis_index("scan")

    @pl.when(chip == 0)
    def _():
        out_ref[...] = state_ref[PART:, :width]

    @pl.when(chip == 1)
    def _():
        lanes = decay_lanes(state_ref[:16, width:], head_of_lane(LANES, width, 6))
        out_ref[...] = (
            lanes * near_ref[:, :width].astype(F32) + state_ref[:PART, :width].astype(F32)
        ).astype(BF16)

    @pl.when(chip == 2)
    def _():
        heads_map = head_of_lane(LANES, width, 6)
        lanes = decay_lanes(near_ref[:16, width:], heads_map)
        entered = lanes * far_ref[:, :width].astype(F32) + near_ref[:, :width].astype(F32)
        own = decay_lanes(state_ref[:16, width:], heads_map)
        out_ref[...] = (own * entered + state_ref[PART:, :width].astype(F32)).astype(BF16)

    @pl.when(chip == 3)
    def _():
        out_ref[...] = jnp.zeros(out_ref.shape, BF16)


def enter_kernel(
    near_ref, far_ref, next_ref, skip_ref, keep_ref, got_ref, decay_ref, mine_ref, send_ref, enter_ref
):
    width = keep_ref.shape[1]
    core = lax.axis_index("band")
    chip = lax.axis_index("scan")
    near = near_ref[:, :width]

    @pl.when(chip == 0)
    def _():
        enter_ref[...] = jnp.zeros(enter_ref.shape, F32)

    @pl.when(chip == 1)
    def _():
        enter_ref[:PART, :] = near.astype(F32)
        enter_ref[PART:, :] = next_ref[...].astype(F32)

    @pl.when(chip > 1)
    def _():
        lanes = decay_lanes(near_ref[:16, width:], head_of_lane(LANES, width, 6))

        @pl.when(chip == 2)
        def _():
            enter_ref[:PART, :] = next_ref[...].astype(F32)
            enter_ref[PART:, :] = lanes * far_ref[:, :width].astype(F32) + near.astype(F32)

        @pl.when(chip == 3)
        def _():
            enter_ref[:PART, :] = lanes * skip_ref[...].astype(F32) + near.astype(F32)
            enter_ref[PART:, :] = next_ref[...].astype(F32)

    share_enter(enter_ref, keep_ref, got_ref, decay_ref, mine_ref, send_ref)


def share_enter(enter_ref, keep_ref, got_ref, decay_ref, mine_ref, send_ref):
    width = keep_ref.shape[1]
    core = lax.axis_index("band")
    heads_map = head_of_lane(LANES, width, 6)
    enter = enter_ref[...]

    @pl.when(core == 0)
    def _():
        mine_ref[...] = enter.astype(BF16)
        send_ref[...] = (decay_lanes(decay_ref[...], heads_map) * enter + keep_ref[...]).astype(BF16)

    @pl.when(core == 1)
    def _():
        send_ref[...] = enter.astype(BF16)
        lanes = decay_lanes(got_ref[:16, width:], heads_map)
        mine_ref[...] = (lanes * enter + got_ref[:, :width].astype(F32)).astype(BF16)


def gathered_kernel(all_ref, keep_ref, got_ref, decay_ref, mine_ref, send_ref, enter_ref):
    width = keep_ref.shape[1]
    chip = lax.axis_index("scan")
    heads_map = head_of_lane(LANES, width, 6)
    enter_ref[...] = jnp.zeros(enter_ref.shape, F32)
    for source in range(all_ref.shape[0]):

        @pl.when(source < chip)
        def _():
            lanes = decay_lanes(all_ref[source, :16, width:], heads_map)
            enter_ref[...] = lanes * enter_ref[...] + all_ref[source, :, :width].astype(F32)

    share_enter(enter_ref, keep_ref, got_ref, decay_ref, mine_ref, send_ref)


def entering_state(keep, got, decay, chips):
    width = keep.shape[1]
    half = jax.ShapeDtypeStruct((HALF, width), BF16)
    state, first, second = local_call(
        chip_kernel,
        "chip_state",
        [
            jax.ShapeDtypeStruct((HALF, width + LANES), BF16),
            jax.ShapeDtypeStruct((PART, width + LANES), BF16),
            jax.ShapeDtypeStruct((PART, width + LANES), BF16),
        ],
        (keep, got, decay),
    )
    enter = pltpu.VMEM((HALF, width), F32)
    if chips != 4:
        gathered = lax.all_gather(state, "scan", axis=0)
        return local_call(
            gathered_kernel, "enter_state", [half, half], (gathered, keep, got, decay), (enter,)
        )
    near = lax.ppermute(first, "scan", [(0, 1), (1, 2), (2, 3)])
    far = lax.ppermute(second, "scan", [(0, 2)])
    (middle,) = local_call(
        middle_kernel, "middle_state", [jax.ShapeDtypeStruct((PART, width), BF16)], (state, near, far)
    )
    following = lax.ppermute(middle, "scan", [(0, 1), (1, 2), (2, 3)])
    skipping = lax.ppermute(middle, "scan", [(1, 3)])
    return local_call(
        enter_kernel,
        "enter_state",
        [half, half],
        (near, far, following, skipping, keep, got, decay),
        (enter,),
    )


def gated_kernel(mine_ref, other_ref, read_ref, gain_ref, base_ref, factor_ref, out_ref, square_ref, sum_ref):
    core = lax.axis_index("band")
    at = pl.program_id(0)
    mine, other = mine_ref[...], other_ref[...]
    is_first = core == 0
    low = jnp.where(is_first, mine.astype(F32), other.astype(F32)).astype(BF16)
    high = jnp.where(is_first, other.astype(F32), mine.astype(F32)).astype(BF16)
    carried = dot(read_ref[...], jnp.concatenate([low, high], axis=0))
    gated = base_ref[...] + factor_ref[...] * carried
    out_ref[...] = (gated * gain_ref[...]).astype(BF16)
    squares = gated * gated
    total = sum(squares[:, k : k + LANES] for k in range(0, squares.shape[1], LANES))

    @pl.when(at == 0)
    def _():
        sum_ref[...] = total

    @pl.when(at > 0)
    def _():
        sum_ref[...] += total

    @pl.when(at == pl.num_programs(0) - 1)
    def _():
        square_ref[...] = jnp.broadcast_to(
            jnp.sum(sum_ref[...].T, axis=0, keepdims=True), square_ref.shape
        )


def gated_part(mine, other, read_proj, norm_gain, base, factor):
    tokens, width = base.shape
    block = column_block(width)
    cols = lambda rows: pl.BlockSpec((rows, block), lambda i: (0, i))
    return pl.pallas_call(
        gated_kernel,
        name="gated_part",
        out_shape=[
            jax.ShapeDtypeStruct((tokens, width), BF16),
            jax.ShapeDtypeStruct((8, tokens), F32),
        ],
        grid=(width // block,),
        in_specs=[
            cols(HALF),
            cols(HALF),
            pl.BlockSpec(read_proj.shape, lambda i: (0, 0)),
            cols(1),
            cols(tokens),
            cols(tokens),
        ],
        out_specs=[cols(tokens), pl.BlockSpec((8, tokens), lambda i: (0, 0))],
        scratch_shapes=[pltpu.VMEM((tokens, LANES), F32)],
        compiler_params=pltpu.CompilerParams(vmem_limit_bytes=24 * MIB),
        cost_estimate=pl.CostEstimate(
            flops=2 * tokens * width * STATE, bytes_accessed=tokens * width * 10, transcendentals=0
        ),
    )(mine, other, read_proj, norm_gain, base, factor)


def project_kernel(where_ref, gated_ref, weight_ref, out_ref):
    out_ref[...] = dot(gated_ref[...], weight_ref[...]).astype(out_ref.dtype)


def project(where, gated, out_weight, count, dtype):
    tokens, width = gated.shape
    return pl.pallas_call(
        project_kernel,
        name="project",
        out_shape=jax.ShapeDtypeStruct((tokens, count * CHUNK), dtype),
        grid_spec=pltpu.PrefetchScalarGridSpec(
            num_scalar_prefetch=1,
            grid=(count,),
            in_specs=[
                pl.BlockSpec((tokens, width), lambda i, where: (0, 0)),
                pl.BlockSpec((width, CHUNK), lambda i, where: (0, where[0] + i)),
            ],
            out_specs=pl.BlockSpec((tokens, CHUNK), lambda i, where: (0, i)),
        ),
        compiler_params=pltpu.CompilerParams(vmem_limit_bytes=16 * MIB),
        cost_estimate=pl.CostEstimate(
            flops=2 * tokens * width * count * CHUNK,
            bytes_accessed=(tokens + count * CHUNK) * width * 2,
            transcendentals=0,
        ),
    )(where, gated, out_weight)


def finish_kernel(squares_ref, other_squares_ref, own_ref, *refs):
    *got_refs, out_ref = refs
    mean = (squares_ref[...] + other_squares_ref[...]) / INNER
    scale = lax.rsqrt(mean[:1] + EPSILON)
    scale = jnp.broadcast_to(scale, (LANES, scale.shape[1])).T
    first = 0
    for got_ref in got_refs:
        for k in range(0, got_ref.shape[1], LANES):
            lanes = slice(first + k, first + k + LANES)
            total = own_ref[:, lanes] + got_ref[:, k : k + LANES].astype(F32)
            out_ref[:, lanes] = (total * scale).astype(BF16)
        first += got_ref.shape[1]


SENDS = (1, 2, 2)


def layer_columns(gated, squares, out_weight, members):
    tokens = gated.shape[0]
    columns = out_weight.shape[1] // members
    if members != 2 or columns != CHUNK * sum(SENDS):
        mean = lax.psum(squares[0], "tensor") / INNER
        partial = dot(gated, out_weight).astype(BF16)
        total = lax.psum_scatter(partial, "tensor", scatter_dimension=1, tiled=True)
        return (total.astype(F32) * lax.rsqrt(mean + EPSILON)[:, None]).astype(BF16)
    member = lax.axis_index("tensor")
    swap = [(0, 1), (1, 0)]
    blocks = columns // CHUNK
    got, first = [], 0
    for count in SENDS:
        where = ((1 - member) * blocks + first)[None].astype(jnp.int32)
        got.append(lax.ppermute(project(where, gated, out_weight, count, BF16), "tensor", swap))
        first += count
    other_squares = lax.ppermute(squares, "tensor", swap)
    own = project((member * blocks)[None].astype(jnp.int32), gated, out_weight, blocks, F32)
    (result,) = local_call(
        finish_kernel,
        "finish",
        [jax.ShapeDtypeStruct((tokens, columns), BF16)],
        (squares, other_squares, own, *got),
    )
    return result


def on_device(
    chips,
    members,
    signal,
    gate_branch,
    write_proj,
    read_proj,
    step_logits,
    valid_mask,
    stretch_band,
    band_offset,
    decay_log,
    step_offset,
    skip_gain,
    norm_gain,
    out_weight,
):
    tokens, width = signal.shape
    heads = decay_log.shape[0]
    running, weight, decay, keep, send = local_call(
        state_kernel,
        "own_state",
        [
            jax.ShapeDtypeStruct((heads, tokens), F32),
            jax.ShapeDtypeStruct((heads, tokens), F32),
            jax.ShapeDtypeStruct((16, LANES), BF16),
            jax.ShapeDtypeStruct((HALF, width), F32),
            jax.ShapeDtypeStruct((HALF, width + LANES), BF16),
        ],
        (
            stretch_band,
            step_logits,
            valid_mask[None],
            band_offset,
            decay_log[None],
            step_offset[None],
            write_proj,
            signal,
        ),
        (pltpu.VMEM((STATE, width), F32),),
        smem=(0,),
        flops=8 * tokens * width * STATE,
    )
    cores = [(0, 1), (1, 0)]
    got = lax.ppermute(send, "band", cores)
    base, factor = local_part(
        running, weight, skip_gain[None], write_proj, read_proj, signal, gate_branch
    )
    mine, give = entering_state(keep, got, decay, chips)
    other = lax.ppermute(give, "band", cores)
    gated, squares = gated_part(mine, other, read_proj, norm_gain[None], base, factor)
    return layer_columns(gated, squares, out_weight, members)


def solution(mesh):
    placed = (
        P(("group", "scan", "band"), "tensor"),
        P(("group", "scan", "band"), "tensor"),
        P(("group", "scan", "band"), None),
        P(("group", "scan", "band"), None),
        P("tensor", ("group", "scan", "band")),
        P(("group", "scan", "band")),
        P(("group", "scan", "band")),
        P(None, "tensor"),
        P("tensor"),
        P("tensor"),
        P("tensor"),
        P("tensor"),
        P("tensor", None),
    )
    return jax.shard_map(
        functools.partial(on_device, mesh.shape["scan"], mesh.shape["tensor"]),
        mesh=mesh,
        in_specs=placed,
        out_specs=P(("group", "scan", "band"), "tensor"),
        check_vma=False,
    )
```

time: 134 us -> 71.6 us (0.53)
  waiting for transfers between devices: 63 us -> 20.1 us
  matrix products: 24.6 us -> 0 us
  Pallas kernels: 0 us -> 21.2 us
  blocking collectives: 17.9 us -> 0 us
  local copies, waits for them, and re-layouts: 4.72 us -> 19.8 us
  between operations: 15 us -> 0.91 us
  starting transfers between devices: 0.04 us -> 9 us
  other arithmetic: 6.85 us -> 0 us
    all_gather x1 -> x0, waiting for transfers between devices: 38.3 us -> none  [on_device(): lax.all_gather(device_pair[1][None].astype(jnp.bfloat16), ('scan', 'band'...]
    reduce_scatter x1 -> x0, waiting for transfers between devices: 24.6 us -> none  [on_device(): lax.psum_scatter(lax.dot_general(out_weight, normed, (((0,), (1,)), ((),...]
    dot_general x8 -> x0, matrix products: 24.6 us -> none  [the longest x1 9.46 us: on_device(): lax.dot_general(out_weight, normed, (((0,), (1,)), ((), ())), preferred_e...]
    pallas_call x0 -> x11, Pallas kernels: none -> 21.2 us  [the longest x1 6.99 us: local_part(): pl.pallas_call(local_kernel, name='local_part', out_shape=[jax.ShapeDtype...]
    ppermute x0 -> x10, waiting for transfers between devices: none -> 20.1 us  [the longest x1 8.33 us: entering_state(): following = lax.ppermute(middle, 'scan', [(0, 1), (1, 2), (2, 3)])]
    unnamed x26 -> x32, local copies, waits for them, and re-layouts: 3.97 us -> 19.8 us
    unnamed x1 -> x0, blocking collectives: 12.8 us -> none
    ppermute x0 -> x10, starting transfers between devices: none -> 9 us  [the longest x3 3.7 us: layer_columns(): lax.ppermute(project(where, gated, out_weight, count, BF16), 'tensor', swap)]
  transfers between devices with their start and end apart: 2 -> 10, of which waited for: 2 -> 4; matrix products, arithmetic and copies ran while one was open for 2% -> 0% of each run, Pallas kernels for 0% -> 17%
where the time goes in v1:
time: 71.6 us; the launch traced here: 71.1 us
  Pallas kernels  21.2 us (30%)
  waiting for transfers between devices  20.1 us (28%)
  local copies, waits for them, and re-layouts  19.8 us (28%)
  starting transfers between devices  9 us (13%)
  between operations  0.91 us (1%)
    unnamed x32, local copies, waits for them, and re-layouts  19.8 us
    ppermute x1, waiting for transfers between devices, entering_state(): following = lax.ppermute(middle, 'scan', [(0, 1), (1, 2), (2, 3)])  8.33 us
    pallas_call x1, Pallas kernels, local_part(): pl.pallas_call(local_kernel, name='local_part', out_shape=[jax.ShapeDtype...  6.99 us
    ppermute x1, waiting for transfers between devices, entering_state(): near = lax.ppermute(first, 'scan', [(0, 1), (1, 2), (2, 3)])  6.33 us
    pallas_call x4, Pallas kernels, project(): pl.pallas_call(project_kernel, name='project', out_shape=jax.ShapeDtypeSt...  6.11 us
    pallas_call x5, Pallas kernels, local_call(): pl.pallas_call(body, name=name, out_shape=outs, in_specs=[pl.BlockSpec(me...  6.02 us
    ppermute x1, waiting for transfers between devices, entering_state(): skipping = lax.ppermute(middle, 'scan', [(1, 3)])  3.81 us
    ppermute x3, starting transfers between devices, layer_columns(): lax.ppermute(project(where, gated, out_weight, count, BF16), 'tensor', swap)  3.7 us
  transfers between devices with their start and end apart: 10, of which 4 were waited for; matrix products, arithmetic and copies ran while one was open for 0% of the time, Pallas kernels for 17%

profile of v1, /device:TPU:24, one launch (start us, length us, event | category | flops | bytes accessed | tf_op | source)
XLA Modules:
  0.0 71.1 jit_solution(7663489617444084865)
XLA Ops:
  0.7 1.3 %copy-done.4 = bf16[256,2560]{1,0:T(8,128)(2,1)S(1)} copy-done((bf16[256,2560]{1,0:T(8,128)(2,1)S(1)}, bf16[256,2560]{1,0:T(8,128)(2,1)}, u32[]{:S(2)}) %copy-start.4) | copy-done | bytes 1310744
  2.0 0.8 %copy-done.7 = bf16[256,128]{1,0:T(8,128)(2,1)S(1)} copy-done((bf16[256,128]{1,0:T(8,128)(2,1)S(1)}, bf16[256,128]{1,0:T(8,128)(2,1)}, u32[]{:S(2)}) %copy-start.7) | copy-done | bytes 65560
  2.8 0.8 %copy-done.9 = f32[40,256]{1,0:T(8,128)S(1)} copy-done((f32[40,256]{1,0:T(8,128)S(1)}, f32[40,256]{1,0:T(8,128)}, u32[]{:S(2)}) %copy-start.9) | copy-done | bytes 40984
  3.6 0.7 copy-done.10
  4.3 0.7 copy-done.11
  5.0 0.7 copy-done.12
  5.6 0.7 copy-done.13
  6.3 3.4 %own_state.1 = (f32[40,256]{1,0:T(8,128)S(1)}, f32[40,256]{1,0:T(8,128)S(1)}, bf16[16,128]{1,0:T(8,128)(2,1)S(1)}, f32[64,2560]{1,0:T(8,128)S(1)}, bf16[64,2688]{1,0:T(8,128)(2,1)S(1)}) custom-call(s32[1]{0:T(128)S(6)} %copy.14.band_ref, f32[40,256]{1,0:T(8,128)S(1)} %copy-done.9, s32[1,256]{1,0:T(1,128)S(1)} %bitcast.8, f32[12,40]{1,0:T(8,128)S(1)} %copy-done.10, ...), custom_call_target="tpu_custom_call" | custom-call | flops 671088640 | bytes 2505924 | tf_op jit(solution)/shard_map/own_state/pallas_call | solution.py:88
  9.8 1.6 %collective-permute-done.got_ref = bf16[64,2688]{1,0:T(8,128)(2,1)S(1)} collective-permute-done((bf16[64,2688]{1,0:T(8,128)(2,1)S(1)}, bf16[64,2688]{1,0:T(8,128)(2,1)S(1)}, u32[]{:S(2)}, u32[]{:S(2)}) %collective-permute-start) | collective-permute-done | bytes 344096 | tf_op jit(solution)/shard_map/ppermute | solution.py:563
  11.4 0.2 chip_state.1
  11.7 1.4 %collective-permute-start.1 = (bf16[32,2688]{1,0:T(8,128)(2,1)S(1)}, bf16[32,2688]{1,0:T(8,128)(2,1)S(1)}, u32[]{:S(2)}, u32[]{:S(2)}) collective-permute-start(bf16[32,2688]{1,0:T(8,128)(2,1)S(1)} %get-tuple-element.22), channel_id=1, source_target_pairs={{0,4},{4,8},{8,12},{1,5},{5,9},{9,13},{2,6},{6,10},{10,14},{3,7},{... | collective-permute-start | bytes 516104 | tf_op jit(solution)/shard_map/ppermute | solution.py:374
  13.2 0.7 collective-permute-start.2
  13.9 6.3 %collective-permute-done.1.near_ref = bf16[32,2688]{1,0:T(8,128)(2,1)S(1)} collective-permute-done((bf16[32,2688]{1,0:T(8,128)(2,1)S(1)}, bf16[32,2688]{1,0:T(8,128)(2,1)S(1)}, u32[]{:S(2)}, u32[]{:S(2)}) %collective-permute-start.1) | collective-permute-done | bytes 172064 | tf_op jit(solution)/shard_map/ppermute | solution.py:374
  20.2 1.3 %collective-permute-start.3 = (bf16[32,2560]{1,0:T(8,128)(2,1)S(1)}, bf16[32,2560]{1,0:T(8,128)(2,1)S(1)}, u32[]{:S(2)}, u32[]{:S(2)}) collective-permute-start(bf16[32,2560]{1,0:T(8,128)(2,1)S(1)} %middle_state.1), channel_id=1, source_target_pairs={{0,4},{4,8},{8,12},{1,5},{5,9},{9,13},{2,6},{6,10},{10,14},{3,7},{... | collective-permute-start | bytes 491528 | tf_op jit(solution)/shard_map/ppermute | solution.py:379
  21.5 1.3 %collective-permute-start.4 = (bf16[32,2560]{1,0:T(8,128)(2,1)S(1)}, bf16[32,2560]{1,0:T(8,128)(2,1)S(1)}, u32[]{:S(2)}, u32[]{:S(2)}) collective-permute-start(bf16[32,2560]{1,0:T(8,128)(2,1)S(1)} %middle_state.1), channel_id=1, source_target_pairs={{4,12},{5,13},{6,14},{7,15},{20,28},{21,29},{22,30},{23,31}} | collective-permute-start | bytes 491528 | tf_op jit(solution)/shard_map/ppermute | solution.py:380
  22.8 8.3 %collective-permute-done.3.next_ref = bf16[32,2560]{1,0:T(8,128)(2,1)S(1)} collective-permute-done((bf16[32,2560]{1,0:T(8,128)(2,1)S(1)}, bf16[32,2560]{1,0:T(8,128)(2,1)S(1)}, u32[]{:S(2)}, u32[]{:S(2)}) %collective-permute-start.3) | collective-permute-done | bytes 163872 | tf_op jit(solution)/shard_map/ppermute | solution.py:379
  31.1 3.8 %collective-permute-done.4.skip_ref = bf16[32,2560]{1,0:T(8,128)(2,1)S(1)} collective-permute-done((bf16[32,2560]{1,0:T(8,128)(2,1)S(1)}, bf16[32,2560]{1,0:T(8,128)(2,1)S(1)}, u32[]{:S(2)}, u32[]{:S(2)}) %collective-permute-start.4) | collective-permute-done | bytes 163872 | tf_op jit(solution)/shard_map/ppermute | solution.py:380
  35.0 1.3 %enter_state.1 = (bf16[64,2560]{1,0:T(8,128)(2,1)S(1)}, bf16[64,2560]{1,0:T(8,128)(2,1)}) custom-call(bf16[32,2688]{1,0:T(8,128)(2,1)S(1)} %collective-permute-done.1.near_ref, bf16[32,2688]{1,0:T(8,128)(2,1)S(1)} %collective-permute-done.2.far_ref, bf16[32,2560]{1,0:T(8,128)(2,1)S(1)} %collective-permute-done.3.next_ref, ...), custom_call_target="tpu_custom_call" | custom-call | bytes 2330624 | tf_op jit(solution)/shard_map/enter_state/pallas_call | solution.py:88
  36.3 7.0 %local_part.1 = (f32[256,2560]{1,0:T(8,128)S(1)}, f32[256,2560]{1,0:T(8,128)S(1)}) custom-call(f32[40,256]{1,0:T(8,128)S(1)} %get-tuple-element.27.running_ref, f32[40,256]{1,0:T(8,128)S(1)} %get-tuple-element.28.weight_ref, f32[1,40]{1,0:T(1,128)S(1)} %bitcast.11, bf16[256,128]{1,0:T(8,128)(2,1)S(1)} %copy-done.8, bf16[256,128]{1,0:T(8,128)(2,1)S(1)} %copy-done.3, ...), custom_call_target="tpu_custom_call" | custom-call | flops 1006632960 | bytes 7864320 | tf_op jit(solution)/shard_map/local_part/pallas_call | solution.py:223
  43.3 2.1 %gated_part.1 = (bf16[256,2560]{1,0:T(8,128)(2,1)S(1)}, f32[8,256]{1,0:T(8,128)S(1)}) custom-call(bf16[64,2560]{1,0:T(8,128)(2,1)S(1)} %get-tuple-element.25.mine_ref, bf16[64,2560]{1,0:T(8,128)(2,1)S(1)} %collective-permute-done.5.other_ref, bf16[256,128]{1,0:T(8,128)(2,1)S(1)} %copy-done.3, f32[1,2560]{1,0:T(1,128)S(1)} %broadcast_in_dim.30.gain_ref, ...), custom_call_target="tpu_custom_call" | custom-call | flops 167772160 | bytes 6553600 | tf_op jit(solution)/shard_map/gated_part/pallas_call | solution.py:422
  45.4 4.7 %copy-done = bf16[2560,2560]{1,0:T(8,128)(2,1)S(1)} copy-done((bf16[2560,2560]{1,0:T(8,128)(2,1)S(1)}, bf16[2560,2560]{1,0:T(8,128)(2,1)}, u32[]{:S(2)}) %copy-start) | copy-done | bytes 13107224
  50.1 1.3 %project.6 = bf16[256,512]{1,0:T(8,128)(2,1)S(1)} custom-call(s32[1]{0:T(128)} %bitcast.6.where_ref, bf16[256,2560]{1,0:T(8,128)(2,1)S(1)} %get-tuple-element.32.gated_ref, bf16[2560,2560]{1,0:T(8,128)(2,1)S(1)} %copy-done), custom_call_target="tpu_custom_call" | custom-call | flops 671088640 | bytes 3932160 | tf_op jit(solution)/shard_map/project/pallas_call | solution.py:453
  51.4 1.6 %collective-permute-start.8 = (bf16[256,512]{1,0:T(8,128)(2,1)S(1)}, bf16[256,512]{1,0:T(8,128)(2,1)S(1)}, u32[]{:S(2)}, u32[]{:S(2)}) collective-permute-start(bf16[256,512]{1,0:T(8,128)(2,1)S(1)} %project.6), channel_id=1, source_target_pairs={{0,2},{2,0},{1,3},{3,1},{4,6},{6,4},{5,7},{7,5},{8,10},{10,8},{9,1... | collective-permute-start | bytes 786440 | tf_op jit(solution)/shard_map/ppermute | solution.py:506
  52.9 1.3 %project.7 = bf16[256,512]{1,0:T(8,128)(2,1)S(1)} custom-call(s32[1]{0:T(128)} %bitcast.7.where_ref, bf16[256,2560]{1,0:T(8,128)(2,1)S(1)} %get-tuple-element.32.gated_ref, bf16[2560,2560]{1,0:T(8,128)(2,1)S(1)} %copy-done), custom_call_target="tpu_custom_call" | custom-call | flops 671088640 | bytes 3932160 | tf_op jit(solution)/shard_map/project/pallas_call | solution.py:453
  54.2 0.6 collective-permute-start.9
  54.8 4.7 %copy-done.1 = bf16[2560,2560]{1,0:T(8,128)(2,1)S(1)} copy-done((bf16[2560,2560]{1,0:T(8,128)(2,1)S(1)}, bf16[2560,2560]{1,0:T(8,128)(2,1)}, u32[]{:S(2)}) %copy-start.1) | copy-done | bytes 13107224
  59.5 0.5 project.5
  60.0 1.5 %collective-permute-start.7 = (bf16[256,256]{1,0:T(8,128)(2,1)S(1)}, bf16[256,256]{1,0:T(8,128)(2,1)S(1)}, u32[]{:S(2)}, u32[]{:S(2)}) collective-permute-start(bf16[256,256]{1,0:T(8,128)(2,1)S(1)} %project.5), channel_id=1, source_target_pairs={{0,2},{2,0},{1,3},{3,1},{4,6},{6,4},{5,7},{7,5},{8,10},{10,8},{9,1... | collective-permute-start | bytes 393224 | tf_op jit(solution)/shard_map/ppermute | solution.py:506
  61.6 0.5 collective-permute-start.6
  62.1 4.7 %copy-done.2 = bf16[2560,2560]{1,0:T(8,128)(2,1)S(1)} copy-done((bf16[2560,2560]{1,0:T(8,128)(2,1)S(1)}, bf16[2560,2560]{1,0:T(8,128)(2,1)}, u32[]{:S(2)}) %copy-start.2) | copy-done | bytes 13107224
  66.8 3.1 %project.4.own_ref = f32[256,1280]{1,0:T(8,128)S(1)} custom-call(s32[1]{0:T(128)} %bitcast.4.where_ref, bf16[256,2560]{1,0:T(8,128)(2,1)S(1)} %get-tuple-element.32.gated_ref, bf16[2560,2560]{1,0:T(8,128)(2,1)S(1)} %copy-done.2), custom_call_target="tpu_custom_call" | custom-call | flops 1677721600 | bytes 7864320 | tf_op jit(solution)/shard_map/project/pallas_call | solution.py:453
  70.0 1.1 %finish.1 = bf16[256,1280]{1,0:T(8,128)(2,1)} custom-call(f32[8,256]{1,0:T(8,128)S(1)} %get-tuple-element.31.squares_ref, f32[8,256]{1,0:T(8,128)S(1)} %collective-permute-done.6.other_squares_ref, f32[256,1280]{1,0:T(8,128)S(1)} %project.4.own_ref, bf16[256,256]{1,0:T(8,128)(2,1)S(1)} %collective-permute-done.7.refs_0_, ...), custom_call_target="tpu_custom_call" | custom-call | bytes 2637824 | tf_op jit(solution)/shard_map/finish/pallas_call | solution.py:88
  (32 shorter events, 0.2 us)
Async XLA Ops:
  0.7 1.3 %copy-start.4 = (bf16[256,2560]{1,0:T(8,128)(2,1)S(1)}, bf16[256,2560]{1,0:T(8,128)(2,1)}, u32[]{:S(2)}) copy-start(bf16[256,2560]{1,0:T(8,128)(2,1)} %signal_ref.3) | copy-start | bytes 3932164
  2.0 0.8 %copy-start.7 = (bf16[256,128]{1,0:T(8,128)(2,1)S(1)}, bf16[256,128]{1,0:T(8,128)(2,1)}, u32[]{:S(2)}) copy-start(bf16[256,128]{1,0:T(8,128)(2,1)} %write_ref.3) | copy-start | bytes 196612
  2.8 0.8 %copy-start.9 = (f32[40,256]{1,0:T(8,128)S(1)}, f32[40,256]{1,0:T(8,128)}, u32[]{:S(2)}) copy-start(f32[40,256]{1,0:T(8,128)} %logits_ref.1) | copy-start | bytes 122884
  3.6 0.7 copy-start.10
  4.3 0.7 copy-start.11
  5.0 0.7 copy-start.12
  5.6 0.7 copy-start.13
  9.7 1.7 %collective-permute-start = (bf16[64,2688]{1,0:T(8,128)(2,1)S(1)}, bf16[64,2688]{1,0:T(8,128)(2,1)S(1)}, u32[]{:S(2)}, u32[]{:S(2)}) collective-permute-start(bf16[64,2688]{1,0:T(8,128)(2,1)S(1)} %get-tuple-element.20), channel_id=1, source_target_pairs={{0,1},{1,0},{2,3},{3,2},{4,5},{5,4},{6,7},{7,6},{8,9},{9,8},{10,11... | collective-permute-start | bytes 1032200 | tf_op jit(solution)/shard_map/ppermute | solution.py:563
  11.4 24.8 %copy-start.6 = (bf16[256,2560]{1,0:T(8,128)(2,1)S(1)}, bf16[256,2560]{1,0:T(8,128)(2,1)}, u32[]{:S(2)}) copy-start(bf16[256,2560]{1,0:T(8,128)(2,1)} %gate_ref.1) | copy-start | bytes 3932164
  11.7 24.5 %copy-start.15 = (f32[2560]{0:T(1024)S(1)}, f32[2560]{0:T(1024)}, u32[]{:S(2)}) copy-start(f32[2560]{0:T(1024)} %param.24) | copy-start | bytes 30724
  11.7 24.6 %copy-start.3 = (bf16[256,128]{1,0:T(8,128)(2,1)S(1)}, bf16[256,128]{1,0:T(8,128)(2,1)}, u32[]{:S(2)}) copy-start(bf16[256,128]{1,0:T(8,128)(2,1)} %read_ref.3) | copy-start | bytes 196612
  11.7 24.5 %copy-start.5 = (bf16[256,2560]{1,0:T(8,128)(2,1)S(1)}, bf16[256,2560]{1,0:T(8,128)(2,1)}, u32[]{:S(2)}) copy-start(bf16[256,2560]{1,0:T(8,128)(2,1)} %signal_ref.3) | copy-start | bytes 3932164
  11.7 24.5 %copy-start.8 = (bf16[256,128]{1,0:T(8,128)(2,1)S(1)}, bf16[256,128]{1,0:T(8,128)(2,1)}, u32[]{:S(2)}) copy-start(bf16[256,128]{1,0:T(8,128)(2,1)} %write_ref.3) | copy-start | bytes 196612
  11.7 24.5 %copy-start.14 = (f32[40]{0:T(128)S(1)}, f32[40]{0:T(128)}, u32[]{:S(2)}) copy-start(f32[40]{0:T(128)} %param.23) | copy-start | bytes 484
  11.7 8.4 %collective-permute-start.1 = (bf16[32,2688]{1,0:T(8,128)(2,1)S(1)}, bf16[32,2688]{1,0:T(8,128)(2,1)S(1)}, u32[]{:S(2)}, u32[]{:S(2)}) collective-permute-start(bf16[32,2688]{1,0:T(8,128)(2,1)S(1)} %get-tuple-element.22), channel_id=1, source_target_pairs={{0,4},{4,8},{8,12},{1,5},{5,9},{9,13},{2,6},{6,10},{10,14},{3,7},{... | collective-permute-start | bytes 516104 | tf_op jit(solution)/shard_map/ppermute | solution.py:374
  13.2 7.0 %collective-permute-start.2 = (bf16[32,2688]{1,0:T(8,128)(2,1)S(1)}, bf16[32,2688]{1,0:T(8,128)(2,1)S(1)}, u32[]{:S(2)}, u32[]{:S(2)}) collective-permute-start(bf16[32,2688]{1,0:T(8,128)(2,1)S(1)} %get-tuple-element.23), channel_id=1, source_target_pairs={{0,8},{1,9},{2,10},{3,11},{16,24},{17,25},{18,26},{19,27}} | collective-permute-start | bytes 516104 | tf_op jit(solution)/shard_map/ppermute | solution.py:375
  20.2 10.9 %collective-permute-start.3 = (bf16[32,2560]{1,0:T(8,128)(2,1)S(1)}, bf16[32,2560]{1,0:T(8,128)(2,1)S(1)}, u32[]{:S(2)}, u32[]{:S(2)}) collective-permute-start(bf16[32,2560]{1,0:T(8,128)(2,1)S(1)} %middle_state.1), channel_id=1, source_target_pairs={{0,4},{4,8},{8,12},{1,5},{5,9},{9,13},{2,6},{6,10},{10,14},{3,7},{... | collective-permute-start | bytes 491528 | tf_op jit(solution)/shard_map/ppermute | solution.py:379
  21.5 13.4 %collective-permute-start.4 = (bf16[32,2560]{1,0:T(8,128)(2,1)S(1)}, bf16[32,2560]{1,0:T(8,128)(2,1)S(1)}, u32[]{:S(2)}, u32[]{:S(2)}) collective-permute-start(bf16[32,2560]{1,0:T(8,128)(2,1)S(1)} %middle_state.1), channel_id=1, source_target_pairs={{4,12},{5,13},{6,14},{7,15},{20,28},{21,29},{22,30},{23,31}} | collective-permute-start | bytes 491528 | tf_op jit(solution)/shard_map/ppermute | solution.py:380
  36.2 7.1 %collective-permute-start.5 = (bf16[64,2560]{1,0:T(8,128)(2,1)}, bf16[64,2560]{1,0:T(8,128)(2,1)S(1)}, u32[]{:S(2)}, u32[]{:S(2)}) collective-permute-start(bf16[64,2560]{1,0:T(8,128)(2,1)} %get-tuple-element.26), channel_id=1, source_target_pairs={{0,1},{1,0},{2,3},{3,2},{4,5},{5,4},{6,7},{7,6},{8,9},{9,8},{10,11... | collective-permute-start | bytes 983048 | tf_op jit(solution)/shard_map/ppermute | solution.py:568
  45.4 4.7 %copy-start = (bf16[2560,2560]{1,0:T(8,128)(2,1)S(1)}, bf16[2560,2560]{1,0:T(8,128)(2,1)}, u32[]{:S(2)}) copy-start(bf16[2560,2560]{1,0:T(8,128)(2,1)} %weight_ref.7) | copy-start | bytes 39321604
  51.4 18.6 %collective-permute-start.8 = (bf16[256,512]{1,0:T(8,128)(2,1)S(1)}, bf16[256,512]{1,0:T(8,128)(2,1)S(1)}, u32[]{:S(2)}, u32[]{:S(2)}) collective-permute-start(bf16[256,512]{1,0:T(8,128)(2,1)S(1)} %project.6), channel_id=1, source_target_pairs={{0,2},{2,0},{1,3},{3,1},{4,6},{6,4},{5,7},{7,5},{8,10},{10,8},{9,1... | collective-permute-start | bytes 786440 | tf_op jit(solution)/shard_map/ppermute | solution.py:506
  54.2 15.8 %collective-permute-start.9 = (bf16[256,512]{1,0:T(8,128)(2,1)S(1)}, bf16[256,512]{1,0:T(8,128)(2,1)S(1)}, u32[]{:S(2)}, u32[]{:S(2)}) collective-permute-start(bf16[256,512]{1,0:T(8,128)(2,1)S(1)} %project.7), channel_id=1, source_target_pairs={{0,2},{2,0},{1,3},{3,1},{4,6},{6,4},{5,7},{7,5},{8,10},{10,8},{9,1... | collective-permute-start | bytes 786440 | tf_op jit(solution)/shard_map/ppermute | solution.py:506
  54.8 4.7 %copy-start.1 = (bf16[2560,2560]{1,0:T(8,128)(2,1)S(1)}, bf16[2560,2560]{1,0:T(8,128)(2,1)}, u32[]{:S(2)}) copy-start(bf16[2560,2560]{1,0:T(8,128)(2,1)} %weight_ref.7) | copy-start | bytes 39321604
  60.0 9.9 %collective-permute-start.7 = (bf16[256,256]{1,0:T(8,128)(2,1)S(1)}, bf16[256,256]{1,0:T(8,128)(2,1)S(1)}, u32[]{:S(2)}, u32[]{:S(2)}) collective-permute-start(bf16[256,256]{1,0:T(8,128)(2,1)S(1)} %project.5), channel_id=1, source_target_pairs={{0,2},{2,0},{1,3},{3,1},{4,6},{6,4},{5,7},{7,5},{8,10},{10,8},{9,1... | collective-permute-start | bytes 393224 | tf_op jit(solution)/shard_map/ppermute | solution.py:506
  61.6 8.4 %collective-permute-start.6 = (f32[8,256]{1,0:T(8,128)S(1)}, f32[8,256]{1,0:T(8,128)S(1)}, u32[]{:S(2)}, u32[]{:S(2)}) collective-permute-start(f32[8,256]{1,0:T(8,128)S(1)} %get-tuple-element.31.squares_ref), channel_id=1, source_target_pairs={{0,2},{2,0},{1,3},{3,1},{4,6},{6,4},{5,7},{7,5},{8,10},{10,8},{9,1... | collective-permute-start | bytes 24584 | tf_op jit(solution)/shard_map/ppermute | solution.py:508
  62.1 4.7 %copy-start.2 = (bf16[2560,2560]{1,0:T(8,128)(2,1)S(1)}, bf16[2560,2560]{1,0:T(8,128)(2,1)}, u32[]{:S(2)}) copy-start(bf16[2560,2560]{1,0:T(8,128)(2,1)} %weight_ref.7) | copy-start | bytes 39321604

commit v2 on v1

v2 whole, which is shorter than its diff:
```python
import functools

import jax
import jax.numpy as jnp
from jax import lax
from jax.experimental import pallas as pl
from jax.experimental.pallas import tpu as pltpu
from jax.sharding import PartitionSpec as P

HEAD_DIM = 64
STATE = 128
HALF = STATE // 2
PART = HALF // 2
STRETCH = 256
BANDS = 12
INNER = 5120
LANES = 128
CHUNK = 256

EPSILON = 1e-05
HIGHEST = lax.Precision.HIGHEST
F32 = jnp.float32
BF16 = jnp.bfloat16
MIB = 1 << 20


def dot(a, b):
    return lax.dot_general(a, b, (((1,), (0,)), ((), ())), preferred_element_type=F32)


def dot_rows(a, b):
    return lax.dot_general(a, b, (((0,), (0,)), ((), ())), preferred_element_type=F32)


def pieces(x):
    high = x.astype(BF16)
    rest = x - high.astype(F32)
    middle = rest.astype(BF16)
    return high, middle, (rest - middle.astype(F32)).astype(BF16)


def head_of_lane(heads, lanes, group, first=0):
    row = lax.broadcasted_iota(jnp.int32, (heads, lanes), 0)
    lane = lax.broadcasted_iota(jnp.int32, (heads, lanes), 1)
    return (row == first + lax.shift_right_logical(lane, group)).astype(F32).astype(BF16)


def spread_tokens(values, heads_map):
    return sum(dot_rows(piece, heads_map) for piece in pieces(values))


def spread_heads(row, heads_map):
    return sum(dot(piece, heads_map) for piece in pieces(jnp.broadcast_to(row, (8, row.shape[1]))))[:1]


def diagonal(rows, lanes):
    return lax.broadcasted_iota(jnp.int32, (rows, lanes), 0) == lax.broadcasted_iota(
        jnp.int32, (rows, lanes), 1
    )


def to_column(row):
    count = row.shape[1]
    return jnp.sum(jnp.where(diagonal(count, count), row, 0.0), axis=1, keepdims=True)


def decay_block(row, rows):
    place = lax.broadcasted_iota(jnp.int32, (rows, LANES), 0)
    high, middle, low = (piece.astype(F32) for piece in pieces(row))
    block = jnp.where(place == 0, high, jnp.where(place == 1, middle, jnp.where(place == 2, low, 0.0)))
    return block.astype(BF16)


def decay_row(block):
    return jnp.sum(block.astype(F32), axis=0, keepdims=True)


def decay_lanes(block, heads_map):
    return jnp.sum(dot(block[:16], heads_map), axis=0, keepdims=True)


def column_block(width):
    return width // 5 if width % (5 * LANES) == 0 else width


def local_call(body, name, outs, args, scratch=(), limit=32 * MIB, flops=0, after=()):
    size = sum(a.size * a.dtype.itemsize for a in args) + sum(o.size * o.dtype.itemsize for o in outs)

    def kernel(*refs):
        body(*refs[: len(args)], *refs[len(args) + len(after) :])

    return pl.pallas_call(
        kernel,
        name=name,
        out_shape=outs,
        in_specs=[pl.BlockSpec(memory_space=pltpu.VMEM)] * len(args)
        + [pl.BlockSpec(memory_space=pl.ANY)] * len(after),
        out_specs=[pl.BlockSpec(memory_space=pltpu.VMEM)] * len(outs),
        scratch_shapes=list(scratch),
        compiler_params=pltpu.CompilerParams(vmem_limit_bytes=limit),
        cost_estimate=pl.CostEstimate(flops=flops, bytes_accessed=size, transcendentals=0),
    )(*args, *after)


def whole(a):
    return pl.BlockSpec(a.shape, lambda i: (0,) * a.ndim)


IN_VMEM = pl.BlockSpec(memory_space=pltpu.VMEM)


def in_hbm(*arrays):
    return [pltpu.with_memory_space_constraint(a, pltpu.HBM) for a in arrays]


def state_kernel(
    band_ref,
    logits_ref,
    mask_ref,
    offset_ref,
    decay_log_ref,
    step_offset_ref,
    write_ref,
    signal_ref,
    running_ref,
    weight_ref,
    decay_ref,
    keep_ref,
    send_ref,
    tail_ref,
    state_ref,
):
    heads, tokens = logits_ref.shape
    block = signal_ref.shape[1]
    width = keep_ref.shape[1]
    core = lax.axis_index("band")
    at = pl.program_id(0)

    @pl.when(at == 0)
    def _():
        offset = to_column(step_offset_ref[...] + offset_ref[pl.ds(band_ref[0], 1), :])
        raw = logits_ref[...] + offset
        step_size = jnp.maximum(raw, 0.0) + jnp.log1p(jnp.exp(-jnp.abs(raw)))
        log_decay = step_size * to_column(-jnp.exp(decay_log_ref[...]))
        earlier = lax.broadcasted_iota(jnp.int32, (tokens, tokens), 0)
        later = lax.broadcasted_iota(jnp.int32, (tokens, tokens), 1)
        running = lax.dot_general(
            log_decay,
            (earlier <= later).astype(F32),
            (((1,), (0,)), ((), ())),
            precision=HIGHEST,
            preferred_element_type=F32,
        )
        weight = step_size * mask_ref[...].astype(F32)
        running_ref[...] = running
        weight_ref[...] = weight
        total = running[:, tokens - 1 : tokens]
        tail_ref[...] = jnp.exp(total - running) * weight
        row = jnp.sum(jnp.where(diagonal(heads, LANES), jnp.exp(total), 0.0), axis=0, keepdims=True)
        send_ref[:, width:] = decay_block(row, HALF)
        decay_ref[...] = decay_block(row, 16)

    heads_map = head_of_lane(heads, block, 6, at * (block // HEAD_DIM))
    scaled = (signal_ref[...].astype(F32) * spread_tokens(tail_ref[...], heads_map)).astype(BF16)
    state_ref[...] = dot_rows(write_ref[...], scaled)
    own = pl.multiple_of(core * HALF, HALF)
    other = pl.multiple_of((1 - core) * HALF, HALF)
    lanes = pl.ds(pl.multiple_of(at * block, LANES), block)
    keep_ref[:, lanes] = state_ref[pl.ds(own, HALF), :]
    send_ref[:, lanes] = state_ref[pl.ds(other, HALF), :].astype(BF16)


def own_state(stretch_band, small, write_proj, signal):
    tokens, width = signal.shape
    heads = small[0].shape[0]
    block = column_block(width)
    return pl.pallas_call(
        state_kernel,
        name="own_state",
        out_shape=[
            jax.ShapeDtypeStruct((heads, tokens), F32),
            jax.ShapeDtypeStruct((heads, tokens), F32),
            jax.ShapeDtypeStruct((16, LANES), BF16),
            jax.ShapeDtypeStruct((HALF, width), F32),
            jax.ShapeDtypeStruct((HALF, width + LANES), BF16),
        ],
        grid=(width // block,),
        in_specs=[pl.BlockSpec(memory_space=pltpu.SMEM)]
        + [whole(a) for a in (*small, write_proj)]
        + [pl.BlockSpec((tokens, block), lambda i: (0, i))],
        out_specs=[IN_VMEM] * 5,
        scratch_shapes=[pltpu.VMEM((heads, tokens), F32), pltpu.VMEM((STATE, block), F32)],
        compiler_params=pltpu.CompilerParams(vmem_limit_bytes=16 * MIB),
        cost_estimate=pl.CostEstimate(
            flops=4 * tokens * width * STATE, bytes_accessed=tokens * width * 2, transcendentals=0
        ),
    )(stretch_band, *in_hbm(*small, write_proj, signal))


def local_kernel(
    running_ref,
    weight_ref,
    decay_ref,
    got_ref,
    after_ref,
    skip_ref,
    write_ref,
    read_ref,
    signal_ref,
    gate_ref,
    base_ref,
    factor_ref,
    lanes_ref,
    scores_ref,
):
    heads, tokens = running_ref.shape
    block = signal_ref.shape[1]
    width = base_ref.shape[1]
    at = pl.program_id(0)
    half = tokens // 2

    @pl.when(at == 0)
    def _():
        scores = lax.dot_general(
            read_ref[...], write_ref[...], (((1,), (1,)), ((), ())), preferred_element_type=F32
        )
        row = lax.broadcasted_iota(jnp.int32, scores.shape, 0)
        lane = lax.broadcasted_iota(jnp.int32, scores.shape, 1)
        scores_ref[...] = jnp.where(row >= lane, scores, 0.0)
        core = lax.axis_index("band")
        mine, got = decay_ref[...].astype(F32), got_ref[:16, width:].astype(F32)
        first = jnp.where(core == 0, mine, got).astype(BF16)
        lanes_ref[...] = jnp.broadcast_to(
            decay_lanes(first, head_of_lane(LANES, width, 6)), lanes_ref.shape
        )

    running = running_ref[...]
    first_head = at * (block // HEAD_DIM)
    wide = spread_tokens(running, head_of_lane(heads, block * 2, 7, first_head))
    heads_map = head_of_lane(heads, block, 6, first_head)
    gate = gate_ref[...].astype(F32)
    gate = gate / (1.0 + jnp.exp(-gate))
    out_lanes = pl.ds(pl.multiple_of(at * block, LANES), block)
    factor_ref[:, out_lanes] = spread_tokens(jnp.exp(running), heads_map) * gate
    skip = spread_heads(skip_ref[...], heads_map)
    low_lanes = lax.broadcasted_iota(jnp.int32, (half, LANES), 1) < HEAD_DIM
    early, late = slice(0, half), slice(half, tokens)
    for pair in range(block // LANES):
        lanes = slice(pair * LANES, (pair + 1) * LANES)
        values = signal_ref[:, lanes]
        top, bottom = [], []
        for k in (2 * pair, 2 * pair + 1):
            row = running_ref[pl.ds(first_head + k, 1), :]
            weight = weight_ref[pl.ds(first_head + k, 1), :]
            column = wide[:, k * LANES : (k + 1) * LANES]

            def mixing(rows, cols):
                span = jnp.minimum(column[rows] - row[:, cols], 0.0)
                return (jnp.exp(span) * scores_ref[rows, cols] * weight[:, cols]).astype(BF16)

            top.append(mixing(early, early))
            bottom.append(jnp.concatenate([mixing(late, early), mixing(late, late)], axis=1))
        top = dot(jnp.concatenate(top, axis=0), values[early])
        bottom = dot(jnp.concatenate(bottom, axis=0), values)
        skipped = values.astype(F32) * skip[:, lanes]
        out_lanes = pl.ds(pl.multiple_of(at * block + pair * LANES, LANES), LANES)
        base_ref[early, out_lanes] = (
            jnp.where(low_lanes, top[:half], top[half:]) + skipped[early]
        ) * gate[early, lanes]
        base_ref[late, out_lanes] = (
            jnp.where(low_lanes, bottom[:half], bottom[half:]) + skipped[late]
        ) * gate[late, lanes]


def local_part(running, weight, decay, got, after, skip_gain, write_proj, read_proj, signal, gate_branch):
    tokens, width = signal.shape
    heads = running.shape[0]
    block = column_block(width)
    cols = pl.BlockSpec((tokens, block), lambda i: (0, i))
    return pl.pallas_call(
        local_kernel,
        name="local_part",
        out_shape=[jax.ShapeDtypeStruct((tokens, width), F32)] * 2
        + [jax.ShapeDtypeStruct((8, width), F32)],
        grid=(width // block,),
        in_specs=[IN_VMEM] * 4
        + [pl.BlockSpec(memory_space=pl.ANY)]
        + [whole(a) for a in (skip_gain, write_proj, read_proj)]
        + [cols, cols],
        out_specs=[IN_VMEM] * 3,
        scratch_shapes=[pltpu.VMEM((tokens, tokens), F32)],
        compiler_params=pltpu.CompilerParams(vmem_limit_bytes=24 * MIB),
        cost_estimate=pl.CostEstimate(
            flops=6 * heads * tokens * tokens * HEAD_DIM,
            bytes_accessed=tokens * width * 12,
            transcendentals=heads * tokens * tokens,
        ),
    )(
        running,
        weight,
        decay,
        got,
        after,
        *in_hbm(skip_gain, write_proj, read_proj, signal, gate_branch),
    )


def stage_kernel(*refs):
    count = (len(refs) - 2) // 2
    copies = [
        pltpu.make_async_copy(refs[i], refs[count + 1 + i], refs[-1].at[i]) for i in range(count)
    ]
    for copy in copies:
        copy.start()
    for copy in copies:
        copy.wait()


def stage(arrays, after):
    size = sum(a.size * a.dtype.itemsize for a in arrays)
    return pl.pallas_call(
        stage_kernel,
        name="stage",
        out_shape=[jax.ShapeDtypeStruct(a.shape, a.dtype) for a in arrays],
        in_specs=[pl.BlockSpec(memory_space=pltpu.HBM)] * len(arrays) + [pl.BlockSpec(memory_space=pl.ANY)],
        out_specs=[IN_VMEM] * len(arrays),
        scratch_shapes=[pltpu.SemaphoreType.DMA((len(arrays),))],
        compiler_params=pltpu.CompilerParams(vmem_limit_bytes=4 * MIB),
        cost_estimate=pl.CostEstimate(flops=0, bytes_accessed=2 * size, transcendentals=0),
    )(*in_hbm(*arrays), after)


def chip_kernel(keep_ref, got_ref, decay_ref, state_ref, first_ref, second_ref):
    width = keep_ref.shape[1]
    core = lax.axis_index("band")
    chip = lax.axis_index("scan")
    heads_map = head_of_lane(LANES, width, 6)
    got_decay = got_ref[:16, width:]
    mine = decay_ref[...]
    later = jnp.where(core == 0, got_decay.astype(F32), mine.astype(F32)).astype(BF16)
    lanes = decay_lanes(later, heads_map)
    got = got_ref[:, :width].astype(F32)
    keep = keep_ref[...]
    early, late = jnp.where(core == 0, keep, got), jnp.where(core == 0, got, keep)
    state_ref[:, :width] = (early * lanes + late).astype(BF16)
    block = decay_block(decay_row(got_decay) * decay_row(mine), PART)
    state_ref[:PART, width:] = block
    state_ref[PART:, width:] = block
    second_ref[...] = state_ref[PART:, :]
    first_ref[...] = state_ref[pl.ds(pl.multiple_of(jnp.where(chip == 1, PART, 0), PART), PART), :]


def middle_kernel(state_ref, near_ref, far_ref, out_ref, lanes_ref):
    width = out_ref.shape[1]
    chip = lax.axis_index("scan")

    @pl.when(chip == 0)
    def _():
        out_ref[...] = state_ref[PART:, :width]

    @pl.when(chip == 1)
    def _():
        lanes = decay_lanes(state_ref[:16, width:], head_of_lane(LANES, width, 6))
        out_ref[...] = (
            lanes * near_ref[:, :width].astype(F32) + state_ref[:PART, :width].astype(F32)
        ).astype(BF16)

    @pl.when(chip > 1)
    def _():
        heads_map = head_of_lane(LANES, width, 6)
        lanes = decay_lanes(near_ref[:16, width:], heads_map)
        lanes_ref[...] = jnp.broadcast_to(lanes, lanes_ref.shape)

        @pl.when(chip == 2)
        def _():
            entered = lanes * far_ref[:, :width].astype(F32) + near_ref[:, :width].astype(F32)
            own = decay_lanes(state_ref[:16, width:], heads_map)
            out_ref[...] = (own * entered + state_ref[PART:, :width].astype(F32)).astype(BF16)


def enter_kernel(
    near_ref, far_ref, next_ref, skip_ref, near_lanes_ref, keep_ref, got_ref, lanes_ref, mine_ref, send_ref
):
    width = keep_ref.shape[1]
    chip = lax.axis_index("scan")

    def parts(first, second):
        enter = jnp.concatenate([first.astype(F32), second.astype(F32)], axis=0)
        share_enter(enter, keep_ref, got_ref, lanes_ref, mine_ref, send_ref)

    @pl.when(chip == 0)
    def _():
        share_enter(jnp.zeros((HALF, width), F32), keep_ref, got_ref, lanes_ref, mine_ref, send_ref)

    @pl.when(chip == 1)
    def _():
        parts(near_ref[:, :width], next_ref[...])

    @pl.when(chip == 2)
    def _():
        near = near_ref[:, :width].astype(F32)
        parts(next_ref[...], near_lanes_ref[:1] * far_ref[:, :width].astype(F32) + near)

    @pl.when(chip == 3)
    def _():
        near = near_ref[:, :width].astype(F32)
        parts(near_lanes_ref[:1] * skip_ref[...].astype(F32) + near, next_ref[...])


def share_enter(enter, keep_ref, got_ref, lanes_ref, mine_ref, send_ref):
    width = keep_ref.shape[1]
    core = lax.axis_index("band")

    @pl.when(core == 0)
    def _():
        mine_ref[...] = enter.astype(BF16)
        send_ref[...] = (lanes_ref[:1] * enter + keep_ref[...]).astype(BF16)

    @pl.when(core == 1)
    def _():
        send_ref[...] = enter.astype(BF16)
        mine_ref[...] = (lanes_ref[:1] * enter + got_ref[:, :width].astype(F32)).astype(BF16)


def gathered_kernel(all_ref, keep_ref, got_ref, lanes_ref, mine_ref, send_ref, enter_ref):
    width = keep_ref.shape[1]
    chip = lax.axis_index("scan")
    heads_map = head_of_lane(LANES, width, 6)
    enter_ref[...] = jnp.zeros(enter_ref.shape, F32)
    for source in range(all_ref.shape[0]):

        @pl.when(source < chip)
        def _():
            lanes = decay_lanes(all_ref[source, :16, width:], heads_map)
            enter_ref[...] = lanes * enter_ref[...] + all_ref[source, :, :width].astype(F32)

    share_enter(enter_ref[...], keep_ref, got_ref, lanes_ref, mine_ref, send_ref)


def chip_state(keep, got, decay):
    width = keep.shape[1]
    return local_call(
        chip_kernel,
        "chip_state",
        [
            jax.ShapeDtypeStruct((HALF, width + LANES), BF16),
            jax.ShapeDtypeStruct((PART, width + LANES), BF16),
            jax.ShapeDtypeStruct((PART, width + LANES), BF16),
        ],
        (keep, got, decay),
    )


def entering_state(chips, state, first, second, keep, got, local, constants):
    width = keep.shape[1]
    half = jax.ShapeDtypeStruct((HALF, width), BF16)
    if chips != 4:
        gathered = lax.all_gather(state, "scan", axis=0)
        base, factor, lanes = local(first)
        mine, give = local_call(
            gathered_kernel,
            "enter_state",
            [half, half],
            (gathered, keep, got, lanes),
            (pltpu.VMEM((HALF, width), F32),),
        )
        return mine, give, base, factor, stage(constants, lanes)
    near = lax.ppermute(first, "scan", [(0, 1), (1, 2), (2, 3)])
    far = lax.ppermute(second, "scan", [(0, 2)])
    base, factor, lanes = local(first)
    middle, near_lanes = local_call(
        middle_kernel,
        "middle_state",
        [jax.ShapeDtypeStruct((PART, width), BF16), jax.ShapeDtypeStruct((8, width), F32)],
        (state, near, far),
        after=(lanes,),
    )
    following = lax.ppermute(middle, "scan", [(0, 1), (1, 2), (2, 3)])
    skipping = lax.ppermute(middle, "scan", [(1, 3)])
    staged = stage(constants, middle)
    mine, give = local_call(
        enter_kernel,
        "enter_state",
        [half, half],
        (near, far, following, skipping, near_lanes, keep, got, lanes),
        after=(staged[0],),
    )
    return mine, give, base, factor, staged


def gated_kernel(mine_ref, other_ref, base_ref, factor_ref, read_ref, gain_ref, out_ref, square_ref):
    core = lax.axis_index("band")
    tokens, width = base_ref.shape
    block = column_block(width)
    is_first = core == 0
    read = read_ref[...]
    sums = jnp.zeros((tokens, LANES), F32)
    for first in range(0, width, block):
        lanes = slice(first, first + block)
        mine, other = mine_ref[:, lanes].astype(F32), other_ref[:, lanes].astype(F32)
        low = jnp.where(is_first, mine, other).astype(BF16)
        high = jnp.where(is_first, other, mine).astype(BF16)
        carried = dot(read, jnp.concatenate([low, high], axis=0))
        gated = base_ref[:, lanes] + factor_ref[:, lanes] * carried
        out_ref[:, lanes] = (gated * gain_ref[:, lanes]).astype(BF16)
        squares = gated * gated
        sums += sum(squares[:, k : k + LANES] for k in range(0, block, LANES))
    square_ref[...] = jnp.broadcast_to(jnp.sum(sums.T, axis=0, keepdims=True), square_ref.shape)


def gated_part(mine, other, base, factor, read_proj, norm_gain):
    tokens, width = base.shape
    return local_call(
        gated_kernel,
        "gated_part",
        [
            jax.ShapeDtypeStruct((tokens, width), BF16),
            jax.ShapeDtypeStruct((8, tokens), F32),
        ],
        (mine, other, base, factor, read_proj, norm_gain),
        flops=2 * tokens * width * STATE,
    )


def project_kernel(other, first, gated_ref, weight_ref, out_ref):
    columns = weight_ref.shape[1] // 2
    member = lax.axis_index("tensor")
    start = (1 - member if other else member) * columns + first
    for k in range(0, out_ref.shape[1], CHUNK):
        lanes = pl.ds(pl.multiple_of(start + k, LANES), CHUNK)
        out_ref[:, k : k + CHUNK] = dot(gated_ref[...], weight_ref[:, lanes]).astype(out_ref.dtype)


def project(other, first, count, dtype, gated, weight, after=()):
    tokens, width = gated.shape
    (result,) = local_call(
        functools.partial(project_kernel, other, first * CHUNK),
        "project",
        [jax.ShapeDtypeStruct((tokens, count * CHUNK), dtype)],
        (gated, weight),
        flops=2 * tokens * width * count * CHUNK,
        after=after,
    )
    return result


def finish_kernel(squares_ref, other_squares_ref, own_ref, *refs):
    *got_refs, out_ref = refs
    mean = (squares_ref[...] + other_squares_ref[...]) / INNER
    scale = lax.rsqrt(mean[:1] + EPSILON)
    scale = jnp.broadcast_to(scale, (LANES, scale.shape[1])).T
    first = 0
    for got_ref in got_refs:
        for k in range(0, got_ref.shape[1], LANES):
            lanes = slice(first + k, first + k + LANES)
            total = own_ref[:, lanes] + got_ref[:, k : k + LANES].astype(F32)
            out_ref[:, lanes] = (total * scale).astype(BF16)
        first += got_ref.shape[1]


SENDS = (1, 2, 2)


def layer_columns(members, gated, squares, weight):
    tokens = gated.shape[0]
    columns = weight.shape[1] // members
    if members != 2 or columns != CHUNK * sum(SENDS):
        mean = lax.psum(squares[0], "tensor") / INNER
        partial = dot(gated, weight).astype(BF16)
        total = lax.psum_scatter(partial, "tensor", scatter_dimension=1, tiled=True)
        return (total.astype(F32) * lax.rsqrt(mean + EPSILON)[:, None]).astype(BF16)
    swap = [(0, 1), (1, 0)]
    got, first, done = [], 0, ()
    for count in SENDS:
        part = project(True, first, count, BF16, gated, weight, done)
        got.append(lax.ppermute(part, "tensor", swap))
        first, done = first + count, (part,)
    other_squares = lax.ppermute(squares, "tensor", swap)
    own = project(False, 0, first, F32, gated, weight, done)
    (result,) = local_call(
        finish_kernel,
        "finish",
        [jax.ShapeDtypeStruct((tokens, columns), BF16)],
        (squares, other_squares, own, *got),
    )
    return result


def on_device(
    chips,
    members,
    signal,
    gate_branch,
    write_proj,
    read_proj,
    step_logits,
    valid_mask,
    stretch_band,
    band_offset,
    decay_log,
    step_offset,
    skip_gain,
    norm_gain,
    out_weight,
):
    small = (step_logits, valid_mask[None], band_offset, decay_log[None], step_offset[None])
    running, weight, decay, keep, send = own_state(stretch_band, small, write_proj, signal)
    cores = [(0, 1), (1, 0)]
    got = lax.ppermute(send, "band", cores)
    state, first, second = chip_state(keep, got, decay)

    def local(after):
        return local_part(
            running,
            weight,
            decay,
            got,
            after,
            skip_gain[None],
            write_proj,
            read_proj,
            signal,
            gate_branch,
        )

    mine, give, base, factor, staged = entering_state(
        chips, state, first, second, keep, got, local, (out_weight, read_proj, norm_gain[None])
    )
    other = lax.ppermute(give, "band", cores)
    weight, read, gain = staged
    gated, squares = gated_part(mine, other, base, factor, read, gain)
    return layer_columns(members, gated, squares, weight)


def solution(mesh):
    placed = (
        P(("group", "scan", "band"), "tensor"),
        P(("group", "scan", "band"), "tensor"),
        P(("group", "scan", "band"), None),
        P(("group", "scan", "band"), None),
        P("tensor", ("group", "scan", "band")),
        P(("group", "scan", "band")),
        P(("group", "scan", "band")),
        P(None, "tensor"),
        P("tensor"),
        P("tensor"),
        P("tensor"),
        P("tensor"),
        P("tensor", None),
    )
    return jax.shard_map(
        functools.partial(on_device, mesh.shape["scan"], mesh.shape["tensor"]),
        mesh=mesh,
        in_specs=placed,
        out_specs=P(("group", "scan", "band"), "tensor"),
        check_vma=False,
    )
```

time: 71.6 us -> 56 us (0.78)
  the two profiles are of different devices: /device:TPU:24 before, /device:TPU:0 now
where the time goes in v2:
time: 56 us; the launch traced here: 55.7 us
  Pallas kernels  23.8 us (42%)
  starting transfers between devices  16.5 us (29%)
  waiting for transfers between devices  14 us (25%)
  between operations  0.82 us (1%)
  local copies, waits for them, and re-layouts  0.61 us (1%)
    ppermute x1, waiting for transfers between devices, layer_columns(): other_squares = lax.ppermute(squares, 'tensor', swap)  11 us
    pallas_call x1, Pallas kernels, local_part(): pl.pallas_call(local_kernel, name='local_part', out_shape=[jax.ShapeDtype...  7.49 us
    pallas_call x9, Pallas kernels, local_call(): pl.pallas_call(kernel, name=name, out_shape=outs, in_specs=[pl.BlockSpec(...  6.44 us
    ppermute x1, starting transfers between devices, entering_state(): far = lax.ppermute(second, 'scan', [(0, 2)])  5.88 us
    pallas_call x1, Pallas kernels, own_state(): pl.pallas_call(state_kernel, name='own_state', out_shape=[jax.ShapeDtypeS...  5.13 us
    pallas_call x1, Pallas kernels, stage(): pl.pallas_call(stage_kernel, name='stage', out_shape=[jax.ShapeDtypeStruc...  4.75 us
    ppermute x1, starting transfers between devices, entering_state(): following = lax.ppermute(middle, 'scan', [(0, 1), (1, 2), (2, 3)])  3.99 us
    ppermute x3, starting transfers between devices, layer_columns(): got.append(lax.ppermute(part, 'tensor', swap))  3.58 us
  transfers between devices with their start and end apart: 10, of which 3 were waited for; matrix products, arithmetic and copies ran while one was open for 1% of the time, Pallas kernels for 25%

profile of v2, /device:TPU:0, one launch (start us, length us, event | category | flops | bytes accessed | tf_op | source)
XLA Modules:
  0.0 55.7 jit_solution(17796746750924918941)
XLA Ops:
  0.7 5.1 %own_state.1 = (f32[40,256]{1,0:T(8,128)S(1)}, f32[40,256]{1,0:T(8,128)S(1)}, bf16[16,128]{1,0:T(8,128)(2,1)S(1)}, f32[64,2560]{1,0:T(8,128)S(1)}, bf16[64,2688]{1,0:T(8,128)(2,1)S(1)}) custom-call(s32[1]{0:T(128)S(6)} %copy.14.band_ref, f32[40,256]{1,0:T(8,128)} %logits_ref.1, s32[1,256]{1,0:T(1,128)} %bitcast.4, f32[12,40]{1,0:T(8,128)} %offset_ref.1, ...), custom_call_target="tpu_custom_call" | custom-call | flops 335544320 | bytes 1310720 | tf_op jit(solution)/shard_map/own_state/pallas_call | solution.py:177
  5.8 0.5 collective-permute-start
  6.3 1.3 %collective-permute-done.refs_1_.got_ref.refs_6_ = bf16[64,2688]{1,0:T(8,128)(2,1)S(1)} collective-permute-done((bf16[64,2688]{1,0:T(8,128)(2,1)S(1)}, bf16[64,2688]{1,0:T(8,128)(2,1)S(1)}, u32[]{:S(2)}, u32[]{:S(2)}) %collective-permute-start) | collective-permute-done | bytes 344096 | tf_op jit(solution)/shard_map/ppermute | solution.py:609
  7.6 0.2 chip_state.1
  7.8 5.9 %collective-permute-start.2 = (bf16[32,2688]{1,0:T(8,128)(2,1)S(1)}, bf16[32,2688]{1,0:T(8,128)(2,1)S(1)}, u32[]{:S(2)}, u32[]{:S(2)}) collective-permute-start(bf16[32,2688]{1,0:T(8,128)(2,1)S(1)} %get-tuple-element.29), channel_id=1, source_target_pairs={{0,8},{1,9},{2,10},{3,11},{16,24},{17,25},{18,26},{19,27}} | collective-permute-start | bytes 516104 | tf_op jit(solution)/shard_map/ppermute | solution.py:469
  13.7 1.3 %collective-permute-start.1 = (bf16[32,2688]{1,0:T(8,128)(2,1)S(1)}, bf16[32,2688]{1,0:T(8,128)(2,1)S(1)}, u32[]{:S(2)}, u32[]{:S(2)}) collective-permute-start(bf16[32,2688]{1,0:T(8,128)(2,1)S(1)} %get-tuple-element.28.after_ref), channel_id=1, source_target_pairs={{0,4},{4,8},{8,12},{1,5},{5,9},{9,13},{2,6},{6,10},{10,14},{3,7},{... | collective-permute-start | bytes 516104 | tf_op jit(solution)/shard_map/ppermute | solution.py:468
  15.0 0.0 copy-start
  15.0 7.5 %local_part.1 = (f32[256,2560]{1,0:T(8,128)S(1)}, f32[256,2560]{1,0:T(8,128)S(1)}, f32[8,2560]{1,0:T(8,128)S(1)}) custom-call(f32[40,256]{1,0:T(8,128)S(1)} %get-tuple-element.31.running_ref, f32[40,256]{1,0:T(8,128)S(1)} %get-tuple-element.32.weight_ref, bf16[16,128]{1,0:T(8,128)(2,1)S(1)} %get-tuple-element.27.refs_2_.decay_ref, ...), custom_call_target="tpu_custom_call" | custom-call | flops 1006632960 | bytes 7864320 | tf_op jit(solution)/shard_map/local_part/pallas_call | solution.py:280
  22.5 0.0 collective-permute-done.2.refs_2_.refs_1_
  22.6 0.0 collective-permute-done.1.refs_1_.refs_0_
  22.6 0.7 %collective-permute-start.4 = (bf16[32,2560]{1,0:T(8,128)(2,1)S(1)}, bf16[32,2560]{1,0:T(8,128)(2,1)S(1)}, u32[]{:S(2)}, u32[]{:S(2)}) collective-permute-start(bf16[32,2560]{1,0:T(8,128)(2,1)S(1)} %get-tuple-element.34.refs_3_), channel_id=1, source_target_pairs={{4,12},{5,13},{6,14},{7,15},{20,28},{21,29},{22,30},{23,31}} | collective-permute-start | bytes 491528 | tf_op jit(solution)/shard_map/ppermute | solution.py:479
  23.3 4.0 %collective-permute-start.3 = (bf16[32,2560]{1,0:T(8,128)(2,1)S(1)}, bf16[32,2560]{1,0:T(8,128)(2,1)S(1)}, u32[]{:S(2)}, u32[]{:S(2)}) collective-permute-start(bf16[32,2560]{1,0:T(8,128)(2,1)S(1)} %get-tuple-element.34.refs_3_), channel_id=1, source_target_pairs={{0,4},{4,8},{8,12},{1,5},{5,9},{9,13},{2,6},{6,10},{10,14},{3,7},{... | collective-permute-start | bytes 491528 | tf_op jit(solution)/shard_map/ppermute | solution.py:478
  27.3 0.6 %broadcast_in_dim.19.refs_2_ = f32[1,2560]{1,0:T(1,128)} reshape(f32[2560]{0:T(1024)S(1)} %copy-done) | data formatting | bytes 20480 | tf_op jit(solution)/shard_map/broadcast_in_dim | solution.py:627
  27.9 4.8 %stage.1 = (bf16[2560,2560]{1,0:T(8,128)(2,1)S(1)}, bf16[256,128]{1,0:T(8,128)(2,1)S(1)}, f32[1,2560]{1,0:T(1,128)S(1)}) custom-call(bf16[2560,2560]{1,0:T(8,128)(2,1)} %refs_0_.1, bf16[256,128]{1,0:T(8,128)(2,1)} %refs_1_.1, f32[1,2560]{1,0:T(1,128)} %broadcast_in_dim.19.refs_2_, bf16[32,2560]{1,0:T(8,128)(2,1)S(1)} %get-tuple-element.34.refs_3_), custom_call_target="tpu_custom_call" | custom-call | bytes 26365952 | tf_op jit(solution)/shard_map/stage/pallas_call | solution.py:321
  32.7 0.0 collective-permute-done.4.refs_3_
  32.7 0.0 collective-permute-done.3.refs_2_
  32.7 0.1 enter_state.1
  32.8 0.1 collective-permute-start.5
  32.9 1.6 %collective-permute-done.5.refs_1_ = bf16[64,2560]{1,0:T(8,128)(2,1)S(1)} collective-permute-done((bf16[64,2560]{1,0:T(8,128)(2,1)S(1)}, bf16[64,2560]{1,0:T(8,128)(2,1)S(1)}, u32[]{:S(2)}, u32[]{:S(2)}) %collective-permute-start.5) | collective-permute-done | bytes 327712 | tf_op jit(solution)/shard_map/ppermute | solution.py:629
  34.5 0.9 %gated_part.1 = (bf16[256,2560]{1,0:T(8,128)(2,1)S(1)}, f32[8,256]{1,0:T(8,128)S(1)}) custom-call(bf16[64,2560]{1,0:T(8,128)(2,1)S(1)} %get-tuple-element.37.refs_0_, bf16[64,2560]{1,0:T(8,128)(2,1)S(1)} %collective-permute-done.5.refs_1_, f32[256,2560]{1,0:T(8,128)S(1)} %get-tuple-element.39.refs_2_, f32[256,2560]{1,0:T(8,128)S(1)} %get-tuple-element.40.refs_3_, ...), custom_call_target="tpu_custom_call" | custom-call | flops 167772160 | bytes 7292928 | tf_op jit(solution)/shard_map/gated_part/pallas_call | solution.py:92
  35.4 0.5 project.4.refs_2_
  35.9 0.9 %project.5.refs_2_ = bf16[256,512]{1,0:T(8,128)(2,1)S(1)} custom-call(bf16[256,2560]{1,0:T(8,128)(2,1)S(1)} %get-tuple-element.44.refs_0_, bf16[2560,2560]{1,0:T(8,128)(2,1)S(1)} %get-tuple-element.36.refs_8_.refs_1_, bf16[256,256]{1,0:T(8,128)(2,1)S(1)} %project.4.refs_2_), custom_call_target="tpu_custom_call" | custom-call | flops 671088640 | bytes 14680064 | tf_op jit(solution)/shard_map/project/pallas_call | solution.py:92
  36.8 0.9 %project.6.refs_2_ = bf16[256,512]{1,0:T(8,128)(2,1)S(1)} custom-call(bf16[256,2560]{1,0:T(8,128)(2,1)S(1)} %get-tuple-element.44.refs_0_, bf16[2560,2560]{1,0:T(8,128)(2,1)S(1)} %get-tuple-element.36.refs_8_.refs_1_, bf16[256,512]{1,0:T(8,128)(2,1)S(1)} %project.5.refs_2_), custom_call_target="tpu_custom_call" | custom-call | flops 671088640 | bytes 14680064 | tf_op jit(solution)/shard_map/project/pallas_call | solution.py:92
  37.6 1.6 %collective-permute-start.9 = (bf16[256,512]{1,0:T(8,128)(2,1)S(1)}, bf16[256,512]{1,0:T(8,128)(2,1)S(1)}, u32[]{:S(2)}, u32[]{:S(2)}) collective-permute-start(bf16[256,512]{1,0:T(8,128)(2,1)S(1)} %project.6.refs_2_), channel_id=1, source_target_pairs={{0,2},{2,0},{1,3},{3,1},{4,6},{6,4},{5,7},{7,5},{8,10},{10,8},{9,1... | collective-permute-start | bytes 786440 | tf_op jit(solution)/shard_map/ppermute | solution.py:576
  39.2 0.5 collective-permute-start.8
  39.7 1.5 %collective-permute-start.7 = (bf16[256,256]{1,0:T(8,128)(2,1)S(1)}, bf16[256,256]{1,0:T(8,128)(2,1)S(1)}, u32[]{:S(2)}, u32[]{:S(2)}) collective-permute-start(bf16[256,256]{1,0:T(8,128)(2,1)S(1)} %project.4.refs_2_), channel_id=1, source_target_pairs={{0,2},{2,0},{1,3},{3,1},{4,6},{6,4},{5,7},{7,5},{8,10},{10,8},{9,1... | collective-permute-start | bytes 393224 | tf_op jit(solution)/shard_map/ppermute | solution.py:576
  41.2 0.5 collective-permute-start.6
  41.8 1.9 %project.7.refs_2_ = f32[256,1280]{1,0:T(8,128)S(1)} custom-call(bf16[256,2560]{1,0:T(8,128)(2,1)S(1)} %get-tuple-element.44.refs_0_, bf16[2560,2560]{1,0:T(8,128)(2,1)S(1)} %get-tuple-element.36.refs_8_.refs_1_, bf16[256,512]{1,0:T(8,128)(2,1)S(1)} %project.6.refs_2_), custom_call_target="tpu_custom_call" | custom-call | flops 1677721600 | bytes 15728640 | tf_op jit(solution)/shard_map/project/pallas_call | solution.py:92
  43.6 11.0 %collective-permute-done.6.refs_1_ = f32[8,256]{1,0:T(8,128)S(1)} collective-permute-done((f32[8,256]{1,0:T(8,128)S(1)}, f32[8,256]{1,0:T(8,128)S(1)}, u32[]{:S(2)}, u32[]{:S(2)}) %collective-permute-start.6) | collective-permute-done | bytes 8224 | tf_op jit(solution)/shard_map/ppermute | solution.py:578
  54.7 0.0 collective-permute-done.7.refs_3_
  54.7 0.0 collective-permute-done.8.refs_4_
  54.7 1.1 %finish.1 = bf16[256,1280]{1,0:T(8,128)(2,1)} custom-call(f32[8,256]{1,0:T(8,128)S(1)} %get-tuple-element.43.refs_0_, f32[8,256]{1,0:T(8,128)S(1)} %collective-permute-done.6.refs_1_, f32[256,1280]{1,0:T(8,128)S(1)} %project.7.refs_2_, bf16[256,256]{1,0:T(8,128)(2,1)S(1)} %collective-permute-done.7.refs_3_, ...), custom_call_target="tpu_custom_call" | custom-call | bytes 2637824 | tf_op jit(solution)/shard_map/finish/pallas_call | solution.py:92
  (3 shorter events, 0.0 us)
Async XLA Ops:
  5.8 1.8 %collective-permute-start = (bf16[64,2688]{1,0:T(8,128)(2,1)S(1)}, bf16[64,2688]{1,0:T(8,128)(2,1)S(1)}, u32[]{:S(2)}, u32[]{:S(2)}) collective-permute-start(bf16[64,2688]{1,0:T(8,128)(2,1)S(1)} %get-tuple-element.26), channel_id=1, source_target_pairs={{0,1},{1,0},{2,3},{3,2},{4,5},{5,4},{6,7},{7,6},{8,9},{9,8},{10,11... | collective-permute-start | bytes 1032200 | tf_op jit(solution)/shard_map/ppermute | solution.py:609
  7.8 14.7 %collective-permute-start.2 = (bf16[32,2688]{1,0:T(8,128)(2,1)S(1)}, bf16[32,2688]{1,0:T(8,128)(2,1)S(1)}, u32[]{:S(2)}, u32[]{:S(2)}) collective-permute-start(bf16[32,2688]{1,0:T(8,128)(2,1)S(1)} %get-tuple-element.29), channel_id=1, source_target_pairs={{0,8},{1,9},{2,10},{3,11},{16,24},{17,25},{18,26},{19,27}} | collective-permute-start | bytes 516104 | tf_op jit(solution)/shard_map/ppermute | solution.py:469
  13.7 8.8 %collective-permute-start.1 = (bf16[32,2688]{1,0:T(8,128)(2,1)S(1)}, bf16[32,2688]{1,0:T(8,128)(2,1)S(1)}, u32[]{:S(2)}, u32[]{:S(2)}) collective-permute-start(bf16[32,2688]{1,0:T(8,128)(2,1)S(1)} %get-tuple-element.28.after_ref), channel_id=1, source_target_pairs={{0,4},{4,8},{8,12},{1,5},{5,9},{9,13},{2,6},{6,10},{10,14},{3,7},{... | collective-permute-start | bytes 516104 | tf_op jit(solution)/shard_map/ppermute | solution.py:468
  15.0 12.3 %copy-start = (f32[2560]{0:T(1024)S(1)}, f32[2560]{0:T(1024)}, u32[]{:S(2)}) copy-start(f32[2560]{0:T(1024)} %param.24) | copy-start | bytes 30724
  22.6 10.1 %collective-permute-start.4 = (bf16[32,2560]{1,0:T(8,128)(2,1)S(1)}, bf16[32,2560]{1,0:T(8,128)(2,1)S(1)}, u32[]{:S(2)}, u32[]{:S(2)}) collective-permute-start(bf16[32,2560]{1,0:T(8,128)(2,1)S(1)} %get-tuple-element.34.refs_3_), channel_id=1, source_target_pairs={{4,12},{5,13},{6,14},{7,15},{20,28},{21,29},{22,30},{23,31}} | collective-permute-start | bytes 491528 | tf_op jit(solution)/shard_map/ppermute | solution.py:479
  23.3 9.4 %collective-permute-start.3 = (bf16[32,2560]{1,0:T(8,128)(2,1)S(1)}, bf16[32,2560]{1,0:T(8,128)(2,1)S(1)}, u32[]{:S(2)}, u32[]{:S(2)}) collective-permute-start(bf16[32,2560]{1,0:T(8,128)(2,1)S(1)} %get-tuple-element.34.refs_3_), channel_id=1, source_target_pairs={{0,4},{4,8},{8,12},{1,5},{5,9},{9,13},{2,6},{6,10},{10,14},{3,7},{... | collective-permute-start | bytes 491528 | tf_op jit(solution)/shard_map/ppermute | solution.py:478
  32.8 1.7 %collective-permute-start.5 = (bf16[64,2560]{1,0:T(8,128)(2,1)S(1)}, bf16[64,2560]{1,0:T(8,128)(2,1)S(1)}, u32[]{:S(2)}, u32[]{:S(2)}) collective-permute-start(bf16[64,2560]{1,0:T(8,128)(2,1)S(1)} %get-tuple-element.38), channel_id=1, source_target_pairs={{0,1},{1,0},{2,3},{3,2},{4,5},{5,4},{6,7},{7,6},{8,9},{9,8},{10,11... | collective-permute-start | bytes 983048 | tf_op jit(solution)/shard_map/ppermute | solution.py:629
  37.6 17.0 %collective-permute-start.9 = (bf16[256,512]{1,0:T(8,128)(2,1)S(1)}, bf16[256,512]{1,0:T(8,128)(2,1)S(1)}, u32[]{:S(2)}, u32[]{:S(2)}) collective-permute-start(bf16[256,512]{1,0:T(8,128)(2,1)S(1)} %project.6.refs_2_), channel_id=1, source_target_pairs={{0,2},{2,0},{1,3},{3,1},{4,6},{6,4},{5,7},{7,5},{8,10},{10,8},{9,1... | collective-permute-start | bytes 786440 | tf_op jit(solution)/shard_map/ppermute | solution.py:576
  39.2 15.5 %collective-permute-start.8 = (bf16[256,512]{1,0:T(8,128)(2,1)S(1)}, bf16[256,512]{1,0:T(8,128)(2,1)S(1)}, u32[]{:S(2)}, u32[]{:S(2)}) collective-permute-start(bf16[256,512]{1,0:T(8,128)(2,1)S(1)} %project.5.refs_2_), channel_id=1, source_target_pairs={{0,2},{2,0},{1,3},{3,1},{4,6},{6,4},{5,7},{7,5},{8,10},{10,8},{9,1... | collective-permute-start | bytes 786440 | tf_op jit(solution)/shard_map/ppermute | solution.py:576
  39.7 14.9 %collective-permute-start.7 = (bf16[256,256]{1,0:T(8,128)(2,1)S(1)}, bf16[256,256]{1,0:T(8,128)(2,1)S(1)}, u32[]{:S(2)}, u32[]{:S(2)}) collective-permute-start(bf16[256,256]{1,0:T(8,128)(2,1)S(1)} %project.4.refs_2_), channel_id=1, source_target_pairs={{0,2},{2,0},{1,3},{3,1},{4,6},{6,4},{5,7},{7,5},{8,10},{10,8},{9,1... | collective-permute-start | bytes 393224 | tf_op jit(solution)/shard_map/ppermute | solution.py:576
  41.2 13.4 %collective-permute-start.6 = (f32[8,256]{1,0:T(8,128)S(1)}, f32[8,256]{1,0:T(8,128)S(1)}, u32[]{:S(2)}, u32[]{:S(2)}) collective-permute-start(f32[8,256]{1,0:T(8,128)S(1)} %get-tuple-element.43.refs_0_), channel_id=1, source_target_pairs={{0,2},{2,0},{1,3},{3,1},{4,6},{6,4},{5,7},{7,5},{8,10},{10,8},{9,1... | collective-permute-start | bytes 24584 | tf_op jit(solution)/shard_map/ppermute | solution.py:578

commit v3 on v2

v3 whole, which is shorter than its diff:
```python
import functools

import jax
import jax.numpy as jnp
from jax import lax
from jax.experimental import pallas as pl
from jax.experimental.pallas import tpu as pltpu
from jax.sharding import PartitionSpec as P

HEAD_DIM = 64
STATE = 128
HALF = STATE // 2
PART = HALF // 2
STRETCH = 256
BANDS = 12
INNER = 5120
LANES = 128

EPSILON = 1e-05
HIGHEST = lax.Precision.HIGHEST
F32 = jnp.float32
BF16 = jnp.bfloat16
MIB = 1 << 20


def dot(a, b):
    return lax.dot_general(a, b, (((1,), (0,)), ((), ())), preferred_element_type=F32)


def pieces(x):
    high = x.astype(BF16)
    rest = x - high.astype(F32)
    middle = rest.astype(BF16)
    return high, middle, (rest - middle.astype(F32)).astype(BF16)


def head_of_lane(heads, lanes, group, first=0):
    row = lax.broadcasted_iota(jnp.int32, (heads, lanes), 0)
    lane = lax.broadcasted_iota(jnp.int32, (heads, lanes), 1)
    return (row == first + lax.shift_right_logical(lane, group)).astype(F32).astype(BF16)


def slot_of(heads):
    return -(-heads // 8) * 8


def piece_rows(values, ref):
    heads = values.shape[0]
    ref[...] = jnp.zeros(ref.shape, F32)
    for k, piece in enumerate(pieces(values)):
        first = k * slot_of(heads)
        ref[first : first + heads, :] = piece.astype(F32)
    return ref[...]


def piece_map(heads, lanes, group, first=0):
    away = (
        lax.broadcasted_iota(jnp.int32, (LANES, lanes), 0)
        - lax.shift_right_logical(lax.broadcasted_iota(jnp.int32, (LANES, lanes), 1), group)
        - first
    )
    slot = slot_of(heads)
    hit = (away == 0) | (away == slot) | (away == 2 * slot)
    return jnp.where(hit, 1.0, 0.0).astype(BF16)


def spread_heads(row, heads_map):
    return sum(dot(piece, heads_map) for piece in pieces(jnp.broadcast_to(row, (8, row.shape[1]))))[:1]


def diagonal(rows, lanes):
    return lax.broadcasted_iota(jnp.int32, (rows, lanes), 0) == lax.broadcasted_iota(
        jnp.int32, (rows, lanes), 1
    )


def to_column(row):
    count = row.shape[1]
    return jnp.sum(jnp.where(diagonal(count, count), row, 0.0), axis=1, keepdims=True)


def decay_block(row, rows):
    place = lax.broadcasted_iota(jnp.int32, (rows, LANES), 0)
    high, middle, low = (piece.astype(F32) for piece in pieces(row))
    block = jnp.where(place == 0, high, jnp.where(place == 1, middle, jnp.where(place == 2, low, 0.0)))
    return block.astype(BF16)


def decay_row(block):
    return jnp.sum(block.astype(F32), axis=0, keepdims=True)


def decay_lanes(block, heads_map):
    return jnp.sum(dot(block[:16], heads_map), axis=0, keepdims=True)


def column_block(width):
    return width // 5 if width % (5 * LANES) == 0 else width


def local_call(body, name, outs, args, scratch=(), limit=8 * MIB, flops=0, after=()):
    size = sum(a.size * a.dtype.itemsize for a in args) + sum(o.size * o.dtype.itemsize for o in outs)

    def kernel(*refs):
        body(*refs[: len(args)], *refs[len(args) + len(after) :])

    return pl.pallas_call(
        kernel,
        name=name,
        out_shape=outs,
        in_specs=[pl.BlockSpec(memory_space=pltpu.VMEM)] * len(args)
        + [pl.BlockSpec(memory_space=pl.ANY)] * len(after),
        out_specs=[pl.BlockSpec(memory_space=pltpu.VMEM)] * len(outs),
        scratch_shapes=list(scratch),
        compiler_params=pltpu.CompilerParams(vmem_limit_bytes=limit),
        cost_estimate=pl.CostEstimate(flops=flops, bytes_accessed=size, transcendentals=0),
    )(*args, *after)


IN_VMEM = pl.BlockSpec(memory_space=pltpu.VMEM)
IN_HBM = pl.BlockSpec(memory_space=pltpu.HBM)
ANYWHERE = pl.BlockSpec(memory_space=pl.ANY)


def in_hbm(*arrays):
    return [pltpu.with_memory_space_constraint(a, pltpu.HBM) for a in arrays]


def state_kernel(
    band_ref,
    logits_hbm,
    mask_hbm,
    offset_hbm,
    decay_log_hbm,
    step_offset_hbm,
    write_hbm,
    read_hbm,
    signal_hbm,
    gate_hbm,
    running_ref,
    weight_ref,
    decay_ref,
    keep_ref,
    send_ref,
    write_ref,
    read_ref,
    signal_ref,
    gate_ref,
    logits_ref,
    mask_ref,
    offset_ref,
    decay_log_ref,
    step_offset_ref,
    rows_ref,
    sems,
    block_sems,
):
    heads, tokens = logits_ref.shape
    width = signal_ref.shape[1]
    block = column_block(width)
    is_first = lax.axis_index("band") == 0
    pairs = (
        (logits_hbm, logits_ref),
        (mask_hbm, mask_ref),
        (offset_hbm, offset_ref),
        (decay_log_hbm, decay_log_ref),
        (step_offset_hbm, step_offset_ref),
        (write_hbm, write_ref),
        (read_hbm, read_ref),
        (gate_hbm, gate_ref),
    )
    copies = [pltpu.make_async_copy(*pair, sems.at[i]) for i, pair in enumerate(pairs)]
    blocks = [
        pltpu.make_async_copy(
            signal_hbm.at[:, pl.ds(first, block)],
            signal_ref.at[:, pl.ds(first, block)],
            block_sems.at[first // block],
        )
        for first in range(0, width, block)
    ]
    for copy in copies[:6] + blocks + copies[6:]:
        copy.start()
    for copy in copies[:6]:
        copy.wait()

    offset = to_column(step_offset_ref[...] + offset_ref[pl.ds(band_ref[0], 1), :])
    raw = logits_ref[...] + offset
    step_size = jnp.maximum(raw, 0.0) + jnp.log1p(jnp.exp(-jnp.abs(raw)))
    log_decay = step_size * to_column(-jnp.exp(decay_log_ref[...]))
    earlier = lax.broadcasted_iota(jnp.int32, (tokens, tokens), 0)
    later = lax.broadcasted_iota(jnp.int32, (tokens, tokens), 1)
    sums = dot(
        piece_rows(log_decay, rows_ref).astype(BF16), jnp.where(earlier <= later, 1.0, 0.0).astype(BF16)
    )
    slot = slot_of(heads)
    running = sums[:heads] + sums[slot : slot + heads] + sums[2 * slot : 2 * slot + heads]
    weight = step_size * mask_ref[...].astype(F32)
    running_ref[...] = running
    weight_ref[...] = weight
    total = running[:, tokens - 1 : tokens]
    row = jnp.sum(jnp.where(diagonal(heads, LANES), jnp.exp(total), 0.0), axis=0, keepdims=True)
    send_ref[:, width:] = decay_block(row, HALF)
    decay_ref[...] = decay_block(row, 16)

    tail = piece_rows(jnp.exp(total - running) * weight, rows_ref).T.astype(BF16)
    write = write_ref[...].astype(F32).T
    low, high = write[:HALF], write[HALF:]
    write = jnp.concatenate(
        [jnp.where(is_first, low, high), jnp.where(is_first, high, low)], axis=0
    ).astype(BF16)
    for copy, first in zip(blocks, range(0, width, block)):
        lanes = slice(first, first + block)
        factors = dot(tail, piece_map(heads, block, 6, first // HEAD_DIM))
        copy.wait()
        state = dot(write, (signal_ref[:, lanes].astype(F32) * factors).astype(BF16))
        keep_ref[:, lanes] = state[:HALF]
        send_ref[:, lanes] = state[HALF:].astype(BF16)
    for copy in copies[6:]:
        copy.wait()


def own_state(stretch_band, small, write_proj, read_proj, signal, gate_branch):
    tokens, width = signal.shape
    heads = small[0].shape[0]
    passed = (write_proj, read_proj, signal, gate_branch)
    return pl.pallas_call(
        state_kernel,
        name="own_state",
        out_shape=[
            jax.ShapeDtypeStruct((heads, tokens), F32),
            jax.ShapeDtypeStruct((heads, tokens), F32),
            jax.ShapeDtypeStruct((16, LANES), BF16),
            jax.ShapeDtypeStruct((HALF, width), F32),
            jax.ShapeDtypeStruct((HALF, width + LANES), BF16),
        ]
        + [jax.ShapeDtypeStruct(a.shape, a.dtype) for a in passed],
        in_specs=[pl.BlockSpec(memory_space=pltpu.SMEM)] + [IN_HBM] * 9,
        out_specs=[IN_VMEM] * 9,
        scratch_shapes=[pltpu.VMEM(a.shape, a.dtype) for a in small]
        + [
            pltpu.VMEM((LANES, tokens), F32),
            pltpu.SemaphoreType.DMA((8,)),
            pltpu.SemaphoreType.DMA((width // column_block(width),)),
        ],
        compiler_params=pltpu.CompilerParams(vmem_limit_bytes=16 * MIB),
        cost_estimate=pl.CostEstimate(
            flops=4 * tokens * width * STATE, bytes_accessed=tokens * width * 2, transcendentals=0
        ),
    )(stretch_band, *in_hbm(*small, *passed))


def local_kernel(
    running_ref,
    weight_ref,
    decay_ref,
    got_ref,
    write_ref,
    read_ref,
    signal_ref,
    gate_ref,
    skip_hbm,
    gain_hbm,
    matrix_hbm,
    after_ref,
    base_ref,
    factor_ref,
    lanes_ref,
    gain_ref,
    matrix_ref,
    scores_ref,
    rows_ref,
    running_pieces_ref,
    decay_pieces_ref,
    skip_ref,
    sems,
):
    heads, tokens = running_ref.shape
    width = base_ref.shape[1]
    block = column_block(width)
    half = tokens // 2
    copies = [
        pltpu.make_async_copy(*pair, sems.at[i])
        for i, pair in enumerate(((skip_hbm, skip_ref), (gain_hbm, gain_ref), (matrix_hbm, matrix_ref)))
    ]
    for copy in copies:
        copy.start()

    scores = lax.dot_general(
        read_ref[...], write_ref[...], (((1,), (1,)), ((), ())), preferred_element_type=F32
    )
    row = lax.broadcasted_iota(jnp.int32, scores.shape, 0)
    lane = lax.broadcasted_iota(jnp.int32, scores.shape, 1)
    scores_ref[...] = jnp.where(row >= lane, scores, 0.0)
    running = running_ref[...]
    running_pieces_ref[...] = piece_rows(running, rows_ref).T.astype(BF16)
    decay_pieces_ref[...] = piece_rows(jnp.exp(running), rows_ref).T.astype(BF16)
    is_first = lax.axis_index("band") == 0
    mine, got = decay_ref[...].astype(F32), got_ref[:16, width:].astype(F32)
    first_core = jnp.where(is_first, mine, got).astype(BF16)
    lanes_ref[...] = jnp.broadcast_to(
        decay_lanes(first_core, head_of_lane(LANES, width, 6)), lanes_ref.shape
    )
    copies[0].wait()
    low_lanes = lax.broadcasted_iota(jnp.int32, (half, LANES), 1) < HEAD_DIM
    early, late = slice(0, half), slice(half, tokens)

    def heads_block(at, _):
        first_head = at * (block // HEAD_DIM)
        out_lanes = pl.ds(pl.multiple_of(at * block, LANES), block)
        wide = dot(running_pieces_ref[...], piece_map(heads, block * 2, 7, first_head))
        gate = gate_ref[:, out_lanes].astype(F32)
        gate = gate / (1.0 + jnp.exp(-gate))
        factor_ref[:, out_lanes] = (
            dot(decay_pieces_ref[...], piece_map(heads, block, 6, first_head)) * gate
        )
        skip = spread_heads(skip_ref[...], head_of_lane(heads, block, 6, first_head))
        for pair in range(block // LANES):
            lanes = slice(pair * LANES, (pair + 1) * LANES)
            out_lanes = pl.ds(pl.multiple_of(at * block + pair * LANES, LANES), LANES)
            values = signal_ref[:, out_lanes]
            top, bottom = [], []
            for k in (2 * pair, 2 * pair + 1):
                row = running_ref[pl.ds(first_head + k, 1), :]
                weight = weight_ref[pl.ds(first_head + k, 1), :]
                column = wide[:, k * LANES : (k + 1) * LANES]

                def mixing(rows, cols):
                    span = jnp.minimum(column[rows] - row[:, cols], 0.0)
                    return (jnp.exp(span) * scores_ref[rows, cols] * weight[:, cols]).astype(BF16)

                top.append(mixing(early, early))
                bottom.append(jnp.concatenate([mixing(late, early), mixing(late, late)], axis=1))
            top = dot(jnp.concatenate(top, axis=0), values[early])
            bottom = dot(jnp.concatenate(bottom, axis=0), values)
            skipped = values.astype(F32) * skip[:, lanes]
            base_ref[early, out_lanes] = (
                jnp.where(low_lanes, top[:half], top[half:]) + skipped[early]
            ) * gate[early, lanes]
            base_ref[late, out_lanes] = (
                jnp.where(low_lanes, bottom[:half], bottom[half:]) + skipped[late]
            ) * gate[late, lanes]
        return 0

    lax.fori_loop(0, width // block, heads_block, 0)
    for copy in copies[1:]:
        copy.wait()


def local_part(resident, constants, after):
    running, signal = resident[0], resident[6]
    skip_gain, norm_gain, out_weight = constants
    tokens, width = signal.shape
    heads = running.shape[0]
    return pl.pallas_call(
        local_kernel,
        name="local_part",
        out_shape=[jax.ShapeDtypeStruct((tokens, width), F32)] * 2
        + [jax.ShapeDtypeStruct((8, width), F32)]
        + [jax.ShapeDtypeStruct(a.shape, a.dtype) for a in (norm_gain, out_weight)],
        in_specs=[IN_VMEM] * len(resident) + [IN_HBM] * len(constants) + [ANYWHERE],
        out_specs=[IN_VMEM] * 5,
        scratch_shapes=[
            pltpu.VMEM((tokens, tokens), F32),
            pltpu.VMEM((LANES, tokens), F32),
            pltpu.VMEM((tokens, LANES), BF16),
            pltpu.VMEM((tokens, LANES), BF16),
            pltpu.VMEM(skip_gain.shape, F32),
            pltpu.SemaphoreType.DMA((3,)),
        ],
        compiler_params=pltpu.CompilerParams(vmem_limit_bytes=16 * MIB),
        cost_estimate=pl.CostEstimate(
            flops=6 * heads * tokens * tokens * HEAD_DIM,
            bytes_accessed=tokens * width * 12,
            transcendentals=heads * tokens * tokens,
        ),
    )(*resident, *in_hbm(*constants), after)


def chip_kernel(keep_ref, got_ref, decay_ref, state_ref, first_ref, second_ref):
    width = keep_ref.shape[1]
    core = lax.axis_index("band")
    chip = lax.axis_index("scan")
    heads_map = head_of_lane(LANES, width, 6)
    got_decay = got_ref[:16, width:]
    mine = decay_ref[...]
    later = jnp.where(core == 0, got_decay.astype(F32), mine.astype(F32)).astype(BF16)
    lanes = decay_lanes(later, heads_map)
    got = got_ref[:, :width].astype(F32)
    keep = keep_ref[...]
    early, late = jnp.where(core == 0, keep, got), jnp.where(core == 0, got, keep)
    state_ref[:, :width] = (early * lanes + late).astype(BF16)
    block = decay_block(decay_row(got_decay) * decay_row(mine), PART)
    state_ref[:PART, width:] = block
    state_ref[PART:, width:] = block
    second_ref[...] = state_ref[PART:, :]
    first_ref[...] = state_ref[pl.ds(pl.multiple_of(jnp.where(chip == 1, PART, 0), PART), PART), :]


def middle_kernel(state_ref, near_ref, far_ref, out_ref, lanes_ref):
    width = out_ref.shape[1]
    chip = lax.axis_index("scan")

    @pl.when(chip == 0)
    def _():
        out_ref[...] = state_ref[PART:, :width]

    @pl.when(chip == 1)
    def _():
        lanes = decay_lanes(state_ref[:16, width:], head_of_lane(LANES, width, 6))
        out_ref[...] = (
            lanes * near_ref[:, :width].astype(F32) + state_ref[:PART, :width].astype(F32)
        ).astype(BF16)

    @pl.when(chip > 1)
    def _():
        heads_map = head_of_lane(LANES, width, 6)
        lanes = decay_lanes(near_ref[:16, width:], heads_map)
        lanes_ref[...] = jnp.broadcast_to(lanes, lanes_ref.shape)

        @pl.when(chip == 2)
        def _():
            entered = lanes * far_ref[:, :width].astype(F32) + near_ref[:, :width].astype(F32)
            own = decay_lanes(state_ref[:16, width:], heads_map)
            out_ref[...] = (own * entered + state_ref[PART:, :width].astype(F32)).astype(BF16)


def enter_kernel(
    near_ref, far_ref, next_ref, skip_ref, near_lanes_ref, keep_ref, got_ref, lanes_ref, mine_ref, send_ref
):
    width = keep_ref.shape[1]
    chip = lax.axis_index("scan")

    def parts(first, second):
        enter = jnp.concatenate([first.astype(F32), second.astype(F32)], axis=0)
        share_enter(enter, keep_ref, got_ref, lanes_ref, mine_ref, send_ref)

    @pl.when(chip == 0)
    def _():
        share_enter(jnp.zeros((HALF, width), F32), keep_ref, got_ref, lanes_ref, mine_ref, send_ref)

    @pl.when(chip == 1)
    def _():
        parts(near_ref[:, :width], next_ref[...])

    @pl.when(chip == 2)
    def _():
        near = near_ref[:, :width].astype(F32)
        parts(next_ref[...], near_lanes_ref[:1] * far_ref[:, :width].astype(F32) + near)

    @pl.when(chip == 3)
    def _():
        near = near_ref[:, :width].astype(F32)
        parts(near_lanes_ref[:1] * skip_ref[...].astype(F32) + near, next_ref[...])


def share_enter(enter, keep_ref, got_ref, lanes_ref, mine_ref, send_ref):
    width = keep_ref.shape[1]
    core = lax.axis_index("band")

    @pl.when(core == 0)
    def _():
        mine_ref[...] = enter.astype(BF16)
        send_ref[...] = (lanes_ref[:1] * enter + keep_ref[...]).astype(BF16)

    @pl.when(core == 1)
    def _():
        send_ref[...] = enter.astype(BF16)
        mine_ref[...] = (lanes_ref[:1] * enter + got_ref[:, :width].astype(F32)).astype(BF16)


def gathered_kernel(all_ref, keep_ref, got_ref, lanes_ref, mine_ref, send_ref, enter_ref):
    width = keep_ref.shape[1]
    chip = lax.axis_index("scan")
    heads_map = head_of_lane(LANES, width, 6)
    enter_ref[...] = jnp.zeros(enter_ref.shape, F32)
    for source in range(all_ref.shape[0]):

        @pl.when(source < chip)
        def _():
            lanes = decay_lanes(all_ref[source, :16, width:], heads_map)
            enter_ref[...] = lanes * enter_ref[...] + all_ref[source, :, :width].astype(F32)

    share_enter(enter_ref[...], keep_ref, got_ref, lanes_ref, mine_ref, send_ref)


def chip_state(keep, got, decay):
    width = keep.shape[1]
    return local_call(
        chip_kernel,
        "chip_state",
        [
            jax.ShapeDtypeStruct((HALF, width + LANES), BF16),
            jax.ShapeDtypeStruct((PART, width + LANES), BF16),
            jax.ShapeDtypeStruct((PART, width + LANES), BF16),
        ],
        (keep, got, decay),
    )


def entering_state(chips, state, first, second, keep, got, local):
    width = keep.shape[1]
    half = jax.ShapeDtypeStruct((HALF, width), BF16)
    if chips != 4:
        gathered = lax.all_gather(state, "scan", axis=0)
        base, factor, lanes, gain, weight = local(first)
        mine, give = local_call(
            gathered_kernel,
            "enter_state",
            [half, half],
            (gathered, keep, got, lanes),
            (pltpu.VMEM((HALF, width), F32),),
        )
        return mine, give, base, factor, gain, weight
    near = lax.ppermute(first, "scan", [(0, 1), (1, 2), (2, 3)])
    far = lax.ppermute(second, "scan", [(0, 2)])
    base, factor, lanes, gain, weight = local(first)
    middle, near_lanes = local_call(
        middle_kernel,
        "middle_state",
        [jax.ShapeDtypeStruct((PART, width), BF16), jax.ShapeDtypeStruct((8, width), F32)],
        (state, near, far),
        after=(lanes,),
    )
    following = lax.ppermute(middle, "scan", [(0, 1), (1, 2), (2, 3)])
    skipping = lax.ppermute(middle, "scan", [(1, 3)])
    mine, give = local_call(
        enter_kernel,
        "enter_state",
        [half, half],
        (near, far, following, skipping, near_lanes, keep, got, lanes),
    )
    return mine, give, base, factor, gain, weight


def gated_kernel(
    mine_ref, other_ref, base_ref, factor_ref, read_ref, gain_ref, weight_ref, out_ref, square_ref, *first_refs
):
    tokens, width = base_ref.shape
    block = column_block(width)
    is_first = lax.axis_index("band") == 0
    read = read_ref[...]
    sums = jnp.zeros((tokens, LANES), F32)
    for first in range(0, width, block):
        lanes = slice(first, first + block)
        mine, other = mine_ref[:, lanes].astype(F32), other_ref[:, lanes].astype(F32)
        low = jnp.where(is_first, mine, other).astype(BF16)
        high = jnp.where(is_first, other, mine).astype(BF16)
        carried = dot(read, jnp.concatenate([low, high], axis=0))
        gated = base_ref[:, lanes] + factor_ref[:, lanes] * carried
        for k in range(0, block, LANES):
            column = gated[:, k : k + LANES]
            row = (first + k) // LANES
            out_ref[:, first + k : first + k + LANES] = (column * gain_ref[row : row + 1, :]).astype(BF16)
            sums += column * column
    for first_ref in first_refs:
        send_kernel(0, out_ref, weight_ref, first_ref)
    square_ref[...] = jnp.broadcast_to(jnp.sum(sums.T, axis=0, keepdims=True), square_ref.shape)


def gated_part(mine, other, base, factor, read_proj, gain, weight, first):
    tokens, width = base.shape
    return local_call(
        gated_kernel,
        "gated_part",
        [
            jax.ShapeDtypeStruct((tokens, width), BF16),
            jax.ShapeDtypeStruct((8, tokens), F32),
        ]
        + [jax.ShapeDtypeStruct((tokens, first), BF16)] * (first > 0),
        (mine, other, base, factor, read_proj, gain, weight),
        flops=2 * tokens * width * STATE,
    )


SENDS = (512, 384, 384)


def columns_of(weight_ref, other, first, count):
    columns = weight_ref.shape[1] // 2
    member = lax.axis_index("tensor")
    start = (1 - member if other else member) * columns + first
    return weight_ref[:, pl.ds(pl.multiple_of(start, LANES), count)]


def send_kernel(first, gated_ref, weight_ref, *refs):
    out_ref = refs[-1]
    tokens, count = gated_ref.shape[0], out_ref.shape[1]
    out_ref[:tokens, :] = dot(gated_ref[...], columns_of(weight_ref, True, first, count)).astype(BF16)
    for square_ref in refs[:-1]:
        out_ref[tokens:, :] = jnp.zeros((16, count), BF16)
        for lane in range(0, tokens, LANES):
            lanes = slice(lane, lane + LANES)
            out_ref[tokens:, lanes] = decay_block(square_ref[:1, lanes], 16)


def own_kernel(gated_ref, weight_ref, out_ref):
    gated, count = gated_ref[...], out_ref.shape[1] // 5
    for first in range(0, out_ref.shape[1], count):
        out_ref[:, first : first + count] = dot(gated, columns_of(weight_ref, False, first, count))


def finish_kernel(squares_ref, own_ref, *refs):
    *got_refs, out_ref, sent_ref, sems = refs
    tokens = own_ref.shape[0]
    other_squares = got_refs[-1][tokens:, :tokens].astype(F32)
    mean = (squares_ref[:1] + jnp.sum(other_squares, axis=0, keepdims=True)) / INNER
    scale = lax.rsqrt(mean + EPSILON)
    scale = jnp.broadcast_to(scale, (LANES, tokens)).T
    first, copies = 0, []
    for got_ref in got_refs:
        count = got_ref.shape[1]
        for lane in range(0, count, LANES):
            lanes = slice(first + lane, first + lane + LANES)
            total = own_ref[:, lanes] + got_ref[:tokens, lane : lane + LANES].astype(F32)
            sent_ref[:, lanes] = (total * scale).astype(BF16)
        lanes = pl.ds(first, count)
        copies.append(
            pltpu.make_async_copy(sent_ref.at[:, lanes], out_ref.at[:, lanes], sems.at[len(copies)])
        )
        copies[-1].start()
        first += count
    for copy in copies:
        copy.wait()


def finish(squares, own, got):
    args = (squares, own, *got)
    return pl.pallas_call(
        finish_kernel,
        name="finish",
        out_shape=jax.ShapeDtypeStruct(own.shape, BF16),
        in_specs=[IN_VMEM] * len(args),
        out_specs=IN_HBM,
        scratch_shapes=[
            pltpu.VMEM(own.shape, BF16),
            pltpu.SemaphoreType.DMA((len(got),)),
        ],
        compiler_params=pltpu.CompilerParams(vmem_limit_bytes=8 * MIB),
    )(*args)


def direct(members, columns):
    return members == 2 and columns == sum(SENDS)


def layer_columns(members, gated, squares, weight, ready):
    columns = weight.shape[1] // members
    if not direct(members, columns):
        mean = lax.psum(squares[0], "tensor") / INNER
        partial = dot(gated, weight).astype(BF16)
        total = lax.psum_scatter(partial, "tensor", scatter_dimension=1, tiled=True)
        return (total.astype(F32) * lax.rsqrt(mean + EPSILON)[:, None]).astype(BF16)
    swap = [(0, 1), (1, 0)]
    tokens = gated.shape[0]
    parts, first = [ready[0]], SENDS[0]
    for count in SENDS[1:]:
        last = first + count == columns
        parts += local_call(
            functools.partial(send_kernel, first),
            "project_other",
            [jax.ShapeDtypeStruct((tokens + 16 * last, count), BF16)],
            (gated, weight) + (squares,) * last,
            after=parts[-1:],
        )
        first += count
    got = [lax.ppermute(part, "tensor", swap) for part in parts]
    (own,) = local_call(
        own_kernel,
        "project_own",
        [jax.ShapeDtypeStruct((tokens, columns), F32)],
        (gated, weight),
        after=parts[-1:],
    )
    return finish(squares, own, got)


def on_device(
    chips,
    members,
    signal,
    gate_branch,
    write_proj,
    read_proj,
    step_logits,
    valid_mask,
    stretch_band,
    band_offset,
    decay_log,
    step_offset,
    skip_gain,
    norm_gain,
    out_weight,
):
    small = (step_logits, valid_mask[None], band_offset, decay_log[None], step_offset[None])
    running, weight, decay, keep, send, *passed = own_state(
        stretch_band, small, write_proj, read_proj, signal, gate_branch
    )
    cores = [(0, 1), (1, 0)]
    got = lax.ppermute(send, "band", cores)
    state, first, second = chip_state(keep, got, decay)
    constants = (skip_gain[None], norm_gain.reshape(-1, LANES), out_weight)

    def local(after):
        return local_part((running, weight, decay, got, *passed), constants, after)

    mine, give, base, factor, gain, matrix = entering_state(
        chips, state, first, second, keep, got, local
    )
    other = lax.ppermute(give, "band", cores)
    ahead = SENDS[0] if direct(members, matrix.shape[1] // members) else 0
    gated, squares, *ready = gated_part(
        mine, other, base, factor, passed[1], gain, matrix, ahead
    )
    return layer_columns(members, gated, squares, matrix, ready)


def solution(mesh):
    placed = (
        P(("group", "scan", "band"), "tensor"),
        P(("group", "scan", "band"), "tensor"),
        P(("group", "scan", "band"), None),
        P(("group", "scan", "band"), None),
        P("tensor", ("group", "scan", "band")),
        P(("group", "scan", "band")),
        P(("group", "scan", "band")),
        P(None, "tensor"),
        P("tensor"),
        P("tensor"),
        P("tensor"),
        P("tensor"),
        P("tensor", None),
    )
    return jax.shard_map(
        functools.partial(on_device, mesh.shape["scan"], mesh.shape["tensor"]),
        mesh=mesh,
        in_specs=placed,
        out_specs=P(("group", "scan", "band"), "tensor"),
        check_vma=False,
    )
```

time: 56 us -> 51 us (0.911)
  the two profiles are of different devices: /device:TPU:0 before, /device:TPU:24 now
where the time goes in v3:
time: 51 us; the launch traced here: 50.8 us
  waiting for transfers between devices  25.6 us (50%)
  Pallas kernels  16.1 us (32%)
  starting transfers between devices  8.31 us (16%)
  between operations  0.77 us (2%)
    ppermute x3, waiting for transfers between devices, layer_columns(): got = [lax.ppermute(part, 'tensor', swap) for part in parts]  9.89 us
    ppermute x1, waiting for transfers between devices, entering_state(): following = lax.ppermute(middle, 'scan', [(0, 1), (1, 2), (2, 3)])  8.27 us
    pallas_call x1, Pallas kernels, local_part(): pl.pallas_call(local_kernel, name='local_part', out_shape=[jax.ShapeDtype...  5.96 us
    pallas_call x7, Pallas kernels, local_call(): pl.pallas_call(kernel, name=name, out_shape=outs, in_specs=[pl.BlockSpec(...  5.72 us
    ppermute x1, waiting for transfers between devices, entering_state(): skipping = lax.ppermute(middle, 'scan', [(1, 3)])  3.81 us
    ppermute x3, starting transfers between devices, layer_columns(): got = [lax.ppermute(part, 'tensor', swap) for part in parts]  3.62 us
    pallas_call x1, Pallas kernels, own_state(): pl.pallas_call(state_kernel, name='own_state', out_shape=[jax.ShapeDtypeS...  3.37 us
    ppermute x1, waiting for transfers between devices, on_device(): got = lax.ppermute(send, 'band', cores)  1.64 us
  transfers between devices with their start and end apart: 9, of which 6 were waited for; matrix products, arithmetic and copies ran while one was open for 0% of the time, Pallas kernels for 19%

profile of v3, /device:TPU:24, one launch (start us, length us, event | category | flops | bytes accessed | tf_op | source)
XLA Modules:
  0.0 50.8 jit_solution(4329376188398485377)
XLA Ops:
  0.7 3.4 %own_state.1 = (f32[40,256]{1,0:T(8,128)S(1)}, f32[40,256]{1,0:T(8,128)S(1)}, bf16[16,128]{1,0:T(8,128)(2,1)S(1)}, f32[64,2560]{1,0:T(8,128)S(1)}, bf16[64,2688]...) custom-call(s32[1]{0:T(128)S(6)} %copy.14.band_ref, ...), custom_call_target="tpu_custom_call" | custom-call | flops 335544320 | bytes 1310720 | tf_op jit(solution)/shard_map/own_state/pallas_call | solution.py:226
  4.0 0.1 collective-permute-start
  4.1 1.6 %collective-permute-done.refs_1_.got_ref.refs_6_ = bf16[64,2688]{1,0:T(8,128)(2,1)S(1)} collective-permute-done((bf16[64,2688]{1,0:T(8,128)(2,1)S(1)}, bf16[64,2688]{1,0:T(8,128)(2,1)S(1)}, u32[]{:S(2)}, u32[]{:S(2)}) %collective-permute-start) | collective-permute-done | bytes 344096 | tf_op jit(solution)/shard_map/ppermute | solution.py:699
  5.8 0.3 chip_state.1
  6.0 1.3 %collective-permute-start.1 = (bf16[32,2688]{1,0:T(8,128)(2,1)S(1)}, bf16[32,2688]{1,0:T(8,128)(2,1)S(1)}, u32[]{:S(2)}, u32[]{:S(2)}) collective-permute-start(bf16[32,2688]{1,0:T(8,128)(2,1)S(1)} %get-tuple-element.32.after_ref), channel_id=1, source_target_pairs={{0,4},{4,8},{8,12},{1,5},{5,9},{9,13},{2,6},{6,10},{10,14},{3,7},{... | collective-permute-start | bytes 516104 | tf_op jit(solution)/shard_map/ppermute | solution.py:514
  7.3 0.7 %collective-permute-start.2 = (bf16[32,2688]{1,0:T(8,128)(2,1)S(1)}, bf16[32,2688]{1,0:T(8,128)(2,1)S(1)}, u32[]{:S(2)}, u32[]{:S(2)}) collective-permute-start(bf16[32,2688]{1,0:T(8,128)(2,1)S(1)} %get-tuple-element.33), channel_id=1, source_target_pairs={{0,8},{1,9},{2,10},{3,11},{16,24},{17,25},{18,26},{19,27}} | collective-permute-start | bytes 516104 | tf_op jit(solution)/shard_map/ppermute | solution.py:515
  8.0 6.0 %local_part.1 = (f32[256,2560]{1,0:T(8,128)S(1)}, f32[256,2560]{1,0:T(8,128)S(1)}, f32[8,2560]{1,0:T(8,128)S(1)}, f32[20,128]{1,0:T(8,128)S(1)}, bf16[2560,2560]{1,0:T(8,128)(2,1)S(1)}) custom-call(f32[40,256]{1,0:T(8,128)S(1)} %get-tuple-element.35.running_ref, f32[40,256]{1,0:T(8,128)S(1)} %get-tuple-element.36.weight_ref, ...), custom_call_target="tpu_custom_call" | custom-call | flops 1006632960 | bytes 7864320 | tf_op jit(solution)/shard_map/local_part/pallas_call | solution.py:354
  14.0 0.4 collective-permute-done.1.refs_1_.refs_0_
  14.3 0.0 collective-permute-done.2.refs_2_.refs_1_
  14.3 0.2 middle_state.1
  14.5 1.3 %collective-permute-start.3 = (bf16[32,2560]{1,0:T(8,128)(2,1)S(1)}, bf16[32,2560]{1,0:T(8,128)(2,1)S(1)}, u32[]{:S(2)}, u32[]{:S(2)}) collective-permute-start(bf16[32,2560]{1,0:T(8,128)(2,1)S(1)} %get-tuple-element.42), channel_id=1, source_target_pairs={{0,4},{4,8},{8,12},{1,5},{5,9},{9,13},{2,6},{6,10},{10,14},{3,7},{... | collective-permute-start | bytes 491528 | tf_op jit(solution)/shard_map/ppermute | solution.py:524
  15.8 1.3 %collective-permute-start.4 = (bf16[32,2560]{1,0:T(8,128)(2,1)S(1)}, bf16[32,2560]{1,0:T(8,128)(2,1)S(1)}, u32[]{:S(2)}, u32[]{:S(2)}) collective-permute-start(bf16[32,2560]{1,0:T(8,128)(2,1)S(1)} %get-tuple-element.42), channel_id=1, source_target_pairs={{4,12},{5,13},{6,14},{7,15},{20,28},{21,29},{22,30},{23,31}} | collective-permute-start | bytes 491528 | tf_op jit(solution)/shard_map/ppermute | solution.py:525
  17.1 8.3 %collective-permute-done.3.refs_2_ = bf16[32,2560]{1,0:T(8,128)(2,1)S(1)} collective-permute-done((bf16[32,2560]{1,0:T(8,128)(2,1)S(1)}, bf16[32,2560]{1,0:T(8,128)(2,1)S(1)}, u32[]{:S(2)}, u32[]{:S(2)}) %collective-permute-start.3) | collective-permute-done | bytes 163872 | tf_op jit(solution)/shard_map/ppermute | solution.py:524
  25.4 3.8 %collective-permute-done.4.refs_3_ = bf16[32,2560]{1,0:T(8,128)(2,1)S(1)} collective-permute-done((bf16[32,2560]{1,0:T(8,128)(2,1)S(1)}, bf16[32,2560]{1,0:T(8,128)(2,1)S(1)}, u32[]{:S(2)}, u32[]{:S(2)}) %collective-permute-start.4) | collective-permute-done | bytes 163872 | tf_op jit(solution)/shard_map/ppermute | solution.py:525
  29.2 0.2 enter_state.1
  29.4 0.1 collective-permute-start.5
  29.4 1.6 %collective-permute-done.5.refs_1_ = bf16[64,2560]{1,0:T(8,128)(2,1)S(1)} collective-permute-done((bf16[64,2560]{1,0:T(8,128)(2,1)S(1)}, bf16[64,2560]{1,0:T(8,128)(2,1)S(1)}, u32[]{:S(2)}, u32[]{:S(2)}) %collective-permute-start.5) | collective-permute-done | bytes 327712 | tf_op jit(solution)/shard_map/ppermute | solution.py:709
  31.1 1.5 %gated_part.1 = (bf16[256,2560]{1,0:T(8,128)(2,1)S(1)}, f32[8,256]{1,0:T(8,128)S(1)}, bf16[256,512]{1,0:T(8,128)(2,1)S(1)}) custom-call(bf16[64,2560]{1,0:T(8,128)(2,1)S(1)} %get-tuple-element.44.refs_0_, bf16[64,2560]{1,0:T(8,128)(2,1)S(1)} %collective-permute-done.5.refs_1_, f32[256,2560]{1,0:T(8,128)S(1)} %get-tuple-element.46.refs_2_, ...), custom_call_target="tpu_custom_call" | custom-call | flops 167772160 | bytes 20662272 | tf_op jit(solution)/shard_map/gated_part/pallas_call | solution.py:107
  32.6 1.5 %collective-permute-start.6 = (bf16[256,512]{1,0:T(8,128)(2,1)S(1)}, bf16[256,512]{1,0:T(8,128)(2,1)S(1)}, u32[]{:S(2)}, u32[]{:S(2)}) collective-permute-start(bf16[256,512]{1,0:T(8,128)(2,1)S(1)} %get-tuple-element.52.refs_2_), channel_id=1, source_target_pairs={{0,2},{2,0},{1,3},{3,1},{4,6},{6,4},{5,7},{7,5},{8,10},{10,8},{9,1... | collective-permute-start | bytes 786440 | tf_op jit(solution)/shard_map/ppermute | solution.py:666
  34.1 0.9 %project_other.2.refs_3_ = bf16[256,384]{1,0:T(8,128)(2,1)S(1)} custom-call(bf16[256,2560]{1,0:T(8,128)(2,1)S(1)} %get-tuple-element.51.refs_0_, bf16[2560,2560]{1,0:T(8,128)(2,1)S(1)} %get-tuple-element.49.refs_6_.refs_1_, bf16[256,512]{1,0:T(8,128)(2,1)S(1)} %get-tuple-element.52.refs_2_), custom_call_target="tpu_custom_call" | custom-call | bytes 14614528 | tf_op jit(solution)/shard_map/project_other/pallas_call | solution.py:107
  35.0 0.9 %project_other.3.refs_2_ = bf16[272,384]{1,0:T(8,128)(2,1)S(1)} custom-call(bf16[256,2560]{1,0:T(8,128)(2,1)S(1)} %get-tuple-element.51.refs_0_, bf16[2560,2560]{1,0:T(8,128)(2,1)S(1)} %get-tuple-element.49.refs_6_.refs_1_, f32[8,256]{1,0:T(8,128)S(1)} %get-tuple-element.50.refs_2_.squares_ref, bf16[256,384]{1,0:T(8,128)(2,1)S(1)} %project_other.2.refs_3_), custom_call_target="tpu_custom_call" | custom-call | bytes 14635008 | tf_op jit(solution)/shard_map/project_other/pallas_call | solution.py:107
  35.9 0.6 %collective-permute-start.8 = (bf16[272,384]{1,0:T(8,128)(2,1)S(1)}, bf16[272,384]{1,0:T(8,128)(2,1)S(1)}, u32[]{:S(2)}, u32[]{:S(2)}) collective-permute-start(bf16[272,384]{1,0:T(8,128)(2,1)S(1)} %project_other.3.refs_2_), channel_id=1, source_target_pairs={{0,2},{2,0},{1,3},{3,1},{4,6},{6,4},{5,7},{7,5},{8,10},{10,8},{9,1... | collective-permute-start | bytes 626696 | tf_op jit(solution)/shard_map/ppermute | solution.py:666
  36.5 1.5 %collective-permute-start.7 = (bf16[256,384]{1,0:T(8,128)(2,1)S(1)}, bf16[256,384]{1,0:T(8,128)(2,1)S(1)}, u32[]{:S(2)}, u32[]{:S(2)}) collective-permute-start(bf16[256,384]{1,0:T(8,128)(2,1)S(1)} %project_other.2.refs_3_), channel_id=1, source_target_pairs={{0,2},{2,0},{1,3},{3,1},{4,6},{6,4},{5,7},{7,5},{8,10},{10,8},{9,1... | collective-permute-start | bytes 589832 | tf_op jit(solution)/shard_map/ppermute | solution.py:666
  38.0 1.9 %project_own.1.own_ref = f32[256,1280]{1,0:T(8,128)S(1)} custom-call(bf16[256,2560]{1,0:T(8,128)(2,1)S(1)} %get-tuple-element.51.refs_0_, bf16[2560,2560]{1,0:T(8,128)(2,1)S(1)} %get-tuple-element.49.refs_6_.refs_1_, bf16[272,384]{1,0:T(8,128)(2,1)S(1)} %project_other.3.refs_2_), custom_call_target="tpu_custom_call" | custom-call | bytes 15728640 | tf_op jit(solution)/shard_map/project_own/pallas_call | solution.py:107
  39.8 9.9 %collective-permute-done.7.refs_1_ = bf16[256,384]{1,0:T(8,128)(2,1)S(1)} collective-permute-done((bf16[256,384]{1,0:T(8,128)(2,1)S(1)}, bf16[256,384]{1,0:T(8,128)(2,1)S(1)}, u32[]{:S(2)}, u32[]{:S(2)}) %collective-permute-start.7) | collective-permute-done | bytes 196640 | tf_op jit(solution)/shard_map/ppermute | solution.py:666
  49.7 0.0 collective-permute-done.8.refs_2_
  49.7 0.0 collective-permute-done.6.refs_0_
  49.7 1.1 %finish.1 = bf16[256,1280]{1,0:T(8,128)(2,1)} custom-call(f32[8,256]{1,0:T(8,128)S(1)} %get-tuple-element.50.refs_2_.squares_ref, f32[256,1280]{1,0:T(8,128)S(1)} %project_own.1.own_ref, bf16[256,512]{1,0:T(8,128)(2,1)S(1)} %collective-permute-done.6.refs_0_, bf16[256,384]{1,0:T(8,128)(2,1)S(1)} %collective-permute-done.7.refs_1_, ...), custom_call_target="tpu_custom_call" | custom-call | tf_op jit(solution)/shard_map/finish/pallas_call | solution.py:628
Async XLA Ops:
  4.0 1.7 %collective-permute-start = (bf16[64,2688]{1,0:T(8,128)(2,1)S(1)}, bf16[64,2688]{1,0:T(8,128)(2,1)S(1)}, u32[]{:S(2)}, u32[]{:S(2)}) collective-permute-start(bf16[64,2688]{1,0:T(8,128)(2,1)S(1)} %get-tuple-element.30), channel_id=1, source_target_pairs={{0,1},{1,0},{2,3},{3,2},{4,5},{5,4},{6,7},{7,6},{8,9},{9,8},{10,11... | collective-permute-start | bytes 1032200 | tf_op jit(solution)/shard_map/ppermute | solution.py:699
  6.0 8.3 %collective-permute-start.1 = (bf16[32,2688]{1,0:T(8,128)(2,1)S(1)}, bf16[32,2688]{1,0:T(8,128)(2,1)S(1)}, u32[]{:S(2)}, u32[]{:S(2)}) collective-permute-start(bf16[32,2688]{1,0:T(8,128)(2,1)S(1)} %get-tuple-element.32.after_ref), channel_id=1, source_target_pairs={{0,4},{4,8},{8,12},{1,5},{5,9},{9,13},{2,6},{6,10},{10,14},{3,7},{... | collective-permute-start | bytes 516104 | tf_op jit(solution)/shard_map/ppermute | solution.py:514
  7.3 7.0 %collective-permute-start.2 = (bf16[32,2688]{1,0:T(8,128)(2,1)S(1)}, bf16[32,2688]{1,0:T(8,128)(2,1)S(1)}, u32[]{:S(2)}, u32[]{:S(2)}) collective-permute-start(bf16[32,2688]{1,0:T(8,128)(2,1)S(1)} %get-tuple-element.33), channel_id=1, source_target_pairs={{0,8},{1,9},{2,10},{3,11},{16,24},{17,25},{18,26},{19,27}} | collective-permute-start | bytes 516104 | tf_op jit(solution)/shard_map/ppermute | solution.py:515
  14.5 10.9 %collective-permute-start.3 = (bf16[32,2560]{1,0:T(8,128)(2,1)S(1)}, bf16[32,2560]{1,0:T(8,128)(2,1)S(1)}, u32[]{:S(2)}, u32[]{:S(2)}) collective-permute-start(bf16[32,2560]{1,0:T(8,128)(2,1)S(1)} %get-tuple-element.42), channel_id=1, source_target_pairs={{0,4},{4,8},{8,12},{1,5},{5,9},{9,13},{2,6},{6,10},{10,14},{3,7},{... | collective-permute-start | bytes 491528 | tf_op jit(solution)/shard_map/ppermute | solution.py:524
  15.8 13.4 %collective-permute-start.4 = (bf16[32,2560]{1,0:T(8,128)(2,1)S(1)}, bf16[32,2560]{1,0:T(8,128)(2,1)S(1)}, u32[]{:S(2)}, u32[]{:S(2)}) collective-permute-start(bf16[32,2560]{1,0:T(8,128)(2,1)S(1)} %get-tuple-element.42), channel_id=1, source_target_pairs={{4,12},{5,13},{6,14},{7,15},{20,28},{21,29},{22,30},{23,31}} | collective-permute-start | bytes 491528 | tf_op jit(solution)/shard_map/ppermute | solution.py:525
  29.4 1.7 %collective-permute-start.5 = (bf16[64,2560]{1,0:T(8,128)(2,1)S(1)}, bf16[64,2560]{1,0:T(8,128)(2,1)S(1)}, u32[]{:S(2)}, u32[]{:S(2)}) collective-permute-start(bf16[64,2560]{1,0:T(8,128)(2,1)S(1)} %get-tuple-element.45), channel_id=1, source_target_pairs={{0,1},{1,0},{2,3},{3,2},{4,5},{5,4},{6,7},{7,6},{8,9},{9,8},{10,11... | collective-permute-start | bytes 983048 | tf_op jit(solution)/shard_map/ppermute | solution.py:709
  32.6 17.1 %collective-permute-start.6 = (bf16[256,512]{1,0:T(8,128)(2,1)S(1)}, bf16[256,512]{1,0:T(8,128)(2,1)S(1)}, u32[]{:S(2)}, u32[]{:S(2)}) collective-permute-start(bf16[256,512]{1,0:T(8,128)(2,1)S(1)} %get-tuple-element.52.refs_2_), channel_id=1, source_target_pairs={{0,2},{2,0},{1,3},{3,1},{4,6},{6,4},{5,7},{7,5},{8,10},{10,8},{9,1... | collective-permute-start | bytes 786440 | tf_op jit(solution)/shard_map/ppermute | solution.py:666
  35.9 13.8 %collective-permute-start.8 = (bf16[272,384]{1,0:T(8,128)(2,1)S(1)}, bf16[272,384]{1,0:T(8,128)(2,1)S(1)}, u32[]{:S(2)}, u32[]{:S(2)}) collective-permute-start(bf16[272,384]{1,0:T(8,128)(2,1)S(1)} %project_other.3.refs_2_), channel_id=1, source_target_pairs={{0,2},{2,0},{1,3},{3,1},{4,6},{6,4},{5,7},{7,5},{8,10},{10,8},{9,1... | collective-permute-start | bytes 626696 | tf_op jit(solution)/shard_map/ppermute | solution.py:666
  36.5 13.2 %collective-permute-start.7 = (bf16[256,384]{1,0:T(8,128)(2,1)S(1)}, bf16[256,384]{1,0:T(8,128)(2,1)S(1)}, u32[]{:S(2)}, u32[]{:S(2)}) collective-permute-start(bf16[256,384]{1,0:T(8,128)(2,1)S(1)} %project_other.2.refs_3_), channel_id=1, source_target_pairs={{0,2},{2,0},{1,3},{3,1},{4,6},{6,4},{5,7},{7,5},{8,10},{10,8},{9,1... | collective-permute-start | bytes 589832 | tf_op jit(solution)/shard_map/ppermute | solution.py:666

commit v4 on v3

--- a/solution.py
+++ b/solution.py
@@ -249,42 +249,10 @@
     )(stretch_band, *in_hbm(*small, *passed))
 
 
-def local_kernel(
-    running_ref,
-    weight_ref,
-    decay_ref,
-    got_ref,
-    write_ref,
-    read_ref,
-    signal_ref,
-    gate_ref,
-    skip_hbm,
-    gain_hbm,
-    matrix_hbm,
-    after_ref,
-    base_ref,
-    factor_ref,
-    lanes_ref,
-    gain_ref,
-    matrix_ref,
-    scores_ref,
-    rows_ref,
-    running_pieces_ref,
-    decay_pieces_ref,
-    skip_ref,
-    sems,
+def prepare_local(
+    running_ref, write_ref, read_ref, decay_ref, got_ref, scores_ref, running_pieces_ref, decay_pieces_ref, lanes_ref, rows_ref
 ):
-    heads, tokens = running_ref.shape
-    width = base_ref.shape[1]
-    block = column_block(width)
-    half = tokens // 2
-    copies = [
-        pltpu.make_async_copy(*pair, sems.at[i])
-        for i, pair in enumerate(((skip_hbm, skip_ref), (gain_hbm, gain_ref), (matrix_hbm, matrix_ref)))
-    ]
-    for copy in copies:
-        copy.start()
-
+    width = lanes_ref.shape[1]
     scores = lax.dot_general(
         read_ref[...], write_ref[...], (((1,), (1,)), ((), ())), preferred_element_type=F32
     )
@@ -294,30 +262,51 @@
     running = running_ref[...]
     running_pieces_ref[...] = piece_rows(running, rows_ref).T.astype(BF16)
     decay_pieces_ref[...] = piece_rows(jnp.exp(running), rows_ref).T.astype(BF16)
-    is_first = lax.axis_index("band") == 0
     mine, got = decay_ref[...].astype(F32), got_ref[:16, width:].astype(F32)
-    first_core = jnp.where(is_first, mine, got).astype(BF16)
+    first_core = jnp.where(lax.axis_index("band") == 0, mine, got).astype(BF16)
     lanes_ref[...] = jnp.broadcast_to(
         decay_lanes(first_core, head_of_lane(LANES, width, 6)), lanes_ref.shape
     )
-    copies[0].wait()
+
+
+def local_heads(
+    first_block,
+    running_ref,
+    weight_ref,
+    signal_ref,
+    gate_ref,
+    scores_ref,
+    running_pieces_ref,
+    decay_pieces_ref,
+    skip_ref,
+    base_ref,
+    factor_ref,
+):
+    heads, tokens = running_ref.shape
+    block = column_block(signal_ref.shape[1])
+    half = tokens // 2
     low_lanes = lax.broadcasted_iota(jnp.int32, (half, LANES), 1) < HEAD_DIM
     early, late = slice(0, half), slice(half, tokens)
 
     def heads_block(at, _):
-        first_head = at * (block // HEAD_DIM)
-        out_lanes = pl.ds(pl.multiple_of(at * block, LANES), block)
+        first_head = (first_block + at) * (block // HEAD_DIM)
+
+        def whole_lanes(lane, count):
+            return pl.ds(pl.multiple_of((first_block + at) * block + lane, LANES), count)
+
+        def part_lanes(lane, count):
+            return pl.ds(pl.multiple_of(at * block + lane, LANES), count)
+
         wide = dot(running_pieces_ref[...], piece_map(heads, block * 2, 7, first_head))
-        gate = gate_ref[:, out_lanes].astype(F32)
+        gate = gate_ref[:, whole_lanes(0, block)].astype(F32)
         gate = gate / (1.0 + jnp.exp(-gate))
-        factor_ref[:, out_lanes] = (
+        factor_ref[:, part_lanes(0, block)] = (
             dot(decay_pieces_ref[...], piece_map(heads, block, 6, first_head)) * gate
         )
         skip = spread_heads(skip_ref[...], head_of_lane(heads, block, 6, first_head))
         for pair in range(block // LANES):
             lanes = slice(pair * LANES, (pair + 1) * LANES)
-            out_lanes = pl.ds(pl.multiple_of(at * block + pair * LANES, LANES), LANES)
-            values = signal_ref[:, out_lanes]
+            values = signal_ref[:, whole_lanes(pair * LANES, LANES)]
             top, bottom = [], []
             for k in (2 * pair, 2 * pair + 1):
                 row = running_ref[pl.ds(first_head + k, 1), :]
@@ -333,6 +322,7 @@
             top = dot(jnp.concatenate(top, axis=0), values[early])
             bottom = dot(jnp.concatenate(bottom, axis=0), values)
             skipped = values.astype(F32) * skip[:, lanes]
+            out_lanes = part_lanes(pair * LANES, LANES)
             base_ref[early, out_lanes] = (
                 jnp.where(low_lanes, top[:half], top[half:]) + skipped[early]
             ) * gate[early, lanes]
@@ -341,39 +331,155 @@
             ) * gate[late, lanes]
         return 0
 
-    lax.fori_loop(0, width // block, heads_block, 0)
+    lax.fori_loop(0, base_ref.shape[1] // block, heads_block, 0)
+
+
+def local_first_kernel(
+    running_ref,
+    weight_ref,
+    signal_ref,
+    gate_ref,
+    write_ref,
+    read_ref,
+    decay_ref,
+    got_ref,
+    skip_hbm,
+    gain_hbm,
+    matrix_hbm,
+    after_ref,
+    base_ref,
+    factor_ref,
+    matrix_ref,
+    gain_ref,
+    scores_ref,
+    running_pieces_ref,
+    decay_pieces_ref,
+    skip_ref,
+    lanes_ref,
+    rows_ref,
+    sems,
+):
+    rows = matrix_ref.shape[0]
+    pairs = (
+        (skip_hbm, skip_ref),
+        (gain_hbm, gain_ref),
+        (matrix_hbm.at[pl.ds(0, rows), :], matrix_ref),
+    )
+    copies = [pltpu.make_async_copy(*pair, sems.at[i]) for i, pair in enumerate(pairs)]
+    for copy in copies:
+        copy.start()
+    prepared = (scores_ref, running_pieces_ref, decay_pieces_ref)
+    prepare_local(running_ref, write_ref, read_ref, decay_ref, got_ref, *prepared, lanes_ref, rows_ref)
+    copies[0].wait()
+    local_heads(
+        0, running_ref, weight_ref, signal_ref, gate_ref, *prepared, skip_ref, base_ref, factor_ref
+    )
     for copy in copies[1:]:
         copy.wait()
 
 
-def local_part(resident, constants, after):
-    running, signal = resident[0], resident[6]
-    skip_gain, norm_gain, out_weight = constants
-    tokens, width = signal.shape
-    heads = running.shape[0]
+def local_rest_kernel(
+    running_ref,
+    weight_ref,
+    signal_ref,
+    gate_ref,
+    scores_ref,
+    running_pieces_ref,
+    decay_pieces_ref,
+    skip_ref,
+    matrix_hbm,
+    after_ref,
+    base_ref,
+    factor_ref,
+    matrix_ref,
+    sem,
+):
+    rows = matrix_ref.shape[0]
+    copy = pltpu.make_async_copy(
+        matrix_hbm.at[pl.ds(matrix_hbm.shape[0] - rows, rows), :], matrix_ref, sem
+    )
+    copy.start()
+    local_heads(
+        (signal_ref.shape[1] - rows) // column_block(signal_ref.shape[1]),
+        running_ref,
+        weight_ref,
+        signal_ref,
+        gate_ref,
+        scores_ref,
+        running_pieces_ref,
+        decay_pieces_ref,
+        skip_ref,
+        base_ref,
+        factor_ref,
+    )
+    copy.wait()
+
+
+def first_columns(width):
+    return 4 * (width // 5) if width % (5 * LANES) == 0 else width // 2
+
+
+def local_call_of(kernel, name, heads, columns, outs, resident, passed, after, scratch):
+    tokens = resident[0].shape[1]
+    matrix = passed[-1]
     return pl.pallas_call(
-        local_kernel,
-        name="local_part",
-        out_shape=[jax.ShapeDtypeStruct((tokens, width), F32)] * 2
-        + [jax.ShapeDtypeStruct((8, width), F32)]
-        + [jax.ShapeDtypeStruct(a.shape, a.dtype) for a in (norm_gain, out_weight)],
-        in_specs=[IN_VMEM] * len(resident) + [IN_HBM] * len(constants) + [ANYWHERE],
-        out_specs=[IN_VMEM] * 5,
-        scratch_shapes=[
-            pltpu.VMEM((tokens, tokens), F32),
-            pltpu.VMEM((LANES, tokens), F32),
-            pltpu.VMEM((tokens, LANES), BF16),
-            pltpu.VMEM((tokens, LANES), BF16),
-            pltpu.VMEM(skip_gain.shape, F32),
-            pltpu.SemaphoreType.DMA((3,)),
-        ],
+        kernel,
+        name=name,
+        out_shape=[jax.ShapeDtypeStruct((tokens, columns), F32)] * 2
+        + [jax.ShapeDtypeStruct((columns, matrix.shape[1]), BF16)]
+        + outs,
+        in_specs=[IN_VMEM] * len(resident) + [IN_HBM] * len(passed) + [ANYWHERE],
+        out_specs=[IN_VMEM] * (3 + len(outs)),
+        scratch_shapes=scratch,
         compiler_params=pltpu.CompilerParams(vmem_limit_bytes=16 * MIB),
         cost_estimate=pl.CostEstimate(
-            flops=6 * heads * tokens * tokens * HEAD_DIM,
-            bytes_accessed=tokens * width * 12,
-            transcendentals=heads * tokens * tokens,
+            flops=6 * columns * tokens * tokens,
+            bytes_accessed=tokens * columns * 12,
+            transcendentals=columns // HEAD_DIM * tokens * tokens,
         ),
-    )(*resident, *in_hbm(*constants), after)
+    )(*resident, *in_hbm(*passed), after)
+
+
+def local_first(values, constants, after):
+    running, signal = values[0], values[2]
+    skip_gain, norm_gain, _ = constants
+    heads, tokens = running.shape
+    width = signal.shape[1]
+    pieces_shape = jax.ShapeDtypeStruct((tokens, LANES), BF16)
+    return local_call_of(
+        local_first_kernel,
+        "local_first",
+        heads,
+        first_columns(width),
+        [
+            jax.ShapeDtypeStruct(norm_gain.shape, F32),
+            jax.ShapeDtypeStruct((tokens, tokens), F32),
+            pieces_shape,
+            pieces_shape,
+            jax.ShapeDtypeStruct(skip_gain.shape, F32),
+            jax.ShapeDtypeStruct((8, width), F32),
+        ],
+        values,
+        constants,
+        after,
+        [pltpu.VMEM((LANES, tokens), F32), pltpu.SemaphoreType.DMA((3,))],
+    )
+
+
+def local_rest(values, prepared, out_weight, after):
+    running, signal = values[0], values[2]
+    width = signal.shape[1]
+    return local_call_of(
+        local_rest_kernel,
+        "local_rest",
+        running.shape[0],
+        width - first_columns(width),
+        [],
+        (*values, *prepared),
+        (out_weight,),
+        after,
+        [pltpu.SemaphoreType.DMA(())],
+    )
 
 
 def chip_kernel(keep_ref, got_ref, decay_ref, state_ref, first_ref, second_ref):
@@ -392,43 +498,62 @@
     block = decay_block(decay_row(got_decay) * decay_row(mine), PART)
     state_ref[:PART, width:] = block
     state_ref[PART:, width:] = block
-    second_ref[...] = state_ref[PART:, :]
-    first_ref[...] = state_ref[pl.ds(pl.multiple_of(jnp.where(chip == 1, PART, 0), PART), PART), :]
-
-
-def middle_kernel(state_ref, near_ref, far_ref, out_ref, lanes_ref):
+
+    def rows(second):
+        return state_ref[pl.ds(pl.multiple_of(jnp.where(second, PART, 0), PART), PART), :]
+
+    first_ref[:, : width + LANES] = rows(chip == 1)
+    first_ref[:, width + LANES :] = jnp.zeros((PART, LANES), BF16)
+    second_ref[...] = rows(chip != 2)
+
+
+def early_kernel(state_ref, near_ref, out_ref):
+    width = out_ref.shape[1] - LANES
+    chip = lax.axis_index("scan")
+    out_ref[:, width:] = jnp.zeros((PART, LANES), BF16)
+
+    @pl.when(chip == 0)
+    def _():
+        out_ref[:, :width] = state_ref[PART:, :width]
+
+    @pl.when(chip == 1)
+    def _():
+        lanes = decay_lanes(state_ref[:16, width : width + LANES], head_of_lane(LANES, width, 6))
+        out_ref[:, :width] = (
+            lanes * near_ref[:, :width].astype(F32) + state_ref[:PART, :width].astype(F32)
+        ).astype(BF16)
+
+
+def middle_kernel(state_ref, near_ref, far_ref, early_ref, out_ref, lanes_ref):
     width = out_ref.shape[1]
     chip = lax.axis_index("scan")
-
-    @pl.when(chip == 0)
-    def _():
-        out_ref[...] = state_ref[PART:, :width]
-
-    @pl.when(chip == 1)
-    def _():
-        lanes = decay_lanes(state_ref[:16, width:], head_of_lane(LANES, width, 6))
-        out_ref[...] = (
-            lanes * near_ref[:, :width].astype(F32) + state_ref[:PART, :width].astype(F32)
-        ).astype(BF16)
-
-    @pl.when(chip > 1)
+    decays = slice(width, width + LANES)
+
+    @pl.when(chip < 2)
+    def _():
+        out_ref[...] = early_ref[:, :width]
+
+    @pl.when(chip == 2)
     def _():
         heads_map = head_of_lane(LANES, width, 6)
-        lanes = decay_lanes(near_ref[:16, width:], heads_map)
+        lanes = decay_lanes(near_ref[:16, decays], heads_map)
         lanes_ref[...] = jnp.broadcast_to(lanes, lanes_ref.shape)
-
-        @pl.when(chip == 2)
-        def _():
-            entered = lanes * far_ref[:, :width].astype(F32) + near_ref[:, :width].astype(F32)
-            own = decay_lanes(state_ref[:16, width:], heads_map)
-            out_ref[...] = (own * entered + state_ref[PART:, :width].astype(F32)).astype(BF16)
+        entered = lanes * far_ref[:, :width].astype(F32) + near_ref[:, :width].astype(F32)
+        own = decay_lanes(state_ref[:16, decays], heads_map)
+        out_ref[...] = (own * entered + state_ref[PART:, :width].astype(F32)).astype(BF16)
+
+    @pl.when(chip == 3)
+    def _():
+        lanes = decay_lanes(far_ref[:16, decays], head_of_lane(LANES, width, 6))
+        lanes_ref[...] = jnp.broadcast_to(lanes, lanes_ref.shape)
 
 
 def enter_kernel(
-    near_ref, far_ref, next_ref, skip_ref, near_lanes_ref, keep_ref, got_ref, lanes_ref, mine_ref, send_ref
+    near_ref, far_ref, early_ref, last_ref, far_lanes_ref, keep_ref, got_ref, lanes_ref, mine_ref, send_ref
 ):
     width = keep_ref.shape[1]
     chip = lax.axis_index("scan")
+    near, far, early = (ref.at[:, pl.ds(0, width)] for ref in (near_ref, far_ref, early_ref))
 
     def parts(first, second):
         enter = jnp.concatenate([first.astype(F32), second.astype(F32)], axis=0)
@@ -440,17 +565,15 @@
 
     @pl.when(chip == 1)
     def _():
-        parts(near_ref[:, :width], next_ref[...])
+        parts(near[...], early[...])
 
     @pl.when(chip == 2)
     def _():
-        near = near_ref[:, :width].astype(F32)
-        parts(next_ref[...], near_lanes_ref[:1] * far_ref[:, :width].astype(F32) + near)
+        parts(last_ref[...], far_lanes_ref[:1] * far[...].astype(F32) + near[...].astype(F32))
 
     @pl.when(chip == 3)
     def _():
-        near = near_ref[:, :width].astype(F32)
-        parts(near_lanes_ref[:1] * skip_ref[...].astype(F32) + near, next_ref[...])
+        parts(far_lanes_ref[:1] * early[...].astype(F32) + far[...].astype(F32), last_ref[...])
 
 
 def share_enter(enter, keep_ref, got_ref, lanes_ref, mine_ref, send_ref):
@@ -490,19 +613,20 @@
         "chip_state",
         [
             jax.ShapeDtypeStruct((HALF, width + LANES), BF16),
-            jax.ShapeDtypeStruct((PART, width + LANES), BF16),
+            jax.ShapeDtypeStruct((PART, width + 2 * LANES), BF16),
             jax.ShapeDtypeStruct((PART, width + LANES), BF16),
         ],
         (keep, got, decay),
     )
 
 
-def entering_state(chips, state, first, second, keep, got, local):
+def entering_state(chips, state, first, second, keep, got, local_one, local_two):
     width = keep.shape[1]
     half = jax.ShapeDtypeStruct((HALF, width), BF16)
     if chips != 4:
         gathered = lax.all_gather(state, "scan", axis=0)
-        base, factor, lanes, gain, weight = local(first)
+        locals_one, lanes = local_one(first)
+        locals_two = local_two(locals_one[0])
         mine, give = local_call(
             gathered_kernel,
             "enter_state",
@@ -510,32 +634,52 @@
             (gathered, keep, got, lanes),
             (pltpu.VMEM((HALF, width), F32),),
         )
-        return mine, give, base, factor, gain, weight
-    near = lax.ppermute(first, "scan", [(0, 1), (1, 2), (2, 3)])
-    far = lax.ppermute(second, "scan", [(0, 2)])
-    base, factor, lanes, gain, weight = local(first)
-    middle, near_lanes = local_call(
+        return mine, give, locals_one, locals_two
+    near = lax.ppermute(first, "scan", [(0, 1), (1, 2)])
+    far = lax.ppermute(second, "scan", [(0, 2), (2, 3)])
+    locals_one, lanes = local_one(first)
+    (ahead,) = local_call(
+        early_kernel,
+        "early_state",
+        [jax.ShapeDtypeStruct((PART, width + LANES), BF16)],
+        (state, near),
+        after=(lanes,),
+    )
+    early = lax.ppermute(ahead, "scan", [(1, 3), (0, 1)])
+    middle, far_lanes = local_call(
         middle_kernel,
         "middle_state",
         [jax.ShapeDtypeStruct((PART, width), BF16), jax.ShapeDtypeStruct((8, width), F32)],
-        (state, near, far),
-        after=(lanes,),
-    )
-    following = lax.ppermute(middle, "scan", [(0, 1), (1, 2), (2, 3)])
-    skipping = lax.ppermute(middle, "scan", [(1, 3)])
+        (state, near, far, ahead),
+    )
+    locals_two = local_two(middle)
+    last = lax.ppermute(middle, "scan", [(1, 2), (2, 3)])
     mine, give = local_call(
         enter_kernel,
         "enter_state",
         [half, half],
-        (near, far, following, skipping, near_lanes, keep, got, lanes),
-    )
-    return mine, give, base, factor, gain, weight
+        (near, far, early, last, far_lanes, keep, got, lanes),
+        after=(locals_two[0],),
+    )
+    return mine, give, locals_one, locals_two
 
 
 def gated_kernel(
-    mine_ref, other_ref, base_ref, factor_ref, read_ref, gain_ref, weight_ref, out_ref, square_ref, *first_refs
+    mine_ref,
+    other_ref,
+    base_ref,
+    base_rest_ref,
+    factor_ref,
+    factor_rest_ref,
+    read_ref,
+    gain_ref,
+    weight_ref,
+    weight_rest_ref,
+    out_ref,
+    square_ref,
+    *first_refs,
 ):
-    tokens, width = base_ref.shape
+    tokens, width = out_ref.shape
     block = column_block(width)
     is_first = lax.axis_index("band") == 0
     read = read_ref[...]
@@ -546,19 +690,23 @@
         low = jnp.where(is_first, mine, other).astype(BF16)
         high = jnp.where(is_first, other, mine).astype(BF16)
         carried = dot(read, jnp.concatenate([low, high], axis=0))
-        gated = base_ref[:, lanes] + factor_ref[:, lanes] * carried
+        base, factor, start = base_ref, factor_ref, first
+        if first >= base_ref.shape[1]:
+            base, factor, start = base_rest_ref, factor_rest_ref, first - base_ref.shape[1]
+        gated = base[:, start : start + block] + factor[:, start : start + block] * carried
         for k in range(0, block, LANES):
             column = gated[:, k : k + LANES]
             row = (first + k) // LANES
             out_ref[:, first + k : first + k + LANES] = (column * gain_ref[row : row + 1, :]).astype(BF16)
             sums += column * column
     for first_ref in first_refs:
-        send_kernel(0, out_ref, weight_ref, first_ref)
+        send_kernel(0, out_ref, weight_ref, weight_rest_ref, first_ref)
     square_ref[...] = jnp.broadcast_to(jnp.sum(sums.T, axis=0, keepdims=True), square_ref.shape)
 
 
-def gated_part(mine, other, base, factor, read_proj, gain, weight, first):
-    tokens, width = base.shape
+def gated_part(mine, other, bases, factors, read_proj, gain, weights, first):
+    tokens = read_proj.shape[0]
+    width = mine.shape[1]
     return local_call(
         gated_kernel,
         "gated_part",
@@ -567,7 +715,7 @@
             jax.ShapeDtypeStruct((8, tokens), F32),
         ]
         + [jax.ShapeDtypeStruct((tokens, first), BF16)] * (first > 0),
-        (mine, other, base, factor, read_proj, gain, weight),
+        (mine, other, *bases, *factors, read_proj, gain, *weights),
         flops=2 * tokens * width * STATE,
     )
 
@@ -575,17 +723,23 @@
 SENDS = (512, 384, 384)
 
 
-def columns_of(weight_ref, other, first, count):
+def project(gated_ref, weight_ref, weight_rest_ref, other, first, count):
     columns = weight_ref.shape[1] // 2
     member = lax.axis_index("tensor")
     start = (1 - member if other else member) * columns + first
-    return weight_ref[:, pl.ds(pl.multiple_of(start, LANES), count)]
-
-
-def send_kernel(first, gated_ref, weight_ref, *refs):
+    lanes = pl.ds(pl.multiple_of(start, LANES), count)
+    rows = weight_ref.shape[0]
+    return dot(gated_ref[:, :rows], weight_ref[:, lanes]) + dot(
+        gated_ref[:, rows:], weight_rest_ref[:, lanes]
+    )
+
+
+def send_kernel(first, gated_ref, weight_ref, weight_rest_ref, *refs):
     out_ref = refs[-1]
     tokens, count = gated_ref.shape[0], out_ref.shape[1]
-    out_ref[:tokens, :] = dot(gated_ref[...], columns_of(weight_ref, True, first, count)).astype(BF16)
+    out_ref[:tokens, :] = project(
+        gated_ref, weight_ref, weight_rest_ref, True, first, count
+    ).astype(BF16)
     for square_ref in refs[:-1]:
         out_ref[tokens:, :] = jnp.zeros((16, count), BF16)
         for lane in range(0, tokens, LANES):
@@ -593,10 +747,12 @@
             out_ref[tokens:, lanes] = decay_block(square_ref[:1, lanes], 16)
 
 
-def own_kernel(gated_ref, weight_ref, out_ref):
-    gated, count = gated_ref[...], out_ref.shape[1] // 5
+def own_kernel(gated_ref, weight_ref, weight_rest_ref, out_ref):
+    count = out_ref.shape[1] // 5
     for first in range(0, out_ref.shape[1], count):
-        out_ref[:, first : first + count] = dot(gated, columns_of(weight_ref, False, first, count))
+        out_ref[:, first : first + count] = project(
+            gated_ref, weight_ref, weight_rest_ref, False, first, count
+        )
 
 
 def finish_kernel(squares_ref, own_ref, *refs):
@@ -643,11 +799,11 @@
     return members == 2 and columns == sum(SENDS)
 
 
-def layer_columns(members, gated, squares, weight, ready):
-    columns = weight.shape[1] // members
+def layer_columns(members, gated, squares, weights, ready):
+    columns = weights[0].shape[1] // members
     if not direct(members, columns):
         mean = lax.psum(squares[0], "tensor") / INNER
-        partial = dot(gated, weight).astype(BF16)
+        partial = dot(gated, jnp.concatenate(weights, axis=0)).astype(BF16)
         total = lax.psum_scatter(partial, "tensor", scatter_dimension=1, tiled=True)
         return (total.astype(F32) * lax.rsqrt(mean + EPSILON)[:, None]).astype(BF16)
     swap = [(0, 1), (1, 0)]
@@ -659,7 +815,7 @@
             functools.partial(send_kernel, first),
             "project_other",
             [jax.ShapeDtypeStruct((tokens + 16 * last, count), BF16)],
-            (gated, weight) + (squares,) * last,
+            (gated, *weights) + (squares,) * last,
             after=parts[-1:],
         )
         first += count
@@ -668,7 +824,7 @@
         own_kernel,
         "project_own",
         [jax.ShapeDtypeStruct((tokens, columns), F32)],
-        (gated, weight),
+        (gated, *weights),
         after=parts[-1:],
     )
     return finish(squares, own, got)
@@ -699,19 +855,30 @@
     got = lax.ppermute(send, "band", cores)
     state, first, second = chip_state(keep, got, decay)
     constants = (skip_gain[None], norm_gain.reshape(-1, LANES), out_weight)
-
-    def local(after):
-        return local_part((running, weight, decay, got, *passed), constants, after)
-
-    mine, give, base, factor, gain, matrix = entering_state(
-        chips, state, first, second, keep, got, local
+    write, read, *streams = passed
+    values = (running, weight, *streams)
+    prepared = []
+
+    def local_one(after):
+        base, factor, matrix, gain, *rest, lanes = local_first(
+            (*values, write, read, decay, got), constants, after
+        )
+        prepared.extend(rest)
+        return (base, factor, matrix, gain), lanes
+
+    def local_two(after):
+        return local_rest(values, prepared, out_weight, after)
+
+    mine, give, (base, factor, matrix, gain), rest = entering_state(
+        chips, state, first, second, keep, got, local_one, local_two
     )
     other = lax.ppermute(give, "band", cores)
     ahead = SENDS[0] if direct(members, matrix.shape[1] // members) else 0
+    weights = (matrix, rest[2])
     gated, squares, *ready = gated_part(
-        mine, other, base, factor, passed[1], gain, matrix, ahead
-    )
-    return layer_columns(members, gated, squares, matrix, ready)
+        mine, other, (base, rest[0]), (factor, rest[1]), read, gain, weights, ahead
+    )
+    return layer_columns(members, gated, squares, weights, ready)
 
 
 def solution(mesh):

time: 51 us -> 48.3 us (0.947); the launches traced: 50.8 us -> 47.4 us
  waiting for transfers between devices: 25.6 us -> 20.9 us
  Pallas kernels: 16.1 us -> 17.3 us
    ppermute x4, waiting for transfers between devices: 12.4 us -> 7.79 us  [the longest x1 7.03 us: entering_state(): last = lax.ppermute(middle, 'scan', [(1, 2), (2, 3)])]
    pallas_call x1 -> x2, Pallas kernels: 5.96 us -> 7.06 us  [local_call_of(): pl.pallas_call(kernel, name=name, out_shape=[jax.ShapeDtypeStruct((tokens...]
    pallas_call x7 -> x8, Pallas kernels: 5.72 us -> 5.84 us  [local_call(): pl.pallas_call(kernel, name=name, out_shape=outs, in_specs=[pl.BlockSpec(...]
  transfers between devices with their start and end apart: 9 -> 9, of which waited for: 6 -> 5; matrix products, arithmetic and copies ran while one was open for 0% -> 0% of each run, Pallas kernels for 19% -> 23%
where the time goes in v4:
time: 48.3 us; the launch traced here: 47.4 us
  waiting for transfers between devices  20.9 us (43%)
  Pallas kernels  17.3 us (36%)
  starting transfers between devices  8.33 us (17%)
  between operations  0.79 us (2%)
    ppermute x3, waiting for transfers between devices, layer_columns(): got = [lax.ppermute(part, 'tensor', swap) for part in parts]  9.88 us
    pallas_call x2, Pallas kernels, local_call_of(): pl.pallas_call(kernel, name=name, out_shape=[jax.ShapeDtypeStruct((tokens...  7.06 us
    ppermute x1, waiting for transfers between devices, entering_state(): last = lax.ppermute(middle, 'scan', [(1, 2), (2, 3)])  7.03 us
    pallas_call x8, Pallas kernels, local_call(): pl.pallas_call(kernel, name=name, out_shape=outs, in_specs=[pl.BlockSpec(...  5.84 us
    ppermute x3, starting transfers between devices, layer_columns(): got = [lax.ppermute(part, 'tensor', swap) for part in parts]  3.64 us
    pallas_call x1, Pallas kernels, own_state(): pl.pallas_call(state_kernel, name='own_state', out_shape=[jax.ShapeDtypeS...  3.35 us
    ppermute x1, waiting for transfers between devices, on_device(): got = lax.ppermute(send, 'band', cores)  1.64 us
    ppermute x1, waiting for transfers between devices, on_device(): other = lax.ppermute(give, 'band', cores)  1.62 us
  transfers between devices with their start and end apart: 9, of which 5 were waited for; matrix products, arithmetic and copies ran while one was open for 0% of the time, Pallas kernels for 23%

profile of v4, /device:TPU:24, one launch (start us, length us, event | category | flops | bytes accessed | tf_op | source)
XLA Modules:
  0.0 47.4 jit_solution(14563891706419808259)
XLA Ops:
  0.7 3.4 %own_state.1 = (f32[40,256]{1,0:T(8,128)S(1)}, f32[40,256]{1,0:T(8,128)S(1)}, bf16[16,128]{1,0:T(8,128)(2,1)S(1)}, f32[64,2560]{1,0:T(8,128)S(1)}, bf16[64,2688]...) custom-call(s32[1]{0:T(128)S(6)} %copy.14.band_ref, ...), custom_call_target="tpu_custom_call" | custom-call | flops 335544320 | bytes 1310720 | tf_op jit(solution)/shard_map/own_state/pallas_call | solution.py:226
  4.0 0.1 collective-permute-start
  4.1 1.6 %collective-permute-done.refs_1_.got_ref.refs_6_ = bf16[64,2688]{1,0:T(8,128)(2,1)S(1)} collective-permute-done((bf16[64,2688]{1,0:T(8,128)(2,1)S(1)}, bf16[64,2688]{1,0:T(8,128)(2,1)S(1)}, u32[]{:S(2)}, u32[]{:S(2)}) %collective-permute-start) | collective-permute-done | bytes 344096 | tf_op jit(solution)/shard_map/ppermute | solution.py:855
  5.7 0.3 chip_state.1
  6.0 0.7 %collective-permute-start.1 = (bf16[32,2816]{1,0:T(8,128)(2,1)S(1)}, bf16[32,2816]{1,0:T(8,128)(2,1)S(1)}, u32[]{:S(2)}, u32[]{:S(2)}) collective-permute-start(bf16[32,2816]{1,0:T(8,128)(2,1)S(1)} %get-tuple-element.39.after_ref), channel_id=1, source_target_pairs={{0,4},{4,8},{1,5},{5,9},{2,6},{6,10},{3,7},{7,11},{16,20},{20,24},... | collective-permute-start | bytes 540680 | tf_op jit(solution)/shard_map/ppermute | solution.py:638
  6.7 1.3 %collective-permute-start.2 = (bf16[32,2688]{1,0:T(8,128)(2,1)S(1)}, bf16[32,2688]{1,0:T(8,128)(2,1)S(1)}, u32[]{:S(2)}, u32[]{:S(2)}) collective-permute-start(bf16[32,2688]{1,0:T(8,128)(2,1)S(1)} %get-tuple-element.40), channel_id=1, source_target_pairs={{0,8},{8,12},{1,9},{9,13},{2,10},{10,14},{3,11},{11,15},{16,24},{2... | collective-permute-start | bytes 516104 | tf_op jit(solution)/shard_map/ppermute | solution.py:639
  8.0 4.9 %local_first.1 = (f32[256,2048]{1,0:T(8,128)S(1)}, f32[256,2048]{1,0:T(8,128)S(1)}, bf16[2048,2560]{1,0:T(8,128)(2,1)S(1)}, f32[20,128]{1,0:T(8,128)S(1)}, f32[2...) custom-call(f32[40,256]{1,0:T(8,128)S(1)} %get-tuple-element.42.runn, ...), custom_call_target="tpu_custom_call" | custom-call | flops 805306368 | bytes 6291456 | tf_op jit(solution)/shard_map/local_first/pallas_call | solution.py:425
  12.9 0.0 collective-permute-done.1.refs_1_.refs_0_
  12.9 1.3 %collective-permute-start.3 = (bf16[32,2688]{1,0:T(8,128)(2,1)S(1)}, bf16[32,2688]{1,0:T(8,128)(2,1)S(1)}, u32[]{:S(2)}, u32[]{:S(2)}) collective-permute-start(bf16[32,2688]{1,0:T(8,128)(2,1)S(1)} %early_state.1.refs_3_), channel_id=1, source_target_pairs={{4,12},{0,4},{5,13},{1,5},{6,14},{2,6},{7,15},{3,7},{20,28},{16,20... | collective-permute-start | bytes 516104 | tf_op jit(solution)/shard_map/ppermute | solution.py:648
  14.2 0.8 %collective-permute-done.2.refs_2_.refs_1_ = bf16[32,2688]{1,0:T(8,128)(2,1)S(1)} collective-permute-done((bf16[32,2688]{1,0:T(8,128)(2,1)S(1)}, bf16[32,2688]{1,0:T(8,128)(2,1)S(1)}, u32[]{:S(2)}, u32[]{:S(2)}) %collective-permute-start.2) | collective-permute-done | bytes 172064 | tf_op jit(solution)/shard_map/ppermute | solution.py:639
  15.0 0.2 middle_state.1
  15.2 1.3 %collective-permute-start.4 = (bf16[32,2560]{1,0:T(8,128)(2,1)S(1)}, bf16[32,2560]{1,0:T(8,128)(2,1)S(1)}, u32[]{:S(2)}, u32[]{:S(2)}) collective-permute-start(bf16[32,2560]{1,0:T(8,128)(2,1)S(1)} %get-tuple-element.49.after_ref), channel_id=1, source_target_pairs={{4,8},{8,12},{5,9},{9,13},{6,10},{10,14},{7,11},{11,15},{20,24},{2... | collective-permute-start | bytes 491528 | tf_op jit(solution)/shard_map/ppermute | solution.py:656
  16.5 2.2 %local_rest.1 = (f32[256,512]{1,0:T(8,128)S(1)}, f32[256,512]{1,0:T(8,128)S(1)}, bf16[512,2560]{1,0:T(8,128)(2,1)S(1)}) custom-call(f32[40,256]{1,0:T(8,128)S(1)} %get-tuple-element.42.running_ref, f32[40,256]{1,0:T(8,128)S(1)} %get-tuple-element.43.weight_ref, bf16[256,2560]{1,0:T(8,128)(2,1)S(1)} %get-tuple-element.44.signal_ref, ...), custom_call_target="tpu_custom_call" | custom-call | flops 201326592 | bytes 1572864 | tf_op jit(solution)/shard_map/local_rest/pallas_call | solution.py:425
  18.6 7.0 %collective-permute-done.4.refs_3_ = bf16[32,2560]{1,0:T(8,128)(2,1)S(1)} collective-permute-done((bf16[32,2560]{1,0:T(8,128)(2,1)S(1)}, bf16[32,2560]{1,0:T(8,128)(2,1)S(1)}, u32[]{:S(2)}, u32[]{:S(2)}) %collective-permute-start.4) | collective-permute-done | bytes 163872 | tf_op jit(solution)/shard_map/ppermute | solution.py:656
  25.6 0.0 collective-permute-done.3.refs_2_
  25.6 0.2 enter_state.1
  25.8 0.1 collective-permute-start.5
  25.9 1.6 %collective-permute-done.5.refs_1_ = bf16[64,2560]{1,0:T(8,128)(2,1)S(1)} collective-permute-done((bf16[64,2560]{1,0:T(8,128)(2,1)S(1)}, bf16[64,2560]{1,0:T(8,128)(2,1)S(1)}, u32[]{:S(2)}, u32[]{:S(2)}) %collective-permute-start.5) | collective-permute-done | bytes 327712 | tf_op jit(solution)/shard_map/ppermute | solution.py:875
  27.5 1.6 %gated_part.1 = (bf16[256,2560]{1,0:T(8,128)(2,1)S(1)}, f32[8,256]{1,0:T(8,128)S(1)}, bf16[256,512]{1,0:T(8,128)(2,1)S(1)}) custom-call(bf16[64,2560]{1,0:T(8,128)(2,1)S(1)} %get-tuple-element.56.refs_0_, bf16[64,2560]{1,0:T(8,128)(2,1)S(1)} %collective-permute-done.5.refs_1_, f32[256,2048]{1,0:T(8,128)S(1)} %get-tuple-element.58.refs_2_, ...), custom_call_target="tpu_custom_call" | custom-call | flops 167772160 | bytes 20662272 | tf_op jit(solution)/shard_map/gated_part/pallas_call | solution.py:107
  29.2 1.5 %collective-permute-start.6 = (bf16[256,512]{1,0:T(8,128)(2,1)S(1)}, bf16[256,512]{1,0:T(8,128)(2,1)S(1)}, u32[]{:S(2)}, u32[]{:S(2)}) collective-permute-start(bf16[256,512]{1,0:T(8,128)(2,1)S(1)} %get-tuple-element.66.refs_3_), channel_id=1, source_target_pairs={{0,2},{2,0},{1,3},{3,1},{4,6},{6,4},{5,7},{7,5},{8,10},{10,8},{9,1... | collective-permute-start | bytes 786440 | tf_op jit(solution)/shard_map/ppermute | solution.py:822
  30.7 0.9 %project_other.2.refs_4_ = bf16[256,384]{1,0:T(8,128)(2,1)S(1)} custom-call(bf16[256,2560]{1,0:T(8,128)(2,1)S(1)} %get-tuple-element.65.refs_0_, bf16[2048,2560]{1,0:T(8,128)(2,1)S(1)} %get-tuple-element.62.refs_8_.refs_1_, bf16[512,2560]{1,0:T(8,128)(2,1)S(1)} %get-tuple-element.63.refs_9_.refs_2_, bf16[256,512]{1,0:T(8,128)(2,1)S(1)} %get-tuple-element.66.refs_3_), custom_call_target="tpu_custom_call" | custom-call | bytes 14614528 | tf_op jit(solution)/shard_map/project_other/pallas_call | solution.py:107
  31.6 0.9 %project_other.3.refs_3_ = bf16[272,384]{1,0:T(8,128)(2,1)S(1)} custom-call(bf16[256,2560]{1,0:T(8,128)(2,1)S(1)} %get-tuple-element.65.refs_0_, bf16[2048,2560]{1,0:T(8,128)(2,1)S(1)} %get-tuple-element.62.refs_8_.refs_1_, bf16[512,2560]{1,0:T(8,128)(2,1)S(1)} %get-tuple-element.63.refs_9_.refs_2_, f32[8,256]{1,0:T(8,128)S(1)} %get-tuple-element.64.refs_3_.squares_ref, ...), custom_call_target="tpu_custom_call" | custom-call | bytes 14635008 | tf_op jit(solution)/shard_map/project_other/pallas_call | solution.py:107
  32.5 0.6 %collective-permute-start.8 = (bf16[272,384]{1,0:T(8,128)(2,1)S(1)}, bf16[272,384]{1,0:T(8,128)(2,1)S(1)}, u32[]{:S(2)}, u32[]{:S(2)}) collective-permute-start(bf16[272,384]{1,0:T(8,128)(2,1)S(1)} %project_other.3.refs_3_), channel_id=1, source_target_pairs={{0,2},{2,0},{1,3},{3,1},{4,6},{6,4},{5,7},{7,5},{8,10},{10,8},{9,1... | collective-permute-start | bytes 626696 | tf_op jit(solution)/shard_map/ppermute | solution.py:822
  33.1 1.5 %collective-permute-start.7 = (bf16[256,384]{1,0:T(8,128)(2,1)S(1)}, bf16[256,384]{1,0:T(8,128)(2,1)S(1)}, u32[]{:S(2)}, u32[]{:S(2)}) collective-permute-start(bf16[256,384]{1,0:T(8,128)(2,1)S(1)} %project_other.2.refs_4_), channel_id=1, source_target_pairs={{0,2},{2,0},{1,3},{3,1},{4,6},{6,4},{5,7},{7,5},{8,10},{10,8},{9,1... | collective-permute-start | bytes 589832 | tf_op jit(solution)/shard_map/ppermute | solution.py:822
  34.6 1.8 %project_own.1.own_ref = f32[256,1280]{1,0:T(8,128)S(1)} custom-call(bf16[256,2560]{1,0:T(8,128)(2,1)S(1)} %get-tuple-element.65.refs_0_, bf16[2048,2560]{1,0:T(8,128)(2,1)S(1)} %get-tuple-element.62.refs_8_.refs_1_, bf16[512,2560]{1,0:T(8,128)(2,1)S(1)} %get-tuple-element.63.refs_9_.refs_2_, bf16[272,384]{1,0:T(8,128)(2,1)S(1)} %project_other.3.refs_3_), custom_call_target="tpu_custom_call" | custom-call | bytes 15728640 | tf_op jit(solution)/shard_map/project_own/pallas_call | solution.py:107
  36.4 9.9 %collective-permute-done.7.refs_1_ = bf16[256,384]{1,0:T(8,128)(2,1)S(1)} collective-permute-done((bf16[256,384]{1,0:T(8,128)(2,1)S(1)}, bf16[256,384]{1,0:T(8,128)(2,1)S(1)}, u32[]{:S(2)}, u32[]{:S(2)}) %collective-permute-start.7) | collective-permute-done | bytes 196640 | tf_op jit(solution)/shard_map/ppermute | solution.py:822
  46.3 0.0 collective-permute-done.8.refs_2_
  46.3 0.0 collective-permute-done.6.refs_0_
  46.3 1.1 %finish.1 = bf16[256,1280]{1,0:T(8,128)(2,1)} custom-call(f32[8,256]{1,0:T(8,128)S(1)} %get-tuple-element.64.refs_3_.squares_ref, f32[256,1280]{1,0:T(8,128)S(1)} %project_own.1.own_ref, bf16[256,512]{1,0:T(8,128)(2,1)S(1)} %collective-permute-done.6.refs_0_, bf16[256,384]{1,0:T(8,128)(2,1)S(1)} %collective-permute-done.7.refs_1_, ...), custom_call_target="tpu_custom_call" | custom-call | tf_op jit(solution)/shard_map/finish/pallas_call | solution.py:784
  (1 shorter events, 0.0 us)
Async XLA Ops:
  4.0 1.7 %collective-permute-start = (bf16[64,2688]{1,0:T(8,128)(2,1)S(1)}, bf16[64,2688]{1,0:T(8,128)(2,1)S(1)}, u32[]{:S(2)}, u32[]{:S(2)}) collective-permute-start(bf16[64,2688]{1,0:T(8,128)(2,1)S(1)} %get-tuple-element.37), channel_id=1, source_target_pairs={{0,1},{1,0},{2,3},{3,2},{4,5},{5,4},{6,7},{7,6},{8,9},{9,8},{10,11... | collective-permute-start | bytes 1032200 | tf_op jit(solution)/shard_map/ppermute | solution.py:855
  6.0 6.9 %collective-permute-start.1 = (bf16[32,2816]{1,0:T(8,128)(2,1)S(1)}, bf16[32,2816]{1,0:T(8,128)(2,1)S(1)}, u32[]{:S(2)}, u32[]{:S(2)}) collective-permute-start(bf16[32,2816]{1,0:T(8,128)(2,1)S(1)} %get-tuple-element.39.after_ref), channel_id=1, source_target_pairs={{0,4},{4,8},{1,5},{5,9},{2,6},{6,10},{3,7},{7,11},{16,20},{20,24},... | collective-permute-start | bytes 540680 | tf_op jit(solution)/shard_map/ppermute | solution.py:638
  6.7 8.3 %collective-permute-start.2 = (bf16[32,2688]{1,0:T(8,128)(2,1)S(1)}, bf16[32,2688]{1,0:T(8,128)(2,1)S(1)}, u32[]{:S(2)}, u32[]{:S(2)}) collective-permute-start(bf16[32,2688]{1,0:T(8,128)(2,1)S(1)} %get-tuple-element.40), channel_id=1, source_target_pairs={{0,8},{8,12},{1,9},{9,13},{2,10},{10,14},{3,11},{11,15},{16,24},{2... | collective-permute-start | bytes 516104 | tf_op jit(solution)/shard_map/ppermute | solution.py:639
  12.9 12.7 %collective-permute-start.3 = (bf16[32,2688]{1,0:T(8,128)(2,1)S(1)}, bf16[32,2688]{1,0:T(8,128)(2,1)S(1)}, u32[]{:S(2)}, u32[]{:S(2)}) collective-permute-start(bf16[32,2688]{1,0:T(8,128)(2,1)S(1)} %early_state.1.refs_3_), channel_id=1, source_target_pairs={{4,12},{0,4},{5,13},{1,5},{6,14},{2,6},{7,15},{3,7},{20,28},{16,20... | collective-permute-start | bytes 516104 | tf_op jit(solution)/shard_map/ppermute | solution.py:648
  15.2 10.5 %collective-permute-start.4 = (bf16[32,2560]{1,0:T(8,128)(2,1)S(1)}, bf16[32,2560]{1,0:T(8,128)(2,1)S(1)}, u32[]{:S(2)}, u32[]{:S(2)}) collective-permute-start(bf16[32,2560]{1,0:T(8,128)(2,1)S(1)} %get-tuple-element.49.after_ref), channel_id=1, source_target_pairs={{4,8},{8,12},{5,9},{9,13},{6,10},{10,14},{7,11},{11,15},{20,24},{2... | collective-permute-start | bytes 491528 | tf_op jit(solution)/shard_map/ppermute | solution.py:656
  25.8 1.7 %collective-permute-start.5 = (bf16[64,2560]{1,0:T(8,128)(2,1)S(1)}, bf16[64,2560]{1,0:T(8,128)(2,1)S(1)}, u32[]{:S(2)}, u32[]{:S(2)}) collective-permute-start(bf16[64,2560]{1,0:T(8,128)(2,1)S(1)} %get-tuple-element.57), channel_id=1, source_target_pairs={{0,1},{1,0},{2,3},{3,2},{4,5},{5,4},{6,7},{7,6},{8,9},{9,8},{10,11... | collective-permute-start | bytes 983048 | tf_op jit(solution)/shard_map/ppermute | solution.py:875
  29.2 17.1 %collective-permute-start.6 = (bf16[256,512]{1,0:T(8,128)(2,1)S(1)}, bf16[256,512]{1,0:T(8,128)(2,1)S(1)}, u32[]{:S(2)}, u32[]{:S(2)}) collective-permute-start(bf16[256,512]{1,0:T(8,128)(2,1)S(1)} %get-tuple-element.66.refs_3_), channel_id=1, source_target_pairs={{0,2},{2,0},{1,3},{3,1},{4,6},{6,4},{5,7},{7,5},{8,10},{10,8},{9,1... | collective-permute-start | bytes 786440 | tf_op jit(solution)/shard_map/ppermute | solution.py:822
  32.5 13.8 %collective-permute-start.8 = (bf16[272,384]{1,0:T(8,128)(2,1)S(1)}, bf16[272,384]{1,0:T(8,128)(2,1)S(1)}, u32[]{:S(2)}, u32[]{:S(2)}) collective-permute-start(bf16[272,384]{1,0:T(8,128)(2,1)S(1)} %project_other.3.refs_3_), channel_id=1, source_target_pairs={{0,2},{2,0},{1,3},{3,1},{4,6},{6,4},{5,7},{7,5},{8,10},{10,8},{9,1... | collective-permute-start | bytes 626696 | tf_op jit(solution)/shard_map/ppermute | solution.py:822
  33.1 13.2 %collective-permute-start.7 = (bf16[256,384]{1,0:T(8,128)(2,1)S(1)}, bf16[256,384]{1,0:T(8,128)(2,1)S(1)}, u32[]{:S(2)}, u32[]{:S(2)}) collective-permute-start(bf16[256,384]{1,0:T(8,128)(2,1)S(1)} %project_other.2.refs_4_), channel_id=1, source_target_pairs={{0,2},{2,0},{1,3},{3,1},{4,6},{6,4},{5,7},{7,5},{8,10},{10,8},{9,1... | collective-permute-start | bytes 589832 | tf_op jit(solution)/shard_map/ppermute | solution.py:822

commit v5 on v4

--- a/solution.py
+++ b/solution.py
@@ -98,7 +98,7 @@
     return width // 5 if width % (5 * LANES) == 0 else width
 
 
-def local_call(body, name, outs, args, scratch=(), limit=8 * MIB, flops=0, after=()):
+def local_call(body, name, outs, args, scratch=(), limit=8 * MIB, flops=0, after=(), aliases=None):
     size = sum(a.size * a.dtype.itemsize for a in args) + sum(o.size * o.dtype.itemsize for o in outs)
 
     def kernel(*refs):
@@ -112,6 +112,7 @@
         + [pl.BlockSpec(memory_space=pl.ANY)] * len(after),
         out_specs=[pl.BlockSpec(memory_space=pltpu.VMEM)] * len(outs),
         scratch_shapes=list(scratch),
+        input_output_aliases=aliases or {},
         compiler_params=pltpu.CompilerParams(vmem_limit_bytes=limit),
         cost_estimate=pl.CostEstimate(flops=flops, bytes_accessed=size, transcendentals=0),
     )(*args, *after)
@@ -343,6 +344,7 @@
     read_ref,
     decay_ref,
     got_ref,
+    state_ref,
     skip_hbm,
     gain_hbm,
     matrix_hbm,
@@ -350,6 +352,7 @@
     base_ref,
     factor_ref,
     matrix_ref,
+    second_ref,
     gain_ref,
     scores_ref,
     running_pieces_ref,
@@ -368,6 +371,8 @@
     copies = [pltpu.make_async_copy(*pair, sems.at[i]) for i, pair in enumerate(pairs)]
     for copy in copies:
         copy.start()
+    upper = lax.axis_index("scan") == 2
+    second_ref[...] = state_ref[pl.ds(pl.multiple_of(jnp.where(upper, 0, PART), PART), PART), :]
     prepared = (scores_ref, running_pieces_ref, decay_pieces_ref)
     prepare_local(running_ref, write_ref, read_ref, decay_ref, got_ref, *prepared, lanes_ref, rows_ref)
     copies[0].wait()
@@ -379,6 +384,8 @@
 
 
 def local_rest_kernel(
+    first_block,
+    first_row,
     running_ref,
     weight_ref,
     signal_ref,
@@ -395,12 +402,10 @@
     sem,
 ):
     rows = matrix_ref.shape[0]
-    copy = pltpu.make_async_copy(
-        matrix_hbm.at[pl.ds(matrix_hbm.shape[0] - rows, rows), :], matrix_ref, sem
-    )
+    copy = pltpu.make_async_copy(matrix_hbm.at[pl.ds(first_row, rows), :], matrix_ref, sem)
     copy.start()
     local_heads(
-        (signal_ref.shape[1] - rows) // column_block(signal_ref.shape[1]),
+        first_block,
         running_ref,
         weight_ref,
         signal_ref,
@@ -415,18 +420,23 @@
     copy.wait()
 
 
-def first_columns(width):
-    return 4 * (width // 5) if width % (5 * LANES) == 0 else width // 2
-
-
-def local_call_of(kernel, name, heads, columns, outs, resident, passed, after, scratch):
-    tokens = resident[0].shape[1]
+def local_shares(width):
+    if width % (10 * LANES):
+        return (width // column_block(width), 0, 0), (width, 0, 0)
+    tenth = width // 10
+    return (1, 2, 2), (tenth, 3 * tenth, 6 * tenth)
+
+
+def local_call_of(kernel, name, part, outs, resident, passed, after, scratch):
+    tokens, width = resident[2].shape
     matrix = passed[-1]
+    blocks, rows = local_shares(width)
+    columns = blocks[part] * column_block(width)
     return pl.pallas_call(
         kernel,
         name=name,
         out_shape=[jax.ShapeDtypeStruct((tokens, columns), F32)] * 2
-        + [jax.ShapeDtypeStruct((columns, matrix.shape[1]), BF16)]
+        + [jax.ShapeDtypeStruct((rows[part], matrix.shape[1]), BF16)]
         + outs,
         in_specs=[IN_VMEM] * len(resident) + [IN_HBM] * len(passed) + [ANYWHERE],
         out_specs=[IN_VMEM] * (3 + len(outs)),
@@ -440,18 +450,17 @@
     )(*resident, *in_hbm(*passed), after)
 
 
-def local_first(values, constants, after):
+def local_first(values, state, constants, after):
     running, signal = values[0], values[2]
     skip_gain, norm_gain, _ = constants
-    heads, tokens = running.shape
-    width = signal.shape[1]
+    tokens, width = signal.shape
     pieces_shape = jax.ShapeDtypeStruct((tokens, LANES), BF16)
     return local_call_of(
         local_first_kernel,
         "local_first",
-        heads,
-        first_columns(width),
+        0,
         [
+            jax.ShapeDtypeStruct((PART, state.shape[1]), BF16),
             jax.ShapeDtypeStruct(norm_gain.shape, F32),
             jax.ShapeDtypeStruct((tokens, tokens), F32),
             pieces_shape,
@@ -459,21 +468,19 @@
             jax.ShapeDtypeStruct(skip_gain.shape, F32),
             jax.ShapeDtypeStruct((8, width), F32),
         ],
-        values,
+        (*values, state),
         constants,
         after,
         [pltpu.VMEM((LANES, tokens), F32), pltpu.SemaphoreType.DMA((3,))],
     )
 
 
-def local_rest(values, prepared, out_weight, after):
-    running, signal = values[0], values[2]
-    width = signal.shape[1]
+def local_rest(part, values, prepared, out_weight, after):
+    blocks, rows = local_shares(values[2].shape[1])
     return local_call_of(
-        local_rest_kernel,
+        functools.partial(local_rest_kernel, sum(blocks[:part]), sum(rows[:part])),
         "local_rest",
-        running.shape[0],
-        width - first_columns(width),
+        part,
         [],
         (*values, *prepared),
         (out_weight,),
@@ -482,7 +489,7 @@
     )
 
 
-def chip_kernel(keep_ref, got_ref, decay_ref, state_ref, first_ref, second_ref):
+def chip_kernel(keep_ref, got_ref, decay_ref, state_ref, first_ref):
     width = keep_ref.shape[1]
     core = lax.axis_index("band")
     chip = lax.axis_index("scan")
@@ -499,96 +506,103 @@
     state_ref[:PART, width:] = block
     state_ref[PART:, width:] = block
 
-    def rows(second):
-        return state_ref[pl.ds(pl.multiple_of(jnp.where(second, PART, 0), PART), PART), :]
-
-    first_ref[:, : width + LANES] = rows(chip == 1)
-    first_ref[:, width + LANES :] = jnp.zeros((PART, LANES), BF16)
-    second_ref[...] = rows(chip != 2)
+    lower = jnp.where(chip == 1, PART, 0)
+    first_ref[...] = state_ref[pl.ds(pl.multiple_of(lower, PART), PART), :]
 
 
 def early_kernel(state_ref, near_ref, out_ref):
-    width = out_ref.shape[1] - LANES
+    width = out_ref.shape[1]
     chip = lax.axis_index("scan")
-    out_ref[:, width:] = jnp.zeros((PART, LANES), BF16)
 
     @pl.when(chip == 0)
     def _():
-        out_ref[:, :width] = state_ref[PART:, :width]
+        out_ref[...] = state_ref[PART:, :width]
 
     @pl.when(chip == 1)
     def _():
-        lanes = decay_lanes(state_ref[:16, width : width + LANES], head_of_lane(LANES, width, 6))
-        out_ref[:, :width] = (
+        lanes = decay_lanes(state_ref[:16, width:], head_of_lane(LANES, width, 6))
+        out_ref[...] = (
             lanes * near_ref[:, :width].astype(F32) + state_ref[:PART, :width].astype(F32)
         ).astype(BF16)
 
 
-def middle_kernel(state_ref, near_ref, far_ref, early_ref, out_ref, lanes_ref):
+def middle_kernel(state_ref, near_ref, far_ref, out_ref, lanes_ref):
     width = out_ref.shape[1]
     chip = lax.axis_index("scan")
-    decays = slice(width, width + LANES)
-
-    @pl.when(chip < 2)
-    def _():
-        out_ref[...] = early_ref[:, :width]
 
     @pl.when(chip == 2)
     def _():
         heads_map = head_of_lane(LANES, width, 6)
-        lanes = decay_lanes(near_ref[:16, decays], heads_map)
+        lanes = decay_lanes(near_ref[:16, width:], heads_map)
         lanes_ref[...] = jnp.broadcast_to(lanes, lanes_ref.shape)
         entered = lanes * far_ref[:, :width].astype(F32) + near_ref[:, :width].astype(F32)
-        own = decay_lanes(state_ref[:16, decays], heads_map)
+        own = decay_lanes(state_ref[:16, width:], heads_map)
         out_ref[...] = (own * entered + state_ref[PART:, :width].astype(F32)).astype(BF16)
 
     @pl.when(chip == 3)
     def _():
-        lanes = decay_lanes(far_ref[:16, decays], head_of_lane(LANES, width, 6))
+        lanes = decay_lanes(far_ref[:16, width:], head_of_lane(LANES, width, 6))
         lanes_ref[...] = jnp.broadcast_to(lanes, lanes_ref.shape)
 
 
 def enter_kernel(
-    near_ref, far_ref, early_ref, last_ref, far_lanes_ref, keep_ref, got_ref, lanes_ref, mine_ref, send_ref
+    near_ref,
+    far_ref,
+    early_ref,
+    next_ref,
+    far_lanes_ref,
+    keep_ref,
+    got_ref,
+    lanes_ref,
+    mine_ref,
+    send_ref,
 ):
     width = keep_ref.shape[1]
     chip = lax.axis_index("scan")
-    near, far, early = (ref.at[:, pl.ds(0, width)] for ref in (near_ref, far_ref, early_ref))
-
-    def parts(first, second):
-        enter = jnp.concatenate([first.astype(F32), second.astype(F32)], axis=0)
-        share_enter(enter, keep_ref, got_ref, lanes_ref, mine_ref, send_ref)
+    near, far = (ref.at[:, pl.ds(0, width)] for ref in (near_ref, far_ref))
+    refs = (keep_ref, got_ref, lanes_ref, mine_ref, send_ref)
 
     @pl.when(chip == 0)
     def _():
-        share_enter(jnp.zeros((HALF, width), F32), keep_ref, got_ref, lanes_ref, mine_ref, send_ref)
+        share_enter(jnp.zeros((HALF, width), F32), 0, *refs)
 
     @pl.when(chip == 1)
     def _():
-        parts(near[...], early[...])
+        share_enter(near[...].astype(F32), 0, *refs)
+        share_enter(early_ref[...].astype(F32), PART, *refs)
 
     @pl.when(chip == 2)
     def _():
-        parts(last_ref[...], far_lanes_ref[:1] * far[...].astype(F32) + near[...].astype(F32))
+        share_enter(next_ref[...].astype(F32), 0, *refs)
+        share_enter(far_lanes_ref[:1] * far[...].astype(F32) + near[...].astype(F32), PART, *refs)
 
     @pl.when(chip == 3)
     def _():
-        parts(far_lanes_ref[:1] * early[...].astype(F32) + far[...].astype(F32), last_ref[...])
-
-
-def share_enter(enter, keep_ref, got_ref, lanes_ref, mine_ref, send_ref):
+        share_enter(far_lanes_ref[:1] * early_ref[...].astype(F32) + far[...].astype(F32), 0, *refs)
+
+
+def enter_last_kernel(last_ref, keep_ref, got_ref, lanes_ref, old_mine, old_send, mine_ref, send_ref):
+    @pl.when(lax.axis_index("scan") == 3)
+    def _():
+        share_enter(
+            last_ref[...].astype(F32), PART, keep_ref, got_ref, lanes_ref, mine_ref, send_ref
+        )
+
+
+def share_enter(enter, first, keep_ref, got_ref, lanes_ref, mine_ref, send_ref):
     width = keep_ref.shape[1]
     core = lax.axis_index("band")
+    rows = slice(first, first + enter.shape[0])
 
     @pl.when(core == 0)
     def _():
-        mine_ref[...] = enter.astype(BF16)
-        send_ref[...] = (lanes_ref[:1] * enter + keep_ref[...]).astype(BF16)
+        mine_ref[rows, :] = enter.astype(BF16)
+        send_ref[rows, :] = (lanes_ref[:1] * enter + keep_ref[rows, :]).astype(BF16)
 
     @pl.when(core == 1)
     def _():
-        send_ref[...] = enter.astype(BF16)
-        mine_ref[...] = (lanes_ref[:1] * enter + got_ref[:, :width].astype(F32)).astype(BF16)
+        send_ref[rows, :] = enter.astype(BF16)
+        mine_ref[rows, :] = (lanes_ref[:1] * enter + got_ref[rows, :width].astype(F32)).astype(BF16)
 
 
 def gathered_kernel(all_ref, keep_ref, got_ref, lanes_ref, mine_ref, send_ref, enter_ref):
@@ -603,7 +617,7 @@
             lanes = decay_lanes(all_ref[source, :16, width:], heads_map)
             enter_ref[...] = lanes * enter_ref[...] + all_ref[source, :, :width].astype(F32)
 
-    share_enter(enter_ref[...], keep_ref, got_ref, lanes_ref, mine_ref, send_ref)
+    share_enter(enter_ref[...], 0, keep_ref, got_ref, lanes_ref, mine_ref, send_ref)
 
 
 def chip_state(keep, got, decay):
@@ -613,109 +627,108 @@
         "chip_state",
         [
             jax.ShapeDtypeStruct((HALF, width + LANES), BF16),
-            jax.ShapeDtypeStruct((PART, width + 2 * LANES), BF16),
             jax.ShapeDtypeStruct((PART, width + LANES), BF16),
         ],
         (keep, got, decay),
     )
 
 
-def entering_state(chips, state, first, second, keep, got, local_one, local_two):
+def entering_state(chips, state, first, keep, got, local):
     width = keep.shape[1]
     half = jax.ShapeDtypeStruct((HALF, width), BF16)
     if chips != 4:
         gathered = lax.all_gather(state, "scan", axis=0)
-        locals_one, lanes = local_one(first)
-        locals_two = local_two(locals_one[0])
-        mine, give = local_call(
+        second, lanes = local(0, first)
+        local(1, second)
+        local(2, second)
+        return local_call(
             gathered_kernel,
             "enter_state",
             [half, half],
             (gathered, keep, got, lanes),
             (pltpu.VMEM((HALF, width), F32),),
         )
-        return mine, give, locals_one, locals_two
     near = lax.ppermute(first, "scan", [(0, 1), (1, 2)])
+    second, lanes = local(0, first)
     far = lax.ppermute(second, "scan", [(0, 2), (2, 3)])
-    locals_one, lanes = local_one(first)
+    done = local(1, second)
     (ahead,) = local_call(
         early_kernel,
         "early_state",
-        [jax.ShapeDtypeStruct((PART, width + LANES), BF16)],
+        [jax.ShapeDtypeStruct((PART, width), BF16)],
         (state, near),
-        after=(lanes,),
+        after=(done,),
     )
     early = lax.ppermute(ahead, "scan", [(1, 3), (0, 1)])
+    following = lax.ppermute(ahead, "scan", [(1, 2)])
     middle, far_lanes = local_call(
         middle_kernel,
         "middle_state",
         [jax.ShapeDtypeStruct((PART, width), BF16), jax.ShapeDtypeStruct((8, width), F32)],
-        (state, near, far, ahead),
-    )
-    locals_two = local_two(middle)
-    last = lax.ppermute(middle, "scan", [(1, 2), (2, 3)])
+        (state, near, far),
+        after=(ahead,),
+    )
+    last = lax.ppermute(middle, "scan", [(2, 3)])
+    done = local(2, middle)
     mine, give = local_call(
         enter_kernel,
         "enter_state",
         [half, half],
-        (near, far, early, last, far_lanes, keep, got, lanes),
-        after=(locals_two[0],),
-    )
-    return mine, give, locals_one, locals_two
-
-
-def gated_kernel(
-    mine_ref,
-    other_ref,
-    base_ref,
-    base_rest_ref,
-    factor_ref,
-    factor_rest_ref,
-    read_ref,
-    gain_ref,
-    weight_ref,
-    weight_rest_ref,
-    out_ref,
-    square_ref,
-    *first_refs,
-):
+        (near, far, early, following, far_lanes, keep, got, lanes),
+        after=(done,),
+    )
+    return local_call(
+        enter_last_kernel,
+        "enter_last",
+        [half, half],
+        (last, keep, got, lanes, mine, give),
+        aliases={4: 0, 5: 1},
+    )
+
+
+def gated_kernel(parts, mine_ref, other_ref, read_ref, gain_ref, *refs):
+    bases, factors, weights = refs[:parts], refs[parts : 2 * parts], refs[2 * parts : 3 * parts]
+    out_ref, square_ref, *first_refs = refs[3 * parts :]
     tokens, width = out_ref.shape
     block = column_block(width)
     is_first = lax.axis_index("band") == 0
     read = read_ref[...]
     sums = jnp.zeros((tokens, LANES), F32)
-    for first in range(0, width, block):
-        lanes = slice(first, first + block)
-        mine, other = mine_ref[:, lanes].astype(F32), other_ref[:, lanes].astype(F32)
-        low = jnp.where(is_first, mine, other).astype(BF16)
-        high = jnp.where(is_first, other, mine).astype(BF16)
-        carried = dot(read, jnp.concatenate([low, high], axis=0))
-        base, factor, start = base_ref, factor_ref, first
-        if first >= base_ref.shape[1]:
-            base, factor, start = base_rest_ref, factor_rest_ref, first - base_ref.shape[1]
-        gated = base[:, start : start + block] + factor[:, start : start + block] * carried
-        for k in range(0, block, LANES):
-            column = gated[:, k : k + LANES]
-            row = (first + k) // LANES
-            out_ref[:, first + k : first + k + LANES] = (column * gain_ref[row : row + 1, :]).astype(BF16)
-            sums += column * column
+    first = 0
+    for base_ref, factor_ref in zip(bases, factors):
+        for start in range(0, base_ref.shape[1], block):
+            lanes = slice(first, first + block)
+            mine, other = mine_ref[:, lanes].astype(F32), other_ref[:, lanes].astype(F32)
+            low = jnp.where(is_first, mine, other).astype(BF16)
+            high = jnp.where(is_first, other, mine).astype(BF16)
+            carried = dot(read, jnp.concatenate([low, high], axis=0))
+            lanes = slice(start, start + block)
+            gated = base_ref[:, lanes] + factor_ref[:, lanes] * carried
+            for k in range(0, block, LANES):
+                column = gated[:, k : k + LANES]
+                row = (first + k) // LANES
+                out_ref[:, first + k : first + k + LANES] = (
+                    column * gain_ref[row : row + 1, :]
+                ).astype(BF16)
+                sums += column * column
+            first += block
     for first_ref in first_refs:
-        send_kernel(0, out_ref, weight_ref, weight_rest_ref, first_ref)
+        send_kernel(0, out_ref, *weights, first_ref)
     square_ref[...] = jnp.broadcast_to(jnp.sum(sums.T, axis=0, keepdims=True), square_ref.shape)
 
 
-def gated_part(mine, other, bases, factors, read_proj, gain, weights, first):
+def gated_part(mine, other, read_proj, gain, bases, factors, weights, first):
     tokens = read_proj.shape[0]
     width = mine.shape[1]
     return local_call(
-        gated_kernel,
+        functools.partial(gated_kernel, len(bases)),
         "gated_part",
         [
             jax.ShapeDtypeStruct((tokens, width), BF16),
             jax.ShapeDtypeStruct((8, tokens), F32),
         ]
         + [jax.ShapeDtypeStruct((tokens, first), BF16)] * (first > 0),
-        (mine, other, *bases, *factors, read_proj, gain, *weights),
+        (mine, other, read_proj, gain, *bases, *factors, *weights),
         flops=2 * tokens * width * STATE,
     )
 
@@ -723,36 +736,36 @@
 SENDS = (512, 384, 384)
 
 
-def project(gated_ref, weight_ref, weight_rest_ref, other, first, count):
-    columns = weight_ref.shape[1] // 2
+def project(gated_ref, weights, other, first, count):
+    columns = weights[0].shape[1] // 2
     member = lax.axis_index("tensor")
     start = (1 - member if other else member) * columns + first
     lanes = pl.ds(pl.multiple_of(start, LANES), count)
-    rows = weight_ref.shape[0]
-    return dot(gated_ref[:, :rows], weight_ref[:, lanes]) + dot(
-        gated_ref[:, rows:], weight_rest_ref[:, lanes]
-    )
-
-
-def send_kernel(first, gated_ref, weight_ref, weight_rest_ref, *refs):
-    out_ref = refs[-1]
+    row, total = 0, None
+    for weight_ref in weights:
+        rows = weight_ref.shape[0]
+        term = dot(gated_ref[:, row : row + rows], weight_ref[:, lanes])
+        row, total = row + rows, term if total is None else total + term
+    return total
+
+
+def send_kernel(first, gated_ref, *refs, squares=False):
+    *refs, out_ref = refs
+    weights = refs[:-1] if squares else refs
     tokens, count = gated_ref.shape[0], out_ref.shape[1]
-    out_ref[:tokens, :] = project(
-        gated_ref, weight_ref, weight_rest_ref, True, first, count
-    ).astype(BF16)
-    for square_ref in refs[:-1]:
+    out_ref[:tokens, :] = project(gated_ref, weights, True, first, count).astype(BF16)
+    if squares:
         out_ref[tokens:, :] = jnp.zeros((16, count), BF16)
         for lane in range(0, tokens, LANES):
             lanes = slice(lane, lane + LANES)
-            out_ref[tokens:, lanes] = decay_block(square_ref[:1, lanes], 16)
-
-
-def own_kernel(gated_ref, weight_ref, weight_rest_ref, out_ref):
+            out_ref[tokens:, lanes] = decay_block(refs[-1][:1, lanes], 16)
+
+
+def own_kernel(gated_ref, *refs):
+    *weights, out_ref = refs
     count = out_ref.shape[1] // 5
     for first in range(0, out_ref.shape[1], count):
-        out_ref[:, first : first + count] = project(
-            gated_ref, weight_ref, weight_rest_ref, False, first, count
-        )
+        out_ref[:, first : first + count] = project(gated_ref, weights, False, first, count)
 
 
 def finish_kernel(squares_ref, own_ref, *refs):
@@ -812,7 +825,7 @@
     for count in SENDS[1:]:
         last = first + count == columns
         parts += local_call(
-            functools.partial(send_kernel, first),
+            functools.partial(send_kernel, first, squares=last),
             "project_other",
             [jax.ShapeDtypeStruct((tokens + 16 * last, count), BF16)],
             (gated, *weights) + (squares,) * last,
@@ -853,30 +866,33 @@
     )
     cores = [(0, 1), (1, 0)]
     got = lax.ppermute(send, "band", cores)
-    state, first, second = chip_state(keep, got, decay)
+    state, first = chip_state(keep, got, decay)
     constants = (skip_gain[None], norm_gain.reshape(-1, LANES), out_weight)
     write, read, *streams = passed
     values = (running, weight, *streams)
-    prepared = []
-
-    def local_one(after):
-        base, factor, matrix, gain, *rest, lanes = local_first(
-            (*values, write, read, decay, got), constants, after
-        )
-        prepared.extend(rest)
-        return (base, factor, matrix, gain), lanes
-
-    def local_two(after):
-        return local_rest(values, prepared, out_weight, after)
-
-    mine, give, (base, factor, matrix, gain), rest = entering_state(
-        chips, state, first, second, keep, got, local_one, local_two
-    )
+    bases, factors, weights, prepared, gains = [], [], [], [], []
+
+    def local(part, after):
+        if not local_shares(signal.shape[1])[0][part]:
+            return after
+        if part:
+            base, factor, matrix = local_rest(part, values, prepared, out_weight, after)
+        else:
+            base, factor, matrix, second, gain, *rest, lanes = local_first(
+                (*values, write, read, decay, got), state, constants, after
+            )
+            prepared.extend(rest)
+            gains.append(gain)
+        bases.append(base)
+        factors.append(factor)
+        weights.append(matrix)
+        return base if part else (second, lanes)
+
+    mine, give = entering_state(chips, state, first, keep, got, local)
     other = lax.ppermute(give, "band", cores)
-    ahead = SENDS[0] if direct(members, matrix.shape[1] // members) else 0
-    weights = (matrix, rest[2])
+    ahead = SENDS[0] if direct(members, out_weight.shape[1] // members) else 0
     gated, squares, *ready = gated_part(
-        mine, other, (base, rest[0]), (factor, rest[1]), read, gain, weights, ahead
+        mine, other, read, gains[0], bases, factors, weights, ahead
     )
     return layer_columns(members, gated, squares, weights, ready)
 

time: 48.3 us -> 47.2 us (0.977)
  waiting for transfers between devices: 20.9 us -> 19.6 us
  starting transfers between devices: 8.33 us -> 8.99 us
    ppermute x1 -> x2, waiting for transfers between devices: 7.03 us -> 3.15 us  [the longest x1 3.15 us: entering_state(): last = lax.ppermute(middle, 'scan', [(2, 3)])]
    ppermute x1, waiting for transfers between devices: 0.76 us -> 2.85 us  [entering_state(): far = lax.ppermute(second, 'scan', [(0, 2), (2, 3)])]
    ppermute x1 -> x2, starting transfers between devices: 1.29 us -> 1.96 us  [the longest x1 1.29 us: entering_state(): last = lax.ppermute(middle, 'scan', [(2, 3)])]
    pallas_call x8 -> x9, Pallas kernels: 5.84 us -> 5.76 us  [local_call(): pl.pallas_call(kernel, name=name, out_shape=outs, in_specs=[pl.BlockSpec(...]
    pallas_call x2 -> x3, Pallas kernels: 7.06 us -> 7.03 us  [local_call_of(): pl.pallas_call(kernel, name=name, out_shape=[jax.ShapeDtypeStruct((tokens...]
  transfers between devices with their start and end apart: 9 -> 10, of which waited for: 5 -> 6; matrix products, arithmetic and copies ran while one was open for 0% -> 0% of each run, Pallas kernels for 23% -> 23%
where the time goes in v5:
time: 47.2 us; the launch traced here: 46.6 us
  waiting for transfers between devices  19.6 us (42%)
  Pallas kernels  17.2 us (36%)
  starting transfers between devices  8.99 us (19%)
  between operations  0.81 us (2%)
    ppermute x3, waiting for transfers between devices, layer_columns(): got = [lax.ppermute(part, 'tensor', swap) for part in parts]  9.9 us
    pallas_call x3, Pallas kernels, local_call_of(): pl.pallas_call(kernel, name=name, out_shape=[jax.ShapeDtypeStruct((tokens...  7.03 us
    pallas_call x9, Pallas kernels, local_call(): pl.pallas_call(kernel, name=name, out_shape=outs, in_specs=[pl.BlockSpec(...  5.76 us
    ppermute x3, starting transfers between devices, layer_columns(): got = [lax.ppermute(part, 'tensor', swap) for part in parts]  3.63 us
    pallas_call x1, Pallas kernels, own_state(): pl.pallas_call(state_kernel, name='own_state', out_shape=[jax.ShapeDtypeS...  3.35 us
    ppermute x1, waiting for transfers between devices, entering_state(): last = lax.ppermute(middle, 'scan', [(2, 3)])  3.15 us
    ppermute x1, waiting for transfers between devices, entering_state(): far = lax.ppermute(second, 'scan', [(0, 2), (2, 3)])  2.85 us
    ppermute x1, waiting for transfers between devices, on_device(): got = lax.ppermute(send, 'band', cores)  1.64 us
  transfers between devices with their start and end apart: 10, of which 6 were waited for; matrix products, arithmetic and copies ran while one was open for 0% of the time, Pallas kernels for 23%

profile of v5, /device:TPU:24, one launch (start us, length us, event | category | flops | bytes accessed | tf_op | source)
XLA Modules:
  0.0 46.6 jit_solution(10854610918912710151)
XLA Ops:
  0.7 3.4 %own_state.1 = (f32[40,256]{1,0:T(8,128)S(1)}, f32[40,256]{1,0:T(8,128)S(1)}, bf16[16,128]{1,0:T(8,128)(2,1)S(1)}, f32[64,2560]{1,0:T(8,128)S(1)}, bf16[64,2688]...) custom-call(s32[1]{0:T(128)S(6)} %copy.18.band_ref, ...), custom_call_target="tpu_custom_call" | custom-call | flops 335544320 | bytes 1310720 | tf_op jit(solution)/shard_map/own_state/pallas_call | solution.py:227
  4.0 0.1 collective-permute-start
  4.1 1.6 %collective-permute-done.refs_1_.got_ref.refs_6_.refs_2_ = bf16[64,2688]{1,0:T(8,128)(2,1)S(1)} collective-permute-done((bf16[64,2688]{1,0:T(8,128)(2,1)S(1)}, bf16[64,2688]{1,0:T(8,128)(2,1)S(1)}, u32[]{:S(2)}, u32[]{:S(2)}) %collective-permute-start) | collective-permute-done | bytes 344096 | tf_op jit(solution)/shard_map/ppermute | solution.py:868
  5.7 0.2 chip_state.1
  6.0 0.7 %collective-permute-start.1 = (bf16[32,2688]{1,0:T(8,128)(2,1)S(1)}, bf16[32,2688]{1,0:T(8,128)(2,1)S(1)}, u32[]{:S(2)}, u32[]{:S(2)}) collective-permute-start(bf16[32,2688]{1,0:T(8,128)(2,1)S(1)} %get-tuple-element.45.after_ref), channel_id=1, source_target_pairs={{0,4},{4,8},{1,5},{5,9},{2,6},{6,10},{3,7},{7,11},{16,20},{20,24},... | collective-permute-start | bytes 516104 | tf_op jit(solution)/shard_map/ppermute | solution.py:651
  6.7 1.7 %local_first.1 = (f32[256,512]{1,0:T(8,128)S(1)}, f32[256,512]{1,0:T(8,128)S(1)}, bf16[256,2560]{1,0:T(8,128)(2,1)S(1)}, bf16[32,2688]{1,0:T(8,128)(2,1)S(1)}, f...) custom-call(f32[40,256]{1,0:T(8,128)S(1)} %get-tuple-element.46.runn, ...), custom_call_target="tpu_custom_call" | custom-call | flops 201326592 | bytes 1572864 | tf_op jit(solution)/shard_map/local_first/pallas_call | solution.py:435
  8.3 1.3 %collective-permute-start.2 = (bf16[32,2688]{1,0:T(8,128)(2,1)S(1)}, bf16[32,2688]{1,0:T(8,128)(2,1)S(1)}, u32[]{:S(2)}, u32[]{:S(2)}) collective-permute-start(bf16[32,2688]{1,0:T(8,128)(2,1)S(1)} %get-tuple-element.52.after_ref), channel_id=1, source_target_pairs={{0,8},{8,12},{1,9},{9,13},{2,10},{10,14},{3,11},{11,15},{16,24},{2... | collective-permute-start | bytes 516104 | tf_op jit(solution)/shard_map/ppermute | solution.py:653
  9.6 2.1 %local_rest.2 = (f32[256,1024]{1,0:T(8,128)S(1)}, f32[256,1024]{1,0:T(8,128)S(1)}, bf16[768,2560]{1,0:T(8,128)(2,1)S(1)}) custom-call(f32[40,256]{1,0:T(8,128)S(1)} %get-tuple-element.46.running_ref, f32[40,256]{1,0:T(8,128)S(1)} %get-tuple-element.47.weight_ref, bf16[256,2560]{1,0:T(8,128)(2,1)S(1)} %get-tuple-element.48.signal_ref, ...), custom_call_target="tpu_custom_call" | custom-call | flops 402653184 | bytes 3145728 | tf_op jit(solution)/shard_map/local_rest/pallas_call | solution.py:435
  11.8 0.0 collective-permute-done.1.refs_1_.refs_0_
  11.8 1.3 %collective-permute-start.4 = (bf16[32,2560]{1,0:T(8,128)(2,1)S(1)}, bf16[32,2560]{1,0:T(8,128)(2,1)S(1)}, u32[]{:S(2)}, u32[]{:S(2)}) collective-permute-start(bf16[32,2560]{1,0:T(8,128)(2,1)S(1)} %early_state.1.refs_3_), channel_id=1, source_target_pairs={{4,12},{0,4},{5,13},{1,5},{6,14},{2,6},{7,15},{3,7},{20,28},{16,20... | collective-permute-start | bytes 491528 | tf_op jit(solution)/shard_map/ppermute | solution.py:662
  13.1 0.7 %collective-permute-start.5 = (bf16[32,2560]{1,0:T(8,128)(2,1)S(1)}, bf16[32,2560]{1,0:T(8,128)(2,1)S(1)}, u32[]{:S(2)}, u32[]{:S(2)}) collective-permute-start(bf16[32,2560]{1,0:T(8,128)(2,1)S(1)} %early_state.1.refs_3_), channel_id=1, source_target_pairs={{4,8},{5,9},{6,10},{7,11},{20,24},{21,25},{22,26},{23,27}} | collective-permute-start | bytes 491528 | tf_op jit(solution)/shard_map/ppermute | solution.py:663
  13.8 2.9 %collective-permute-done.2.refs_2_.refs_1_ = bf16[32,2688]{1,0:T(8,128)(2,1)S(1)} collective-permute-done((bf16[32,2688]{1,0:T(8,128)(2,1)S(1)}, bf16[32,2688]{1,0:T(8,128)(2,1)S(1)}, u32[]{:S(2)}, u32[]{:S(2)}) %collective-permute-start.2) | collective-permute-done | bytes 172064 | tf_op jit(solution)/shard_map/ppermute | solution.py:653
  16.6 0.2 middle_state.1
  16.8 1.3 %collective-permute-start.3 = (bf16[32,2560]{1,0:T(8,128)(2,1)S(1)}, bf16[32,2560]{1,0:T(8,128)(2,1)S(1)}, u32[]{:S(2)}, u32[]{:S(2)}) collective-permute-start(bf16[32,2560]{1,0:T(8,128)(2,1)S(1)} %get-tuple-element.58.after_ref), channel_id=1, source_target_pairs={{8,12},{9,13},{10,14},{11,15},{24,28},{25,29},{26,30},{27,31}} | collective-permute-start | bytes 491528 | tf_op jit(solution)/shard_map/ppermute | solution.py:671
  18.1 3.2 %local_rest.3 = (f32[256,1024]{1,0:T(8,128)S(1)}, f32[256,1024]{1,0:T(8,128)S(1)}, bf16[1536,2560]{1,0:T(8,128)(2,1)S(1)}) custom-call(f32[40,256]{1,0:T(8,128)S(1)} %get-tuple-element.46.running_ref, f32[40,256]{1,0:T(8,128)S(1)} %get-tuple-element.47.weight_ref, bf16[256,2560]{1,0:T(8,128)(2,1)S(1)} %get-tuple-element.48.signal_ref, ...), custom_call_target="tpu_custom_call" | custom-call | flops 402653184 | bytes 3145728 | tf_op jit(solution)/shard_map/local_rest/pallas_call | solution.py:435
  21.4 0.4 collective-permute-done.4.refs_2_
  21.8 0.0 collective-permute-done.5.refs_3_
  21.8 0.1 enter_state.1
  21.9 3.1 %collective-permute-done.3.refs_0_ = bf16[32,2560]{1,0:T(8,128)(2,1)S(1)} collective-permute-done((bf16[32,2560]{1,0:T(8,128)(2,1)S(1)}, bf16[32,2560]{1,0:T(8,128)(2,1)S(1)}, u32[]{:S(2)}, u32[]{:S(2)}) %collective-permute-start.3) | collective-permute-done | bytes 163872 | tf_op jit(solution)/shard_map/ppermute | solution.py:671
  25.1 0.1 enter_last.1
  25.1 0.1 collective-permute-start.6
  25.2 1.6 %collective-permute-done.6.refs_1_ = bf16[64,2560]{1,0:T(8,128)(2,1)S(1)} collective-permute-done((bf16[64,2560]{1,0:T(8,128)(2,1)S(1)}, bf16[64,2560]{1,0:T(8,128)(2,1)S(1)}, u32[]{:S(2)}, u32[]{:S(2)}) %collective-permute-start.6) | collective-permute-done | bytes 327712 | tf_op jit(solution)/shard_map/ppermute | solution.py:892
  26.8 1.6 %gated_part.1 = (bf16[256,2560]{1,0:T(8,128)(2,1)S(1)}, f32[8,256]{1,0:T(8,128)S(1)}, bf16[256,512]{1,0:T(8,128)(2,1)S(1)}) custom-call(bf16[64,2560]{1,0:T(8,128)(2,1)S(1)} %get-tuple-element.64.refs_0_, bf16[64,2560]{1,0:T(8,128)(2,1)S(1)} %collective-permute-done.6.refs_1_, bf16[256,128]{1,0:T(8,128)(2,1)S(1)} %get-tuple-element.51.read_ref.refs_2_, ...), custom_call_target="tpu_custom_call" | custom-call | flops 167772160 | bytes 20662272 | tf_op jit(solution)/shard_map/gated_part/pallas_call | solution.py:107
  28.4 1.5 %collective-permute-start.7 = (bf16[256,512]{1,0:T(8,128)(2,1)S(1)}, bf16[256,512]{1,0:T(8,128)(2,1)S(1)}, u32[]{:S(2)}, u32[]{:S(2)}) collective-permute-start(bf16[256,512]{1,0:T(8,128)(2,1)S(1)} %get-tuple-element.76.refs_4_), channel_id=1, source_target_pairs={{0,2},{2,0},{1,3},{3,1},{4,6},{6,4},{5,7},{7,5},{8,10},{10,8},{9,1... | collective-permute-start | bytes 786440 | tf_op jit(solution)/shard_map/ppermute | solution.py:835
  30.0 0.8 %project_other.2.refs_5_ = bf16[256,384]{1,0:T(8,128)(2,1)S(1)} custom-call(bf16[256,2560]{1,0:T(8,128)(2,1)S(1)} %get-tuple-element.75.refs_0_, bf16[256,2560]{1,0:T(8,128)(2,1)S(1)} %get-tuple-element.71.refs_10_.refs_1_, bf16[768,2560]{1,0:T(8,128)(2,1)S(1)} %get-tuple-element.72.refs_11_.refs_2_, ...), custom_call_target="tpu_custom_call" | custom-call | bytes 14614528 | tf_op jit(solution)/shard_map/project_other/pallas_call | solution.py:107
  30.8 0.9 %project_other.3.refs_4_ = bf16[272,384]{1,0:T(8,128)(2,1)S(1)} custom-call(bf16[256,2560]{1,0:T(8,128)(2,1)S(1)} %get-tuple-element.75.refs_0_, bf16[256,2560]{1,0:T(8,128)(2,1)S(1)} %get-tuple-element.71.refs_10_.refs_1_, bf16[768,2560]{1,0:T(8,128)(2,1)S(1)} %get-tuple-element.72.refs_11_.refs_2_, ...), custom_call_target="tpu_custom_call" | custom-call | bytes 14635008 | tf_op jit(solution)/shard_map/project_other/pallas_call | solution.py:107
  31.7 0.6 %collective-permute-start.9 = (bf16[272,384]{1,0:T(8,128)(2,1)S(1)}, bf16[272,384]{1,0:T(8,128)(2,1)S(1)}, u32[]{:S(2)}, u32[]{:S(2)}) collective-permute-start(bf16[272,384]{1,0:T(8,128)(2,1)S(1)} %project_other.3.refs_4_), channel_id=1, source_target_pairs={{0,2},{2,0},{1,3},{3,1},{4,6},{6,4},{5,7},{7,5},{8,10},{10,8},{9,1... | collective-permute-start | bytes 626696 | tf_op jit(solution)/shard_map/ppermute | solution.py:835
  32.3 1.5 %collective-permute-start.8 = (bf16[256,384]{1,0:T(8,128)(2,1)S(1)}, bf16[256,384]{1,0:T(8,128)(2,1)S(1)}, u32[]{:S(2)}, u32[]{:S(2)}) collective-permute-start(bf16[256,384]{1,0:T(8,128)(2,1)S(1)} %project_other.2.refs_5_), channel_id=1, source_target_pairs={{0,2},{2,0},{1,3},{3,1},{4,6},{6,4},{5,7},{7,5},{8,10},{10,8},{9,1... | collective-permute-start | bytes 589832 | tf_op jit(solution)/shard_map/ppermute | solution.py:835
  33.8 1.9 %project_own.1.own_ref = f32[256,1280]{1,0:T(8,128)S(1)} custom-call(bf16[256,2560]{1,0:T(8,128)(2,1)S(1)} %get-tuple-element.75.refs_0_, bf16[256,2560]{1,0:T(8,128)(2,1)S(1)} %get-tuple-element.71.refs_10_.refs_1_, bf16[768,2560]{1,0:T(8,128)(2,1)S(1)} %get-tuple-element.72.refs_11_.refs_2_, bf16[1536,2560]{1,0:T(8,128)(2,1)S(1)} %get-tuple-element.73.refs_12_.refs_3_, ...), custom_call_target="tpu_custom_call" | custom-call | bytes 15728640 | tf_op jit(solution)/shard_map/project_own/pallas_call | solution.py:107
  35.6 9.9 %collective-permute-done.8.refs_1_ = bf16[256,384]{1,0:T(8,128)(2,1)S(1)} collective-permute-done((bf16[256,384]{1,0:T(8,128)(2,1)S(1)}, bf16[256,384]{1,0:T(8,128)(2,1)S(1)}, u32[]{:S(2)}, u32[]{:S(2)}) %collective-permute-start.8) | collective-permute-done | bytes 196640 | tf_op jit(solution)/shard_map/ppermute | solution.py:835
  45.5 0.0 collective-permute-done.9.refs_2_
  45.5 1.1 %finish.1 = bf16[256,1280]{1,0:T(8,128)(2,1)} custom-call(f32[8,256]{1,0:T(8,128)S(1)} %get-tuple-element.74.refs_4_.squares_ref, f32[256,1280]{1,0:T(8,128)S(1)} %project_own.1.own_ref, bf16[256,512]{1,0:T(8,128)(2,1)S(1)} %collective-permute-done.7.refs_0_, bf16[256,384]{1,0:T(8,128)(2,1)S(1)} %collective-permute-done.8.refs_1_, ...), custom_call_target="tpu_custom_call" | custom-call | tf_op jit(solution)/shard_map/finish/pallas_call | solution.py:797
  (2 shorter events, 0.0 us)
Async XLA Ops:
  4.0 1.7 %collective-permute-start = (bf16[64,2688]{1,0:T(8,128)(2,1)S(1)}, bf16[64,2688]{1,0:T(8,128)(2,1)S(1)}, u32[]{:S(2)}, u32[]{:S(2)}) collective-permute-start(bf16[64,2688]{1,0:T(8,128)(2,1)S(1)} %get-tuple-element.42), channel_id=1, source_target_pairs={{0,1},{1,0},{2,3},{3,2},{4,5},{5,4},{6,7},{7,6},{8,9},{9,8},{10,11... | collective-permute-start | bytes 1032200 | tf_op jit(solution)/shard_map/ppermute | solution.py:868
  6.0 5.8 %collective-permute-start.1 = (bf16[32,2688]{1,0:T(8,128)(2,1)S(1)}, bf16[32,2688]{1,0:T(8,128)(2,1)S(1)}, u32[]{:S(2)}, u32[]{:S(2)}) collective-permute-start(bf16[32,2688]{1,0:T(8,128)(2,1)S(1)} %get-tuple-element.45.after_ref), channel_id=1, source_target_pairs={{0,4},{4,8},{1,5},{5,9},{2,6},{6,10},{3,7},{7,11},{16,20},{20,24},... | collective-permute-start | bytes 516104 | tf_op jit(solution)/shard_map/ppermute | solution.py:651
  8.3 8.3 %collective-permute-start.2 = (bf16[32,2688]{1,0:T(8,128)(2,1)S(1)}, bf16[32,2688]{1,0:T(8,128)(2,1)S(1)}, u32[]{:S(2)}, u32[]{:S(2)}) collective-permute-start(bf16[32,2688]{1,0:T(8,128)(2,1)S(1)} %get-tuple-element.52.after_ref), channel_id=1, source_target_pairs={{0,8},{8,12},{1,9},{9,13},{2,10},{10,14},{3,11},{11,15},{16,24},{2... | collective-permute-start | bytes 516104 | tf_op jit(solution)/shard_map/ppermute | solution.py:653
  11.8 10.0 %collective-permute-start.4 = (bf16[32,2560]{1,0:T(8,128)(2,1)S(1)}, bf16[32,2560]{1,0:T(8,128)(2,1)S(1)}, u32[]{:S(2)}, u32[]{:S(2)}) collective-permute-start(bf16[32,2560]{1,0:T(8,128)(2,1)S(1)} %early_state.1.refs_3_), channel_id=1, source_target_pairs={{4,12},{0,4},{5,13},{1,5},{6,14},{2,6},{7,15},{3,7},{20,28},{16,20... | collective-permute-start | bytes 491528 | tf_op jit(solution)/shard_map/ppermute | solution.py:662
  13.1 8.7 %collective-permute-start.5 = (bf16[32,2560]{1,0:T(8,128)(2,1)S(1)}, bf16[32,2560]{1,0:T(8,128)(2,1)S(1)}, u32[]{:S(2)}, u32[]{:S(2)}) collective-permute-start(bf16[32,2560]{1,0:T(8,128)(2,1)S(1)} %early_state.1.refs_3_), channel_id=1, source_target_pairs={{4,8},{5,9},{6,10},{7,11},{20,24},{21,25},{22,26},{23,27}} | collective-permute-start | bytes 491528 | tf_op jit(solution)/shard_map/ppermute | solution.py:663
  16.8 8.3 %collective-permute-start.3 = (bf16[32,2560]{1,0:T(8,128)(2,1)S(1)}, bf16[32,2560]{1,0:T(8,128)(2,1)S(1)}, u32[]{:S(2)}, u32[]{:S(2)}) collective-permute-start(bf16[32,2560]{1,0:T(8,128)(2,1)S(1)} %get-tuple-element.58.after_ref), channel_id=1, source_target_pairs={{8,12},{9,13},{10,14},{11,15},{24,28},{25,29},{26,30},{27,31}} | collective-permute-start | bytes 491528 | tf_op jit(solution)/shard_map/ppermute | solution.py:671
  25.1 1.7 %collective-permute-start.6 = (bf16[64,2560]{1,0:T(8,128)(2,1)S(1)}, bf16[64,2560]{1,0:T(8,128)(2,1)S(1)}, u32[]{:S(2)}, u32[]{:S(2)}) collective-permute-start(bf16[64,2560]{1,0:T(8,128)(2,1)S(1)} %get-tuple-element.65), channel_id=1, source_target_pairs={{0,1},{1,0},{2,3},{3,2},{4,5},{5,4},{6,7},{7,6},{8,9},{9,8},{10,11... | collective-permute-start | bytes 983048 | tf_op jit(solution)/shard_map/ppermute | solution.py:892
  28.4 17.1 %collective-permute-start.7 = (bf16[256,512]{1,0:T(8,128)(2,1)S(1)}, bf16[256,512]{1,0:T(8,128)(2,1)S(1)}, u32[]{:S(2)}, u32[]{:S(2)}) collective-permute-start(bf16[256,512]{1,0:T(8,128)(2,1)S(1)} %get-tuple-element.76.refs_4_), channel_id=1, source_target_pairs={{0,2},{2,0},{1,3},{3,1},{4,6},{6,4},{5,7},{7,5},{8,10},{10,8},{9,1... | collective-permute-start | bytes 786440 | tf_op jit(solution)/shard_map/ppermute | solution.py:835
  31.7 13.9 %collective-permute-start.9 = (bf16[272,384]{1,0:T(8,128)(2,1)S(1)}, bf16[272,384]{1,0:T(8,128)(2,1)S(1)}, u32[]{:S(2)}, u32[]{:S(2)}) collective-permute-start(bf16[272,384]{1,0:T(8,128)(2,1)S(1)} %project_other.3.refs_4_), channel_id=1, source_target_pairs={{0,2},{2,0},{1,3},{3,1},{4,6},{6,4},{5,7},{7,5},{8,10},{10,8},{9,1... | collective-permute-start | bytes 626696 | tf_op jit(solution)/shard_map/ppermute | solution.py:835
  32.3 13.2 %collective-permute-start.8 = (bf16[256,384]{1,0:T(8,128)(2,1)S(1)}, bf16[256,384]{1,0:T(8,128)(2,1)S(1)}, u32[]{:S(2)}, u32[]{:S(2)}) collective-permute-start(bf16[256,384]{1,0:T(8,128)(2,1)S(1)} %project_other.2.refs_5_), channel_id=1, source_target_pairs={{0,2},{2,0},{1,3},{3,1},{4,6},{6,4},{5,7},{7,5},{8,10},{10,8},{9,1... | collective-permute-start | bytes 589832 | tf_op jit(solution)/shard_map/ppermute | solution.py:835

commit v6 on v5

--- a/solution.py
+++ b/solution.py
@@ -53,15 +53,16 @@
     return ref[...]
 
 
-def piece_map(heads, lanes, group, first=0):
-    away = (
-        lax.broadcasted_iota(jnp.int32, (LANES, lanes), 0)
-        - lax.shift_right_logical(lax.broadcasted_iota(jnp.int32, (LANES, lanes), 1), group)
-        - first
-    )
+def piece_away(heads, lanes, group):
     slot = slot_of(heads)
-    hit = (away == 0) | (away == slot) | (away == 2 * slot)
-    return jnp.where(hit, 1.0, 0.0).astype(BF16)
+    row = lax.broadcasted_iota(jnp.int32, (LANES, lanes), 0)
+    head = row - jnp.where(row >= 2 * slot, 2 * slot, jnp.where(row >= slot, slot, 0))
+    head = jnp.where(row < 3 * slot, head, -LANES)
+    return head - lax.shift_right_logical(lax.broadcasted_iota(jnp.int32, (LANES, lanes), 1), group)
+
+
+def piece_map(away, first):
+    return jnp.where(away == first, 1.0, 0.0).astype(BF16)
 
 
 def spread_heads(row, heads_map):
@@ -90,8 +91,12 @@
     return jnp.sum(block.astype(F32), axis=0, keepdims=True)
 
 
+def decay_map(heads, width):
+    return head_of_lane(-(-heads // 16) * 16, width, 6)
+
+
 def decay_lanes(block, heads_map):
-    return jnp.sum(dot(block[:16], heads_map), axis=0, keepdims=True)
+    return jnp.sum(dot(block[:16, : heads_map.shape[0]], heads_map), axis=0, keepdims=True)
 
 
 def column_block(width):
@@ -153,6 +158,7 @@
     decay_log_ref,
     step_offset_ref,
     rows_ref,
+    factors_ref,
     sems,
     block_sems,
 ):
@@ -209,11 +215,15 @@
     write = jnp.concatenate(
         [jnp.where(is_first, low, high), jnp.where(is_first, high, low)], axis=0
     ).astype(BF16)
-    for copy, first in zip(blocks, range(0, width, block)):
+    away = piece_away(heads, block, 6)
+    for first in range(0, width, block):
+        factors_ref[:, first : first + block] = dot(tail, piece_map(away, first // HEAD_DIM))
+    for copy in blocks:
+        copy.wait()
+    for first in range(0, width, block):
         lanes = slice(first, first + block)
-        factors = dot(tail, piece_map(heads, block, 6, first // HEAD_DIM))
-        copy.wait()
-        state = dot(write, (signal_ref[:, lanes].astype(F32) * factors).astype(BF16))
+        scaled = (signal_ref[:, lanes].astype(F32) * factors_ref[:, lanes]).astype(BF16)
+        state = dot(write, scaled)
         keep_ref[:, lanes] = state[:HALF]
         send_ref[:, lanes] = state[HALF:].astype(BF16)
     for copy in copies[6:]:
@@ -240,6 +250,7 @@
         scratch_shapes=[pltpu.VMEM(a.shape, a.dtype) for a in small]
         + [
             pltpu.VMEM((LANES, tokens), F32),
+            pltpu.VMEM((tokens, width), F32),
             pltpu.SemaphoreType.DMA((8,)),
             pltpu.SemaphoreType.DMA((width // column_block(width),)),
         ],
@@ -266,7 +277,7 @@
     mine, got = decay_ref[...].astype(F32), got_ref[:16, width:].astype(F32)
     first_core = jnp.where(lax.axis_index("band") == 0, mine, got).astype(BF16)
     lanes_ref[...] = jnp.broadcast_to(
-        decay_lanes(first_core, head_of_lane(LANES, width, 6)), lanes_ref.shape
+        decay_lanes(first_core, decay_map(width // HEAD_DIM, width)), lanes_ref.shape
     )
 
 
@@ -289,6 +300,8 @@
     low_lanes = lax.broadcasted_iota(jnp.int32, (half, LANES), 1) < HEAD_DIM
     early, late = slice(0, half), slice(half, tokens)
 
+    wide_away, away = piece_away(heads, 2 * block, 7), piece_away(heads, block, 6)
+
     def heads_block(at, _):
         first_head = (first_block + at) * (block // HEAD_DIM)
 
@@ -298,11 +311,11 @@
         def part_lanes(lane, count):
             return pl.ds(pl.multiple_of(at * block + lane, LANES), count)
 
-        wide = dot(running_pieces_ref[...], piece_map(heads, block * 2, 7, first_head))
+        wide = dot(running_pieces_ref[...], piece_map(wide_away, first_head))
         gate = gate_ref[:, whole_lanes(0, block)].astype(F32)
         gate = gate / (1.0 + jnp.exp(-gate))
         factor_ref[:, part_lanes(0, block)] = (
-            dot(decay_pieces_ref[...], piece_map(heads, block, 6, first_head)) * gate
+            dot(decay_pieces_ref[...], piece_map(away, first_head)) * gate
         )
         skip = spread_heads(skip_ref[...], head_of_lane(heads, block, 6, first_head))
         for pair in range(block // LANES):
@@ -493,7 +506,7 @@
     width = keep_ref.shape[1]
     core = lax.axis_index("band")
     chip = lax.axis_index("scan")
-    heads_map = head_of_lane(LANES, width, 6)
+    heads_map = decay_map(width // HEAD_DIM, width)
     got_decay = got_ref[:16, width:]
     mine = decay_ref[...]
     later = jnp.where(core == 0, got_decay.astype(F32), mine.astype(F32)).astype(BF16)
@@ -520,7 +533,7 @@
 
     @pl.when(chip == 1)
     def _():
-        lanes = decay_lanes(state_ref[:16, width:], head_of_lane(LANES, width, 6))
+        lanes = decay_lanes(state_ref[:16, width:], decay_map(width // HEAD_DIM, width))
         out_ref[...] = (
             lanes * near_ref[:, :width].astype(F32) + state_ref[:PART, :width].astype(F32)
         ).astype(BF16)
@@ -532,7 +545,7 @@
 
     @pl.when(chip == 2)
     def _():
-        heads_map = head_of_lane(LANES, width, 6)
+        heads_map = decay_map(width // HEAD_DIM, width)
         lanes = decay_lanes(near_ref[:16, width:], heads_map)
         lanes_ref[...] = jnp.broadcast_to(lanes, lanes_ref.shape)
         entered = lanes * far_ref[:, :width].astype(F32) + near_ref[:, :width].astype(F32)
@@ -541,7 +554,7 @@
 
     @pl.when(chip == 3)
     def _():
-        lanes = decay_lanes(far_ref[:16, width:], head_of_lane(LANES, width, 6))
+        lanes = decay_lanes(far_ref[:16, width:], decay_map(width // HEAD_DIM, width))
         lanes_ref[...] = jnp.broadcast_to(lanes, lanes_ref.shape)
 
 
@@ -608,7 +621,7 @@
 def gathered_kernel(all_ref, keep_ref, got_ref, lanes_ref, mine_ref, send_ref, enter_ref):
     width = keep_ref.shape[1]
     chip = lax.axis_index("scan")
-    heads_map = head_of_lane(LANES, width, 6)
+    heads_map = decay_map(width // HEAD_DIM, width)
     enter_ref[...] = jnp.zeros(enter_ref.shape, F32)
     for source in range(all_ref.shape[0]):
 
@@ -712,9 +725,13 @@
                 ).astype(BF16)
                 sums += column * column
             first += block
+    square_ref[...] = jnp.broadcast_to(jnp.sum(sums.T, axis=0, keepdims=True), square_ref.shape)
     for first_ref in first_refs:
         send_kernel(0, out_ref, *weights, first_ref)
-    square_ref[...] = jnp.broadcast_to(jnp.sum(sums.T, axis=0, keepdims=True), square_ref.shape)
+        first_ref[tokens:, :] = jnp.zeros((16, first_ref.shape[1]), BF16)
+        for lane in range(0, tokens, LANES):
+            lanes = slice(lane, lane + LANES)
+            first_ref[tokens:, lanes] = decay_block(square_ref[:1, lanes], 16)
 
 
 def gated_part(mine, other, read_proj, gain, bases, factors, weights, first):
@@ -727,7 +744,7 @@
             jax.ShapeDtypeStruct((tokens, width), BF16),
             jax.ShapeDtypeStruct((8, tokens), F32),
         ]
-        + [jax.ShapeDtypeStruct((tokens, first), BF16)] * (first > 0),
+        + [jax.ShapeDtypeStruct((tokens + 16, first), BF16)] * (first > 0),
         (mine, other, read_proj, gain, *bases, *factors, *weights),
         flops=2 * tokens * width * STATE,
     )
@@ -749,16 +766,10 @@
     return total
 
 
-def send_kernel(first, gated_ref, *refs, squares=False):
-    *refs, out_ref = refs
-    weights = refs[:-1] if squares else refs
+def send_kernel(first, gated_ref, *refs):
+    *weights, out_ref = refs
     tokens, count = gated_ref.shape[0], out_ref.shape[1]
     out_ref[:tokens, :] = project(gated_ref, weights, True, first, count).astype(BF16)
-    if squares:
-        out_ref[tokens:, :] = jnp.zeros((16, count), BF16)
-        for lane in range(0, tokens, LANES):
-            lanes = slice(lane, lane + LANES)
-            out_ref[tokens:, lanes] = decay_block(refs[-1][:1, lanes], 16)
 
 
 def own_kernel(gated_ref, *refs):
@@ -768,44 +779,71 @@
         out_ref[:, first : first + count] = project(gated_ref, weights, False, first, count)
 
 
-def finish_kernel(squares_ref, own_ref, *refs):
-    *got_refs, out_ref, sent_ref, sems = refs
+def finish_columns(first, got_refs, own_ref, scale, out_ref, sent_ref, sems):
     tokens = own_ref.shape[0]
-    other_squares = got_refs[-1][tokens:, :tokens].astype(F32)
-    mean = (squares_ref[:1] + jnp.sum(other_squares, axis=0, keepdims=True)) / INNER
-    scale = lax.rsqrt(mean + EPSILON)
-    scale = jnp.broadcast_to(scale, (LANES, tokens)).T
-    first, copies = 0, []
+    copies, place = [], 0
     for got_ref in got_refs:
         count = got_ref.shape[1]
         for lane in range(0, count, LANES):
-            lanes = slice(first + lane, first + lane + LANES)
-            total = own_ref[:, lanes] + got_ref[:tokens, lane : lane + LANES].astype(F32)
-            sent_ref[:, lanes] = (total * scale).astype(BF16)
-        lanes = pl.ds(first, count)
+            own_lanes = slice(first + place + lane, first + place + lane + LANES)
+            total = own_ref[:, own_lanes] + got_ref[:tokens, lane : lane + LANES].astype(F32)
+            sent_ref[:, place + lane : place + lane + LANES] = (total * scale).astype(BF16)
         copies.append(
-            pltpu.make_async_copy(sent_ref.at[:, lanes], out_ref.at[:, lanes], sems.at[len(copies)])
+            pltpu.make_async_copy(
+                sent_ref.at[:, pl.ds(place, count)],
+                out_ref.at[:, pl.ds(first + place, count)],
+                sems.at[len(copies)],
+            )
         )
         copies[-1].start()
-        first += count
+        place += count
     for copy in copies:
         copy.wait()
 
 
+def finish_first_kernel(squares_ref, own_ref, got_ref, out_ref, scale_ref, sent_ref, sems):
+    tokens = own_ref.shape[0]
+    other_squares = got_ref[tokens:, :tokens].astype(F32)
+    mean = (squares_ref[:1] + jnp.sum(other_squares, axis=0, keepdims=True)) / INNER
+    scale = lax.rsqrt(mean + EPSILON)
+    scale_ref[...] = jnp.broadcast_to(scale, (LANES, tokens)).T
+    finish_columns(0, [got_ref], own_ref, scale_ref[...], out_ref, sent_ref, sems)
+
+
+def finish_rest_kernel(scale_ref, own_ref, *refs):
+    *got_refs, old_ref, out_ref, sent_ref, sems = refs
+    first = own_ref.shape[1] - sent_ref.shape[1]
+    finish_columns(first, got_refs, own_ref, scale_ref[...], out_ref, sent_ref, sems)
+
+
 def finish(squares, own, got):
-    args = (squares, own, *got)
+    tokens, columns = own.shape
+    first = got[0].shape[1]
+    shape = jax.ShapeDtypeStruct(own.shape, BF16)
+    params = pltpu.CompilerParams(vmem_limit_bytes=8 * MIB)
+    begun, scale = pl.pallas_call(
+        finish_first_kernel,
+        name="finish_first",
+        out_shape=[shape, jax.ShapeDtypeStruct((tokens, LANES), F32)],
+        in_specs=[IN_VMEM] * 3,
+        out_specs=[IN_HBM, IN_VMEM],
+        scratch_shapes=[pltpu.VMEM((tokens, first), BF16), pltpu.SemaphoreType.DMA((1,))],
+        compiler_params=params,
+    )(squares, own, got[0])
+    args = (scale, own, *got[1:])
     return pl.pallas_call(
-        finish_kernel,
-        name="finish",
-        out_shape=jax.ShapeDtypeStruct(own.shape, BF16),
-        in_specs=[IN_VMEM] * len(args),
+        finish_rest_kernel,
+        name="finish_rest",
+        out_shape=shape,
+        in_specs=[IN_VMEM] * len(args) + [IN_HBM],
         out_specs=IN_HBM,
+        input_output_aliases={len(args): 0},
         scratch_shapes=[
-            pltpu.VMEM(own.shape, BF16),
-            pltpu.SemaphoreType.DMA((len(got),)),
+            pltpu.VMEM((tokens, columns - first), BF16),
+            pltpu.SemaphoreType.DMA((len(got) - 1,)),
         ],
-        compiler_params=pltpu.CompilerParams(vmem_limit_bytes=8 * MIB),
-    )(*args)
+        compiler_params=params,
+    )(*args, begun)
 
 
 def direct(members, columns):
@@ -823,12 +861,11 @@
     tokens = gated.shape[0]
     parts, first = [ready[0]], SENDS[0]
     for count in SENDS[1:]:
-        last = first + count == columns
         parts += local_call(
-            functools.partial(send_kernel, first, squares=last),
+            functools.partial(send_kernel, first),
             "project_other",
-            [jax.ShapeDtypeStruct((tokens + 16 * last, count), BF16)],
-            (gated, *weights) + (squares,) * last,
+            [jax.ShapeDtypeStruct((tokens, count), BF16)],
+            (gated, *weights),
             after=parts[-1:],
         )
         first += count

time: 47.2 us -> 46.1 us (0.977)
  waiting for transfers between devices: 19.6 us -> 18.8 us
    pallas_call x1, Pallas kernels: 3.35 us -> 2.46 us  [own_state(): pl.pallas_call(state_kernel, name='own_state', out_shape=[jax.ShapeDtypeS...]
    ppermute x3, waiting for transfers between devices: 9.9 us -> 9.1 us  [layer_columns(): got = [lax.ppermute(part, 'tensor', swap) for part in parts]]
    pallas_call x1 -> x2, Pallas kernels: 1.05 us -> 1.68 us  [the longest x1 0.85 us: finish(): pl.pallas_call(finish_first_kernel, name='finish_first', out_shape=[shape...]
  transfers between devices with their start and end apart: 10 -> 10, of which waited for: 6 -> 8; matrix products, arithmetic and copies ran while one was open for 0% -> 0% of each run, Pallas kernels for 23% -> 26%
where the time goes in v6:
time: 46.1 us; the launch traced here: 45.5 us
  waiting for transfers between devices  18.8 us (41%)
  Pallas kernels  16.9 us (37%)
  starting transfers between devices  9 us (20%)
  between operations  0.82 us (2%)
    ppermute x3, waiting for transfers between devices, layer_columns(): got = [lax.ppermute(part, 'tensor', swap) for part in parts]  9.1 us
    pallas_call x3, Pallas kernels, local_call_of(): pl.pallas_call(kernel, name=name, out_shape=[jax.ShapeDtypeStruct((tokens...  6.99 us
    pallas_call x9, Pallas kernels, local_call(): pl.pallas_call(kernel, name=name, out_shape=outs, in_specs=[pl.BlockSpec(...  5.74 us
    ppermute x3, starting transfers between devices, layer_columns(): got = [lax.ppermute(part, 'tensor', swap) for part in parts]  3.64 us
    ppermute x1, waiting for transfers between devices, entering_state(): last = lax.ppermute(middle, 'scan', [(2, 3)])  3.09 us
    ppermute x1, waiting for transfers between devices, entering_state(): far = lax.ppermute(second, 'scan', [(0, 2), (2, 3)])  2.86 us
    pallas_call x1, Pallas kernels, own_state(): pl.pallas_call(state_kernel, name='own_state', out_shape=[jax.ShapeDtypeS...  2.46 us
    ppermute x1, waiting for transfers between devices, on_device(): got = lax.ppermute(send, 'band', cores)  1.64 us
  transfers between devices with their start and end apart: 10, of which 8 were waited for; matrix products, arithmetic and copies ran while one was open for 0% of the time, Pallas kernels for 26%

profile of v6, /device:TPU:24, one launch (start us, length us, event | category | flops | bytes accessed | tf_op | source)
XLA Modules:
  0.0 45.5 jit_solution(4828229115138278961)
XLA Ops:
  0.7 2.5 %own_state.1 = (f32[40,256]{1,0:T(8,128)S(1)}, f32[40,256]{1,0:T(8,128)S(1)}, bf16[16,128]{1,0:T(8,128)(2,1)S(1)}, f32[64,2560]{1,0:T(8,128)S(1)}, bf16[64,2688]...) custom-call(s32[1]{0:T(128)S(6)} %copy.20.band_ref, ...), custom_call_target="tpu_custom_call" | custom-call | flops 335544320 | bytes 1310720 | tf_op jit(solution)/shard_map/own_state/pallas_call | solution.py:237
  3.1 0.1 collective-permute-start
  3.2 1.6 %collective-permute-done.refs_1_.got_ref.refs_6_.refs_2_ = bf16[64,2688]{1,0:T(8,128)(2,1)S(1)} collective-permute-done((bf16[64,2688]{1,0:T(8,128)(2,1)S(1)}, bf16[64,2688]{1,0:T(8,128)(2,1)S(1)}, u32[]{:S(2)}, u32[]{:S(2)}) %collective-permute-start) | collective-permute-done | bytes 344096 | tf_op jit(solution)/shard_map/ppermute | solution.py:905
  4.8 0.2 chip_state.1
  5.1 0.7 %collective-permute-start.1 = (bf16[32,2688]{1,0:T(8,128)(2,1)S(1)}, bf16[32,2688]{1,0:T(8,128)(2,1)S(1)}, u32[]{:S(2)}, u32[]{:S(2)}) collective-permute-start(bf16[32,2688]{1,0:T(8,128)(2,1)S(1)} %get-tuple-element.47.after_ref), channel_id=1, source_target_pairs={{0,4},{4,8},{1,5},{5,9},{2,6},{6,10},{3,7},{7,11},{16,20},{20,24},... | collective-permute-start | bytes 516104 | tf_op jit(solution)/shard_map/ppermute | solution.py:664
  5.8 1.6 %local_first.1 = (f32[256,512]{1,0:T(8,128)S(1)}, f32[256,512]{1,0:T(8,128)S(1)}, bf16[256,2560]{1,0:T(8,128)(2,1)S(1)}, bf16[32,2688]{1,0:T(8,128)(2,1)S(1)}, f...) custom-call(f32[40,256]{1,0:T(8,128)S(1)} %get-tuple-element.48.runn, ...), custom_call_target="tpu_custom_call" | custom-call | flops 201326592 | bytes 1572864 | tf_op jit(solution)/shard_map/local_first/pallas_call | solution.py:448
  7.4 1.3 %collective-permute-start.2 = (bf16[32,2688]{1,0:T(8,128)(2,1)S(1)}, bf16[32,2688]{1,0:T(8,128)(2,1)S(1)}, u32[]{:S(2)}, u32[]{:S(2)}) collective-permute-start(bf16[32,2688]{1,0:T(8,128)(2,1)S(1)} %get-tuple-element.54.after_ref), channel_id=1, source_target_pairs={{0,8},{8,12},{1,9},{9,13},{2,10},{10,14},{3,11},{11,15},{16,24},{2... | collective-permute-start | bytes 516104 | tf_op jit(solution)/shard_map/ppermute | solution.py:666
  8.7 2.1 %local_rest.2 = (f32[256,1024]{1,0:T(8,128)S(1)}, f32[256,1024]{1,0:T(8,128)S(1)}, bf16[768,2560]{1,0:T(8,128)(2,1)S(1)}) custom-call(f32[40,256]{1,0:T(8,128)S(1)} %get-tuple-element.48.running_ref, f32[40,256]{1,0:T(8,128)S(1)} %get-tuple-element.49.weight_ref, bf16[256,2560]{1,0:T(8,128)(2,1)S(1)} %get-tuple-element.50.signal_ref, ...), custom_call_target="tpu_custom_call" | custom-call | flops 402653184 | bytes 3145728 | tf_op jit(solution)/shard_map/local_rest/pallas_call | solution.py:448
  10.9 1.3 %collective-permute-start.4 = (bf16[32,2560]{1,0:T(8,128)(2,1)S(1)}, bf16[32,2560]{1,0:T(8,128)(2,1)S(1)}, u32[]{:S(2)}, u32[]{:S(2)}) collective-permute-start(bf16[32,2560]{1,0:T(8,128)(2,1)S(1)} %early_state.1.refs_3_), channel_id=1, source_target_pairs={{4,12},{0,4},{5,13},{1,5},{6,14},{2,6},{7,15},{3,7},{20,28},{16,20... | collective-permute-start | bytes 491528 | tf_op jit(solution)/shard_map/ppermute | solution.py:675
  12.2 0.7 %collective-permute-start.5 = (bf16[32,2560]{1,0:T(8,128)(2,1)S(1)}, bf16[32,2560]{1,0:T(8,128)(2,1)S(1)}, u32[]{:S(2)}, u32[]{:S(2)}) collective-permute-start(bf16[32,2560]{1,0:T(8,128)(2,1)S(1)} %early_state.1.refs_3_), channel_id=1, source_target_pairs={{4,8},{5,9},{6,10},{7,11},{20,24},{21,25},{22,26},{23,27}} | collective-permute-start | bytes 491528 | tf_op jit(solution)/shard_map/ppermute | solution.py:676
  12.8 2.9 %collective-permute-done.2.refs_2_.refs_1_ = bf16[32,2688]{1,0:T(8,128)(2,1)S(1)} collective-permute-done((bf16[32,2688]{1,0:T(8,128)(2,1)S(1)}, bf16[32,2688]{1,0:T(8,128)(2,1)S(1)}, u32[]{:S(2)}, u32[]{:S(2)}) %collective-permute-start.2) | collective-permute-done | bytes 172064 | tf_op jit(solution)/shard_map/ppermute | solution.py:666
  15.7 0.2 middle_state.1
  15.9 1.3 %collective-permute-start.3 = (bf16[32,2560]{1,0:T(8,128)(2,1)S(1)}, bf16[32,2560]{1,0:T(8,128)(2,1)S(1)}, u32[]{:S(2)}, u32[]{:S(2)}) collective-permute-start(bf16[32,2560]{1,0:T(8,128)(2,1)S(1)} %get-tuple-element.60.after_ref), channel_id=1, source_target_pairs={{8,12},{9,13},{10,14},{11,15},{24,28},{25,29},{26,30},{27,31}} | collective-permute-start | bytes 491528 | tf_op jit(solution)/shard_map/ppermute | solution.py:684
  17.2 3.2 %local_rest.3 = (f32[256,1024]{1,0:T(8,128)S(1)}, f32[256,1024]{1,0:T(8,128)S(1)}, bf16[1536,2560]{1,0:T(8,128)(2,1)S(1)}) custom-call(f32[40,256]{1,0:T(8,128)S(1)} %get-tuple-element.48.running_ref, f32[40,256]{1,0:T(8,128)S(1)} %get-tuple-element.49.weight_ref, bf16[256,2560]{1,0:T(8,128)(2,1)S(1)} %get-tuple-element.50.signal_ref, ...), custom_call_target="tpu_custom_call" | custom-call | flops 402653184 | bytes 3145728 | tf_op jit(solution)/shard_map/local_rest/pallas_call | solution.py:448
  20.4 0.5 %collective-permute-done.4.refs_2_ = bf16[32,2560]{1,0:T(8,128)(2,1)S(1)} collective-permute-done((bf16[32,2560]{1,0:T(8,128)(2,1)S(1)}, bf16[32,2560]{1,0:T(8,128)(2,1)S(1)}, u32[]{:S(2)}, u32[]{:S(2)}) %collective-permute-start.4) | collective-permute-done | bytes 163872 | tf_op jit(solution)/shard_map/ppermute | solution.py:675
  20.9 0.1 enter_state.1
  21.0 3.1 %collective-permute-done.3.refs_0_ = bf16[32,2560]{1,0:T(8,128)(2,1)S(1)} collective-permute-done((bf16[32,2560]{1,0:T(8,128)(2,1)S(1)}, bf16[32,2560]{1,0:T(8,128)(2,1)S(1)}, u32[]{:S(2)}, u32[]{:S(2)}) %collective-permute-start.3) | collective-permute-done | bytes 163872 | tf_op jit(solution)/shard_map/ppermute | solution.py:684
  24.1 0.1 enter_last.1
  24.2 0.1 collective-permute-start.6
  24.3 1.6 %collective-permute-done.6.refs_1_ = bf16[64,2560]{1,0:T(8,128)(2,1)S(1)} collective-permute-done((bf16[64,2560]{1,0:T(8,128)(2,1)S(1)}, bf16[64,2560]{1,0:T(8,128)(2,1)S(1)}, u32[]{:S(2)}, u32[]{:S(2)}) %collective-permute-start.6) | collective-permute-done | bytes 327712 | tf_op jit(solution)/shard_map/ppermute | solution.py:929
  25.9 1.6 %gated_part.1 = (bf16[256,2560]{1,0:T(8,128)(2,1)S(1)}, f32[8,256]{1,0:T(8,128)S(1)}, bf16[272,512]{1,0:T(8,128)(2,1)S(1)}) custom-call(bf16[64,2560]{1,0:T(8,128)(2,1)S(1)} %get-tuple-element.66.refs_0_, bf16[64,2560]{1,0:T(8,128)(2,1)S(1)} %collective-permute-done.6.refs_1_, bf16[256,128]{1,0:T(8,128)(2,1)S(1)} %get-tuple-element.53.read_ref.refs_2_, ...), custom_call_target="tpu_custom_call" | custom-call | flops 167772160 | bytes 20678656 | tf_op jit(solution)/shard_map/gated_part/pallas_call | solution.py:112
  27.5 1.6 %collective-permute-start.7 = (bf16[272,512]{1,0:T(8,128)(2,1)S(1)}, bf16[272,512]{1,0:T(8,128)(2,1)S(1)}, u32[]{:S(2)}, u32[]{:S(2)}) collective-permute-start(bf16[272,512]{1,0:T(8,128)(2,1)S(1)} %get-tuple-element.78.refs_4_), channel_id=1, source_target_pairs={{0,2},{2,0},{1,3},{3,1},{4,6},{6,4},{5,7},{7,5},{8,10},{10,8},{9,1... | collective-permute-start | bytes 835592 | tf_op jit(solution)/shard_map/ppermute | solution.py:872
  29.0 0.8 %project_other.2.refs_4_ = bf16[256,384]{1,0:T(8,128)(2,1)S(1)} custom-call(bf16[256,2560]{1,0:T(8,128)(2,1)S(1)} %get-tuple-element.77.refs_0_, bf16[256,2560]{1,0:T(8,128)(2,1)S(1)} %get-tuple-element.73.refs_10_.refs_1_, bf16[768,2560]{1,0:T(8,128)(2,1)S(1)} %get-tuple-element.74.refs_11_.refs_2_, ...), custom_call_target="tpu_custom_call" | custom-call | bytes 14614528 | tf_op jit(solution)/shard_map/project_other/pallas_call | solution.py:112
  29.9 0.9 %project_other.3.refs_4_ = bf16[256,384]{1,0:T(8,128)(2,1)S(1)} custom-call(bf16[256,2560]{1,0:T(8,128)(2,1)S(1)} %get-tuple-element.77.refs_0_, bf16[256,2560]{1,0:T(8,128)(2,1)S(1)} %get-tuple-element.73.refs_10_.refs_1_, bf16[768,2560]{1,0:T(8,128)(2,1)S(1)} %get-tuple-element.74.refs_11_.refs_2_, ...), custom_call_target="tpu_custom_call" | custom-call | bytes 14614528 | tf_op jit(solution)/shard_map/project_other/pallas_call | solution.py:112
  30.7 0.6 %collective-permute-start.9 = (bf16[256,384]{1,0:T(8,128)(2,1)S(1)}, bf16[256,384]{1,0:T(8,128)(2,1)S(1)}, u32[]{:S(2)}, u32[]{:S(2)}) collective-permute-start(bf16[256,384]{1,0:T(8,128)(2,1)S(1)} %project_other.3.refs_4_), channel_id=1, source_target_pairs={{0,2},{2,0},{1,3},{3,1},{4,6},{6,4},{5,7},{7,5},{8,10},{10,8},{9,1... | collective-permute-start | bytes 589832 | tf_op jit(solution)/shard_map/ppermute | solution.py:872
  31.4 1.5 %collective-permute-start.8 = (bf16[256,384]{1,0:T(8,128)(2,1)S(1)}, bf16[256,384]{1,0:T(8,128)(2,1)S(1)}, u32[]{:S(2)}, u32[]{:S(2)}) collective-permute-start(bf16[256,384]{1,0:T(8,128)(2,1)S(1)} %project_other.2.refs_4_), channel_id=1, source_target_pairs={{0,2},{2,0},{1,3},{3,1},{4,6},{6,4},{5,7},{7,5},{8,10},{10,8},{9,1... | collective-permute-start | bytes 589832 | tf_op jit(solution)/shard_map/ppermute | solution.py:872
  32.8 1.9 %project_own.1.own_ref = f32[256,1280]{1,0:T(8,128)S(1)} custom-call(bf16[256,2560]{1,0:T(8,128)(2,1)S(1)} %get-tuple-element.77.refs_0_, bf16[256,2560]{1,0:T(8,128)(2,1)S(1)} %get-tuple-element.73.refs_10_.refs_1_, bf16[768,2560]{1,0:T(8,128)(2,1)S(1)} %get-tuple-element.74.refs_11_.refs_2_, bf16[1536,2560]{1,0:T(8,128)(2,1)S(1)} %get-tuple-element.75.refs_12_.refs_3_, ...), custom_call_target="tpu_custom_call" | custom-call | bytes 15728640 | tf_op jit(solution)/shard_map/project_own/pallas_call | solution.py:112
  34.7 2.3 %collective-permute-done.7.got_ref = bf16[272,512]{1,0:T(8,128)(2,1)S(1)} collective-permute-done((bf16[272,512]{1,0:T(8,128)(2,1)S(1)}, bf16[272,512]{1,0:T(8,128)(2,1)S(1)}, u32[]{:S(2)}, u32[]{:S(2)}) %collective-permute-start.7) | collective-permute-done | bytes 278560 | tf_op jit(solution)/shard_map/ppermute | solution.py:872
  37.0 0.8 %finish_first.1 = (bf16[256,1280]{1,0:T(8,128)(2,1)}, f32[256,128]{1,0:T(8,128)S(1)}) custom-call(f32[8,256]{1,0:T(8,128)S(1)} %get-tuple-element.76.squares_ref, f32[256,1280]{1,0:T(8,128)S(1)} %project_own.1.own_ref, bf16[272,512]{1,0:T(8,128)(2,1)S(1)} %collective-permute-done.7.got_ref), custom_call_target="tpu_custom_call" | custom-call | tf_op jit(solution)/shard_map/finish_first/pallas_call | solution.py:824
  37.9 3.4 %collective-permute-done.9.refs_1_ = bf16[256,384]{1,0:T(8,128)(2,1)S(1)} collective-permute-done((bf16[256,384]{1,0:T(8,128)(2,1)S(1)}, bf16[256,384]{1,0:T(8,128)(2,1)S(1)}, u32[]{:S(2)}, u32[]{:S(2)}) %collective-permute-start.9) | collective-permute-done | bytes 196640 | tf_op jit(solution)/shard_map/ppermute | solution.py:872
  41.2 3.4 %collective-permute-done.8.refs_0_ = bf16[256,384]{1,0:T(8,128)(2,1)S(1)} collective-permute-done((bf16[256,384]{1,0:T(8,128)(2,1)S(1)}, bf16[256,384]{1,0:T(8,128)(2,1)S(1)}, u32[]{:S(2)}, u32[]{:S(2)}) %collective-permute-start.8) | collective-permute-done | bytes 196640 | tf_op jit(solution)/shard_map/ppermute | solution.py:872
  44.7 0.8 %finish_rest.1 = bf16[256,1280]{1,0:T(8,128)(2,1)} custom-call(f32[256,128]{1,0:T(8,128)S(1)} %get-tuple-element.79.scale_ref, f32[256,1280]{1,0:T(8,128)S(1)} %project_own.1.own_ref, bf16[256,384]{1,0:T(8,128)(2,1)S(1)} %collective-permute-done.8.refs_0_, bf16[256,384]{1,0:T(8,128)(2,1)S(1)} %collective-permute-done.9.refs_1_, ...), custom_call_target="tpu_custom_call", output_to_operand_aliasing={{}: (4, {})} | custom-call | tf_op jit(solution)/shard_map/finish_rest/pallas_call | solution.py:834
  (3 shorter events, 0.0 us)
Async XLA Ops:
  3.1 1.7 %collective-permute-start = (bf16[64,2688]{1,0:T(8,128)(2,1)S(1)}, bf16[64,2688]{1,0:T(8,128)(2,1)S(1)}, u32[]{:S(2)}, u32[]{:S(2)}) collective-permute-start(bf16[64,2688]{1,0:T(8,128)(2,1)S(1)} %get-tuple-element.44), channel_id=1, source_target_pairs={{0,1},{1,0},{2,3},{3,2},{4,5},{5,4},{6,7},{7,6},{8,9},{9,8},{10,11... | collective-permute-start | bytes 1032200 | tf_op jit(solution)/shard_map/ppermute | solution.py:905
  5.1 5.7 %collective-permute-start.1 = (bf16[32,2688]{1,0:T(8,128)(2,1)S(1)}, bf16[32,2688]{1,0:T(8,128)(2,1)S(1)}, u32[]{:S(2)}, u32[]{:S(2)}) collective-permute-start(bf16[32,2688]{1,0:T(8,128)(2,1)S(1)} %get-tuple-element.47.after_ref), channel_id=1, source_target_pairs={{0,4},{4,8},{1,5},{5,9},{2,6},{6,10},{3,7},{7,11},{16,20},{20,24},... | collective-permute-start | bytes 516104 | tf_op jit(solution)/shard_map/ppermute | solution.py:664
  7.4 8.3 %collective-permute-start.2 = (bf16[32,2688]{1,0:T(8,128)(2,1)S(1)}, bf16[32,2688]{1,0:T(8,128)(2,1)S(1)}, u32[]{:S(2)}, u32[]{:S(2)}) collective-permute-start(bf16[32,2688]{1,0:T(8,128)(2,1)S(1)} %get-tuple-element.54.after_ref), channel_id=1, source_target_pairs={{0,8},{8,12},{1,9},{9,13},{2,10},{10,14},{3,11},{11,15},{16,24},{2... | collective-permute-start | bytes 516104 | tf_op jit(solution)/shard_map/ppermute | solution.py:666
  10.9 10.0 %collective-permute-start.4 = (bf16[32,2560]{1,0:T(8,128)(2,1)S(1)}, bf16[32,2560]{1,0:T(8,128)(2,1)S(1)}, u32[]{:S(2)}, u32[]{:S(2)}) collective-permute-start(bf16[32,2560]{1,0:T(8,128)(2,1)S(1)} %early_state.1.refs_3_), channel_id=1, source_target_pairs={{4,12},{0,4},{5,13},{1,5},{6,14},{2,6},{7,15},{3,7},{20,28},{16,20... | collective-permute-start | bytes 491528 | tf_op jit(solution)/shard_map/ppermute | solution.py:675
  12.2 8.7 %collective-permute-start.5 = (bf16[32,2560]{1,0:T(8,128)(2,1)S(1)}, bf16[32,2560]{1,0:T(8,128)(2,1)S(1)}, u32[]{:S(2)}, u32[]{:S(2)}) collective-permute-start(bf16[32,2560]{1,0:T(8,128)(2,1)S(1)} %early_state.1.refs_3_), channel_id=1, source_target_pairs={{4,8},{5,9},{6,10},{7,11},{20,24},{21,25},{22,26},{23,27}} | collective-permute-start | bytes 491528 | tf_op jit(solution)/shard_map/ppermute | solution.py:676
  15.9 8.3 %collective-permute-start.3 = (bf16[32,2560]{1,0:T(8,128)(2,1)S(1)}, bf16[32,2560]{1,0:T(8,128)(2,1)S(1)}, u32[]{:S(2)}, u32[]{:S(2)}) collective-permute-start(bf16[32,2560]{1,0:T(8,128)(2,1)S(1)} %get-tuple-element.60.after_ref), channel_id=1, source_target_pairs={{8,12},{9,13},{10,14},{11,15},{24,28},{25,29},{26,30},{27,31}} | collective-permute-start | bytes 491528 | tf_op jit(solution)/shard_map/ppermute | solution.py:684
  24.2 1.7 %collective-permute-start.6 = (bf16[64,2560]{1,0:T(8,128)(2,1)S(1)}, bf16[64,2560]{1,0:T(8,128)(2,1)S(1)}, u32[]{:S(2)}, u32[]{:S(2)}) collective-permute-start(bf16[64,2560]{1,0:T(8,128)(2,1)S(1)} %get-tuple-element.67), channel_id=1, source_target_pairs={{0,1},{1,0},{2,3},{3,2},{4,5},{5,4},{6,7},{7,6},{8,9},{9,8},{10,11... | collective-permute-start | bytes 983048 | tf_op jit(solution)/shard_map/ppermute | solution.py:929
  27.5 9.6 %collective-permute-start.7 = (bf16[272,512]{1,0:T(8,128)(2,1)S(1)}, bf16[272,512]{1,0:T(8,128)(2,1)S(1)}, u32[]{:S(2)}, u32[]{:S(2)}) collective-permute-start(bf16[272,512]{1,0:T(8,128)(2,1)S(1)} %get-tuple-element.78.refs_4_), channel_id=1, source_target_pairs={{0,2},{2,0},{1,3},{3,1},{4,6},{6,4},{5,7},{7,5},{8,10},{10,8},{9,1... | collective-permute-start | bytes 835592 | tf_op jit(solution)/shard_map/ppermute | solution.py:872
  30.7 10.5 %collective-permute-start.9 = (bf16[256,384]{1,0:T(8,128)(2,1)S(1)}, bf16[256,384]{1,0:T(8,128)(2,1)S(1)}, u32[]{:S(2)}, u32[]{:S(2)}) collective-permute-start(bf16[256,384]{1,0:T(8,128)(2,1)S(1)} %project_other.3.refs_4_), channel_id=1, source_target_pairs={{0,2},{2,0},{1,3},{3,1},{4,6},{6,4},{5,7},{7,5},{8,10},{10,8},{9,1... | collective-permute-start | bytes 589832 | tf_op jit(solution)/shard_map/ppermute | solution.py:872
  31.4 13.3 %collective-permute-start.8 = (bf16[256,384]{1,0:T(8,128)(2,1)S(1)}, bf16[256,384]{1,0:T(8,128)(2,1)S(1)}, u32[]{:S(2)}, u32[]{:S(2)}) collective-permute-start(bf16[256,384]{1,0:T(8,128)(2,1)S(1)} %project_other.2.refs_4_), channel_id=1, source_target_pairs={{0,2},{2,0},{1,3},{3,1},{4,6},{6,4},{5,7},{7,5},{8,10},{10,8},{9,1... | collective-permute-start | bytes 589832 | tf_op jit(solution)/shard_map/ppermute | solution.py:872

commit v7 on v6

--- a/solution.py
+++ b/solution.py
@@ -366,6 +366,7 @@
     factor_ref,
     matrix_ref,
     second_ref,
+    halves_ref,
     gain_ref,
     scores_ref,
     running_pieces_ref,
@@ -384,6 +385,9 @@
     copies = [pltpu.make_async_copy(*pair, sems.at[i]) for i, pair in enumerate(pairs)]
     for copy in copies:
         copy.start()
+    read = read_ref[...].astype(F32)
+    swapped = jnp.concatenate([read[:, HALF:], read[:, :HALF]], axis=1)
+    halves_ref[...] = jnp.where(lax.axis_index("band") == 0, read, swapped).astype(BF16)
     upper = lax.axis_index("scan") == 2
     second_ref[...] = state_ref[pl.ds(pl.multiple_of(jnp.where(upper, 0, PART), PART), PART), :]
     prepared = (scores_ref, running_pieces_ref, decay_pieces_ref)
@@ -474,6 +478,7 @@
         0,
         [
             jax.ShapeDtypeStruct((PART, state.shape[1]), BF16),
+            jax.ShapeDtypeStruct((tokens, STATE), BF16),
             jax.ShapeDtypeStruct(norm_gain.shape, F32),
             jax.ShapeDtypeStruct((tokens, tokens), F32),
             pieces_shape,
@@ -704,17 +709,13 @@
     out_ref, square_ref, *first_refs = refs[3 * parts :]
     tokens, width = out_ref.shape
     block = column_block(width)
-    is_first = lax.axis_index("band") == 0
     read = read_ref[...]
     sums = jnp.zeros((tokens, LANES), F32)
     first = 0
     for base_ref, factor_ref in zip(bases, factors):
         for start in range(0, base_ref.shape[1], block):
             lanes = slice(first, first + block)
-            mine, other = mine_ref[:, lanes].astype(F32), other_ref[:, lanes].astype(F32)
-            low = jnp.where(is_first, mine, other).astype(BF16)
-            high = jnp.where(is_first, other, mine).astype(BF16)
-            carried = dot(read, jnp.concatenate([low, high], axis=0))
+            carried = dot(read, jnp.concatenate([mine_ref[:, lanes], other_ref[:, lanes]], axis=0))
             lanes = slice(start, start + block)
             gated = base_ref[:, lanes] + factor_ref[:, lanes] * carried
             for k in range(0, block, LANES):
@@ -725,13 +726,11 @@
                 ).astype(BF16)
                 sums += column * column
             first += block
-    square_ref[...] = jnp.broadcast_to(jnp.sum(sums.T, axis=0, keepdims=True), square_ref.shape)
     for first_ref in first_refs:
         send_kernel(0, out_ref, *weights, first_ref)
-        first_ref[tokens:, :] = jnp.zeros((16, first_ref.shape[1]), BF16)
-        for lane in range(0, tokens, LANES):
-            lanes = slice(lane, lane + LANES)
-            first_ref[tokens:, lanes] = decay_block(square_ref[:1, lanes], 16)
+    squares = jnp.sum(sums.T, axis=0, keepdims=True)
+    for row in range(tokens // LANES):
+        square_ref[row : row + 1, :] = squares[:, row * LANES : (row + 1) * LANES]
 
 
 def gated_part(mine, other, read_proj, gain, bases, factors, weights, first):
@@ -742,15 +741,16 @@
         "gated_part",
         [
             jax.ShapeDtypeStruct((tokens, width), BF16),
-            jax.ShapeDtypeStruct((8, tokens), F32),
+            jax.ShapeDtypeStruct((tokens // LANES, LANES), F32),
         ]
-        + [jax.ShapeDtypeStruct((tokens + 16, first), BF16)] * (first > 0),
+        + [jax.ShapeDtypeStruct((tokens, first), BF16)] * (first > 0),
         (mine, other, read_proj, gain, *bases, *factors, *weights),
         flops=2 * tokens * width * STATE,
     )
 
 
-SENDS = (512, 384, 384)
+SENDS = (256, 384, 384, 256)
+FINISH_FLOPS = 2 * 10**9
 
 
 def project(gated_ref, weights, other, first, count):
@@ -768,8 +768,8 @@
 
 def send_kernel(first, gated_ref, *refs):
     *weights, out_ref = refs
-    tokens, count = gated_ref.shape[0], out_ref.shape[1]
-    out_ref[:tokens, :] = project(gated_ref, weights, True, first, count).astype(BF16)
+    count = out_ref.shape[1]
+    out_ref[...] = project(gated_ref, weights, True, first, count).astype(BF16)
 
 
 def own_kernel(gated_ref, *refs):
@@ -779,71 +779,42 @@
         out_ref[:, first : first + count] = project(gated_ref, weights, False, first, count)
 
 
-def finish_columns(first, got_refs, own_ref, scale, out_ref, sent_ref, sems):
-    tokens = own_ref.shape[0]
-    copies, place = [], 0
-    for got_ref in got_refs:
-        count = got_ref.shape[1]
-        for lane in range(0, count, LANES):
-            own_lanes = slice(first + place + lane, first + place + lane + LANES)
-            total = own_ref[:, own_lanes] + got_ref[:tokens, lane : lane + LANES].astype(F32)
-            sent_ref[:, place + lane : place + lane + LANES] = (total * scale).astype(BF16)
-        copies.append(
-            pltpu.make_async_copy(
-                sent_ref.at[:, pl.ds(place, count)],
-                out_ref.at[:, pl.ds(first + place, count)],
-                sems.at[len(copies)],
-            )
-        )
-        copies[-1].start()
-        place += count
-    for copy in copies:
-        copy.wait()
-
-
-def finish_first_kernel(squares_ref, own_ref, got_ref, out_ref, scale_ref, sent_ref, sems):
-    tokens = own_ref.shape[0]
-    other_squares = got_ref[tokens:, :tokens].astype(F32)
-    mean = (squares_ref[:1] + jnp.sum(other_squares, axis=0, keepdims=True)) / INNER
+def finish_kernel(first, squares_ref, other_squares_ref, own_ref, got_ref, *refs):
+    out_ref, sent_ref, sem = refs[-3:]
+    tokens, count = got_ref.shape
+    mean = (squares_ref[...] + other_squares_ref[...]) / INNER
     scale = lax.rsqrt(mean + EPSILON)
-    scale_ref[...] = jnp.broadcast_to(scale, (LANES, tokens)).T
-    finish_columns(0, [got_ref], own_ref, scale_ref[...], out_ref, sent_ref, sems)
-
-
-def finish_rest_kernel(scale_ref, own_ref, *refs):
-    *got_refs, old_ref, out_ref, sent_ref, sems = refs
-    first = own_ref.shape[1] - sent_ref.shape[1]
-    finish_columns(first, got_refs, own_ref, scale_ref[...], out_ref, sent_ref, sems)
-
-
-def finish(squares, own, got):
-    tokens, columns = own.shape
-    first = got[0].shape[1]
-    shape = jax.ShapeDtypeStruct(own.shape, BF16)
-    params = pltpu.CompilerParams(vmem_limit_bytes=8 * MIB)
-    begun, scale = pl.pallas_call(
-        finish_first_kernel,
-        name="finish_first",
-        out_shape=[shape, jax.ShapeDtypeStruct((tokens, LANES), F32)],
-        in_specs=[IN_VMEM] * 3,
-        out_specs=[IN_HBM, IN_VMEM],
-        scratch_shapes=[pltpu.VMEM((tokens, first), BF16), pltpu.SemaphoreType.DMA((1,))],
-        compiler_params=params,
-    )(squares, own, got[0])
-    args = (scale, own, *got[1:])
-    return pl.pallas_call(
-        finish_rest_kernel,
-        name="finish_rest",
-        out_shape=shape,
-        in_specs=[IN_VMEM] * len(args) + [IN_HBM],
-        out_specs=IN_HBM,
-        input_output_aliases={len(args): 0},
-        scratch_shapes=[
-            pltpu.VMEM((tokens, columns - first), BF16),
-            pltpu.SemaphoreType.DMA((len(got) - 1,)),
-        ],
-        compiler_params=params,
-    )(*args, begun)
+    scale = jnp.concatenate(
+        [jnp.broadcast_to(scale[k : k + 1], (LANES, LANES)).T for k in range(tokens // LANES)], axis=0
+    )
+    for lane in range(0, count, LANES):
+        lanes = slice(lane, lane + LANES)
+        total = own_ref[:, first + lane : first + lane + LANES] + got_ref[:, lanes].astype(F32)
+        sent_ref[:, lanes] = (total * scale).astype(BF16)
+    copy = pltpu.make_async_copy(sent_ref, out_ref.at[:, pl.ds(first, count)], sem)
+    copy.start()
+    copy.wait()
+
+
+def finish(squares, other_squares, own, got):
+    result, first = [], 0
+    for part in got:
+        args = (squares, other_squares, own, part)
+        result = [
+            pl.pallas_call(
+                functools.partial(finish_kernel, first),
+                name="finish",
+                out_shape=jax.ShapeDtypeStruct(own.shape, BF16),
+                in_specs=[IN_VMEM] * len(args) + [IN_HBM] * len(result),
+                out_specs=IN_HBM,
+                input_output_aliases={len(args): 0} if result else {},
+                scratch_shapes=[pltpu.VMEM(part.shape, BF16), pltpu.SemaphoreType.DMA(())],
+                compiler_params=pltpu.CompilerParams(vmem_limit_bytes=8 * MIB),
+                cost_estimate=pl.CostEstimate(flops=FINISH_FLOPS, bytes_accessed=0, transcendentals=0),
+            )(*args, *result)
+        ]
+        first += part.shape[1]
+    return result[0]
 
 
 def direct(members, columns):
@@ -853,7 +824,7 @@
 def layer_columns(members, gated, squares, weights, ready):
     columns = weights[0].shape[1] // members
     if not direct(members, columns):
-        mean = lax.psum(squares[0], "tensor") / INNER
+        mean = lax.psum(squares.reshape(-1), "tensor") / INNER
         partial = dot(gated, jnp.concatenate(weights, axis=0)).astype(BF16)
         total = lax.psum_scatter(partial, "tensor", scatter_dimension=1, tiled=True)
         return (total.astype(F32) * lax.rsqrt(mean + EPSILON)[:, None]).astype(BF16)
@@ -870,6 +841,7 @@
         )
         first += count
     got = [lax.ppermute(part, "tensor", swap) for part in parts]
+    other_squares = lax.ppermute(squares, "tensor", swap)
     (own,) = local_call(
         own_kernel,
         "project_own",
@@ -877,7 +849,7 @@
         (gated, *weights),
         after=parts[-1:],
     )
-    return finish(squares, own, got)
+    return finish(squares, other_squares, own, got)
 
 
 def on_device(
@@ -907,7 +879,7 @@
     constants = (skip_gain[None], norm_gain.reshape(-1, LANES), out_weight)
     write, read, *streams = passed
     values = (running, weight, *streams)
-    bases, factors, weights, prepared, gains = [], [], [], [], []
+    bases, factors, weights, prepared, halves, gains = [], [], [], [], [], []
 
     def local(part, after):
         if not local_shares(signal.shape[1])[0][part]:
@@ -915,11 +887,12 @@
         if part:
             base, factor, matrix = local_rest(part, values, prepared, out_weight, after)
         else:
-            base, factor, matrix, second, gain, *rest, lanes = local_first(
+            base, factor, matrix, second, *kept, lanes = local_first(
                 (*values, write, read, decay, got), state, constants, after
             )
-            prepared.extend(rest)
-            gains.append(gain)
+            halves.append(kept[0])
+            gains.append(kept[1])
+            prepared.extend(kept[2:])
         bases.append(base)
         factors.append(factor)
         weights.append(matrix)
@@ -929,7 +902,7 @@
     other = lax.ppermute(give, "band", cores)
     ahead = SENDS[0] if direct(members, out_weight.shape[1] // members) else 0
     gated, squares, *ready = gated_part(
-        mine, other, read, gains[0], bases, factors, weights, ahead
+        mine, other, halves[0], gains[0], bases, factors, weights, ahead
     )
     return layer_columns(members, gated, squares, weights, ready)
 

time: 46.1 us -> 45.4 us (0.985)
  waiting for transfers between devices: 18.8 us -> 14.2 us
  starting transfers between devices: 9 us -> 11.2 us
  Pallas kernels: 16.9 us -> 18.5 us
    ppermute x3 -> x4, waiting for transfers between devices: 9.1 us -> 3.94 us  [layer_columns(): got = [lax.ppermute(part, 'tensor', swap) for part in parts]]
    ppermute x0 -> x1, starting transfers between devices: none -> 1.5 us  [layer_columns(): other_squares = lax.ppermute(squares, 'tensor', swap)]
    pallas_call x2 -> x4, Pallas kernels: 1.68 us -> 3.18 us  [finish(): pl.pallas_call(functools.partial(finish_kernel, first), name='finish', ou...]
    ppermute x3 -> x4, starting transfers between devices: 3.64 us -> 4.33 us  [layer_columns(): got = [lax.ppermute(part, 'tensor', swap) for part in parts]]
    ppermute x0 -> x1, waiting for transfers between devices: none -> 0.56 us  [layer_columns(): other_squares = lax.ppermute(squares, 'tensor', swap)]
    pallas_call x9 -> x10, Pallas kernels: 5.74 us -> 5.87 us  [local_call(): pl.pallas_call(kernel, name=name, out_shape=outs, in_specs=[pl.BlockSpec(...]
  transfers between devices with their start and end apart: 10 -> 12, of which waited for: 8 -> 8; matrix products, arithmetic and copies ran while one was open for 0% -> 0% of each run, Pallas kernels for 26% -> 31%
where the time goes in v7:
time: 45.4 us; the launch traced here: 44.8 us
  Pallas kernels  18.5 us (41%)
  waiting for transfers between devices  14.2 us (31%)
  starting transfers between devices  11.2 us (25%)
  between operations  0.85 us (2%)
    pallas_call x3, Pallas kernels, local_call_of(): pl.pallas_call(kernel, name=name, out_shape=[jax.ShapeDtypeStruct((tokens...  7.02 us
    pallas_call x10, Pallas kernels, local_call(): pl.pallas_call(kernel, name=name, out_shape=outs, in_specs=[pl.BlockSpec(...  5.87 us
    ppermute x4, starting transfers between devices, layer_columns(): got = [lax.ppermute(part, 'tensor', swap) for part in parts]  4.33 us
    ppermute x4, waiting for transfers between devices, layer_columns(): got = [lax.ppermute(part, 'tensor', swap) for part in parts]  3.94 us
    pallas_call x4, Pallas kernels, finish(): pl.pallas_call(functools.partial(finish_kernel, first), name='finish', ou...  3.18 us
    ppermute x1, waiting for transfers between devices, entering_state(): last = lax.ppermute(middle, 'scan', [(2, 3)])  3.13 us
    ppermute x1, waiting for transfers between devices, entering_state(): far = lax.ppermute(second, 'scan', [(0, 2), (2, 3)])  2.85 us
    pallas_call x1, Pallas kernels, own_state(): pl.pallas_call(state_kernel, name='own_state', out_shape=[jax.ShapeDtypeS...  2.46 us
  transfers between devices with their start and end apart: 12, of which 8 were waited for; matrix products, arithmetic and copies ran while one was open for 0% of the time, Pallas kernels for 31%

profile of v7, /device:TPU:24, one launch (start us, length us, event | category | flops | bytes accessed | tf_op | source)
XLA Modules:
  0.0 44.8 jit_solution(12145724044005594320)
XLA Ops:
  0.7 2.5 %own_state.1 = (f32[40,256]{1,0:T(8,128)S(1)}, f32[40,256]{1,0:T(8,128)S(1)}, bf16[16,128]{1,0:T(8,128)(2,1)S(1)}, f32[64,2560]{1,0:T(8,128)S(1)}, bf16[64,2688]...) custom-call(s32[1]{0:T(128)S(6)} %copy.24.band_ref, ...), custom_call_target="tpu_custom_call" | custom-call | flops 335544320 | bytes 1310720 | tf_op jit(solution)/shard_map/own_state/pallas_call | solution.py:237
  3.2 1.6 %collective-permute-done.refs_1_.got_ref.refs_6_.refs_2_ = bf16[64,2688]{1,0:T(8,128)(2,1)S(1)} collective-permute-done((bf16[64,2688]{1,0:T(8,128)(2,1)S(1)}, bf16[64,2688]{1,0:T(8,128)(2,1)S(1)}, u32[]{:S(2)}, u32[]{:S(2)}) %collective-permute-start) | collective-permute-done | bytes 344096 | tf_op jit(solution)/shard_map/ppermute | solution.py:877
  4.8 0.2 chip_state.1
  5.1 0.7 %collective-permute-start.1 = (bf16[32,2688]{1,0:T(8,128)(2,1)S(1)}, bf16[32,2688]{1,0:T(8,128)(2,1)S(1)}, u32[]{:S(2)}, u32[]{:S(2)}) collective-permute-start(bf16[32,2688]{1,0:T(8,128)(2,1)S(1)} %get-tuple-element.46.after_ref), channel_id=1, source_target_pairs={{0,4},{4,8},{1,5},{5,9},{2,6},{6,10},{3,7},{7,11},{16,20},{20,24},... | collective-permute-start | bytes 516104 | tf_op jit(solution)/shard_map/ppermute | solution.py:669
  5.8 1.6 %local_first.1 = (f32[256,512]{1,0:T(8,128)S(1)}, f32[256,512]{1,0:T(8,128)S(1)}, bf16[256,2560]{1,0:T(8,128)(2,1)S(1)}, bf16[32,2688]{1,0:T(8,128)(2,1)S(1)}, b...) custom-call(f32[40,256]{1,0:T(8,128)S(1)} %get-tuple-element.47.runn, ...), custom_call_target="tpu_custom_call" | custom-call | flops 201326592 | bytes 1572864 | tf_op jit(solution)/shard_map/local_first/pallas_call | solution.py:452
  7.4 1.3 %collective-permute-start.2 = (bf16[32,2688]{1,0:T(8,128)(2,1)S(1)}, bf16[32,2688]{1,0:T(8,128)(2,1)S(1)}, u32[]{:S(2)}, u32[]{:S(2)}) collective-permute-start(bf16[32,2688]{1,0:T(8,128)(2,1)S(1)} %get-tuple-element.53.after_ref), channel_id=1, source_target_pairs={{0,8},{8,12},{1,9},{9,13},{2,10},{10,14},{3,11},{11,15},{16,24},{2... | collective-permute-start | bytes 516104 | tf_op jit(solution)/shard_map/ppermute | solution.py:671
  8.7 2.1 %local_rest.2 = (f32[256,1024]{1,0:T(8,128)S(1)}, f32[256,1024]{1,0:T(8,128)S(1)}, bf16[768,2560]{1,0:T(8,128)(2,1)S(1)}) custom-call(f32[40,256]{1,0:T(8,128)S(1)} %get-tuple-element.47.running_ref, f32[40,256]{1,0:T(8,128)S(1)} %get-tuple-element.48.weight_ref, bf16[256,2560]{1,0:T(8,128)(2,1)S(1)} %get-tuple-element.49.signal_ref, ...), custom_call_target="tpu_custom_call" | custom-call | flops 402653184 | bytes 3145728 | tf_op jit(solution)/shard_map/local_rest/pallas_call | solution.py:452
  10.9 1.3 %collective-permute-start.4 = (bf16[32,2560]{1,0:T(8,128)(2,1)S(1)}, bf16[32,2560]{1,0:T(8,128)(2,1)S(1)}, u32[]{:S(2)}, u32[]{:S(2)}) collective-permute-start(bf16[32,2560]{1,0:T(8,128)(2,1)S(1)} %early_state.1.refs_3_), channel_id=1, source_target_pairs={{4,12},{0,4},{5,13},{1,5},{6,14},{2,6},{7,15},{3,7},{20,28},{16,20... | collective-permute-start | bytes 491528 | tf_op jit(solution)/shard_map/ppermute | solution.py:680
  12.2 0.7 %collective-permute-start.5 = (bf16[32,2560]{1,0:T(8,128)(2,1)S(1)}, bf16[32,2560]{1,0:T(8,128)(2,1)S(1)}, u32[]{:S(2)}, u32[]{:S(2)}) collective-permute-start(bf16[32,2560]{1,0:T(8,128)(2,1)S(1)} %early_state.1.refs_3_), channel_id=1, source_target_pairs={{4,8},{5,9},{6,10},{7,11},{20,24},{21,25},{22,26},{23,27}} | collective-permute-start | bytes 491528 | tf_op jit(solution)/shard_map/ppermute | solution.py:681
  12.9 2.9 %collective-permute-done.2.refs_2_.refs_1_ = bf16[32,2688]{1,0:T(8,128)(2,1)S(1)} collective-permute-done((bf16[32,2688]{1,0:T(8,128)(2,1)S(1)}, bf16[32,2688]{1,0:T(8,128)(2,1)S(1)}, u32[]{:S(2)}, u32[]{:S(2)}) %collective-permute-start.2) | collective-permute-done | bytes 172064 | tf_op jit(solution)/shard_map/ppermute | solution.py:671
  15.9 1.3 %collective-permute-start.3 = (bf16[32,2560]{1,0:T(8,128)(2,1)S(1)}, bf16[32,2560]{1,0:T(8,128)(2,1)S(1)}, u32[]{:S(2)}, u32[]{:S(2)}) collective-permute-start(bf16[32,2560]{1,0:T(8,128)(2,1)S(1)} %get-tuple-element.59.after_ref), channel_id=1, source_target_pairs={{8,12},{9,13},{10,14},{11,15},{24,28},{25,29},{26,30},{27,31}} | collective-permute-start | bytes 491528 | tf_op jit(solution)/shard_map/ppermute | solution.py:689
  17.2 3.2 %local_rest.3 = (f32[256,1024]{1,0:T(8,128)S(1)}, f32[256,1024]{1,0:T(8,128)S(1)}, bf16[1536,2560]{1,0:T(8,128)(2,1)S(1)}) custom-call(f32[40,256]{1,0:T(8,128)S(1)} %get-tuple-element.47.running_ref, f32[40,256]{1,0:T(8,128)S(1)} %get-tuple-element.48.weight_ref, bf16[256,2560]{1,0:T(8,128)(2,1)S(1)} %get-tuple-element.49.signal_ref, ...), custom_call_target="tpu_custom_call" | custom-call | flops 402653184 | bytes 3145728 | tf_op jit(solution)/shard_map/local_rest/pallas_call | solution.py:452
  20.5 0.4 %collective-permute-done.4.refs_2_ = bf16[32,2560]{1,0:T(8,128)(2,1)S(1)} collective-permute-done((bf16[32,2560]{1,0:T(8,128)(2,1)S(1)}, bf16[32,2560]{1,0:T(8,128)(2,1)S(1)}, u32[]{:S(2)}, u32[]{:S(2)}) %collective-permute-start.4) | collective-permute-done | bytes 163872 | tf_op jit(solution)/shard_map/ppermute | solution.py:680
  21.0 3.1 %collective-permute-done.3.refs_0_ = bf16[32,2560]{1,0:T(8,128)(2,1)S(1)} collective-permute-done((bf16[32,2560]{1,0:T(8,128)(2,1)S(1)}, bf16[32,2560]{1,0:T(8,128)(2,1)S(1)}, u32[]{:S(2)}, u32[]{:S(2)}) %collective-permute-start.3) | collective-permute-done | bytes 163872 | tf_op jit(solution)/shard_map/ppermute | solution.py:689
  24.3 1.6 %collective-permute-done.6.refs_1_ = bf16[64,2560]{1,0:T(8,128)(2,1)S(1)} collective-permute-done((bf16[64,2560]{1,0:T(8,128)(2,1)S(1)}, bf16[64,2560]{1,0:T(8,128)(2,1)S(1)}, u32[]{:S(2)}, u32[]{:S(2)}) %collective-permute-start.6) | collective-permute-done | bytes 327712 | tf_op jit(solution)/shard_map/ppermute | solution.py:902
  25.9 1.2 %gated_part.1 = (bf16[256,2560]{1,0:T(8,128)(2,1)S(1)}, f32[2,128]{1,0:T(2,128)S(1)}, bf16[256,256]{1,0:T(8,128)(2,1)S(1)}) custom-call(bf16[64,2560]{1,0:T(8,128)(2,1)S(1)} %get-tuple-element.65.refs_0_, bf16[64,2560]{1,0:T(8,128)(2,1)S(1)} %collective-permute-done.6.refs_1_, bf16[256,128]{1,0:T(8,128)(2,1)S(1)} %get-tuple-element.67.refs_2_, ...), custom_call_target="tpu_custom_call" | custom-call | flops 167772160 | bytes 20524032 | tf_op jit(solution)/shard_map/gated_part/pallas_call | solution.py:112
  27.1 1.6 %collective-permute-start.11 = (bf16[256,256]{1,0:T(8,128)(2,1)S(1)}, bf16[256,256]{1,0:T(8,128)(2,1)S(1)}, u32[]{:S(2)}, u32[]{:S(2)}) collective-permute-start(bf16[256,256]{1,0:T(8,128)(2,1)S(1)} %get-tuple-element.78.refs_4_), channel_id=1, source_target_pairs={{0,2},{2,0},{1,3},{3,1},{4,6},{6,4},{5,7},{7,5},{8,10},{10,8},{9,1... | collective-permute-start | bytes 393224 | tf_op jit(solution)/shard_map/ppermute | solution.py:843
  28.7 0.8 %project_other.3.refs_4_ = bf16[256,384]{1,0:T(8,128)(2,1)S(1)} custom-call(bf16[256,2560]{1,0:T(8,128)(2,1)S(1)} %get-tuple-element.77.refs_0_, bf16[256,2560]{1,0:T(8,128)(2,1)S(1)} %get-tuple-element.73.refs_10_.refs_1_, bf16[768,2560]{1,0:T(8,128)(2,1)S(1)} %get-tuple-element.74.refs_11_.refs_2_, ...), custom_call_target="tpu_custom_call" | custom-call | bytes 14614528 | tf_op jit(solution)/shard_map/project_other/pallas_call | solution.py:112
  29.6 0.6 %collective-permute-start.10 = (bf16[256,384]{1,0:T(8,128)(2,1)S(1)}, bf16[256,384]{1,0:T(8,128)(2,1)S(1)}, u32[]{:S(2)}, u32[]{:S(2)}) collective-permute-start(bf16[256,384]{1,0:T(8,128)(2,1)S(1)} %project_other.3.refs_4_), channel_id=1, source_target_pairs={{0,2},{2,0},{1,3},{3,1},{4,6},{6,4},{5,7},{7,5},{8,10},{10,8},{9,1... | collective-permute-start | bytes 589832 | tf_op jit(solution)/shard_map/ppermute | solution.py:843
  30.1 1.5 %collective-permute-start.7 = (f32[2,128]{1,0:T(2,128)S(1)}, f32[2,128]{1,0:T(2,128)S(1)}, u32[]{:S(2)}, u32[]{:S(2)}) collective-permute-start(f32[2,128]{1,0:T(2,128)S(1)} %get-tuple-element.76.squares_ref), channel_id=1, source_target_pairs={{0,2},{2,0},{1,3},{3,1},{4,6},{6,4},{5,7},{7,5},{8,10},{10,8},{9,1... | collective-permute-start | bytes 3080 | tf_op jit(solution)/shard_map/ppermute | solution.py:844
  31.6 0.8 %project_other.4.refs_4_ = bf16[256,384]{1,0:T(8,128)(2,1)S(1)} custom-call(bf16[256,2560]{1,0:T(8,128)(2,1)S(1)} %get-tuple-element.77.refs_0_, bf16[256,2560]{1,0:T(8,128)(2,1)S(1)} %get-tuple-element.73.refs_10_.refs_1_, bf16[768,2560]{1,0:T(8,128)(2,1)S(1)} %get-tuple-element.74.refs_11_.refs_2_, ...), custom_call_target="tpu_custom_call" | custom-call | bytes 14614528 | tf_op jit(solution)/shard_map/project_other/pallas_call | solution.py:112
  32.5 0.5 %project_other.5.refs_4_ = bf16[256,256]{1,0:T(8,128)(2,1)S(1)} custom-call(bf16[256,2560]{1,0:T(8,128)(2,1)S(1)} %get-tuple-element.77.refs_0_, bf16[256,2560]{1,0:T(8,128)(2,1)S(1)} %get-tuple-element.73.refs_10_.refs_1_, bf16[768,2560]{1,0:T(8,128)(2,1)S(1)} %get-tuple-element.74.refs_11_.refs_2_, ...), custom_call_target="tpu_custom_call" | custom-call | bytes 14548992 | tf_op jit(solution)/shard_map/project_other/pallas_call | solution.py:112
  33.0 0.6 %collective-permute-start.9 = (bf16[256,384]{1,0:T(8,128)(2,1)S(1)}, bf16[256,384]{1,0:T(8,128)(2,1)S(1)}, u32[]{:S(2)}, u32[]{:S(2)}) collective-permute-start(bf16[256,384]{1,0:T(8,128)(2,1)S(1)} %project_other.4.refs_4_), channel_id=1, source_target_pairs={{0,2},{2,0},{1,3},{3,1},{4,6},{6,4},{5,7},{7,5},{8,10},{10,8},{9,1... | collective-permute-start | bytes 589832 | tf_op jit(solution)/shard_map/ppermute | solution.py:843
  33.6 1.9 %project_own.1.own_ref = f32[256,1280]{1,0:T(8,128)S(1)} custom-call(bf16[256,2560]{1,0:T(8,128)(2,1)S(1)} %get-tuple-element.77.refs_0_, bf16[256,2560]{1,0:T(8,128)(2,1)S(1)} %get-tuple-element.73.refs_10_.refs_1_, bf16[768,2560]{1,0:T(8,128)(2,1)S(1)} %get-tuple-element.74.refs_11_.refs_2_, bf16[1536,2560]{1,0:T(8,128)(2,1)S(1)} %get-tuple-element.75.refs_12_.refs_3_, ...), custom_call_target="tpu_custom_call" | custom-call | bytes 15728640 | tf_op jit(solution)/shard_map/project_own/pallas_call | solution.py:112
  35.5 1.6 %collective-permute-start.8 = (bf16[256,256]{1,0:T(8,128)(2,1)S(1)}, bf16[256,256]{1,0:T(8,128)(2,1)S(1)}, u32[]{:S(2)}, u32[]{:S(2)}) collective-permute-start(bf16[256,256]{1,0:T(8,128)(2,1)S(1)} %project_other.5.refs_4_), channel_id=1, source_target_pairs={{0,2},{2,0},{1,3},{3,1},{4,6},{6,4},{5,7},{7,5},{8,10},{10,8},{9,1... | collective-permute-start | bytes 393224 | tf_op jit(solution)/shard_map/ppermute | solution.py:843
  37.1 0.6 %collective-permute-done.7.other_squares_ref = f32[2,128]{1,0:T(2,128)S(1)} collective-permute-done((f32[2,128]{1,0:T(2,128)S(1)}, f32[2,128]{1,0:T(2,128)S(1)}, u32[]{:S(2)}, u32[]{:S(2)}) %collective-permute-start.7) | collective-permute-done | bytes 1056 | tf_op jit(solution)/shard_map/ppermute | solution.py:844
  37.6 0.8 %finish.4.refs_0_ = bf16[256,1280]{1,0:T(8,128)(2,1)} custom-call(f32[2,128]{1,0:T(2,128)S(1)} %get-tuple-element.76.squares_ref, f32[2,128]{1,0:T(2,128)S(1)} %collective-permute-done.7.other_squares_ref, f32[256,1280]{1,0:T(8,128)S(1)} %project_own.1.own_ref, bf16[256,256]{1,0:T(8,128)(2,1)S(1)} %collective-permute-done.11.got_ref), custom_call_target="tpu_custom_call" | custom-call | flops 2000000000 | tf_op jit(solution)/shard_map/finish/pallas_call | solution.py:804
  38.4 0.8 %finish.5.refs_0_ = bf16[256,1280]{1,0:T(8,128)(2,1)} custom-call(f32[2,128]{1,0:T(2,128)S(1)} %get-tuple-element.76.squares_ref, f32[2,128]{1,0:T(2,128)S(1)} %collective-permute-done.7.other_squares_ref, f32[256,1280]{1,0:T(8,128)S(1)} %project_own.1.own_ref, bf16[256,384]{1,0:T(8,128)(2,1)S(1)} %collective-permute-done.10.got_ref, ...), custom_call_target="tpu_custom_call", output_to_operand_aliasing={{}: (4, {})} | custom-call | flops 2000000000 | tf_op jit(solution)/shard_map/finish/pallas_call | solution.py:804
  39.2 2.6 %collective-permute-done.9.got_ref = bf16[256,384]{1,0:T(8,128)(2,1)S(1)} collective-permute-done((bf16[256,384]{1,0:T(8,128)(2,1)S(1)}, bf16[256,384]{1,0:T(8,128)(2,1)S(1)}, u32[]{:S(2)}, u32[]{:S(2)}) %collective-permute-start.9) | collective-permute-done | bytes 196640 | tf_op jit(solution)/shard_map/ppermute | solution.py:843
  41.8 0.8 %finish.6.refs_0_ = bf16[256,1280]{1,0:T(8,128)(2,1)} custom-call(f32[2,128]{1,0:T(2,128)S(1)} %get-tuple-element.76.squares_ref, f32[2,128]{1,0:T(2,128)S(1)} %collective-permute-done.7.other_squares_ref, f32[256,1280]{1,0:T(8,128)S(1)} %project_own.1.own_ref, bf16[256,384]{1,0:T(8,128)(2,1)S(1)} %collective-permute-done.9.got_ref, ...), custom_call_target="tpu_custom_call", output_to_operand_aliasing={{}: (4, {})} | custom-call | flops 2000000000 | tf_op jit(solution)/shard_map/finish/pallas_call | solution.py:804
  42.6 1.4 %collective-permute-done.8.got_ref = bf16[256,256]{1,0:T(8,128)(2,1)S(1)} collective-permute-done((bf16[256,256]{1,0:T(8,128)(2,1)S(1)}, bf16[256,256]{1,0:T(8,128)(2,1)S(1)}, u32[]{:S(2)}, u32[]{:S(2)}) %collective-permute-start.8) | collective-permute-done | bytes 131104 | tf_op jit(solution)/shard_map/ppermute | solution.py:843
  44.0 0.8 %finish.7 = bf16[256,1280]{1,0:T(8,128)(2,1)} custom-call(f32[2,128]{1,0:T(2,128)S(1)} %get-tuple-element.76.squares_ref, f32[2,128]{1,0:T(2,128)S(1)} %collective-permute-done.7.other_squares_ref, f32[256,1280]{1,0:T(8,128)S(1)} %project_own.1.own_ref, bf16[256,256]{1,0:T(8,128)(2,1)S(1)} %collective-permute-done.8.got_ref, ...), custom_call_target="tpu_custom_call", output_to_operand_aliasing={{}: (4, {})} | custom-call | flops 2000000000 | tf_op jit(solution)/shard_map/finish/pallas_call | solution.py:804
  (10 shorter events, 0.5 us)
Async XLA Ops:
  3.1 1.7 %collective-permute-start = (bf16[64,2688]{1,0:T(8,128)(2,1)S(1)}, bf16[64,2688]{1,0:T(8,128)(2,1)S(1)}, u32[]{:S(2)}, u32[]{:S(2)}) collective-permute-start(bf16[64,2688]{1,0:T(8,128)(2,1)S(1)} %get-tuple-element.43), channel_id=1, source_target_pairs={{0,1},{1,0},{2,3},{3,2},{4,5},{5,4},{6,7},{7,6},{8,9},{9,8},{10,11... | collective-permute-start | bytes 1032200 | tf_op jit(solution)/shard_map/ppermute | solution.py:877
  5.1 5.8 %collective-permute-start.1 = (bf16[32,2688]{1,0:T(8,128)(2,1)S(1)}, bf16[32,2688]{1,0:T(8,128)(2,1)S(1)}, u32[]{:S(2)}, u32[]{:S(2)}) collective-permute-start(bf16[32,2688]{1,0:T(8,128)(2,1)S(1)} %get-tuple-element.46.after_ref), channel_id=1, source_target_pairs={{0,4},{4,8},{1,5},{5,9},{2,6},{6,10},{3,7},{7,11},{16,20},{20,24},... | collective-permute-start | bytes 516104 | tf_op jit(solution)/shard_map/ppermute | solution.py:669
  7.4 8.3 %collective-permute-start.2 = (bf16[32,2688]{1,0:T(8,128)(2,1)S(1)}, bf16[32,2688]{1,0:T(8,128)(2,1)S(1)}, u32[]{:S(2)}, u32[]{:S(2)}) collective-permute-start(bf16[32,2688]{1,0:T(8,128)(2,1)S(1)} %get-tuple-element.53.after_ref), channel_id=1, source_target_pairs={{0,8},{8,12},{1,9},{9,13},{2,10},{10,14},{3,11},{11,15},{16,24},{2... | collective-permute-start | bytes 516104 | tf_op jit(solution)/shard_map/ppermute | solution.py:671
  10.9 10.0 %collective-permute-start.4 = (bf16[32,2560]{1,0:T(8,128)(2,1)S(1)}, bf16[32,2560]{1,0:T(8,128)(2,1)S(1)}, u32[]{:S(2)}, u32[]{:S(2)}) collective-permute-start(bf16[32,2560]{1,0:T(8,128)(2,1)S(1)} %early_state.1.refs_3_), channel_id=1, source_target_pairs={{4,12},{0,4},{5,13},{1,5},{6,14},{2,6},{7,15},{3,7},{20,28},{16,20... | collective-permute-start | bytes 491528 | tf_op jit(solution)/shard_map/ppermute | solution.py:680
  12.2 8.7 %collective-permute-start.5 = (bf16[32,2560]{1,0:T(8,128)(2,1)S(1)}, bf16[32,2560]{1,0:T(8,128)(2,1)S(1)}, u32[]{:S(2)}, u32[]{:S(2)}) collective-permute-start(bf16[32,2560]{1,0:T(8,128)(2,1)S(1)} %early_state.1.refs_3_), channel_id=1, source_target_pairs={{4,8},{5,9},{6,10},{7,11},{20,24},{21,25},{22,26},{23,27}} | collective-permute-start | bytes 491528 | tf_op jit(solution)/shard_map/ppermute | solution.py:681
  15.9 8.3 %collective-permute-start.3 = (bf16[32,2560]{1,0:T(8,128)(2,1)S(1)}, bf16[32,2560]{1,0:T(8,128)(2,1)S(1)}, u32[]{:S(2)}, u32[]{:S(2)}) collective-permute-start(bf16[32,2560]{1,0:T(8,128)(2,1)S(1)} %get-tuple-element.59.after_ref), channel_id=1, source_target_pairs={{8,12},{9,13},{10,14},{11,15},{24,28},{25,29},{26,30},{27,31}} | collective-permute-start | bytes 491528 | tf_op jit(solution)/shard_map/ppermute | solution.py:689
  24.2 1.7 %collective-permute-start.6 = (bf16[64,2560]{1,0:T(8,128)(2,1)S(1)}, bf16[64,2560]{1,0:T(8,128)(2,1)S(1)}, u32[]{:S(2)}, u32[]{:S(2)}) collective-permute-start(bf16[64,2560]{1,0:T(8,128)(2,1)S(1)} %get-tuple-element.66), channel_id=1, source_target_pairs={{0,1},{1,0},{2,3},{3,2},{4,5},{5,4},{6,7},{7,6},{8,9},{9,8},{10,11... | collective-permute-start | bytes 983048 | tf_op jit(solution)/shard_map/ppermute | solution.py:902
  27.1 10.5 %collective-permute-start.11 = (bf16[256,256]{1,0:T(8,128)(2,1)S(1)}, bf16[256,256]{1,0:T(8,128)(2,1)S(1)}, u32[]{:S(2)}, u32[]{:S(2)}) collective-permute-start(bf16[256,256]{1,0:T(8,128)(2,1)S(1)} %get-tuple-element.78.refs_4_), channel_id=1, source_target_pairs={{0,2},{2,0},{1,3},{3,1},{4,6},{6,4},{5,7},{7,5},{8,10},{10,8},{9,1... | collective-permute-start | bytes 393224 | tf_op jit(solution)/shard_map/ppermute | solution.py:843
  29.6 8.9 %collective-permute-start.10 = (bf16[256,384]{1,0:T(8,128)(2,1)S(1)}, bf16[256,384]{1,0:T(8,128)(2,1)S(1)}, u32[]{:S(2)}, u32[]{:S(2)}) collective-permute-start(bf16[256,384]{1,0:T(8,128)(2,1)S(1)} %project_other.3.refs_4_), channel_id=1, source_target_pairs={{0,2},{2,0},{1,3},{3,1},{4,6},{6,4},{5,7},{7,5},{8,10},{10,8},{9,1... | collective-permute-start | bytes 589832 | tf_op jit(solution)/shard_map/ppermute | solution.py:843
  30.1 7.5 %collective-permute-start.7 = (f32[2,128]{1,0:T(2,128)S(1)}, f32[2,128]{1,0:T(2,128)S(1)}, u32[]{:S(2)}, u32[]{:S(2)}) collective-permute-start(f32[2,128]{1,0:T(2,128)S(1)} %get-tuple-element.76.squares_ref), channel_id=1, source_target_pairs={{0,2},{2,0},{1,3},{3,1},{4,6},{6,4},{5,7},{7,5},{8,10},{10,8},{9,1... | collective-permute-start | bytes 3080 | tf_op jit(solution)/shard_map/ppermute | solution.py:844
  33.0 8.8 %collective-permute-start.9 = (bf16[256,384]{1,0:T(8,128)(2,1)S(1)}, bf16[256,384]{1,0:T(8,128)(2,1)S(1)}, u32[]{:S(2)}, u32[]{:S(2)}) collective-permute-start(bf16[256,384]{1,0:T(8,128)(2,1)S(1)} %project_other.4.refs_4_), channel_id=1, source_target_pairs={{0,2},{2,0},{1,3},{3,1},{4,6},{6,4},{5,7},{7,5},{8,10},{10,8},{9,1... | collective-permute-start | bytes 589832 | tf_op jit(solution)/shard_map/ppermute | solution.py:843
  35.5 8.5 %collective-permute-start.8 = (bf16[256,256]{1,0:T(8,128)(2,1)S(1)}, bf16[256,256]{1,0:T(8,128)(2,1)S(1)}, u32[]{:S(2)}, u32[]{:S(2)}) collective-permute-start(bf16[256,256]{1,0:T(8,128)(2,1)S(1)} %project_other.5.refs_4_), channel_id=1, source_target_pairs={{0,2},{2,0},{1,3},{3,1},{4,6},{6,4},{5,7},{7,5},{8,10},{10,8},{9,1... | collective-permute-start | bytes 393224 | tf_op jit(solution)/shard_map/ppermute | solution.py:843

commit v8 on v7

--- a/solution.py
+++ b/solution.py
@@ -349,6 +349,7 @@
 
 
 def local_first_kernel(
+    chips,
     running_ref,
     weight_ref,
     signal_ref,
@@ -387,7 +388,12 @@
         copy.start()
     read = read_ref[...].astype(F32)
     swapped = jnp.concatenate([read[:, HALF:], read[:, :HALF]], axis=1)
-    halves_ref[...] = jnp.where(lax.axis_index("band") == 0, read, swapped).astype(BF16)
+    read = jnp.where(lax.axis_index("band") == 0, read, swapped)
+    if chips == 4:
+        late = HALF + PART
+        turned = jnp.concatenate([read[:, :HALF], read[:, late:], read[:, HALF:late]], axis=1)
+        read = jnp.where(lax.axis_index("scan") == 2, turned, read)
+    halves_ref[...] = read.astype(BF16)
     upper = lax.axis_index("scan") == 2
     second_ref[...] = state_ref[pl.ds(pl.multiple_of(jnp.where(upper, 0, PART), PART), PART), :]
     prepared = (scores_ref, running_pieces_ref, decay_pieces_ref)
@@ -441,7 +447,7 @@
     if width % (10 * LANES):
         return (width // column_block(width), 0, 0), (width, 0, 0)
     tenth = width // 10
-    return (1, 2, 2), (tenth, 3 * tenth, 6 * tenth)
+    return (1, 2, 2), (tenth, 4 * tenth, 5 * tenth)
 
 
 def local_call_of(kernel, name, part, outs, resident, passed, after, scratch):
@@ -467,13 +473,13 @@
     )(*resident, *in_hbm(*passed), after)
 
 
-def local_first(values, state, constants, after):
+def local_first(chips, values, state, constants, after):
     running, signal = values[0], values[2]
     skip_gain, norm_gain, _ = constants
     tokens, width = signal.shape
     pieces_shape = jax.ShapeDtypeStruct((tokens, LANES), BF16)
     return local_call_of(
-        local_first_kernel,
+        functools.partial(local_first_kernel, chips),
         "local_first",
         0,
         [
@@ -563,17 +569,8 @@
         lanes_ref[...] = jnp.broadcast_to(lanes, lanes_ref.shape)
 
 
-def enter_kernel(
-    near_ref,
-    far_ref,
-    early_ref,
-    next_ref,
-    far_lanes_ref,
-    keep_ref,
-    got_ref,
-    lanes_ref,
-    mine_ref,
-    send_ref,
+def enter_first_kernel(
+    near_ref, far_ref, early_ref, far_lanes_ref, keep_ref, got_ref, lanes_ref, mine_ref, send_ref
 ):
     width = keep_ref.shape[1]
     chip = lax.axis_index("scan")
@@ -582,44 +579,61 @@
 
     @pl.when(chip == 0)
     def _():
-        share_enter(jnp.zeros((HALF, width), F32), 0, *refs)
+        share_enter(jnp.zeros((PART, width), F32), 0, 0, *refs)
 
     @pl.when(chip == 1)
     def _():
-        share_enter(near[...].astype(F32), 0, *refs)
-        share_enter(early_ref[...].astype(F32), PART, *refs)
+        share_enter(near[...].astype(F32), 0, 0, *refs)
 
     @pl.when(chip == 2)
     def _():
-        share_enter(next_ref[...].astype(F32), 0, *refs)
-        share_enter(far_lanes_ref[:1] * far[...].astype(F32) + near[...].astype(F32), PART, *refs)
+        enter = far_lanes_ref[:1] * far[...].astype(F32) + near[...].astype(F32)
+        share_enter(enter, PART, 0, *refs)
 
     @pl.when(chip == 3)
     def _():
-        share_enter(far_lanes_ref[:1] * early_ref[...].astype(F32) + far[...].astype(F32), 0, *refs)
-
-
-def enter_last_kernel(last_ref, keep_ref, got_ref, lanes_ref, old_mine, old_send, mine_ref, send_ref):
-    @pl.when(lax.axis_index("scan") == 3)
-    def _():
-        share_enter(
-            last_ref[...].astype(F32), PART, keep_ref, got_ref, lanes_ref, mine_ref, send_ref
-        )
-
-
-def share_enter(enter, first, keep_ref, got_ref, lanes_ref, mine_ref, send_ref):
+        enter = far_lanes_ref[:1] * early_ref[...].astype(F32) + far[...].astype(F32)
+        share_enter(enter, 0, 0, *refs)
+
+
+def enter_rest_kernel(
+    early_ref, next_ref, last_ref, keep_ref, got_ref, lanes_ref, old_ref, mine_ref, send_ref
+):
+    width = keep_ref.shape[1]
+    chip = lax.axis_index("scan")
+    refs = (keep_ref, got_ref, lanes_ref, mine_ref, send_ref)
+
+    @pl.when(chip == 0)
+    def _():
+        share_enter(jnp.zeros((PART, width), F32), PART, 0, *refs)
+
+    @pl.when(chip == 1)
+    def _():
+        share_enter(early_ref[...].astype(F32), PART, 0, *refs)
+
+    @pl.when(chip == 2)
+    def _():
+        share_enter(next_ref[...].astype(F32), 0, 0, *refs)
+
+    @pl.when(chip == 3)
+    def _():
+        share_enter(last_ref[...].astype(F32), PART, 0, *refs)
+
+
+def share_enter(enter, first, place, keep_ref, got_ref, lanes_ref, mine_ref, send_ref):
     width = keep_ref.shape[1]
     core = lax.axis_index("band")
     rows = slice(first, first + enter.shape[0])
+    sent = slice(place, place + enter.shape[0])
 
     @pl.when(core == 0)
     def _():
         mine_ref[rows, :] = enter.astype(BF16)
-        send_ref[rows, :] = (lanes_ref[:1] * enter + keep_ref[rows, :]).astype(BF16)
+        send_ref[sent, :] = (lanes_ref[:1] * enter + keep_ref[rows, :]).astype(BF16)
 
     @pl.when(core == 1)
     def _():
-        send_ref[rows, :] = enter.astype(BF16)
+        send_ref[sent, :] = enter.astype(BF16)
         mine_ref[rows, :] = (lanes_ref[:1] * enter + got_ref[rows, :width].astype(F32)).astype(BF16)
 
 
@@ -635,7 +649,7 @@
             lanes = decay_lanes(all_ref[source, :16, width:], heads_map)
             enter_ref[...] = lanes * enter_ref[...] + all_ref[source, :, :width].astype(F32)
 
-    share_enter(enter_ref[...], 0, keep_ref, got_ref, lanes_ref, mine_ref, send_ref)
+    share_enter(enter_ref[...], 0, 0, keep_ref, got_ref, lanes_ref, mine_ref, send_ref)
 
 
 def chip_state(keep, got, decay):
@@ -654,18 +668,21 @@
 def entering_state(chips, state, first, keep, got, local):
     width = keep.shape[1]
     half = jax.ShapeDtypeStruct((HALF, width), BF16)
+    part = jax.ShapeDtypeStruct((PART, width), BF16)
+    cores = [(0, 1), (1, 0)]
     if chips != 4:
         gathered = lax.all_gather(state, "scan", axis=0)
         second, lanes = local(0, first)
         local(1, second)
         local(2, second)
-        return local_call(
+        mine, give = local_call(
             gathered_kernel,
             "enter_state",
             [half, half],
             (gathered, keep, got, lanes),
             (pltpu.VMEM((HALF, width), F32),),
         )
+        return mine, lax.ppermute(give, "band", cores)
     near = lax.ppermute(first, "scan", [(0, 1), (1, 2)])
     second, lanes = local(0, first)
     far = lax.ppermute(second, "scan", [(0, 2), (2, 3)])
@@ -689,22 +706,26 @@
     last = lax.ppermute(middle, "scan", [(2, 3)])
     done = local(2, middle)
     mine, give = local_call(
-        enter_kernel,
-        "enter_state",
-        [half, half],
-        (near, far, early, following, far_lanes, keep, got, lanes),
+        enter_first_kernel,
+        "enter_first",
+        [half, part],
+        (near, far, early, far_lanes, keep, got, lanes),
         after=(done,),
     )
-    return local_call(
-        enter_last_kernel,
-        "enter_last",
-        [half, half],
-        (last, keep, got, lanes, mine, give),
-        aliases={4: 0, 5: 1},
-    )
-
-
-def gated_kernel(parts, mine_ref, other_ref, read_ref, gain_ref, *refs):
+    other = lax.ppermute(give, "band", cores)
+    mine, give = local_call(
+        enter_rest_kernel,
+        "enter_rest",
+        [half, part],
+        (early, following, last, keep, got, lanes, mine),
+        after=(other,),
+        aliases={6: 0},
+    )
+    return mine, other, lax.ppermute(give, "band", cores)
+
+
+def gated_kernel(states, parts, *refs):
+    state_refs, (read_ref, gain_ref, *refs) = refs[:states], refs[states:]
     bases, factors, weights = refs[:parts], refs[parts : 2 * parts], refs[2 * parts : 3 * parts]
     out_ref, square_ref, *first_refs = refs[3 * parts :]
     tokens, width = out_ref.shape
@@ -715,7 +736,7 @@
     for base_ref, factor_ref in zip(bases, factors):
         for start in range(0, base_ref.shape[1], block):
             lanes = slice(first, first + block)
-            carried = dot(read, jnp.concatenate([mine_ref[:, lanes], other_ref[:, lanes]], axis=0))
+            carried = dot(read, jnp.concatenate([ref[:, lanes] for ref in state_refs], axis=0))
             lanes = slice(start, start + block)
             gated = base_ref[:, lanes] + factor_ref[:, lanes] * carried
             for k in range(0, block, LANES):
@@ -733,18 +754,18 @@
         square_ref[row : row + 1, :] = squares[:, row * LANES : (row + 1) * LANES]
 
 
-def gated_part(mine, other, read_proj, gain, bases, factors, weights, first):
+def gated_part(states, read_proj, gain, bases, factors, weights, first):
     tokens = read_proj.shape[0]
-    width = mine.shape[1]
+    width = states[0].shape[1]
     return local_call(
-        functools.partial(gated_kernel, len(bases)),
+        functools.partial(gated_kernel, len(states), len(bases)),
         "gated_part",
         [
             jax.ShapeDtypeStruct((tokens, width), BF16),
             jax.ShapeDtypeStruct((tokens // LANES, LANES), F32),
         ]
         + [jax.ShapeDtypeStruct((tokens, first), BF16)] * (first > 0),
-        (mine, other, read_proj, gain, *bases, *factors, *weights),
+        (*states, read_proj, gain, *bases, *factors, *weights),
         flops=2 * tokens * width * STATE,
     )
 
@@ -888,7 +909,7 @@
             base, factor, matrix = local_rest(part, values, prepared, out_weight, after)
         else:
             base, factor, matrix, second, *kept, lanes = local_first(
-                (*values, write, read, decay, got), state, constants, after
+                chips, (*values, write, read, decay, got), state, constants, after
             )
             halves.append(kept[0])
             gains.append(kept[1])
@@ -898,11 +919,10 @@
         weights.append(matrix)
         return base if part else (second, lanes)
 
-    mine, give = entering_state(chips, state, first, keep, got, local)
-    other = lax.ppermute(give, "band", cores)
+    states = entering_state(chips, state, first, keep, got, local)
     ahead = SENDS[0] if direct(members, out_weight.shape[1] // members) else 0
     gated, squares, *ready = gated_part(
-        mine, other, halves[0], gains[0], bases, factors, weights, ahead
+        states, halves[0], gains[0], bases, factors, weights, ahead
     )
     return layer_columns(members, gated, squares, weights, ready)
 

time: 45.4 us -> 45.2 us (level)
    ppermute x1, waiting for transfers between devices: 0.45 us -> 1.02 us  [entering_state(): early = lax.ppermute(ahead, 'scan', [(1, 3), (0, 1)])]
    ppermute x1 -> x2, waiting for transfers between devices: 1.62 us -> 1.38 us  [the longest x1 1.38 us: entering_state(): return (mine, other, lax.ppermute(give, 'band', cores))]
  transfers between devices with their start and end apart: 12 -> 13, of which waited for: 8 -> 8; matrix products, arithmetic and copies ran while one was open for 0% -> 0% of each run, Pallas kernels for 31% -> 31%
where the time goes in v8:
time: 45.2 us; the launch traced here: 44.6 us
  Pallas kernels  18.6 us (41%)
  waiting for transfers between devices  13.9 us (31%)
  starting transfers between devices  11.2 us (25%)
  between operations  0.86 us (2%)
    pallas_call x3, Pallas kernels, local_call_of(): pl.pallas_call(kernel, name=name, out_shape=[jax.ShapeDtypeStruct((tokens...  7.07 us
    pallas_call x10, Pallas kernels, local_call(): pl.pallas_call(kernel, name=name, out_shape=outs, in_specs=[pl.BlockSpec(...  5.89 us
    ppermute x4, starting transfers between devices, layer_columns(): got = [lax.ppermute(part, 'tensor', swap) for part in parts]  4.33 us
    ppermute x4, waiting for transfers between devices, layer_columns(): got = [lax.ppermute(part, 'tensor', swap) for part in parts]  3.9 us
    pallas_call x4, Pallas kernels, finish(): pl.pallas_call(functools.partial(finish_kernel, first), name='finish', ou...  3.18 us
    ppermute x1, waiting for transfers between devices, entering_state(): last = lax.ppermute(middle, 'scan', [(2, 3)])  2.85 us
    ppermute x1, waiting for transfers between devices, entering_state(): far = lax.ppermute(second, 'scan', [(0, 2), (2, 3)])  2.48 us
    pallas_call x1, Pallas kernels, own_state(): pl.pallas_call(state_kernel, name='own_state', out_shape=[jax.ShapeDtypeS...  2.46 us
  transfers between devices with their start and end apart: 13, of which 8 were waited for; matrix products, arithmetic and copies ran while one was open for 0% of the time, Pallas kernels for 31%

profile of v8, /device:TPU:24, one launch (start us, length us, event | category | flops | bytes accessed | tf_op | source)
XLA Modules:
  0.0 44.6 jit_solution(17608354152527242447)
XLA Ops:
  0.7 2.5 %own_state.1 = (f32[40,256]{1,0:T(8,128)S(1)}, f32[40,256]{1,0:T(8,128)S(1)}, bf16[16,128]{1,0:T(8,128)(2,1)S(1)}, f32[64,2560]{1,0:T(8,128)S(1)}, bf16[64,2688]...) custom-call(s32[1]{0:T(128)S(6)} %copy.22.band_ref, ...), custom_call_target="tpu_custom_call" | custom-call | flops 335544320 | bytes 1310720 | tf_op jit(solution)/shard_map/own_state/pallas_call | solution.py:237
  3.2 1.6 %collective-permute-done.refs_1_.got_ref.refs_5_.refs_4_ = bf16[64,2688]{1,0:T(8,128)(2,1)S(1)} collective-permute-done((bf16[64,2688]{1,0:T(8,128)(2,1)S(1)}, bf16[64,2688]{1,0:T(8,128)(2,1)S(1)}, u32[]{:S(2)}, u32[]{:S(2)}) %collective-permute-start) | collective-permute-done | bytes 344096 | tf_op jit(solution)/shard_map/ppermute | solution.py:898
  4.8 0.2 chip_state.1
  5.1 0.7 %collective-permute-start.1 = (bf16[32,2688]{1,0:T(8,128)(2,1)S(1)}, bf16[32,2688]{1,0:T(8,128)(2,1)S(1)}, u32[]{:S(2)}, u32[]{:S(2)}) collective-permute-start(bf16[32,2688]{1,0:T(8,128)(2,1)S(1)} %get-tuple-element.46.after_ref), channel_id=1, source_target_pairs={{0,4},{4,8},{1,5},{5,9},{2,6},{6,10},{3,7},{7,11},{16,20},{20,24},... | collective-permute-start | bytes 516104 | tf_op jit(solution)/shard_map/ppermute | solution.py:686
  5.8 1.7 %local_first.1 = (f32[256,512]{1,0:T(8,128)S(1)}, f32[256,512]{1,0:T(8,128)S(1)}, bf16[256,2560]{1,0:T(8,128)(2,1)S(1)}, bf16[32,2688]{1,0:T(8,128)(2,1)S(1)}, b...) custom-call(f32[40,256]{1,0:T(8,128)S(1)} %get-tuple-element.47.runn, ...), custom_call_target="tpu_custom_call" | custom-call | flops 201326592 | bytes 1572864 | tf_op jit(solution)/shard_map/local_first/pallas_call | solution.py:458
  7.5 1.3 %collective-permute-start.4 = (bf16[32,2688]{1,0:T(8,128)(2,1)S(1)}, bf16[32,2688]{1,0:T(8,128)(2,1)S(1)}, u32[]{:S(2)}, u32[]{:S(2)}) collective-permute-start(bf16[32,2688]{1,0:T(8,128)(2,1)S(1)} %get-tuple-element.57.after_ref), channel_id=1, source_target_pairs={{0,8},{8,12},{1,9},{9,13},{2,10},{10,14},{3,11},{11,15},{16,24},{2... | collective-permute-start | bytes 516104 | tf_op jit(solution)/shard_map/ppermute | solution.py:688
  8.8 2.5 %local_rest.2 = (f32[256,1024]{1,0:T(8,128)S(1)}, f32[256,1024]{1,0:T(8,128)S(1)}, bf16[1024,2560]{1,0:T(8,128)(2,1)S(1)}) custom-call(f32[40,256]{1,0:T(8,128)S(1)} %get-tuple-element.47.running_ref, f32[40,256]{1,0:T(8,128)S(1)} %get-tuple-element.48.weight_ref, bf16[256,2560]{1,0:T(8,128)(2,1)S(1)} %get-tuple-element.49.signal_ref, ...), custom_call_target="tpu_custom_call" | custom-call | flops 402653184 | bytes 3145728 | tf_op jit(solution)/shard_map/local_rest/pallas_call | solution.py:458
  11.3 1.3 %collective-permute-start.2 = (bf16[32,2560]{1,0:T(8,128)(2,1)S(1)}, bf16[32,2560]{1,0:T(8,128)(2,1)S(1)}, u32[]{:S(2)}, u32[]{:S(2)}) collective-permute-start(bf16[32,2560]{1,0:T(8,128)(2,1)S(1)} %early_state.1.refs_3_), channel_id=1, source_target_pairs={{4,12},{0,4},{5,13},{1,5},{6,14},{2,6},{7,15},{3,7},{20,28},{16,20... | collective-permute-start | bytes 491528 | tf_op jit(solution)/shard_map/ppermute | solution.py:697
  12.6 0.7 %collective-permute-start.3 = (bf16[32,2560]{1,0:T(8,128)(2,1)S(1)}, bf16[32,2560]{1,0:T(8,128)(2,1)S(1)}, u32[]{:S(2)}, u32[]{:S(2)}) collective-permute-start(bf16[32,2560]{1,0:T(8,128)(2,1)S(1)} %early_state.1.refs_3_), channel_id=1, source_target_pairs={{4,8},{5,9},{6,10},{7,11},{20,24},{21,25},{22,26},{23,27}} | collective-permute-start | bytes 491528 | tf_op jit(solution)/shard_map/ppermute | solution.py:698
  13.3 2.5 %collective-permute-done.4.refs_2_.refs_1_ = bf16[32,2688]{1,0:T(8,128)(2,1)S(1)} collective-permute-done((bf16[32,2688]{1,0:T(8,128)(2,1)S(1)}, bf16[32,2688]{1,0:T(8,128)(2,1)S(1)}, u32[]{:S(2)}, u32[]{:S(2)}) %collective-permute-start.4) | collective-permute-done | bytes 172064 | tf_op jit(solution)/shard_map/ppermute | solution.py:688
  15.9 1.3 %collective-permute-start.5 = (bf16[32,2560]{1,0:T(8,128)(2,1)S(1)}, bf16[32,2560]{1,0:T(8,128)(2,1)S(1)}, u32[]{:S(2)}, u32[]{:S(2)}) collective-permute-start(bf16[32,2560]{1,0:T(8,128)(2,1)S(1)} %get-tuple-element.59.after_ref), channel_id=1, source_target_pairs={{8,12},{9,13},{10,14},{11,15},{24,28},{25,29},{26,30},{27,31}} | collective-permute-start | bytes 491528 | tf_op jit(solution)/shard_map/ppermute | solution.py:706
  17.2 2.9 %local_rest.3 = (f32[256,1024]{1,0:T(8,128)S(1)}, f32[256,1024]{1,0:T(8,128)S(1)}, bf16[1280,2560]{1,0:T(8,128)(2,1)S(1)}) custom-call(f32[40,256]{1,0:T(8,128)S(1)} %get-tuple-element.47.running_ref, f32[40,256]{1,0:T(8,128)S(1)} %get-tuple-element.48.weight_ref, bf16[256,2560]{1,0:T(8,128)(2,1)S(1)} %get-tuple-element.49.signal_ref, ...), custom_call_target="tpu_custom_call" | custom-call | flops 402653184 | bytes 3145728 | tf_op jit(solution)/shard_map/local_rest/pallas_call | solution.py:458
  20.1 1.0 %collective-permute-done.2.refs_2_.refs_0_ = bf16[32,2560]{1,0:T(8,128)(2,1)S(1)} collective-permute-done((bf16[32,2560]{1,0:T(8,128)(2,1)S(1)}, bf16[32,2560]{1,0:T(8,128)(2,1)S(1)}, u32[]{:S(2)}, u32[]{:S(2)}) %collective-permute-start.2) | collective-permute-done | bytes 163872 | tf_op jit(solution)/shard_map/ppermute | solution.py:697
  21.4 2.9 %collective-permute-done.5.refs_2_ = bf16[32,2560]{1,0:T(8,128)(2,1)S(1)} collective-permute-done((bf16[32,2560]{1,0:T(8,128)(2,1)S(1)}, bf16[32,2560]{1,0:T(8,128)(2,1)S(1)}, u32[]{:S(2)}, u32[]{:S(2)}) %collective-permute-start.5) | collective-permute-done | bytes 163872 | tf_op jit(solution)/shard_map/ppermute | solution.py:706
  24.4 1.4 %collective-permute-done.7.refs_2_ = bf16[32,2560]{1,0:T(8,128)(2,1)S(1)} collective-permute-done((bf16[32,2560]{1,0:T(8,128)(2,1)S(1)}, bf16[32,2560]{1,0:T(8,128)(2,1)S(1)}, u32[]{:S(2)}, u32[]{:S(2)}) %collective-permute-start.7) | collective-permute-done | bytes 163872 | tf_op jit(solution)/shard_map/ppermute | solution.py:724
  25.8 1.2 %gated_part.1 = (bf16[256,2560]{1,0:T(8,128)(2,1)S(1)}, f32[2,128]{1,0:T(2,128)S(1)}, bf16[256,256]{1,0:T(8,128)(2,1)S(1)}) custom-call(bf16[64,2560]{1,0:T(8,128)(2,1)S(1)} %get-tuple-element.65.refs_0_, bf16[32,2560]{1,0:T(8,128)(2,1)S(1)} %collective-permute-done.6.refs_7_.refs_1_, bf16[32,2560]{1,0:T(8,128)(2,1)S(1)} %collective-permute-done.7.refs_2_, ...), custom_call_target="tpu_custom_call" | custom-call | flops 167772160 | bytes 20524032 | tf_op jit(solution)/shard_map/gated_part/pallas_call | solution.py:112
  27.0 1.5 %collective-permute-start.12 = (bf16[256,256]{1,0:T(8,128)(2,1)S(1)}, bf16[256,256]{1,0:T(8,128)(2,1)S(1)}, u32[]{:S(2)}, u32[]{:S(2)}) collective-permute-start(bf16[256,256]{1,0:T(8,128)(2,1)S(1)} %get-tuple-element.78.refs_4_), channel_id=1, source_target_pairs={{0,2},{2,0},{1,3},{3,1},{4,6},{6,4},{5,7},{7,5},{8,10},{10,8},{9,1... | collective-permute-start | bytes 393224 | tf_op jit(solution)/shard_map/ppermute | solution.py:864
  28.5 0.8 %project_other.3.refs_4_ = bf16[256,384]{1,0:T(8,128)(2,1)S(1)} custom-call(bf16[256,2560]{1,0:T(8,128)(2,1)S(1)} %get-tuple-element.77.refs_0_, bf16[256,2560]{1,0:T(8,128)(2,1)S(1)} %get-tuple-element.73.refs_11_.refs_1_, bf16[1024,2560]{1,0:T(8,128)(2,1)S(1)} %get-tuple-element.74.refs_12_.refs_2_, ...), custom_call_target="tpu_custom_call" | custom-call | bytes 14614528 | tf_op jit(solution)/shard_map/project_other/pallas_call | solution.py:112
  29.4 0.6 %collective-permute-start.11 = (bf16[256,384]{1,0:T(8,128)(2,1)S(1)}, bf16[256,384]{1,0:T(8,128)(2,1)S(1)}, u32[]{:S(2)}, u32[]{:S(2)}) collective-permute-start(bf16[256,384]{1,0:T(8,128)(2,1)S(1)} %project_other.3.refs_4_), channel_id=1, source_target_pairs={{0,2},{2,0},{1,3},{3,1},{4,6},{6,4},{5,7},{7,5},{8,10},{10,8},{9,1... | collective-permute-start | bytes 589832 | tf_op jit(solution)/shard_map/ppermute | solution.py:864
  30.0 1.5 %collective-permute-start.8 = (f32[2,128]{1,0:T(2,128)S(1)}, f32[2,128]{1,0:T(2,128)S(1)}, u32[]{:S(2)}, u32[]{:S(2)}) collective-permute-start(f32[2,128]{1,0:T(2,128)S(1)} %get-tuple-element.76.squares_ref), channel_id=1, source_target_pairs={{0,2},{2,0},{1,3},{3,1},{4,6},{6,4},{5,7},{7,5},{8,10},{10,8},{9,1... | collective-permute-start | bytes 3080 | tf_op jit(solution)/shard_map/ppermute | solution.py:865
  31.4 0.8 %project_other.4.refs_4_ = bf16[256,384]{1,0:T(8,128)(2,1)S(1)} custom-call(bf16[256,2560]{1,0:T(8,128)(2,1)S(1)} %get-tuple-element.77.refs_0_, bf16[256,2560]{1,0:T(8,128)(2,1)S(1)} %get-tuple-element.73.refs_11_.refs_1_, bf16[1024,2560]{1,0:T(8,128)(2,1)S(1)} %get-tuple-element.74.refs_12_.refs_2_, ...), custom_call_target="tpu_custom_call" | custom-call | bytes 14614528 | tf_op jit(solution)/shard_map/project_other/pallas_call | solution.py:112
  32.3 0.5 %project_other.5.refs_4_ = bf16[256,256]{1,0:T(8,128)(2,1)S(1)} custom-call(bf16[256,2560]{1,0:T(8,128)(2,1)S(1)} %get-tuple-element.77.refs_0_, bf16[256,2560]{1,0:T(8,128)(2,1)S(1)} %get-tuple-element.73.refs_11_.refs_1_, bf16[1024,2560]{1,0:T(8,128)(2,1)S(1)} %get-tuple-element.74.refs_12_.refs_2_, ...), custom_call_target="tpu_custom_call" | custom-call | bytes 14548992 | tf_op jit(solution)/shard_map/project_other/pallas_call | solution.py:112
  32.8 0.6 %collective-permute-start.10 = (bf16[256,384]{1,0:T(8,128)(2,1)S(1)}, bf16[256,384]{1,0:T(8,128)(2,1)S(1)}, u32[]{:S(2)}, u32[]{:S(2)}) collective-permute-start(bf16[256,384]{1,0:T(8,128)(2,1)S(1)} %project_other.4.refs_4_), channel_id=1, source_target_pairs={{0,2},{2,0},{1,3},{3,1},{4,6},{6,4},{5,7},{7,5},{8,10},{10,8},{9,1... | collective-permute-start | bytes 589832 | tf_op jit(solution)/shard_map/ppermute | solution.py:864
  33.4 1.9 %project_own.1.own_ref = f32[256,1280]{1,0:T(8,128)S(1)} custom-call(bf16[256,2560]{1,0:T(8,128)(2,1)S(1)} %get-tuple-element.77.refs_0_, bf16[256,2560]{1,0:T(8,128)(2,1)S(1)} %get-tuple-element.73.refs_11_.refs_1_, bf16[1024,2560]{1,0:T(8,128)(2,1)S(1)} %get-tuple-element.74.refs_12_.refs_2_, bf16[1280,2560]{1,0:T(8,128)(2,1)S(1)} %get-tuple-element.75.refs_13_.refs_3_, ...), custom_call_target="tpu_custom_call" | custom-call | bytes 15728640 | tf_op jit(solution)/shard_map/project_own/pallas_call | solution.py:112
  35.3 1.6 %collective-permute-start.9 = (bf16[256,256]{1,0:T(8,128)(2,1)S(1)}, bf16[256,256]{1,0:T(8,128)(2,1)S(1)}, u32[]{:S(2)}, u32[]{:S(2)}) collective-permute-start(bf16[256,256]{1,0:T(8,128)(2,1)S(1)} %project_other.5.refs_4_), channel_id=1, source_target_pairs={{0,2},{2,0},{1,3},{3,1},{4,6},{6,4},{5,7},{7,5},{8,10},{10,8},{9,1... | collective-permute-start | bytes 393224 | tf_op jit(solution)/shard_map/ppermute | solution.py:864
  36.9 0.6 %collective-permute-done.8.other_squares_ref = f32[2,128]{1,0:T(2,128)S(1)} collective-permute-done((f32[2,128]{1,0:T(2,128)S(1)}, f32[2,128]{1,0:T(2,128)S(1)}, u32[]{:S(2)}, u32[]{:S(2)}) %collective-permute-start.8) | collective-permute-done | bytes 1056 | tf_op jit(solution)/shard_map/ppermute | solution.py:865
  37.5 0.8 %finish.4.refs_0_ = bf16[256,1280]{1,0:T(8,128)(2,1)} custom-call(f32[2,128]{1,0:T(2,128)S(1)} %get-tuple-element.76.squares_ref, f32[2,128]{1,0:T(2,128)S(1)} %collective-permute-done.8.other_squares_ref, f32[256,1280]{1,0:T(8,128)S(1)} %project_own.1.own_ref, bf16[256,256]{1,0:T(8,128)(2,1)S(1)} %collective-permute-done.12.got_ref), custom_call_target="tpu_custom_call" | custom-call | flops 2000000000 | tf_op jit(solution)/shard_map/finish/pallas_call | solution.py:825
  38.3 0.8 %finish.5.refs_0_ = bf16[256,1280]{1,0:T(8,128)(2,1)} custom-call(f32[2,128]{1,0:T(2,128)S(1)} %get-tuple-element.76.squares_ref, f32[2,128]{1,0:T(2,128)S(1)} %collective-permute-done.8.other_squares_ref, f32[256,1280]{1,0:T(8,128)S(1)} %project_own.1.own_ref, bf16[256,384]{1,0:T(8,128)(2,1)S(1)} %collective-permute-done.11.got_ref, ...), custom_call_target="tpu_custom_call", output_to_operand_aliasing={{}: (4, {})} | custom-call | flops 2000000000 | tf_op jit(solution)/shard_map/finish/pallas_call | solution.py:825
  39.1 2.6 %collective-permute-done.10.got_ref = bf16[256,384]{1,0:T(8,128)(2,1)S(1)} collective-permute-done((bf16[256,384]{1,0:T(8,128)(2,1)S(1)}, bf16[256,384]{1,0:T(8,128)(2,1)S(1)}, u32[]{:S(2)}, u32[]{:S(2)}) %collective-permute-start.10) | collective-permute-done | bytes 196640 | tf_op jit(solution)/shard_map/ppermute | solution.py:864
  41.7 0.8 %finish.6.refs_0_ = bf16[256,1280]{1,0:T(8,128)(2,1)} custom-call(f32[2,128]{1,0:T(2,128)S(1)} %get-tuple-element.76.squares_ref, f32[2,128]{1,0:T(2,128)S(1)} %collective-permute-done.8.other_squares_ref, f32[256,1280]{1,0:T(8,128)S(1)} %project_own.1.own_ref, bf16[256,384]{1,0:T(8,128)(2,1)S(1)} %collective-permute-done.10.got_ref, ...), custom_call_target="tpu_custom_call", output_to_operand_aliasing={{}: (4, {})} | custom-call | flops 2000000000 | tf_op jit(solution)/shard_map/finish/pallas_call | solution.py:825
  42.5 1.3 %collective-permute-done.9.got_ref = bf16[256,256]{1,0:T(8,128)(2,1)S(1)} collective-permute-done((bf16[256,256]{1,0:T(8,128)(2,1)S(1)}, bf16[256,256]{1,0:T(8,128)(2,1)S(1)}, u32[]{:S(2)}, u32[]{:S(2)}) %collective-permute-start.9) | collective-permute-done | bytes 131104 | tf_op jit(solution)/shard_map/ppermute | solution.py:864
  43.8 0.8 %finish.7 = bf16[256,1280]{1,0:T(8,128)(2,1)} custom-call(f32[2,128]{1,0:T(2,128)S(1)} %get-tuple-element.76.squares_ref, f32[2,128]{1,0:T(2,128)S(1)} %collective-permute-done.8.other_squares_ref, f32[256,1280]{1,0:T(8,128)S(1)} %project_own.1.own_ref, bf16[256,256]{1,0:T(8,128)(2,1)S(1)} %collective-permute-done.9.got_ref, ...), custom_call_target="tpu_custom_call", output_to_operand_aliasing={{}: (4, {})} | custom-call | flops 2000000000 | tf_op jit(solution)/shard_map/finish/pallas_call | solution.py:825
  (12 shorter events, 0.6 us)
Async XLA Ops:
  3.1 1.7 %collective-permute-start = (bf16[64,2688]{1,0:T(8,128)(2,1)S(1)}, bf16[64,2688]{1,0:T(8,128)(2,1)S(1)}, u32[]{:S(2)}, u32[]{:S(2)}) collective-permute-start(bf16[64,2688]{1,0:T(8,128)(2,1)S(1)} %get-tuple-element.43), channel_id=1, source_target_pairs={{0,1},{1,0},{2,3},{3,2},{4,5},{5,4},{6,7},{7,6},{8,9},{9,8},{10,11... | collective-permute-start | bytes 1032200 | tf_op jit(solution)/shard_map/ppermute | solution.py:898
  5.1 6.2 %collective-permute-start.1 = (bf16[32,2688]{1,0:T(8,128)(2,1)S(1)}, bf16[32,2688]{1,0:T(8,128)(2,1)S(1)}, u32[]{:S(2)}, u32[]{:S(2)}) collective-permute-start(bf16[32,2688]{1,0:T(8,128)(2,1)S(1)} %get-tuple-element.46.after_ref), channel_id=1, source_target_pairs={{0,4},{4,8},{1,5},{5,9},{2,6},{6,10},{3,7},{7,11},{16,20},{20,24},... | collective-permute-start | bytes 516104 | tf_op jit(solution)/shard_map/ppermute | solution.py:686
  7.5 8.3 %collective-permute-start.4 = (bf16[32,2688]{1,0:T(8,128)(2,1)S(1)}, bf16[32,2688]{1,0:T(8,128)(2,1)S(1)}, u32[]{:S(2)}, u32[]{:S(2)}) collective-permute-start(bf16[32,2688]{1,0:T(8,128)(2,1)S(1)} %get-tuple-element.57.after_ref), channel_id=1, source_target_pairs={{0,8},{8,12},{1,9},{9,13},{2,10},{10,14},{3,11},{11,15},{16,24},{2... | collective-permute-start | bytes 516104 | tf_op jit(solution)/shard_map/ppermute | solution.py:688
  11.3 9.8 %collective-permute-start.2 = (bf16[32,2560]{1,0:T(8,128)(2,1)S(1)}, bf16[32,2560]{1,0:T(8,128)(2,1)S(1)}, u32[]{:S(2)}, u32[]{:S(2)}) collective-permute-start(bf16[32,2560]{1,0:T(8,128)(2,1)S(1)} %early_state.1.refs_3_), channel_id=1, source_target_pairs={{4,12},{0,4},{5,13},{1,5},{6,14},{2,6},{7,15},{3,7},{20,28},{16,20... | collective-permute-start | bytes 491528 | tf_op jit(solution)/shard_map/ppermute | solution.py:697
  12.6 11.6 %collective-permute-start.3 = (bf16[32,2560]{1,0:T(8,128)(2,1)S(1)}, bf16[32,2560]{1,0:T(8,128)(2,1)S(1)}, u32[]{:S(2)}, u32[]{:S(2)}) collective-permute-start(bf16[32,2560]{1,0:T(8,128)(2,1)S(1)} %early_state.1.refs_3_), channel_id=1, source_target_pairs={{4,8},{5,9},{6,10},{7,11},{20,24},{21,25},{22,26},{23,27}} | collective-permute-start | bytes 491528 | tf_op jit(solution)/shard_map/ppermute | solution.py:698
  15.9 8.3 %collective-permute-start.5 = (bf16[32,2560]{1,0:T(8,128)(2,1)S(1)}, bf16[32,2560]{1,0:T(8,128)(2,1)S(1)}, u32[]{:S(2)}, u32[]{:S(2)}) collective-permute-start(bf16[32,2560]{1,0:T(8,128)(2,1)S(1)} %get-tuple-element.59.after_ref), channel_id=1, source_target_pairs={{8,12},{9,13},{10,14},{11,15},{24,28},{25,29},{26,30},{27,31}} | collective-permute-start | bytes 491528 | tf_op jit(solution)/shard_map/ppermute | solution.py:706
  21.3 2.9 %collective-permute-start.6 = (bf16[32,2560]{1,0:T(8,128)(2,1)S(1)}, bf16[32,2560]{1,0:T(8,128)(2,1)S(1)}, u32[]{:S(2)}, u32[]{:S(2)}) collective-permute-start(bf16[32,2560]{1,0:T(8,128)(2,1)S(1)} %get-tuple-element.64), channel_id=1, source_target_pairs={{0,1},{1,0},{2,3},{3,2},{4,5},{5,4},{6,7},{7,6},{8,9},{9,8},{10,11... | collective-permute-start | bytes 491528 | tf_op jit(solution)/shard_map/ppermute | solution.py:715
  24.3 1.5 %collective-permute-start.7 = (bf16[32,2560]{1,0:T(8,128)(2,1)S(1)}, bf16[32,2560]{1,0:T(8,128)(2,1)S(1)}, u32[]{:S(2)}, u32[]{:S(2)}) collective-permute-start(bf16[32,2560]{1,0:T(8,128)(2,1)S(1)} %get-tuple-element.66), channel_id=1, source_target_pairs={{0,1},{1,0},{2,3},{3,2},{4,5},{5,4},{6,7},{7,6},{8,9},{9,8},{10,11... | collective-permute-start | bytes 491528 | tf_op jit(solution)/shard_map/ppermute | solution.py:724
  27.0 10.5 %collective-permute-start.12 = (bf16[256,256]{1,0:T(8,128)(2,1)S(1)}, bf16[256,256]{1,0:T(8,128)(2,1)S(1)}, u32[]{:S(2)}, u32[]{:S(2)}) collective-permute-start(bf16[256,256]{1,0:T(8,128)(2,1)S(1)} %get-tuple-element.78.refs_4_), channel_id=1, source_target_pairs={{0,2},{2,0},{1,3},{3,1},{4,6},{6,4},{5,7},{7,5},{8,10},{10,8},{9,1... | collective-permute-start | bytes 393224 | tf_op jit(solution)/shard_map/ppermute | solution.py:864
  29.4 8.9 %collective-permute-start.11 = (bf16[256,384]{1,0:T(8,128)(2,1)S(1)}, bf16[256,384]{1,0:T(8,128)(2,1)S(1)}, u32[]{:S(2)}, u32[]{:S(2)}) collective-permute-start(bf16[256,384]{1,0:T(8,128)(2,1)S(1)} %project_other.3.refs_4_), channel_id=1, source_target_pairs={{0,2},{2,0},{1,3},{3,1},{4,6},{6,4},{5,7},{7,5},{8,10},{10,8},{9,1... | collective-permute-start | bytes 589832 | tf_op jit(solution)/shard_map/ppermute | solution.py:864
  30.0 7.5 %collective-permute-start.8 = (f32[2,128]{1,0:T(2,128)S(1)}, f32[2,128]{1,0:T(2,128)S(1)}, u32[]{:S(2)}, u32[]{:S(2)}) collective-permute-start(f32[2,128]{1,0:T(2,128)S(1)} %get-tuple-element.76.squares_ref), channel_id=1, source_target_pairs={{0,2},{2,0},{1,3},{3,1},{4,6},{6,4},{5,7},{7,5},{8,10},{10,8},{9,1... | collective-permute-start | bytes 3080 | tf_op jit(solution)/shard_map/ppermute | solution.py:865
  32.8 8.8 %collective-permute-start.10 = (bf16[256,384]{1,0:T(8,128)(2,1)S(1)}, bf16[256,384]{1,0:T(8,128)(2,1)S(1)}, u32[]{:S(2)}, u32[]{:S(2)}) collective-permute-start(bf16[256,384]{1,0:T(8,128)(2,1)S(1)} %project_other.4.refs_4_), channel_id=1, source_target_pairs={{0,2},{2,0},{1,3},{3,1},{4,6},{6,4},{5,7},{7,5},{8,10},{10,8},{9,1... | collective-permute-start | bytes 589832 | tf_op jit(solution)/shard_map/ppermute | solution.py:864
  35.3 8.5 %collective-permute-start.9 = (bf16[256,256]{1,0:T(8,128)(2,1)S(1)}, bf16[256,256]{1,0:T(8,128)(2,1)S(1)}, u32[]{:S(2)}, u32[]{:S(2)}) collective-permute-start(bf16[256,256]{1,0:T(8,128)(2,1)S(1)} %project_other.5.refs_4_), channel_id=1, source_target_pairs={{0,2},{2,0},{1,3},{3,1},{4,6},{6,4},{5,7},{7,5},{8,10},{10,8},{9,1... | collective-permute-start | bytes 393224 | tf_op jit(solution)/shard_map/ppermute | solution.py:864

commit v9 on v8

--- a/solution.py
+++ b/solution.py
@@ -534,9 +534,10 @@
     first_ref[...] = state_ref[pl.ds(pl.multiple_of(lower, PART), PART), :]
 
 
-def early_kernel(state_ref, near_ref, out_ref):
+def early_kernel(state_ref, near_ref, out_ref, lanes_ref):
     width = out_ref.shape[1]
     chip = lax.axis_index("scan")
+    heads_map = decay_map(width // HEAD_DIM, width)
 
     @pl.when(chip == 0)
     def _():
@@ -544,33 +545,44 @@
 
     @pl.when(chip == 1)
     def _():
-        lanes = decay_lanes(state_ref[:16, width:], decay_map(width // HEAD_DIM, width))
+        lanes = decay_lanes(state_ref[:16, width:], heads_map)
         out_ref[...] = (
             lanes * near_ref[:, :width].astype(F32) + state_ref[:PART, :width].astype(F32)
         ).astype(BF16)
 
-
-def middle_kernel(state_ref, near_ref, far_ref, out_ref, lanes_ref):
+    @pl.when(chip == 2)
+    def _():
+        for first, ref in ((0, near_ref), (8, state_ref)):
+            lanes = decay_lanes(ref[:16, width:], heads_map)
+            lanes_ref[first : first + 8, :] = jnp.broadcast_to(lanes, (8, width))
+
+
+def middle_kernel(state_ref, near_ref, far_ref, lanes_ref, out_ref, far_lanes_ref):
     width = out_ref.shape[1]
     chip = lax.axis_index("scan")
 
+    @pl.when(chip == 3)
+    def _():
+        lanes = decay_lanes(far_ref[:16, width:], decay_map(width // HEAD_DIM, width))
+        far_lanes_ref[...] = jnp.broadcast_to(lanes, far_lanes_ref.shape)
+
     @pl.when(chip == 2)
     def _():
-        heads_map = decay_map(width // HEAD_DIM, width)
-        lanes = decay_lanes(near_ref[:16, width:], heads_map)
-        lanes_ref[...] = jnp.broadcast_to(lanes, lanes_ref.shape)
-        entered = lanes * far_ref[:, :width].astype(F32) + near_ref[:, :width].astype(F32)
-        own = decay_lanes(state_ref[:16, width:], heads_map)
-        out_ref[...] = (own * entered + state_ref[PART:, :width].astype(F32)).astype(BF16)
-
-    @pl.when(chip == 3)
-    def _():
-        lanes = decay_lanes(far_ref[:16, width:], decay_map(width // HEAD_DIM, width))
-        lanes_ref[...] = jnp.broadcast_to(lanes, lanes_ref.shape)
+        entered = lanes_ref[:1] * far_ref[:, :width].astype(F32) + near_ref[:, :width].astype(F32)
+        out_ref[...] = (lanes_ref[8:9] * entered + state_ref[PART:, :width].astype(F32)).astype(BF16)
 
 
 def enter_first_kernel(
-    near_ref, far_ref, early_ref, far_lanes_ref, keep_ref, got_ref, lanes_ref, mine_ref, send_ref
+    near_ref,
+    far_ref,
+    early_ref,
+    near_lanes_ref,
+    far_lanes_ref,
+    keep_ref,
+    got_ref,
+    lanes_ref,
+    mine_ref,
+    send_ref,
 ):
     width = keep_ref.shape[1]
     chip = lax.axis_index("scan")
@@ -587,7 +599,7 @@
 
     @pl.when(chip == 2)
     def _():
-        enter = far_lanes_ref[:1] * far[...].astype(F32) + near[...].astype(F32)
+        enter = near_lanes_ref[:1] * far[...].astype(F32) + near[...].astype(F32)
         share_enter(enter, PART, 0, *refs)
 
     @pl.when(chip == 3)
@@ -687,10 +699,10 @@
     second, lanes = local(0, first)
     far = lax.ppermute(second, "scan", [(0, 2), (2, 3)])
     done = local(1, second)
-    (ahead,) = local_call(
+    ahead, near_lanes = local_call(
         early_kernel,
         "early_state",
-        [jax.ShapeDtypeStruct((PART, width), BF16)],
+        [part, jax.ShapeDtypeStruct((16, width), F32)],
         (state, near),
         after=(done,),
     )
@@ -699,8 +711,8 @@
     middle, far_lanes = local_call(
         middle_kernel,
         "middle_state",
-        [jax.ShapeDtypeStruct((PART, width), BF16), jax.ShapeDtypeStruct((8, width), F32)],
-        (state, near, far),
+        [part, jax.ShapeDtypeStruct((8, width), F32)],
+        (state, near, far, near_lanes),
         after=(ahead,),
     )
     last = lax.ppermute(middle, "scan", [(2, 3)])
@@ -709,7 +721,7 @@
         enter_first_kernel,
         "enter_first",
         [half, part],
-        (near, far, early, far_lanes, keep, got, lanes),
+        (near, far, early, near_lanes, far_lanes, keep, got, lanes),
         after=(done,),
     )
     other = lax.ppermute(give, "band", cores)

time: 45.2 us -> 45.2 us (level)
  no operation moved by 1% of the time
where the time goes in v9:
time: 45.2 us; the launch traced here: 44.6 us
  Pallas kernels  18.6 us (41%)
  waiting for transfers between devices  13.9 us (31%)
  starting transfers between devices  11.2 us (25%)
  between operations  0.86 us (2%)
    pallas_call x3, Pallas kernels, local_call_of(): pl.pallas_call(kernel, name=name, out_shape=[jax.ShapeDtypeStruct((tokens...  7.07 us
    pallas_call x10, Pallas kernels, local_call(): pl.pallas_call(kernel, name=name, out_shape=outs, in_specs=[pl.BlockSpec(...  5.9 us
    ppermute x4, starting transfers between devices, layer_columns(): got = [lax.ppermute(part, 'tensor', swap) for part in parts]  4.33 us
    ppermute x4, waiting for transfers between devices, layer_columns(): got = [lax.ppermute(part, 'tensor', swap) for part in parts]  3.9 us
    pallas_call x4, Pallas kernels, finish(): pl.pallas_call(functools.partial(finish_kernel, first), name='finish', ou...  3.18 us
    ppermute x1, waiting for transfers between devices, entering_state(): last = lax.ppermute(middle, 'scan', [(2, 3)])  2.84 us
    ppermute x1, waiting for transfers between devices, entering_state(): far = lax.ppermute(second, 'scan', [(0, 2), (2, 3)])  2.48 us
    pallas_call x1, Pallas kernels, own_state(): pl.pallas_call(state_kernel, name='own_state', out_shape=[jax.ShapeDtypeS...  2.46 us
  transfers between devices with their start and end apart: 13, of which 8 were waited for; matrix products, arithmetic and copies ran while one was open for 0% of the time, Pallas kernels for 31%

profile of v9, /device:TPU:24, one launch (start us, length us, event | category | flops | bytes accessed | tf_op | source)
XLA Modules:
  0.0 44.6 jit_solution(4772662845739722593)
XLA Ops:
  0.7 2.5 %own_state.1 = (f32[40,256]{1,0:T(8,128)S(1)}, f32[40,256]{1,0:T(8,128)S(1)}, bf16[16,128]{1,0:T(8,128)(2,1)S(1)}, f32[64,2560]{1,0:T(8,128)S(1)}, bf16[64,2688]...) custom-call(s32[1]{0:T(128)S(6)} %copy.22.band_ref, ...), custom_call_target="tpu_custom_call" | custom-call | flops 335544320 | bytes 1310720 | tf_op jit(solution)/shard_map/own_state/pallas_call | solution.py:237
  3.2 1.6 %collective-permute-done.refs_1_.got_ref.refs_6_.refs_4_ = bf16[64,2688]{1,0:T(8,128)(2,1)S(1)} collective-permute-done((bf16[64,2688]{1,0:T(8,128)(2,1)S(1)}, bf16[64,2688]{1,0:T(8,128)(2,1)S(1)}, u32[]{:S(2)}, u32[]{:S(2)}) %collective-permute-start) | collective-permute-done | bytes 344096 | tf_op jit(solution)/shard_map/ppermute | solution.py:910
  4.8 0.2 chip_state.1
  5.1 0.7 %collective-permute-start.1 = (bf16[32,2688]{1,0:T(8,128)(2,1)S(1)}, bf16[32,2688]{1,0:T(8,128)(2,1)S(1)}, u32[]{:S(2)}, u32[]{:S(2)}) collective-permute-start(bf16[32,2688]{1,0:T(8,128)(2,1)S(1)} %get-tuple-element.48.after_ref), channel_id=1, source_target_pairs={{0,4},{4,8},{1,5},{5,9},{2,6},{6,10},{3,7},{7,11},{16,20},{20,24},... | collective-permute-start | bytes 516104 | tf_op jit(solution)/shard_map/ppermute | solution.py:698
  5.8 1.7 %local_first.1 = (f32[256,512]{1,0:T(8,128)S(1)}, f32[256,512]{1,0:T(8,128)S(1)}, bf16[256,2560]{1,0:T(8,128)(2,1)S(1)}, bf16[32,2688]{1,0:T(8,128)(2,1)S(1)}, b...) custom-call(f32[40,256]{1,0:T(8,128)S(1)} %get-tuple-element.49.runn, ...), custom_call_target="tpu_custom_call" | custom-call | flops 201326592 | bytes 1572864 | tf_op jit(solution)/shard_map/local_first/pallas_call | solution.py:458
  7.5 1.3 %collective-permute-start.4 = (bf16[32,2688]{1,0:T(8,128)(2,1)S(1)}, bf16[32,2688]{1,0:T(8,128)(2,1)S(1)}, u32[]{:S(2)}, u32[]{:S(2)}) collective-permute-start(bf16[32,2688]{1,0:T(8,128)(2,1)S(1)} %get-tuple-element.59.after_ref), channel_id=1, source_target_pairs={{0,8},{8,12},{1,9},{9,13},{2,10},{10,14},{3,11},{11,15},{16,24},{2... | collective-permute-start | bytes 516104 | tf_op jit(solution)/shard_map/ppermute | solution.py:700
  8.8 2.5 %local_rest.2 = (f32[256,1024]{1,0:T(8,128)S(1)}, f32[256,1024]{1,0:T(8,128)S(1)}, bf16[1024,2560]{1,0:T(8,128)(2,1)S(1)}) custom-call(f32[40,256]{1,0:T(8,128)S(1)} %get-tuple-element.49.running_ref, f32[40,256]{1,0:T(8,128)S(1)} %get-tuple-element.50.weight_ref, bf16[256,2560]{1,0:T(8,128)(2,1)S(1)} %get-tuple-element.51.signal_ref, ...), custom_call_target="tpu_custom_call" | custom-call | flops 402653184 | bytes 3145728 | tf_op jit(solution)/shard_map/local_rest/pallas_call | solution.py:458
  11.3 1.3 %collective-permute-start.2 = (bf16[32,2560]{1,0:T(8,128)(2,1)S(1)}, bf16[32,2560]{1,0:T(8,128)(2,1)S(1)}, u32[]{:S(2)}, u32[]{:S(2)}) collective-permute-start(bf16[32,2560]{1,0:T(8,128)(2,1)S(1)} %get-tuple-element.61.refs_4_), channel_id=1, source_target_pairs={{4,12},{0,4},{5,13},{1,5},{6,14},{2,6},{7,15},{3,7},{20,28},{16,20... | collective-permute-start | bytes 491528 | tf_op jit(solution)/shard_map/ppermute | solution.py:709
  12.6 0.7 %collective-permute-start.3 = (bf16[32,2560]{1,0:T(8,128)(2,1)S(1)}, bf16[32,2560]{1,0:T(8,128)(2,1)S(1)}, u32[]{:S(2)}, u32[]{:S(2)}) collective-permute-start(bf16[32,2560]{1,0:T(8,128)(2,1)S(1)} %get-tuple-element.61.refs_4_), channel_id=1, source_target_pairs={{4,8},{5,9},{6,10},{7,11},{20,24},{21,25},{22,26},{23,27}} | collective-permute-start | bytes 491528 | tf_op jit(solution)/shard_map/ppermute | solution.py:710
  13.3 2.5 %collective-permute-done.4.refs_2_.refs_1_ = bf16[32,2688]{1,0:T(8,128)(2,1)S(1)} collective-permute-done((bf16[32,2688]{1,0:T(8,128)(2,1)S(1)}, bf16[32,2688]{1,0:T(8,128)(2,1)S(1)}, u32[]{:S(2)}, u32[]{:S(2)}) %collective-permute-start.4) | collective-permute-done | bytes 172064 | tf_op jit(solution)/shard_map/ppermute | solution.py:700
  16.0 1.3 %collective-permute-start.5 = (bf16[32,2560]{1,0:T(8,128)(2,1)S(1)}, bf16[32,2560]{1,0:T(8,128)(2,1)S(1)}, u32[]{:S(2)}, u32[]{:S(2)}) collective-permute-start(bf16[32,2560]{1,0:T(8,128)(2,1)S(1)} %get-tuple-element.63.after_ref), channel_id=1, source_target_pairs={{8,12},{9,13},{10,14},{11,15},{24,28},{25,29},{26,30},{27,31}} | collective-permute-start | bytes 491528 | tf_op jit(solution)/shard_map/ppermute | solution.py:718
  17.3 2.9 %local_rest.3 = (f32[256,1024]{1,0:T(8,128)S(1)}, f32[256,1024]{1,0:T(8,128)S(1)}, bf16[1280,2560]{1,0:T(8,128)(2,1)S(1)}) custom-call(f32[40,256]{1,0:T(8,128)S(1)} %get-tuple-element.49.running_ref, f32[40,256]{1,0:T(8,128)S(1)} %get-tuple-element.50.weight_ref, bf16[256,2560]{1,0:T(8,128)(2,1)S(1)} %get-tuple-element.51.signal_ref, ...), custom_call_target="tpu_custom_call" | custom-call | flops 402653184 | bytes 3145728 | tf_op jit(solution)/shard_map/local_rest/pallas_call | solution.py:458
  20.1 1.0 %collective-permute-done.2.refs_2_.refs_0_ = bf16[32,2560]{1,0:T(8,128)(2,1)S(1)} collective-permute-done((bf16[32,2560]{1,0:T(8,128)(2,1)S(1)}, bf16[32,2560]{1,0:T(8,128)(2,1)S(1)}, u32[]{:S(2)}, u32[]{:S(2)}) %collective-permute-start.2) | collective-permute-done | bytes 163872 | tf_op jit(solution)/shard_map/ppermute | solution.py:709
  21.4 2.8 %collective-permute-done.5.refs_2_ = bf16[32,2560]{1,0:T(8,128)(2,1)S(1)} collective-permute-done((bf16[32,2560]{1,0:T(8,128)(2,1)S(1)}, bf16[32,2560]{1,0:T(8,128)(2,1)S(1)}, u32[]{:S(2)}, u32[]{:S(2)}) %collective-permute-start.5) | collective-permute-done | bytes 163872 | tf_op jit(solution)/shard_map/ppermute | solution.py:718
  24.4 1.4 %collective-permute-done.7.refs_2_ = bf16[32,2560]{1,0:T(8,128)(2,1)S(1)} collective-permute-done((bf16[32,2560]{1,0:T(8,128)(2,1)S(1)}, bf16[32,2560]{1,0:T(8,128)(2,1)S(1)}, u32[]{:S(2)}, u32[]{:S(2)}) %collective-permute-start.7) | collective-permute-done | bytes 163872 | tf_op jit(solution)/shard_map/ppermute | solution.py:736
  25.8 1.2 %gated_part.1 = (bf16[256,2560]{1,0:T(8,128)(2,1)S(1)}, f32[2,128]{1,0:T(2,128)S(1)}, bf16[256,256]{1,0:T(8,128)(2,1)S(1)}) custom-call(bf16[64,2560]{1,0:T(8,128)(2,1)S(1)} %get-tuple-element.69.refs_0_, bf16[32,2560]{1,0:T(8,128)(2,1)S(1)} %collective-permute-done.6.refs_7_.refs_1_, bf16[32,2560]{1,0:T(8,128)(2,1)S(1)} %collective-permute-done.7.refs_2_, ...), custom_call_target="tpu_custom_call" | custom-call | flops 167772160 | bytes 20524032 | tf_op jit(solution)/shard_map/gated_part/pallas_call | solution.py:112
  27.0 1.5 %collective-permute-start.12 = (bf16[256,256]{1,0:T(8,128)(2,1)S(1)}, bf16[256,256]{1,0:T(8,128)(2,1)S(1)}, u32[]{:S(2)}, u32[]{:S(2)}) collective-permute-start(bf16[256,256]{1,0:T(8,128)(2,1)S(1)} %get-tuple-element.82.refs_4_), channel_id=1, source_target_pairs={{0,2},{2,0},{1,3},{3,1},{4,6},{6,4},{5,7},{7,5},{8,10},{10,8},{9,1... | collective-permute-start | bytes 393224 | tf_op jit(solution)/shard_map/ppermute | solution.py:876
  28.5 0.8 %project_other.3.refs_4_ = bf16[256,384]{1,0:T(8,128)(2,1)S(1)} custom-call(bf16[256,2560]{1,0:T(8,128)(2,1)S(1)} %get-tuple-element.81.refs_0_, bf16[256,2560]{1,0:T(8,128)(2,1)S(1)} %get-tuple-element.77.refs_11_.refs_1_, bf16[1024,2560]{1,0:T(8,128)(2,1)S(1)} %get-tuple-element.78.refs_12_.refs_2_, ...), custom_call_target="tpu_custom_call" | custom-call | bytes 14614528 | tf_op jit(solution)/shard_map/project_other/pallas_call | solution.py:112
  29.4 0.6 %collective-permute-start.11 = (bf16[256,384]{1,0:T(8,128)(2,1)S(1)}, bf16[256,384]{1,0:T(8,128)(2,1)S(1)}, u32[]{:S(2)}, u32[]{:S(2)}) collective-permute-start(bf16[256,384]{1,0:T(8,128)(2,1)S(1)} %project_other.3.refs_4_), channel_id=1, source_target_pairs={{0,2},{2,0},{1,3},{3,1},{4,6},{6,4},{5,7},{7,5},{8,10},{10,8},{9,1... | collective-permute-start | bytes 589832 | tf_op jit(solution)/shard_map/ppermute | solution.py:876
  30.0 1.5 %collective-permute-start.8 = (f32[2,128]{1,0:T(2,128)S(1)}, f32[2,128]{1,0:T(2,128)S(1)}, u32[]{:S(2)}, u32[]{:S(2)}) collective-permute-start(f32[2,128]{1,0:T(2,128)S(1)} %get-tuple-element.80.squares_ref), channel_id=1, source_target_pairs={{0,2},{2,0},{1,3},{3,1},{4,6},{6,4},{5,7},{7,5},{8,10},{10,8},{9,1... | collective-permute-start | bytes 3080 | tf_op jit(solution)/shard_map/ppermute | solution.py:877
  31.4 0.8 %project_other.4.refs_4_ = bf16[256,384]{1,0:T(8,128)(2,1)S(1)} custom-call(bf16[256,2560]{1,0:T(8,128)(2,1)S(1)} %get-tuple-element.81.refs_0_, bf16[256,2560]{1,0:T(8,128)(2,1)S(1)} %get-tuple-element.77.refs_11_.refs_1_, bf16[1024,2560]{1,0:T(8,128)(2,1)S(1)} %get-tuple-element.78.refs_12_.refs_2_, ...), custom_call_target="tpu_custom_call" | custom-call | bytes 14614528 | tf_op jit(solution)/shard_map/project_other/pallas_call | solution.py:112
  32.3 0.5 %project_other.5.refs_4_ = bf16[256,256]{1,0:T(8,128)(2,1)S(1)} custom-call(bf16[256,2560]{1,0:T(8,128)(2,1)S(1)} %get-tuple-element.81.refs_0_, bf16[256,2560]{1,0:T(8,128)(2,1)S(1)} %get-tuple-element.77.refs_11_.refs_1_, bf16[1024,2560]{1,0:T(8,128)(2,1)S(1)} %get-tuple-element.78.refs_12_.refs_2_, ...), custom_call_target="tpu_custom_call" | custom-call | bytes 14548992 | tf_op jit(solution)/shard_map/project_other/pallas_call | solution.py:112
  32.8 0.6 %collective-permute-start.10 = (bf16[256,384]{1,0:T(8,128)(2,1)S(1)}, bf16[256,384]{1,0:T(8,128)(2,1)S(1)}, u32[]{:S(2)}, u32[]{:S(2)}) collective-permute-start(bf16[256,384]{1,0:T(8,128)(2,1)S(1)} %project_other.4.refs_4_), channel_id=1, source_target_pairs={{0,2},{2,0},{1,3},{3,1},{4,6},{6,4},{5,7},{7,5},{8,10},{10,8},{9,1... | collective-permute-start | bytes 589832 | tf_op jit(solution)/shard_map/ppermute | solution.py:876
  33.4 1.9 %project_own.1.own_ref = f32[256,1280]{1,0:T(8,128)S(1)} custom-call(bf16[256,2560]{1,0:T(8,128)(2,1)S(1)} %get-tuple-element.81.refs_0_, bf16[256,2560]{1,0:T(8,128)(2,1)S(1)} %get-tuple-element.77.refs_11_.refs_1_, bf16[1024,2560]{1,0:T(8,128)(2,1)S(1)} %get-tuple-element.78.refs_12_.refs_2_, bf16[1280,2560]{1,0:T(8,128)(2,1)S(1)} %get-tuple-element.79.refs_13_.refs_3_, ...), custom_call_target="tpu_custom_call" | custom-call | bytes 15728640 | tf_op jit(solution)/shard_map/project_own/pallas_call | solution.py:112
  35.3 1.6 %collective-permute-start.9 = (bf16[256,256]{1,0:T(8,128)(2,1)S(1)}, bf16[256,256]{1,0:T(8,128)(2,1)S(1)}, u32[]{:S(2)}, u32[]{:S(2)}) collective-permute-start(bf16[256,256]{1,0:T(8,128)(2,1)S(1)} %project_other.5.refs_4_), channel_id=1, source_target_pairs={{0,2},{2,0},{1,3},{3,1},{4,6},{6,4},{5,7},{7,5},{8,10},{10,8},{9,1... | collective-permute-start | bytes 393224 | tf_op jit(solution)/shard_map/ppermute | solution.py:876
  36.9 0.6 %collective-permute-done.8.other_squares_ref = f32[2,128]{1,0:T(2,128)S(1)} collective-permute-done((f32[2,128]{1,0:T(2,128)S(1)}, f32[2,128]{1,0:T(2,128)S(1)}, u32[]{:S(2)}, u32[]{:S(2)}) %collective-permute-start.8) | collective-permute-done | bytes 1056 | tf_op jit(solution)/shard_map/ppermute | solution.py:877
  37.5 0.8 %finish.4.refs_0_ = bf16[256,1280]{1,0:T(8,128)(2,1)} custom-call(f32[2,128]{1,0:T(2,128)S(1)} %get-tuple-element.80.squares_ref, f32[2,128]{1,0:T(2,128)S(1)} %collective-permute-done.8.other_squares_ref, f32[256,1280]{1,0:T(8,128)S(1)} %project_own.1.own_ref, bf16[256,256]{1,0:T(8,128)(2,1)S(1)} %collective-permute-done.12.got_ref), custom_call_target="tpu_custom_call" | custom-call | flops 2000000000 | tf_op jit(solution)/shard_map/finish/pallas_call | solution.py:837
  38.3 0.8 %finish.5.refs_0_ = bf16[256,1280]{1,0:T(8,128)(2,1)} custom-call(f32[2,128]{1,0:T(2,128)S(1)} %get-tuple-element.80.squares_ref, f32[2,128]{1,0:T(2,128)S(1)} %collective-permute-done.8.other_squares_ref, f32[256,1280]{1,0:T(8,128)S(1)} %project_own.1.own_ref, bf16[256,384]{1,0:T(8,128)(2,1)S(1)} %collective-permute-done.11.got_ref, ...), custom_call_target="tpu_custom_call", output_to_operand_aliasing={{}: (4, {})} | custom-call | flops 2000000000 | tf_op jit(solution)/shard_map/finish/pallas_call | solution.py:837
  39.1 2.6 %collective-permute-done.10.got_ref = bf16[256,384]{1,0:T(8,128)(2,1)S(1)} collective-permute-done((bf16[256,384]{1,0:T(8,128)(2,1)S(1)}, bf16[256,384]{1,0:T(8,128)(2,1)S(1)}, u32[]{:S(2)}, u32[]{:S(2)}) %collective-permute-start.10) | collective-permute-done | bytes 196640 | tf_op jit(solution)/shard_map/ppermute | solution.py:876
  41.7 0.8 %finish.6.refs_0_ = bf16[256,1280]{1,0:T(8,128)(2,1)} custom-call(f32[2,128]{1,0:T(2,128)S(1)} %get-tuple-element.80.squares_ref, f32[2,128]{1,0:T(2,128)S(1)} %collective-permute-done.8.other_squares_ref, f32[256,1280]{1,0:T(8,128)S(1)} %project_own.1.own_ref, bf16[256,384]{1,0:T(8,128)(2,1)S(1)} %collective-permute-done.10.got_ref, ...), custom_call_target="tpu_custom_call", output_to_operand_aliasing={{}: (4, {})} | custom-call | flops 2000000000 | tf_op jit(solution)/shard_map/finish/pallas_call | solution.py:837
  42.5 1.3 %collective-permute-done.9.got_ref = bf16[256,256]{1,0:T(8,128)(2,1)S(1)} collective-permute-done((bf16[256,256]{1,0:T(8,128)(2,1)S(1)}, bf16[256,256]{1,0:T(8,128)(2,1)S(1)}, u32[]{:S(2)}, u32[]{:S(2)}) %collective-permute-start.9) | collective-permute-done | bytes 131104 | tf_op jit(solution)/shard_map/ppermute | solution.py:876
  43.8 0.8 %finish.7 = bf16[256,1280]{1,0:T(8,128)(2,1)} custom-call(f32[2,128]{1,0:T(2,128)S(1)} %get-tuple-element.80.squares_ref, f32[2,128]{1,0:T(2,128)S(1)} %collective-permute-done.8.other_squares_ref, f32[256,1280]{1,0:T(8,128)S(1)} %project_own.1.own_ref, bf16[256,256]{1,0:T(8,128)(2,1)S(1)} %collective-permute-done.9.got_ref, ...), custom_call_target="tpu_custom_call", output_to_operand_aliasing={{}: (4, {})} | custom-call | flops 2000000000 | tf_op jit(solution)/shard_map/finish/pallas_call | solution.py:837
  (12 shorter events, 0.6 us)
Async XLA Ops:
  3.1 1.7 %collective-permute-start = (bf16[64,2688]{1,0:T(8,128)(2,1)S(1)}, bf16[64,2688]{1,0:T(8,128)(2,1)S(1)}, u32[]{:S(2)}, u32[]{:S(2)}) collective-permute-start(bf16[64,2688]{1,0:T(8,128)(2,1)S(1)} %get-tuple-element.45), channel_id=1, source_target_pairs={{0,1},{1,0},{2,3},{3,2},{4,5},{5,4},{6,7},{7,6},{8,9},{9,8},{10,11... | collective-permute-start | bytes 1032200 | tf_op jit(solution)/shard_map/ppermute | solution.py:910
  5.1 6.2 %collective-permute-start.1 = (bf16[32,2688]{1,0:T(8,128)(2,1)S(1)}, bf16[32,2688]{1,0:T(8,128)(2,1)S(1)}, u32[]{:S(2)}, u32[]{:S(2)}) collective-permute-start(bf16[32,2688]{1,0:T(8,128)(2,1)S(1)} %get-tuple-element.48.after_ref), channel_id=1, source_target_pairs={{0,4},{4,8},{1,5},{5,9},{2,6},{6,10},{3,7},{7,11},{16,20},{20,24},... | collective-permute-start | bytes 516104 | tf_op jit(solution)/shard_map/ppermute | solution.py:698
  7.5 8.3 %collective-permute-start.4 = (bf16[32,2688]{1,0:T(8,128)(2,1)S(1)}, bf16[32,2688]{1,0:T(8,128)(2,1)S(1)}, u32[]{:S(2)}, u32[]{:S(2)}) collective-permute-start(bf16[32,2688]{1,0:T(8,128)(2,1)S(1)} %get-tuple-element.59.after_ref), channel_id=1, source_target_pairs={{0,8},{8,12},{1,9},{9,13},{2,10},{10,14},{3,11},{11,15},{16,24},{2... | collective-permute-start | bytes 516104 | tf_op jit(solution)/shard_map/ppermute | solution.py:700
  11.3 9.8 %collective-permute-start.2 = (bf16[32,2560]{1,0:T(8,128)(2,1)S(1)}, bf16[32,2560]{1,0:T(8,128)(2,1)S(1)}, u32[]{:S(2)}, u32[]{:S(2)}) collective-permute-start(bf16[32,2560]{1,0:T(8,128)(2,1)S(1)} %get-tuple-element.61.refs_4_), channel_id=1, source_target_pairs={{4,12},{0,4},{5,13},{1,5},{6,14},{2,6},{7,15},{3,7},{20,28},{16,20... | collective-permute-start | bytes 491528 | tf_op jit(solution)/shard_map/ppermute | solution.py:709
  12.6 11.6 %collective-permute-start.3 = (bf16[32,2560]{1,0:T(8,128)(2,1)S(1)}, bf16[32,2560]{1,0:T(8,128)(2,1)S(1)}, u32[]{:S(2)}, u32[]{:S(2)}) collective-permute-start(bf16[32,2560]{1,0:T(8,128)(2,1)S(1)} %get-tuple-element.61.refs_4_), channel_id=1, source_target_pairs={{4,8},{5,9},{6,10},{7,11},{20,24},{21,25},{22,26},{23,27}} | collective-permute-start | bytes 491528 | tf_op jit(solution)/shard_map/ppermute | solution.py:710
  16.0 8.3 %collective-permute-start.5 = (bf16[32,2560]{1,0:T(8,128)(2,1)S(1)}, bf16[32,2560]{1,0:T(8,128)(2,1)S(1)}, u32[]{:S(2)}, u32[]{:S(2)}) collective-permute-start(bf16[32,2560]{1,0:T(8,128)(2,1)S(1)} %get-tuple-element.63.after_ref), channel_id=1, source_target_pairs={{8,12},{9,13},{10,14},{11,15},{24,28},{25,29},{26,30},{27,31}} | collective-permute-start | bytes 491528 | tf_op jit(solution)/shard_map/ppermute | solution.py:718
  21.3 2.9 %collective-permute-start.6 = (bf16[32,2560]{1,0:T(8,128)(2,1)S(1)}, bf16[32,2560]{1,0:T(8,128)(2,1)S(1)}, u32[]{:S(2)}, u32[]{:S(2)}) collective-permute-start(bf16[32,2560]{1,0:T(8,128)(2,1)S(1)} %get-tuple-element.68), channel_id=1, source_target_pairs={{0,1},{1,0},{2,3},{3,2},{4,5},{5,4},{6,7},{7,6},{8,9},{9,8},{10,11... | collective-permute-start | bytes 491528 | tf_op jit(solution)/shard_map/ppermute | solution.py:727
  24.3 1.5 %collective-permute-start.7 = (bf16[32,2560]{1,0:T(8,128)(2,1)S(1)}, bf16[32,2560]{1,0:T(8,128)(2,1)S(1)}, u32[]{:S(2)}, u32[]{:S(2)}) collective-permute-start(bf16[32,2560]{1,0:T(8,128)(2,1)S(1)} %get-tuple-element.70), channel_id=1, source_target_pairs={{0,1},{1,0},{2,3},{3,2},{4,5},{5,4},{6,7},{7,6},{8,9},{9,8},{10,11... | collective-permute-start | bytes 491528 | tf_op jit(solution)/shard_map/ppermute | solution.py:736
  27.0 10.5 %collective-permute-start.12 = (bf16[256,256]{1,0:T(8,128)(2,1)S(1)}, bf16[256,256]{1,0:T(8,128)(2,1)S(1)}, u32[]{:S(2)}, u32[]{:S(2)}) collective-permute-start(bf16[256,256]{1,0:T(8,128)(2,1)S(1)} %get-tuple-element.82.refs_4_), channel_id=1, source_target_pairs={{0,2},{2,0},{1,3},{3,1},{4,6},{6,4},{5,7},{7,5},{8,10},{10,8},{9,1... | collective-permute-start | bytes 393224 | tf_op jit(solution)/shard_map/ppermute | solution.py:876
  29.4 8.9 %collective-permute-start.11 = (bf16[256,384]{1,0:T(8,128)(2,1)S(1)}, bf16[256,384]{1,0:T(8,128)(2,1)S(1)}, u32[]{:S(2)}, u32[]{:S(2)}) collective-permute-start(bf16[256,384]{1,0:T(8,128)(2,1)S(1)} %project_other.3.refs_4_), channel_id=1, source_target_pairs={{0,2},{2,0},{1,3},{3,1},{4,6},{6,4},{5,7},{7,5},{8,10},{10,8},{9,1... | collective-permute-start | bytes 589832 | tf_op jit(solution)/shard_map/ppermute | solution.py:876
  30.0 7.5 %collective-permute-start.8 = (f32[2,128]{1,0:T(2,128)S(1)}, f32[2,128]{1,0:T(2,128)S(1)}, u32[]{:S(2)}, u32[]{:S(2)}) collective-permute-start(f32[2,128]{1,0:T(2,128)S(1)} %get-tuple-element.80.squares_ref), channel_id=1, source_target_pairs={{0,2},{2,0},{1,3},{3,1},{4,6},{6,4},{5,7},{7,5},{8,10},{10,8},{9,1... | collective-permute-start | bytes 3080 | tf_op jit(solution)/shard_map/ppermute | solution.py:877
  32.8 8.8 %collective-permute-start.10 = (bf16[256,384]{1,0:T(8,128)(2,1)S(1)}, bf16[256,384]{1,0:T(8,128)(2,1)S(1)}, u32[]{:S(2)}, u32[]{:S(2)}) collective-permute-start(bf16[256,384]{1,0:T(8,128)(2,1)S(1)} %project_other.4.refs_4_), channel_id=1, source_target_pairs={{0,2},{2,0},{1,3},{3,1},{4,6},{6,4},{5,7},{7,5},{8,10},{10,8},{9,1... | collective-permute-start | bytes 589832 | tf_op jit(solution)/shard_map/ppermute | solution.py:876
  35.3 8.5 %collective-permute-start.9 = (bf16[256,256]{1,0:T(8,128)(2,1)S(1)}, bf16[256,256]{1,0:T(8,128)(2,1)S(1)}, u32[]{:S(2)}, u32[]{:S(2)}) collective-permute-start(bf16[256,256]{1,0:T(8,128)(2,1)S(1)} %project_other.5.refs_4_), channel_id=1, source_target_pairs={{0,2},{2,0},{1,3},{3,1},{4,6},{6,4},{5,7},{7,5},{8,10},{10,8},{9,1... | collective-permute-start | bytes 393224 | tf_op jit(solution)/shard_map/ppermute | solution.py:876

commit v10 on v8

--- a/solution.py
+++ b/solution.py
@@ -770,7 +770,7 @@
     )
 
 
-SENDS = (256, 384, 384, 256)
+SENDS = (256, 512, 384, 128)
 FINISH_FLOPS = 2 * 10**9
 
 

time: 45.2 us -> 45.2 us (level)
    ppermute x1, waiting for transfers between devices: 0.64 us -> 2.13 us  [layer_columns(): other_squares = lax.ppermute(squares, 'tensor', swap)]
    ppermute x4, waiting for transfers between devices: 3.9 us -> 2.54 us  [layer_columns(): got = [lax.ppermute(part, 'tensor', swap) for part in parts]]
  transfers between devices with their start and end apart: 13 -> 13, of which waited for: 8 -> 7; matrix products, arithmetic and copies ran while one was open for 0% -> 0% of each run, Pallas kernels for 31% -> 31%
where the time goes in v10:
time: 45.2 us; the launch traced here: 44.7 us
  Pallas kernels  18.5 us (41%)
  waiting for transfers between devices  14.1 us (31%)
  starting transfers between devices  11.2 us (25%)
  between operations  0.87 us (2%)
    pallas_call x3, Pallas kernels, local_call_of(): pl.pallas_call(kernel, name=name, out_shape=[jax.ShapeDtypeStruct((tokens...  7.07 us
    pallas_call x10, Pallas kernels, local_call(): pl.pallas_call(kernel, name=name, out_shape=outs, in_specs=[pl.BlockSpec(...  5.83 us
    ppermute x4, starting transfers between devices, layer_columns(): got = [lax.ppermute(part, 'tensor', swap) for part in parts]  4.32 us
    pallas_call x4, Pallas kernels, finish(): pl.pallas_call(functools.partial(finish_kernel, first), name='finish', ou...  3.18 us
    ppermute x1, waiting for transfers between devices, entering_state(): last = lax.ppermute(middle, 'scan', [(2, 3)])  2.85 us
    ppermute x4, waiting for transfers between devices, layer_columns(): got = [lax.ppermute(part, 'tensor', swap) for part in parts]  2.54 us
    ppermute x1, waiting for transfers between devices, entering_state(): far = lax.ppermute(second, 'scan', [(0, 2), (2, 3)])  2.48 us
    pallas_call x1, Pallas kernels, own_state(): pl.pallas_call(state_kernel, name='own_state', out_shape=[jax.ShapeDtypeS...  2.46 us
  transfers between devices with their start and end apart: 13, of which 7 were waited for; matrix products, arithmetic and copies ran while one was open for 0% of the time, Pallas kernels for 31%

profile of v10, /device:TPU:24, one launch (start us, length us, event | category | flops | bytes accessed | tf_op | source)
XLA Modules:
  0.0 44.7 jit_solution(9527459646089061262)
XLA Ops:
  0.7 2.5 %own_state.1 = (f32[40,256]{1,0:T(8,128)S(1)}, f32[40,256]{1,0:T(8,128)S(1)}, bf16[16,128]{1,0:T(8,128)(2,1)S(1)}, f32[64,2560]{1,0:T(8,128)S(1)}, bf16[64,2688]...) custom-call(s32[1]{0:T(128)S(6)} %copy.22.band_ref, ...), custom_call_target="tpu_custom_call" | custom-call | flops 335544320 | bytes 1310720 | tf_op jit(solution)/shard_map/own_state/pallas_call | solution.py:237
  3.2 1.6 %collective-permute-done.refs_1_.got_ref.refs_5_.refs_4_ = bf16[64,2688]{1,0:T(8,128)(2,1)S(1)} collective-permute-done((bf16[64,2688]{1,0:T(8,128)(2,1)S(1)}, bf16[64,2688]{1,0:T(8,128)(2,1)S(1)}, u32[]{:S(2)}, u32[]{:S(2)}) %collective-permute-start) | collective-permute-done | bytes 344096 | tf_op jit(solution)/shard_map/ppermute | solution.py:898
  4.8 0.2 chip_state.1
  5.1 0.7 %collective-permute-start.1 = (bf16[32,2688]{1,0:T(8,128)(2,1)S(1)}, bf16[32,2688]{1,0:T(8,128)(2,1)S(1)}, u32[]{:S(2)}, u32[]{:S(2)}) collective-permute-start(bf16[32,2688]{1,0:T(8,128)(2,1)S(1)} %get-tuple-element.46.after_ref), channel_id=1, source_target_pairs={{0,4},{4,8},{1,5},{5,9},{2,6},{6,10},{3,7},{7,11},{16,20},{20,24},... | collective-permute-start | bytes 516104 | tf_op jit(solution)/shard_map/ppermute | solution.py:686
  5.8 1.7 %local_first.1 = (f32[256,512]{1,0:T(8,128)S(1)}, f32[256,512]{1,0:T(8,128)S(1)}, bf16[256,2560]{1,0:T(8,128)(2,1)S(1)}, bf16[32,2688]{1,0:T(8,128)(2,1)S(1)}, b...) custom-call(f32[40,256]{1,0:T(8,128)S(1)} %get-tuple-element.47.runn, ...), custom_call_target="tpu_custom_call" | custom-call | flops 201326592 | bytes 1572864 | tf_op jit(solution)/shard_map/local_first/pallas_call | solution.py:458
  7.5 1.3 %collective-permute-start.4 = (bf16[32,2688]{1,0:T(8,128)(2,1)S(1)}, bf16[32,2688]{1,0:T(8,128)(2,1)S(1)}, u32[]{:S(2)}, u32[]{:S(2)}) collective-permute-start(bf16[32,2688]{1,0:T(8,128)(2,1)S(1)} %get-tuple-element.57.after_ref), channel_id=1, source_target_pairs={{0,8},{8,12},{1,9},{9,13},{2,10},{10,14},{3,11},{11,15},{16,24},{2... | collective-permute-start | bytes 516104 | tf_op jit(solution)/shard_map/ppermute | solution.py:688
  8.8 2.5 %local_rest.2 = (f32[256,1024]{1,0:T(8,128)S(1)}, f32[256,1024]{1,0:T(8,128)S(1)}, bf16[1024,2560]{1,0:T(8,128)(2,1)S(1)}) custom-call(f32[40,256]{1,0:T(8,128)S(1)} %get-tuple-element.47.running_ref, f32[40,256]{1,0:T(8,128)S(1)} %get-tuple-element.48.weight_ref, bf16[256,2560]{1,0:T(8,128)(2,1)S(1)} %get-tuple-element.49.signal_ref, ...), custom_call_target="tpu_custom_call" | custom-call | flops 402653184 | bytes 3145728 | tf_op jit(solution)/shard_map/local_rest/pallas_call | solution.py:458
  11.3 1.3 %collective-permute-start.2 = (bf16[32,2560]{1,0:T(8,128)(2,1)S(1)}, bf16[32,2560]{1,0:T(8,128)(2,1)S(1)}, u32[]{:S(2)}, u32[]{:S(2)}) collective-permute-start(bf16[32,2560]{1,0:T(8,128)(2,1)S(1)} %early_state.1.refs_3_), channel_id=1, source_target_pairs={{4,12},{0,4},{5,13},{1,5},{6,14},{2,6},{7,15},{3,7},{20,28},{16,20... | collective-permute-start | bytes 491528 | tf_op jit(solution)/shard_map/ppermute | solution.py:697
  12.6 0.7 %collective-permute-start.3 = (bf16[32,2560]{1,0:T(8,128)(2,1)S(1)}, bf16[32,2560]{1,0:T(8,128)(2,1)S(1)}, u32[]{:S(2)}, u32[]{:S(2)}) collective-permute-start(bf16[32,2560]{1,0:T(8,128)(2,1)S(1)} %early_state.1.refs_3_), channel_id=1, source_target_pairs={{4,8},{5,9},{6,10},{7,11},{20,24},{21,25},{22,26},{23,27}} | collective-permute-start | bytes 491528 | tf_op jit(solution)/shard_map/ppermute | solution.py:698
  13.3 2.5 %collective-permute-done.4.refs_2_.refs_1_ = bf16[32,2688]{1,0:T(8,128)(2,1)S(1)} collective-permute-done((bf16[32,2688]{1,0:T(8,128)(2,1)S(1)}, bf16[32,2688]{1,0:T(8,128)(2,1)S(1)}, u32[]{:S(2)}, u32[]{:S(2)}) %collective-permute-start.4) | collective-permute-done | bytes 172064 | tf_op jit(solution)/shard_map/ppermute | solution.py:688
  15.8 0.2 middle_state.1
  16.0 1.3 %collective-permute-start.5 = (bf16[32,2560]{1,0:T(8,128)(2,1)S(1)}, bf16[32,2560]{1,0:T(8,128)(2,1)S(1)}, u32[]{:S(2)}, u32[]{:S(2)}) collective-permute-start(bf16[32,2560]{1,0:T(8,128)(2,1)S(1)} %get-tuple-element.59.after_ref), channel_id=1, source_target_pairs={{8,12},{9,13},{10,14},{11,15},{24,28},{25,29},{26,30},{27,31}} | collective-permute-start | bytes 491528 | tf_op jit(solution)/shard_map/ppermute | solution.py:706
  17.3 2.9 %local_rest.3 = (f32[256,1024]{1,0:T(8,128)S(1)}, f32[256,1024]{1,0:T(8,128)S(1)}, bf16[1280,2560]{1,0:T(8,128)(2,1)S(1)}) custom-call(f32[40,256]{1,0:T(8,128)S(1)} %get-tuple-element.47.running_ref, f32[40,256]{1,0:T(8,128)S(1)} %get-tuple-element.48.weight_ref, bf16[256,2560]{1,0:T(8,128)(2,1)S(1)} %get-tuple-element.49.signal_ref, ...), custom_call_target="tpu_custom_call" | custom-call | flops 402653184 | bytes 3145728 | tf_op jit(solution)/shard_map/local_rest/pallas_call | solution.py:458
  20.1 1.0 %collective-permute-done.2.refs_2_.refs_0_ = bf16[32,2560]{1,0:T(8,128)(2,1)S(1)} collective-permute-done((bf16[32,2560]{1,0:T(8,128)(2,1)S(1)}, bf16[32,2560]{1,0:T(8,128)(2,1)S(1)}, u32[]{:S(2)}, u32[]{:S(2)}) %collective-permute-start.2) | collective-permute-done | bytes 163872 | tf_op jit(solution)/shard_map/ppermute | solution.py:697
  21.4 2.9 %collective-permute-done.5.refs_2_ = bf16[32,2560]{1,0:T(8,128)(2,1)S(1)} collective-permute-done((bf16[32,2560]{1,0:T(8,128)(2,1)S(1)}, bf16[32,2560]{1,0:T(8,128)(2,1)S(1)}, u32[]{:S(2)}, u32[]{:S(2)}) %collective-permute-start.5) | collective-permute-done | bytes 163872 | tf_op jit(solution)/shard_map/ppermute | solution.py:706
  24.4 1.4 %collective-permute-done.7.refs_2_ = bf16[32,2560]{1,0:T(8,128)(2,1)S(1)} collective-permute-done((bf16[32,2560]{1,0:T(8,128)(2,1)S(1)}, bf16[32,2560]{1,0:T(8,128)(2,1)S(1)}, u32[]{:S(2)}, u32[]{:S(2)}) %collective-permute-start.7) | collective-permute-done | bytes 163872 | tf_op jit(solution)/shard_map/ppermute | solution.py:724
  25.8 1.2 %gated_part.1 = (bf16[256,2560]{1,0:T(8,128)(2,1)S(1)}, f32[2,128]{1,0:T(2,128)S(1)}, bf16[256,256]{1,0:T(8,128)(2,1)S(1)}) custom-call(bf16[64,2560]{1,0:T(8,128)(2,1)S(1)} %get-tuple-element.65.refs_0_, bf16[32,2560]{1,0:T(8,128)(2,1)S(1)} %collective-permute-done.6.refs_7_.refs_1_, bf16[32,2560]{1,0:T(8,128)(2,1)S(1)} %collective-permute-done.7.refs_2_, ...), custom_call_target="tpu_custom_call" | custom-call | flops 167772160 | bytes 20524032 | tf_op jit(solution)/shard_map/gated_part/pallas_call | solution.py:112
  26.9 1.5 %collective-permute-start.12 = (bf16[256,256]{1,0:T(8,128)(2,1)S(1)}, bf16[256,256]{1,0:T(8,128)(2,1)S(1)}, u32[]{:S(2)}, u32[]{:S(2)}) collective-permute-start(bf16[256,256]{1,0:T(8,128)(2,1)S(1)} %get-tuple-element.78.refs_4_), channel_id=1, source_target_pairs={{0,2},{2,0},{1,3},{3,1},{4,6},{6,4},{5,7},{7,5},{8,10},{10,8},{9,1... | collective-permute-start | bytes 393224 | tf_op jit(solution)/shard_map/ppermute | solution.py:864
  28.4 0.8 %project_other.3.refs_4_ = bf16[256,512]{1,0:T(8,128)(2,1)S(1)} custom-call(bf16[256,2560]{1,0:T(8,128)(2,1)S(1)} %get-tuple-element.77.refs_0_, bf16[256,2560]{1,0:T(8,128)(2,1)S(1)} %get-tuple-element.73.refs_11_.refs_1_, bf16[1024,2560]{1,0:T(8,128)(2,1)S(1)} %get-tuple-element.74.refs_12_.refs_2_, ...), custom_call_target="tpu_custom_call" | custom-call | bytes 14680064 | tf_op jit(solution)/shard_map/project_other/pallas_call | solution.py:112
  29.3 0.6 %collective-permute-start.11 = (bf16[256,512]{1,0:T(8,128)(2,1)S(1)}, bf16[256,512]{1,0:T(8,128)(2,1)S(1)}, u32[]{:S(2)}, u32[]{:S(2)}) collective-permute-start(bf16[256,512]{1,0:T(8,128)(2,1)S(1)} %project_other.3.refs_4_), channel_id=1, source_target_pairs={{0,2},{2,0},{1,3},{3,1},{4,6},{6,4},{5,7},{7,5},{8,10},{10,8},{9,1... | collective-permute-start | bytes 786440 | tf_op jit(solution)/shard_map/ppermute | solution.py:864
  29.9 1.4 %collective-permute-start.8 = (f32[2,128]{1,0:T(2,128)S(1)}, f32[2,128]{1,0:T(2,128)S(1)}, u32[]{:S(2)}, u32[]{:S(2)}) collective-permute-start(f32[2,128]{1,0:T(2,128)S(1)} %get-tuple-element.76.squares_ref), channel_id=1, source_target_pairs={{0,2},{2,0},{1,3},{3,1},{4,6},{6,4},{5,7},{7,5},{8,10},{10,8},{9,1... | collective-permute-start | bytes 3080 | tf_op jit(solution)/shard_map/ppermute | solution.py:865
  31.4 0.8 %project_other.4.refs_4_ = bf16[256,384]{1,0:T(8,128)(2,1)S(1)} custom-call(bf16[256,2560]{1,0:T(8,128)(2,1)S(1)} %get-tuple-element.77.refs_0_, bf16[256,2560]{1,0:T(8,128)(2,1)S(1)} %get-tuple-element.73.refs_11_.refs_1_, bf16[1024,2560]{1,0:T(8,128)(2,1)S(1)} %get-tuple-element.74.refs_12_.refs_2_, ...), custom_call_target="tpu_custom_call" | custom-call | bytes 14614528 | tf_op jit(solution)/shard_map/project_other/pallas_call | solution.py:112
  32.2 0.5 %project_other.5.refs_4_ = bf16[256,128]{1,0:T(8,128)(2,1)S(1)} custom-call(bf16[256,2560]{1,0:T(8,128)(2,1)S(1)} %get-tuple-element.77.refs_0_, bf16[256,2560]{1,0:T(8,128)(2,1)S(1)} %get-tuple-element.73.refs_11_.refs_1_, bf16[1024,2560]{1,0:T(8,128)(2,1)S(1)} %get-tuple-element.74.refs_12_.refs_2_, ...), custom_call_target="tpu_custom_call" | custom-call | bytes 14483456 | tf_op jit(solution)/shard_map/project_other/pallas_call | solution.py:112
  32.8 0.7 %collective-permute-start.10 = (bf16[256,384]{1,0:T(8,128)(2,1)S(1)}, bf16[256,384]{1,0:T(8,128)(2,1)S(1)}, u32[]{:S(2)}, u32[]{:S(2)}) collective-permute-start(bf16[256,384]{1,0:T(8,128)(2,1)S(1)} %project_other.4.refs_4_), channel_id=1, source_target_pairs={{0,2},{2,0},{1,3},{3,1},{4,6},{6,4},{5,7},{7,5},{8,10},{10,8},{9,1... | collective-permute-start | bytes 589832 | tf_op jit(solution)/shard_map/ppermute | solution.py:864
  33.4 1.9 %project_own.1.own_ref = f32[256,1280]{1,0:T(8,128)S(1)} custom-call(bf16[256,2560]{1,0:T(8,128)(2,1)S(1)} %get-tuple-element.77.refs_0_, bf16[256,2560]{1,0:T(8,128)(2,1)S(1)} %get-tuple-element.73.refs_11_.refs_1_, bf16[1024,2560]{1,0:T(8,128)(2,1)S(1)} %get-tuple-element.74.refs_12_.refs_2_, bf16[1280,2560]{1,0:T(8,128)(2,1)S(1)} %get-tuple-element.75.refs_13_.refs_3_, ...), custom_call_target="tpu_custom_call" | custom-call | bytes 15728640 | tf_op jit(solution)/shard_map/project_own/pallas_call | solution.py:112
  35.3 1.5 %collective-permute-start.9 = (bf16[256,128]{1,0:T(8,128)(2,1)S(1)}, bf16[256,128]{1,0:T(8,128)(2,1)S(1)}, u32[]{:S(2)}, u32[]{:S(2)}) collective-permute-start(bf16[256,128]{1,0:T(8,128)(2,1)S(1)} %project_other.5.refs_4_), channel_id=1, source_target_pairs={{0,2},{2,0},{1,3},{3,1},{4,6},{6,4},{5,7},{7,5},{8,10},{10,8},{9,1... | collective-permute-start | bytes 196616 | tf_op jit(solution)/shard_map/ppermute | solution.py:864
  36.8 2.1 %collective-permute-done.8.other_squares_ref = f32[2,128]{1,0:T(2,128)S(1)} collective-permute-done((f32[2,128]{1,0:T(2,128)S(1)}, f32[2,128]{1,0:T(2,128)S(1)}, u32[]{:S(2)}, u32[]{:S(2)}) %collective-permute-start.8) | collective-permute-done | bytes 1056 | tf_op jit(solution)/shard_map/ppermute | solution.py:865
  38.9 0.8 %finish.4.refs_0_ = bf16[256,1280]{1,0:T(8,128)(2,1)} custom-call(f32[2,128]{1,0:T(2,128)S(1)} %get-tuple-element.76.squares_ref, f32[2,128]{1,0:T(2,128)S(1)} %collective-permute-done.8.other_squares_ref, f32[256,1280]{1,0:T(8,128)S(1)} %project_own.1.own_ref, bf16[256,256]{1,0:T(8,128)(2,1)S(1)} %collective-permute-done.12.got_ref), custom_call_target="tpu_custom_call" | custom-call | flops 2000000000 | tf_op jit(solution)/shard_map/finish/pallas_call | solution.py:825
  39.7 0.8 %finish.5.refs_0_ = bf16[256,1280]{1,0:T(8,128)(2,1)} custom-call(f32[2,128]{1,0:T(2,128)S(1)} %get-tuple-element.76.squares_ref, f32[2,128]{1,0:T(2,128)S(1)} %collective-permute-done.8.other_squares_ref, f32[256,1280]{1,0:T(8,128)S(1)} %project_own.1.own_ref, bf16[256,512]{1,0:T(8,128)(2,1)S(1)} %collective-permute-done.11.got_ref, ...), custom_call_target="tpu_custom_call", output_to_operand_aliasing={{}: (4, {})} | custom-call | flops 2000000000 | tf_op jit(solution)/shard_map/finish/pallas_call | solution.py:825
  40.6 2.5 %collective-permute-done.10.got_ref = bf16[256,384]{1,0:T(8,128)(2,1)S(1)} collective-permute-done((bf16[256,384]{1,0:T(8,128)(2,1)S(1)}, bf16[256,384]{1,0:T(8,128)(2,1)S(1)}, u32[]{:S(2)}, u32[]{:S(2)}) %collective-permute-start.10) | collective-permute-done | bytes 196640 | tf_op jit(solution)/shard_map/ppermute | solution.py:864
  43.1 0.8 %finish.6.refs_0_ = bf16[256,1280]{1,0:T(8,128)(2,1)} custom-call(f32[2,128]{1,0:T(2,128)S(1)} %get-tuple-element.76.squares_ref, f32[2,128]{1,0:T(2,128)S(1)} %collective-permute-done.8.other_squares_ref, f32[256,1280]{1,0:T(8,128)S(1)} %project_own.1.own_ref, bf16[256,384]{1,0:T(8,128)(2,1)S(1)} %collective-permute-done.10.got_ref, ...), custom_call_target="tpu_custom_call", output_to_operand_aliasing={{}: (4, {})} | custom-call | flops 2000000000 | tf_op jit(solution)/shard_map/finish/pallas_call | solution.py:825
  43.9 0.8 %finish.7 = bf16[256,1280]{1,0:T(8,128)(2,1)} custom-call(f32[2,128]{1,0:T(2,128)S(1)} %get-tuple-element.76.squares_ref, f32[2,128]{1,0:T(2,128)S(1)} %collective-permute-done.8.other_squares_ref, f32[256,1280]{1,0:T(8,128)S(1)} %project_own.1.own_ref, bf16[256,128]{1,0:T(8,128)(2,1)S(1)} %collective-permute-done.9.got_ref, ...), custom_call_target="tpu_custom_call", output_to_operand_aliasing={{}: (4, {})} | custom-call | flops 2000000000 | tf_op jit(solution)/shard_map/finish/pallas_call | solution.py:825
  (12 shorter events, 0.4 us)
Async XLA Ops:
  3.1 1.7 %collective-permute-start = (bf16[64,2688]{1,0:T(8,128)(2,1)S(1)}, bf16[64,2688]{1,0:T(8,128)(2,1)S(1)}, u32[]{:S(2)}, u32[]{:S(2)}) collective-permute-start(bf16[64,2688]{1,0:T(8,128)(2,1)S(1)} %get-tuple-element.43), channel_id=1, source_target_pairs={{0,1},{1,0},{2,3},{3,2},{4,5},{5,4},{6,7},{7,6},{8,9},{9,8},{10,11... | collective-permute-start | bytes 1032200 | tf_op jit(solution)/shard_map/ppermute | solution.py:898
  5.1 6.2 %collective-permute-start.1 = (bf16[32,2688]{1,0:T(8,128)(2,1)S(1)}, bf16[32,2688]{1,0:T(8,128)(2,1)S(1)}, u32[]{:S(2)}, u32[]{:S(2)}) collective-permute-start(bf16[32,2688]{1,0:T(8,128)(2,1)S(1)} %get-tuple-element.46.after_ref), channel_id=1, source_target_pairs={{0,4},{4,8},{1,5},{5,9},{2,6},{6,10},{3,7},{7,11},{16,20},{20,24},... | collective-permute-start | bytes 516104 | tf_op jit(solution)/shard_map/ppermute | solution.py:686
  7.5 8.3 %collective-permute-start.4 = (bf16[32,2688]{1,0:T(8,128)(2,1)S(1)}, bf16[32,2688]{1,0:T(8,128)(2,1)S(1)}, u32[]{:S(2)}, u32[]{:S(2)}) collective-permute-start(bf16[32,2688]{1,0:T(8,128)(2,1)S(1)} %get-tuple-element.57.after_ref), channel_id=1, source_target_pairs={{0,8},{8,12},{1,9},{9,13},{2,10},{10,14},{3,11},{11,15},{16,24},{2... | collective-permute-start | bytes 516104 | tf_op jit(solution)/shard_map/ppermute | solution.py:688
  11.3 9.8 %collective-permute-start.2 = (bf16[32,2560]{1,0:T(8,128)(2,1)S(1)}, bf16[32,2560]{1,0:T(8,128)(2,1)S(1)}, u32[]{:S(2)}, u32[]{:S(2)}) collective-permute-start(bf16[32,2560]{1,0:T(8,128)(2,1)S(1)} %early_state.1.refs_3_), channel_id=1, source_target_pairs={{4,12},{0,4},{5,13},{1,5},{6,14},{2,6},{7,15},{3,7},{20,28},{16,20... | collective-permute-start | bytes 491528 | tf_op jit(solution)/shard_map/ppermute | solution.py:697
  12.6 11.6 %collective-permute-start.3 = (bf16[32,2560]{1,0:T(8,128)(2,1)S(1)}, bf16[32,2560]{1,0:T(8,128)(2,1)S(1)}, u32[]{:S(2)}, u32[]{:S(2)}) collective-permute-start(bf16[32,2560]{1,0:T(8,128)(2,1)S(1)} %early_state.1.refs_3_), channel_id=1, source_target_pairs={{4,8},{5,9},{6,10},{7,11},{20,24},{21,25},{22,26},{23,27}} | collective-permute-start | bytes 491528 | tf_op jit(solution)/shard_map/ppermute | solution.py:698
  16.0 8.3 %collective-permute-start.5 = (bf16[32,2560]{1,0:T(8,128)(2,1)S(1)}, bf16[32,2560]{1,0:T(8,128)(2,1)S(1)}, u32[]{:S(2)}, u32[]{:S(2)}) collective-permute-start(bf16[32,2560]{1,0:T(8,128)(2,1)S(1)} %get-tuple-element.59.after_ref), channel_id=1, source_target_pairs={{8,12},{9,13},{10,14},{11,15},{24,28},{25,29},{26,30},{27,31}} | collective-permute-start | bytes 491528 | tf_op jit(solution)/shard_map/ppermute | solution.py:706
  21.3 2.9 %collective-permute-start.6 = (bf16[32,2560]{1,0:T(8,128)(2,1)S(1)}, bf16[32,2560]{1,0:T(8,128)(2,1)S(1)}, u32[]{:S(2)}, u32[]{:S(2)}) collective-permute-start(bf16[32,2560]{1,0:T(8,128)(2,1)S(1)} %get-tuple-element.64), channel_id=1, source_target_pairs={{0,1},{1,0},{2,3},{3,2},{4,5},{5,4},{6,7},{7,6},{8,9},{9,8},{10,11... | collective-permute-start | bytes 491528 | tf_op jit(solution)/shard_map/ppermute | solution.py:715
  24.3 1.5 %collective-permute-start.7 = (bf16[32,2560]{1,0:T(8,128)(2,1)S(1)}, bf16[32,2560]{1,0:T(8,128)(2,1)S(1)}, u32[]{:S(2)}, u32[]{:S(2)}) collective-permute-start(bf16[32,2560]{1,0:T(8,128)(2,1)S(1)} %get-tuple-element.66), channel_id=1, source_target_pairs={{0,1},{1,0},{2,3},{3,2},{4,5},{5,4},{6,7},{7,6},{8,9},{9,8},{10,11... | collective-permute-start | bytes 491528 | tf_op jit(solution)/shard_map/ppermute | solution.py:724
  26.9 12.0 %collective-permute-start.12 = (bf16[256,256]{1,0:T(8,128)(2,1)S(1)}, bf16[256,256]{1,0:T(8,128)(2,1)S(1)}, u32[]{:S(2)}, u32[]{:S(2)}) collective-permute-start(bf16[256,256]{1,0:T(8,128)(2,1)S(1)} %get-tuple-element.78.refs_4_), channel_id=1, source_target_pairs={{0,2},{2,0},{1,3},{3,1},{4,6},{6,4},{5,7},{7,5},{8,10},{10,8},{9,1... | collective-permute-start | bytes 393224 | tf_op jit(solution)/shard_map/ppermute | solution.py:864
  29.3 10.4 %collective-permute-start.11 = (bf16[256,512]{1,0:T(8,128)(2,1)S(1)}, bf16[256,512]{1,0:T(8,128)(2,1)S(1)}, u32[]{:S(2)}, u32[]{:S(2)}) collective-permute-start(bf16[256,512]{1,0:T(8,128)(2,1)S(1)} %project_other.3.refs_4_), channel_id=1, source_target_pairs={{0,2},{2,0},{1,3},{3,1},{4,6},{6,4},{5,7},{7,5},{8,10},{10,8},{9,1... | collective-permute-start | bytes 786440 | tf_op jit(solution)/shard_map/ppermute | solution.py:864
  29.9 9.0 %collective-permute-start.8 = (f32[2,128]{1,0:T(2,128)S(1)}, f32[2,128]{1,0:T(2,128)S(1)}, u32[]{:S(2)}, u32[]{:S(2)}) collective-permute-start(f32[2,128]{1,0:T(2,128)S(1)} %get-tuple-element.76.squares_ref), channel_id=1, source_target_pairs={{0,2},{2,0},{1,3},{3,1},{4,6},{6,4},{5,7},{7,5},{8,10},{10,8},{9,1... | collective-permute-start | bytes 3080 | tf_op jit(solution)/shard_map/ppermute | solution.py:865
  32.8 10.3 %collective-permute-start.10 = (bf16[256,384]{1,0:T(8,128)(2,1)S(1)}, bf16[256,384]{1,0:T(8,128)(2,1)S(1)}, u32[]{:S(2)}, u32[]{:S(2)}) collective-permute-start(bf16[256,384]{1,0:T(8,128)(2,1)S(1)} %project_other.4.refs_4_), channel_id=1, source_target_pairs={{0,2},{2,0},{1,3},{3,1},{4,6},{6,4},{5,7},{7,5},{8,10},{10,8},{9,1... | collective-permute-start | bytes 589832 | tf_op jit(solution)/shard_map/ppermute | solution.py:864
  35.3 8.6 %collective-permute-start.9 = (bf16[256,128]{1,0:T(8,128)(2,1)S(1)}, bf16[256,128]{1,0:T(8,128)(2,1)S(1)}, u32[]{:S(2)}, u32[]{:S(2)}) collective-permute-start(bf16[256,128]{1,0:T(8,128)(2,1)S(1)} %project_other.5.refs_4_), channel_id=1, source_target_pairs={{0,2},{2,0},{1,3},{3,1},{4,6},{6,4},{5,7},{7,5},{8,10},{10,8},{9,1... | collective-permute-start | bytes 196616 | tf_op jit(solution)/shard_map/ppermute | solution.py:864

commit v11 on v9

--- a/solution.py
+++ b/solution.py
@@ -782,7 +782,7 @@
     )
 
 
-SENDS = (256, 384, 384, 256)
+SENDS = (256, 512, 384, 128)
 FINISH_FLOPS = 2 * 10**9
 
 

time: 45.2 us -> 45.2 us (level)
    ppermute x1, waiting for transfers between devices: 0.64 us -> 2.13 us  [layer_columns(): other_squares = lax.ppermute(squares, 'tensor', swap)]
    ppermute x4, waiting for transfers between devices: 3.9 us -> 2.54 us  [layer_columns(): got = [lax.ppermute(part, 'tensor', swap) for part in parts]]
  transfers between devices with their start and end apart: 13 -> 13, of which waited for: 8 -> 7; matrix products, arithmetic and copies ran while one was open for 0% -> 0% of each run, Pallas kernels for 31% -> 31%
where the time goes in v11:
time: 45.2 us; the launch traced here: 44.7 us
  Pallas kernels  18.6 us (41%)
  waiting for transfers between devices  14 us (31%)
  starting transfers between devices  11.2 us (25%)
  between operations  0.87 us (2%)
    pallas_call x3, Pallas kernels, local_call_of(): pl.pallas_call(kernel, name=name, out_shape=[jax.ShapeDtypeStruct((tokens...  7.07 us
    pallas_call x10, Pallas kernels, local_call(): pl.pallas_call(kernel, name=name, out_shape=outs, in_specs=[pl.BlockSpec(...  5.84 us
    ppermute x4, starting transfers between devices, layer_columns(): got = [lax.ppermute(part, 'tensor', swap) for part in parts]  4.33 us
    pallas_call x4, Pallas kernels, finish(): pl.pallas_call(functools.partial(finish_kernel, first), name='finish', ou...  3.18 us
    ppermute x1, waiting for transfers between devices, entering_state(): last = lax.ppermute(middle, 'scan', [(2, 3)])  2.85 us
    ppermute x4, waiting for transfers between devices, layer_columns(): got = [lax.ppermute(part, 'tensor', swap) for part in parts]  2.54 us
    ppermute x1, waiting for transfers between devices, entering_state(): far = lax.ppermute(second, 'scan', [(0, 2), (2, 3)])  2.48 us
    pallas_call x1, Pallas kernels, own_state(): pl.pallas_call(state_kernel, name='own_state', out_shape=[jax.ShapeDtypeS...  2.46 us
  transfers between devices with their start and end apart: 13, of which 7 were waited for; matrix products, arithmetic and copies ran while one was open for 0% of the time, Pallas kernels for 31%

profile of v11, /device:TPU:24, one launch (start us, length us, event | category | flops | bytes accessed | tf_op | source)
XLA Modules:
  0.0 44.7 jit_solution(13030870663757946902)
XLA Ops:
  0.7 2.5 %own_state.1 = (f32[40,256]{1,0:T(8,128)S(1)}, f32[40,256]{1,0:T(8,128)S(1)}, bf16[16,128]{1,0:T(8,128)(2,1)S(1)}, f32[64,2560]{1,0:T(8,128)S(1)}, bf16[64,2688]...) custom-call(s32[1]{0:T(128)S(6)} %copy.22.band_ref, ...), custom_call_target="tpu_custom_call" | custom-call | flops 335544320 | bytes 1310720 | tf_op jit(solution)/shard_map/own_state/pallas_call | solution.py:237
  3.2 1.6 %collective-permute-done.refs_1_.got_ref.refs_6_.refs_4_ = bf16[64,2688]{1,0:T(8,128)(2,1)S(1)} collective-permute-done((bf16[64,2688]{1,0:T(8,128)(2,1)S(1)}, bf16[64,2688]{1,0:T(8,128)(2,1)S(1)}, u32[]{:S(2)}, u32[]{:S(2)}) %collective-permute-start) | collective-permute-done | bytes 344096 | tf_op jit(solution)/shard_map/ppermute | solution.py:910
  4.8 0.2 chip_state.1
  5.1 0.7 %collective-permute-start.1 = (bf16[32,2688]{1,0:T(8,128)(2,1)S(1)}, bf16[32,2688]{1,0:T(8,128)(2,1)S(1)}, u32[]{:S(2)}, u32[]{:S(2)}) collective-permute-start(bf16[32,2688]{1,0:T(8,128)(2,1)S(1)} %get-tuple-element.48.after_ref), channel_id=1, source_target_pairs={{0,4},{4,8},{1,5},{5,9},{2,6},{6,10},{3,7},{7,11},{16,20},{20,24},... | collective-permute-start | bytes 516104 | tf_op jit(solution)/shard_map/ppermute | solution.py:698
  5.8 1.7 %local_first.1 = (f32[256,512]{1,0:T(8,128)S(1)}, f32[256,512]{1,0:T(8,128)S(1)}, bf16[256,2560]{1,0:T(8,128)(2,1)S(1)}, bf16[32,2688]{1,0:T(8,128)(2,1)S(1)}, b...) custom-call(f32[40,256]{1,0:T(8,128)S(1)} %get-tuple-element.49.runn, ...), custom_call_target="tpu_custom_call" | custom-call | flops 201326592 | bytes 1572864 | tf_op jit(solution)/shard_map/local_first/pallas_call | solution.py:458
  7.5 1.3 %collective-permute-start.4 = (bf16[32,2688]{1,0:T(8,128)(2,1)S(1)}, bf16[32,2688]{1,0:T(8,128)(2,1)S(1)}, u32[]{:S(2)}, u32[]{:S(2)}) collective-permute-start(bf16[32,2688]{1,0:T(8,128)(2,1)S(1)} %get-tuple-element.59.after_ref), channel_id=1, source_target_pairs={{0,8},{8,12},{1,9},{9,13},{2,10},{10,14},{3,11},{11,15},{16,24},{2... | collective-permute-start | bytes 516104 | tf_op jit(solution)/shard_map/ppermute | solution.py:700
  8.8 2.5 %local_rest.2 = (f32[256,1024]{1,0:T(8,128)S(1)}, f32[256,1024]{1,0:T(8,128)S(1)}, bf16[1024,2560]{1,0:T(8,128)(2,1)S(1)}) custom-call(f32[40,256]{1,0:T(8,128)S(1)} %get-tuple-element.49.running_ref, f32[40,256]{1,0:T(8,128)S(1)} %get-tuple-element.50.weight_ref, bf16[256,2560]{1,0:T(8,128)(2,1)S(1)} %get-tuple-element.51.signal_ref, ...), custom_call_target="tpu_custom_call" | custom-call | flops 402653184 | bytes 3145728 | tf_op jit(solution)/shard_map/local_rest/pallas_call | solution.py:458
  11.3 1.3 %collective-permute-start.2 = (bf16[32,2560]{1,0:T(8,128)(2,1)S(1)}, bf16[32,2560]{1,0:T(8,128)(2,1)S(1)}, u32[]{:S(2)}, u32[]{:S(2)}) collective-permute-start(bf16[32,2560]{1,0:T(8,128)(2,1)S(1)} %get-tuple-element.61.refs_4_), channel_id=1, source_target_pairs={{4,12},{0,4},{5,13},{1,5},{6,14},{2,6},{7,15},{3,7},{20,28},{16,20... | collective-permute-start | bytes 491528 | tf_op jit(solution)/shard_map/ppermute | solution.py:709
  12.6 0.7 %collective-permute-start.3 = (bf16[32,2560]{1,0:T(8,128)(2,1)S(1)}, bf16[32,2560]{1,0:T(8,128)(2,1)S(1)}, u32[]{:S(2)}, u32[]{:S(2)}) collective-permute-start(bf16[32,2560]{1,0:T(8,128)(2,1)S(1)} %get-tuple-element.61.refs_4_), channel_id=1, source_target_pairs={{4,8},{5,9},{6,10},{7,11},{20,24},{21,25},{22,26},{23,27}} | collective-permute-start | bytes 491528 | tf_op jit(solution)/shard_map/ppermute | solution.py:710
  13.3 2.5 %collective-permute-done.4.refs_2_.refs_1_ = bf16[32,2688]{1,0:T(8,128)(2,1)S(1)} collective-permute-done((bf16[32,2688]{1,0:T(8,128)(2,1)S(1)}, bf16[32,2688]{1,0:T(8,128)(2,1)S(1)}, u32[]{:S(2)}, u32[]{:S(2)}) %collective-permute-start.4) | collective-permute-done | bytes 172064 | tf_op jit(solution)/shard_map/ppermute | solution.py:700
  15.8 0.2 middle_state.1
  16.0 1.3 %collective-permute-start.5 = (bf16[32,2560]{1,0:T(8,128)(2,1)S(1)}, bf16[32,2560]{1,0:T(8,128)(2,1)S(1)}, u32[]{:S(2)}, u32[]{:S(2)}) collective-permute-start(bf16[32,2560]{1,0:T(8,128)(2,1)S(1)} %get-tuple-element.63.after_ref), channel_id=1, source_target_pairs={{8,12},{9,13},{10,14},{11,15},{24,28},{25,29},{26,30},{27,31}} | collective-permute-start | bytes 491528 | tf_op jit(solution)/shard_map/ppermute | solution.py:718
  17.3 2.9 %local_rest.3 = (f32[256,1024]{1,0:T(8,128)S(1)}, f32[256,1024]{1,0:T(8,128)S(1)}, bf16[1280,2560]{1,0:T(8,128)(2,1)S(1)}) custom-call(f32[40,256]{1,0:T(8,128)S(1)} %get-tuple-element.49.running_ref, f32[40,256]{1,0:T(8,128)S(1)} %get-tuple-element.50.weight_ref, bf16[256,2560]{1,0:T(8,128)(2,1)S(1)} %get-tuple-element.51.signal_ref, ...), custom_call_target="tpu_custom_call" | custom-call | flops 402653184 | bytes 3145728 | tf_op jit(solution)/shard_map/local_rest/pallas_call | solution.py:458
  20.1 1.0 %collective-permute-done.2.refs_2_.refs_0_ = bf16[32,2560]{1,0:T(8,128)(2,1)S(1)} collective-permute-done((bf16[32,2560]{1,0:T(8,128)(2,1)S(1)}, bf16[32,2560]{1,0:T(8,128)(2,1)S(1)}, u32[]{:S(2)}, u32[]{:S(2)}) %collective-permute-start.2) | collective-permute-done | bytes 163872 | tf_op jit(solution)/shard_map/ppermute | solution.py:709
  21.4 2.8 %collective-permute-done.5.refs_2_ = bf16[32,2560]{1,0:T(8,128)(2,1)S(1)} collective-permute-done((bf16[32,2560]{1,0:T(8,128)(2,1)S(1)}, bf16[32,2560]{1,0:T(8,128)(2,1)S(1)}, u32[]{:S(2)}, u32[]{:S(2)}) %collective-permute-start.5) | collective-permute-done | bytes 163872 | tf_op jit(solution)/shard_map/ppermute | solution.py:718
  24.4 1.4 %collective-permute-done.7.refs_2_ = bf16[32,2560]{1,0:T(8,128)(2,1)S(1)} collective-permute-done((bf16[32,2560]{1,0:T(8,128)(2,1)S(1)}, bf16[32,2560]{1,0:T(8,128)(2,1)S(1)}, u32[]{:S(2)}, u32[]{:S(2)}) %collective-permute-start.7) | collective-permute-done | bytes 163872 | tf_op jit(solution)/shard_map/ppermute | solution.py:736
  25.8 1.2 %gated_part.1 = (bf16[256,2560]{1,0:T(8,128)(2,1)S(1)}, f32[2,128]{1,0:T(2,128)S(1)}, bf16[256,256]{1,0:T(8,128)(2,1)S(1)}) custom-call(bf16[64,2560]{1,0:T(8,128)(2,1)S(1)} %get-tuple-element.69.refs_0_, bf16[32,2560]{1,0:T(8,128)(2,1)S(1)} %collective-permute-done.6.refs_7_.refs_1_, bf16[32,2560]{1,0:T(8,128)(2,1)S(1)} %collective-permute-done.7.refs_2_, ...), custom_call_target="tpu_custom_call" | custom-call | flops 167772160 | bytes 20524032 | tf_op jit(solution)/shard_map/gated_part/pallas_call | solution.py:112
  26.9 1.5 %collective-permute-start.12 = (bf16[256,256]{1,0:T(8,128)(2,1)S(1)}, bf16[256,256]{1,0:T(8,128)(2,1)S(1)}, u32[]{:S(2)}, u32[]{:S(2)}) collective-permute-start(bf16[256,256]{1,0:T(8,128)(2,1)S(1)} %get-tuple-element.82.refs_4_), channel_id=1, source_target_pairs={{0,2},{2,0},{1,3},{3,1},{4,6},{6,4},{5,7},{7,5},{8,10},{10,8},{9,1... | collective-permute-start | bytes 393224 | tf_op jit(solution)/shard_map/ppermute | solution.py:876
  28.4 0.8 %project_other.3.refs_4_ = bf16[256,512]{1,0:T(8,128)(2,1)S(1)} custom-call(bf16[256,2560]{1,0:T(8,128)(2,1)S(1)} %get-tuple-element.81.refs_0_, bf16[256,2560]{1,0:T(8,128)(2,1)S(1)} %get-tuple-element.77.refs_11_.refs_1_, bf16[1024,2560]{1,0:T(8,128)(2,1)S(1)} %get-tuple-element.78.refs_12_.refs_2_, ...), custom_call_target="tpu_custom_call" | custom-call | bytes 14680064 | tf_op jit(solution)/shard_map/project_other/pallas_call | solution.py:112
  29.3 0.6 %collective-permute-start.11 = (bf16[256,512]{1,0:T(8,128)(2,1)S(1)}, bf16[256,512]{1,0:T(8,128)(2,1)S(1)}, u32[]{:S(2)}, u32[]{:S(2)}) collective-permute-start(bf16[256,512]{1,0:T(8,128)(2,1)S(1)} %project_other.3.refs_4_), channel_id=1, source_target_pairs={{0,2},{2,0},{1,3},{3,1},{4,6},{6,4},{5,7},{7,5},{8,10},{10,8},{9,1... | collective-permute-start | bytes 786440 | tf_op jit(solution)/shard_map/ppermute | solution.py:876
  29.9 1.4 %collective-permute-start.8 = (f32[2,128]{1,0:T(2,128)S(1)}, f32[2,128]{1,0:T(2,128)S(1)}, u32[]{:S(2)}, u32[]{:S(2)}) collective-permute-start(f32[2,128]{1,0:T(2,128)S(1)} %get-tuple-element.80.squares_ref), channel_id=1, source_target_pairs={{0,2},{2,0},{1,3},{3,1},{4,6},{6,4},{5,7},{7,5},{8,10},{10,8},{9,1... | collective-permute-start | bytes 3080 | tf_op jit(solution)/shard_map/ppermute | solution.py:877
  31.4 0.8 %project_other.4.refs_4_ = bf16[256,384]{1,0:T(8,128)(2,1)S(1)} custom-call(bf16[256,2560]{1,0:T(8,128)(2,1)S(1)} %get-tuple-element.81.refs_0_, bf16[256,2560]{1,0:T(8,128)(2,1)S(1)} %get-tuple-element.77.refs_11_.refs_1_, bf16[1024,2560]{1,0:T(8,128)(2,1)S(1)} %get-tuple-element.78.refs_12_.refs_2_, ...), custom_call_target="tpu_custom_call" | custom-call | bytes 14614528 | tf_op jit(solution)/shard_map/project_other/pallas_call | solution.py:112
  32.2 0.5 %project_other.5.refs_4_ = bf16[256,128]{1,0:T(8,128)(2,1)S(1)} custom-call(bf16[256,2560]{1,0:T(8,128)(2,1)S(1)} %get-tuple-element.81.refs_0_, bf16[256,2560]{1,0:T(8,128)(2,1)S(1)} %get-tuple-element.77.refs_11_.refs_1_, bf16[1024,2560]{1,0:T(8,128)(2,1)S(1)} %get-tuple-element.78.refs_12_.refs_2_, ...), custom_call_target="tpu_custom_call" | custom-call | bytes 14483456 | tf_op jit(solution)/shard_map/project_other/pallas_call | solution.py:112
  32.7 0.7 %collective-permute-start.10 = (bf16[256,384]{1,0:T(8,128)(2,1)S(1)}, bf16[256,384]{1,0:T(8,128)(2,1)S(1)}, u32[]{:S(2)}, u32[]{:S(2)}) collective-permute-start(bf16[256,384]{1,0:T(8,128)(2,1)S(1)} %project_other.4.refs_4_), channel_id=1, source_target_pairs={{0,2},{2,0},{1,3},{3,1},{4,6},{6,4},{5,7},{7,5},{8,10},{10,8},{9,1... | collective-permute-start | bytes 589832 | tf_op jit(solution)/shard_map/ppermute | solution.py:876
  33.4 1.9 %project_own.1.own_ref = f32[256,1280]{1,0:T(8,128)S(1)} custom-call(bf16[256,2560]{1,0:T(8,128)(2,1)S(1)} %get-tuple-element.81.refs_0_, bf16[256,2560]{1,0:T(8,128)(2,1)S(1)} %get-tuple-element.77.refs_11_.refs_1_, bf16[1024,2560]{1,0:T(8,128)(2,1)S(1)} %get-tuple-element.78.refs_12_.refs_2_, bf16[1280,2560]{1,0:T(8,128)(2,1)S(1)} %get-tuple-element.79.refs_13_.refs_3_, ...), custom_call_target="tpu_custom_call" | custom-call | bytes 15728640 | tf_op jit(solution)/shard_map/project_own/pallas_call | solution.py:112
  35.3 1.5 %collective-permute-start.9 = (bf16[256,128]{1,0:T(8,128)(2,1)S(1)}, bf16[256,128]{1,0:T(8,128)(2,1)S(1)}, u32[]{:S(2)}, u32[]{:S(2)}) collective-permute-start(bf16[256,128]{1,0:T(8,128)(2,1)S(1)} %project_other.5.refs_4_), channel_id=1, source_target_pairs={{0,2},{2,0},{1,3},{3,1},{4,6},{6,4},{5,7},{7,5},{8,10},{10,8},{9,1... | collective-permute-start | bytes 196616 | tf_op jit(solution)/shard_map/ppermute | solution.py:876
  36.8 2.1 %collective-permute-done.8.other_squares_ref = f32[2,128]{1,0:T(2,128)S(1)} collective-permute-done((f32[2,128]{1,0:T(2,128)S(1)}, f32[2,128]{1,0:T(2,128)S(1)}, u32[]{:S(2)}, u32[]{:S(2)}) %collective-permute-start.8) | collective-permute-done | bytes 1056 | tf_op jit(solution)/shard_map/ppermute | solution.py:877
  38.9 0.8 %finish.4.refs_0_ = bf16[256,1280]{1,0:T(8,128)(2,1)} custom-call(f32[2,128]{1,0:T(2,128)S(1)} %get-tuple-element.80.squares_ref, f32[2,128]{1,0:T(2,128)S(1)} %collective-permute-done.8.other_squares_ref, f32[256,1280]{1,0:T(8,128)S(1)} %project_own.1.own_ref, bf16[256,256]{1,0:T(8,128)(2,1)S(1)} %collective-permute-done.12.got_ref), custom_call_target="tpu_custom_call" | custom-call | flops 2000000000 | tf_op jit(solution)/shard_map/finish/pallas_call | solution.py:837
  39.7 0.8 %finish.5.refs_0_ = bf16[256,1280]{1,0:T(8,128)(2,1)} custom-call(f32[2,128]{1,0:T(2,128)S(1)} %get-tuple-element.80.squares_ref, f32[2,128]{1,0:T(2,128)S(1)} %collective-permute-done.8.other_squares_ref, f32[256,1280]{1,0:T(8,128)S(1)} %project_own.1.own_ref, bf16[256,512]{1,0:T(8,128)(2,1)S(1)} %collective-permute-done.11.got_ref, ...), custom_call_target="tpu_custom_call", output_to_operand_aliasing={{}: (4, {})} | custom-call | flops 2000000000 | tf_op jit(solution)/shard_map/finish/pallas_call | solution.py:837
  40.6 2.5 %collective-permute-done.10.got_ref = bf16[256,384]{1,0:T(8,128)(2,1)S(1)} collective-permute-done((bf16[256,384]{1,0:T(8,128)(2,1)S(1)}, bf16[256,384]{1,0:T(8,128)(2,1)S(1)}, u32[]{:S(2)}, u32[]{:S(2)}) %collective-permute-start.10) | collective-permute-done | bytes 196640 | tf_op jit(solution)/shard_map/ppermute | solution.py:876
  43.1 0.8 %finish.6.refs_0_ = bf16[256,1280]{1,0:T(8,128)(2,1)} custom-call(f32[2,128]{1,0:T(2,128)S(1)} %get-tuple-element.80.squares_ref, f32[2,128]{1,0:T(2,128)S(1)} %collective-permute-done.8.other_squares_ref, f32[256,1280]{1,0:T(8,128)S(1)} %project_own.1.own_ref, bf16[256,384]{1,0:T(8,128)(2,1)S(1)} %collective-permute-done.10.got_ref, ...), custom_call_target="tpu_custom_call", output_to_operand_aliasing={{}: (4, {})} | custom-call | flops 2000000000 | tf_op jit(solution)/shard_map/finish/pallas_call | solution.py:837
  43.9 0.8 %finish.7 = bf16[256,1280]{1,0:T(8,128)(2,1)} custom-call(f32[2,128]{1,0:T(2,128)S(1)} %get-tuple-element.80.squares_ref, f32[2,128]{1,0:T(2,128)S(1)} %collective-permute-done.8.other_squares_ref, f32[256,1280]{1,0:T(8,128)S(1)} %project_own.1.own_ref, bf16[256,128]{1,0:T(8,128)(2,1)S(1)} %collective-permute-done.9.got_ref, ...), custom_call_target="tpu_custom_call", output_to_operand_aliasing={{}: (4, {})} | custom-call | flops 2000000000 | tf_op jit(solution)/shard_map/finish/pallas_call | solution.py:837
  (12 shorter events, 0.4 us)
Async XLA Ops:
  3.1 1.7 %collective-permute-start = (bf16[64,2688]{1,0:T(8,128)(2,1)S(1)}, bf16[64,2688]{1,0:T(8,128)(2,1)S(1)}, u32[]{:S(2)}, u32[]{:S(2)}) collective-permute-start(bf16[64,2688]{1,0:T(8,128)(2,1)S(1)} %get-tuple-element.45), channel_id=1, source_target_pairs={{0,1},{1,0},{2,3},{3,2},{4,5},{5,4},{6,7},{7,6},{8,9},{9,8},{10,11... | collective-permute-start | bytes 1032200 | tf_op jit(solution)/shard_map/ppermute | solution.py:910
  5.1 6.2 %collective-permute-start.1 = (bf16[32,2688]{1,0:T(8,128)(2,1)S(1)}, bf16[32,2688]{1,0:T(8,128)(2,1)S(1)}, u32[]{:S(2)}, u32[]{:S(2)}) collective-permute-start(bf16[32,2688]{1,0:T(8,128)(2,1)S(1)} %get-tuple-element.48.after_ref), channel_id=1, source_target_pairs={{0,4},{4,8},{1,5},{5,9},{2,6},{6,10},{3,7},{7,11},{16,20},{20,24},... | collective-permute-start | bytes 516104 | tf_op jit(solution)/shard_map/ppermute | solution.py:698
  7.5 8.3 %collective-permute-start.4 = (bf16[32,2688]{1,0:T(8,128)(2,1)S(1)}, bf16[32,2688]{1,0:T(8,128)(2,1)S(1)}, u32[]{:S(2)}, u32[]{:S(2)}) collective-permute-start(bf16[32,2688]{1,0:T(8,128)(2,1)S(1)} %get-tuple-element.59.after_ref), channel_id=1, source_target_pairs={{0,8},{8,12},{1,9},{9,13},{2,10},{10,14},{3,11},{11,15},{16,24},{2... | collective-permute-start | bytes 516104 | tf_op jit(solution)/shard_map/ppermute | solution.py:700
  11.3 9.8 %collective-permute-start.2 = (bf16[32,2560]{1,0:T(8,128)(2,1)S(1)}, bf16[32,2560]{1,0:T(8,128)(2,1)S(1)}, u32[]{:S(2)}, u32[]{:S(2)}) collective-permute-start(bf16[32,2560]{1,0:T(8,128)(2,1)S(1)} %get-tuple-element.61.refs_4_), channel_id=1, source_target_pairs={{4,12},{0,4},{5,13},{1,5},{6,14},{2,6},{7,15},{3,7},{20,28},{16,20... | collective-permute-start | bytes 491528 | tf_op jit(solution)/shard_map/ppermute | solution.py:709
  12.6 11.6 %collective-permute-start.3 = (bf16[32,2560]{1,0:T(8,128)(2,1)S(1)}, bf16[32,2560]{1,0:T(8,128)(2,1)S(1)}, u32[]{:S(2)}, u32[]{:S(2)}) collective-permute-start(bf16[32,2560]{1,0:T(8,128)(2,1)S(1)} %get-tuple-element.61.refs_4_), channel_id=1, source_target_pairs={{4,8},{5,9},{6,10},{7,11},{20,24},{21,25},{22,26},{23,27}} | collective-permute-start | bytes 491528 | tf_op jit(solution)/shard_map/ppermute | solution.py:710
  16.0 8.3 %collective-permute-start.5 = (bf16[32,2560]{1,0:T(8,128)(2,1)S(1)}, bf16[32,2560]{1,0:T(8,128)(2,1)S(1)}, u32[]{:S(2)}, u32[]{:S(2)}) collective-permute-start(bf16[32,2560]{1,0:T(8,128)(2,1)S(1)} %get-tuple-element.63.after_ref), channel_id=1, source_target_pairs={{8,12},{9,13},{10,14},{11,15},{24,28},{25,29},{26,30},{27,31}} | collective-permute-start | bytes 491528 | tf_op jit(solution)/shard_map/ppermute | solution.py:718
  21.3 2.9 %collective-permute-start.6 = (bf16[32,2560]{1,0:T(8,128)(2,1)S(1)}, bf16[32,2560]{1,0:T(8,128)(2,1)S(1)}, u32[]{:S(2)}, u32[]{:S(2)}) collective-permute-start(bf16[32,2560]{1,0:T(8,128)(2,1)S(1)} %get-tuple-element.68), channel_id=1, source_target_pairs={{0,1},{1,0},{2,3},{3,2},{4,5},{5,4},{6,7},{7,6},{8,9},{9,8},{10,11... | collective-permute-start | bytes 491528 | tf_op jit(solution)/shard_map/ppermute | solution.py:727
  24.3 1.5 %collective-permute-start.7 = (bf16[32,2560]{1,0:T(8,128)(2,1)S(1)}, bf16[32,2560]{1,0:T(8,128)(2,1)S(1)}, u32[]{:S(2)}, u32[]{:S(2)}) collective-permute-start(bf16[32,2560]{1,0:T(8,128)(2,1)S(1)} %get-tuple-element.70), channel_id=1, source_target_pairs={{0,1},{1,0},{2,3},{3,2},{4,5},{5,4},{6,7},{7,6},{8,9},{9,8},{10,11... | collective-permute-start | bytes 491528 | tf_op jit(solution)/shard_map/ppermute | solution.py:736
  26.9 12.0 %collective-permute-start.12 = (bf16[256,256]{1,0:T(8,128)(2,1)S(1)}, bf16[256,256]{1,0:T(8,128)(2,1)S(1)}, u32[]{:S(2)}, u32[]{:S(2)}) collective-permute-start(bf16[256,256]{1,0:T(8,128)(2,1)S(1)} %get-tuple-element.82.refs_4_), channel_id=1, source_target_pairs={{0,2},{2,0},{1,3},{3,1},{4,6},{6,4},{5,7},{7,5},{8,10},{10,8},{9,1... | collective-permute-start | bytes 393224 | tf_op jit(solution)/shard_map/ppermute | solution.py:876
  29.3 10.4 %collective-permute-start.11 = (bf16[256,512]{1,0:T(8,128)(2,1)S(1)}, bf16[256,512]{1,0:T(8,128)(2,1)S(1)}, u32[]{:S(2)}, u32[]{:S(2)}) collective-permute-start(bf16[256,512]{1,0:T(8,128)(2,1)S(1)} %project_other.3.refs_4_), channel_id=1, source_target_pairs={{0,2},{2,0},{1,3},{3,1},{4,6},{6,4},{5,7},{7,5},{8,10},{10,8},{9,1... | collective-permute-start | bytes 786440 | tf_op jit(solution)/shard_map/ppermute | solution.py:876
  29.9 9.0 %collective-permute-start.8 = (f32[2,128]{1,0:T(2,128)S(1)}, f32[2,128]{1,0:T(2,128)S(1)}, u32[]{:S(2)}, u32[]{:S(2)}) collective-permute-start(f32[2,128]{1,0:T(2,128)S(1)} %get-tuple-element.80.squares_ref), channel_id=1, source_target_pairs={{0,2},{2,0},{1,3},{3,1},{4,6},{6,4},{5,7},{7,5},{8,10},{10,8},{9,1... | collective-permute-start | bytes 3080 | tf_op jit(solution)/shard_map/ppermute | solution.py:877
  32.7 10.3 %collective-permute-start.10 = (bf16[256,384]{1,0:T(8,128)(2,1)S(1)}, bf16[256,384]{1,0:T(8,128)(2,1)S(1)}, u32[]{:S(2)}, u32[]{:S(2)}) collective-permute-start(bf16[256,384]{1,0:T(8,128)(2,1)S(1)} %project_other.4.refs_4_), channel_id=1, source_target_pairs={{0,2},{2,0},{1,3},{3,1},{4,6},{6,4},{5,7},{7,5},{8,10},{10,8},{9,1... | collective-permute-start | bytes 589832 | tf_op jit(solution)/shard_map/ppermute | solution.py:876
  35.3 8.6 %collective-permute-start.9 = (bf16[256,128]{1,0:T(8,128)(2,1)S(1)}, bf16[256,128]{1,0:T(8,128)(2,1)S(1)}, u32[]{:S(2)}, u32[]{:S(2)}) collective-permute-start(bf16[256,128]{1,0:T(8,128)(2,1)S(1)} %project_other.5.refs_4_), channel_id=1, source_target_pairs={{0,2},{2,0},{1,3},{3,1},{4,6},{6,4},{5,7},{7,5},{8,10},{10,8},{9,1... | collective-permute-start | bytes 196616 | tf_op jit(solution)/shard_map/ppermute | solution.py:876
